TPU v7x, 32 devices: a whole 2x2x4 slice. The times are simulated.
32 devices in a mesh: fx: 2 (over x), fy: 4 (over z), fz: 4 (over y, core).
Axes of the slice: x: 2, y: 2, z: 4, core: 2. Of those that a mesh axis runs over, the one named last changes fastest.
Arguments:
- density: float32 [16, 32, 512], P('fx', 'fy', 'fz'), may hold values from 0.8 to 1.25
- velocity: float32 [3, 16, 32, 512], P(None, 'fx', 'fy', 'fz'), may hold values from -2 to 2
- pressure: float32 [16, 32, 512], P('fx', 'fy', 'fz'), may hold values from 0.7 to 1.4
- acoustic: float32 [512, 4, 512], P(('fx', 'fy', 'fz')), may hold values from -6 to 6
- sound_speed: float32 [512], P(('fx', 'fy', 'fz')), may hold values from 0.5 to 2
- derivative: float32 [8, 8], replicated, may hold values from -2 to 2
- mode_basis: float32 [8, 8], replicated, may hold values from -2 to 2
- neighbours: int32 [512, 6], P(('fx', 'fy', 'fz')), may hold values from 0 to 511, as said below
- block_owner: int32 [2, 4, 4, 16, 1], P('fx', 'fy', 'fz'), may hold values from 0 to 3; in each aligned block of 16 rows (0 to 15, 16 to 31, ..., all dimensions but the last counted through in order) at most 8 rows name the same one
- block_element: int32 [2, 4, 4, 16], P('fx', 'fy', 'fz'), may hold values from 0 to 15
Outputs:
- flow_state: float32 [5, 16, 32, 512], P(None, 'fx', 'fy', 'fz')
- sound_state: float32 [512, 4, 512], P(('fx', 'fy', 'fz'))
Inputs may be any that keep to these rules, and one draw needn't show every extreme that they name: `neighbours`: across faces -x, -y, -z the neighbour of element e lies in e - 16 to e, across faces +x, +y, +z in e to e + 16. `block_owner`: the 16 blocks of one flow device name one fy index at most 8 times.
All inputs are finite; a program needn't handle non-finite values.
Results may differ from a plain program's by a relative error of at most 0.0001.
Values sent between devices are 32-bit elements; how exact they have to be, the bound alone decides.
No kernel may reach another device: no remote copies, remote signals or barrier semaphores. Data moves between devices by JAX's collectives and lax.ppermute only.
A program may use at most 64 MiB of HBM per device.

v0:
```python
import jax
import jax.numpy as jnp
from jax import lax
from jax.sharding import PartitionSpec as P

HEAT_RATIO = 1.4
TIME_STEP = 0.1
VISCOSITY = 0.05
PENALTY = 0.5
HIGHEST = lax.Precision.HIGHEST


def padded_2(cells, sides, width, closed):
    for axis, dim in sides:
        count = lax.axis_size(axis)
        ends = count if closed else count - 1
        head = lax.slice_in_dim(cells, 0, width, axis=dim)
        tail = lax.slice_in_dim(cells, cells.shape[dim] - width, cells.shape[dim], axis=dim)
        cells = jnp.concatenate(
            [
                lax.ppermute(tail, axis, [(i, (i + 1) % count) for i in range(ends)]),
                cells,
                lax.ppermute(head, axis, [((i + 1) % count, i) for i in range(ends)]),
            ],
            axis=dim,
        )
    return cells


def cut_range(values, along, start_at, stop_at):
    return lax.slice_in_dim(values, start_at, stop_at, axis=along + 1)


def interior(padded, along):
    for other in range(3):
        if other != along:
            padded = cut_range(padded, other, 1, padded.shape[other + 1] - 1)
    return padded


def flow_section(padded):
    center = padded[:, 1:-1, 1:-1, 1:-1]
    velocity_mid = center[1:4] / center[0]
    flow_rate = jnp.zeros_like(center)
    laplace = jnp.zeros_like(velocity_mid)
    slopes = []
    for along in range(3):
        stripe = interior(padded, along)
        length = stripe.shape[along + 1]
        velocity_cells = stripe[1:4] / stripe[0]
        pressure_cells = (HEAT_RATIO - 1.0) * (
            stripe[4] - 0.5 * jnp.sum(stripe[1:4] * velocity_cells, 0)
        )
        signal_speed = (
            jnp.abs(velocity_cells[along])
            + jnp.sqrt(HEAT_RATIO * jnp.abs(pressure_cells) / stripe[0])
        )[None]
        unit_axis = (jnp.arange(3) == along).astype(jnp.float32)
        momentum_flux = (
            stripe[1:4] * velocity_cells[along] + unit_axis[:, None, None, None] * pressure_cells
        )
        fluxes = jnp.concatenate(
            [
                stripe[1 + along][None],
                momentum_flux,
                ((stripe[4] + pressure_cells) * velocity_cells[along])[None],
            ],
            0,
        )
        wave_speed = jnp.maximum(
            cut_range(signal_speed, along, 0, length - 1), cut_range(signal_speed, along, 1, length)
        )
        face_flux = 0.5 * (
            cut_range(fluxes, along, 0, length - 1) + cut_range(fluxes, along, 1, length)
        ) - 0.5 * wave_speed * (
            cut_range(stripe, along, 1, length) - cut_range(stripe, along, 0, length - 1)
        )
        flow_rate = flow_rate - (
            cut_range(face_flux, along, 1, length - 1) - cut_range(face_flux, along, 0, length - 2)
        )
        laplace = (
            laplace
            + cut_range(stripe[1:4], along, 2, length)
            + cut_range(stripe[1:4], along, 0, length - 2)
            - 2.0 * center[1:4]
        )
        slopes.append(
            0.5
            * (
                cut_range(velocity_cells, along, 2, length)
                - cut_range(velocity_cells, along, 0, length - 2)
            )
        )
    empty_row = jnp.zeros_like(center[:1])
    flow_rate = flow_rate + VISCOSITY * jnp.concatenate([empty_row, laplace, empty_row], 0)
    vorticity = jnp.stack(
        [slopes[1][2] - slopes[2][1], slopes[2][0] - slopes[0][2], slopes[0][1] - slopes[1][0]]
    )
    lamb_vector = jnp.stack(
        [
            vorticity[1] * velocity_mid[2] - vorticity[2] * velocity_mid[1],
            vorticity[2] * velocity_mid[0] - vorticity[0] * velocity_mid[2],
            vorticity[0] * velocity_mid[1] - vorticity[1] * velocity_mid[0],
        ]
    )
    return (flow_rate, lamb_vector)


def conserved(density, velocity, pressure):
    energy = pressure / (HEAT_RATIO - 1.0) + 0.5 * density * jnp.sum(velocity * velocity, 0)
    return jnp.concatenate([density[None], density[None] * velocity, energy[None]], 0)


def apply_cube(fields, first_matrix, inner_table):
    row_count = fields.shape[0]
    cube = fields.reshape(row_count, 8, 64)
    along_first = jnp.einsum("xa,rab->rxb", first_matrix, cube, precision=HIGHEST).reshape(
        row_count * 8, 64
    )
    return jnp.dot(along_first, inner_table, precision=HIGHEST).reshape(row_count, 512)


def nodal_slopes(fields, derivative):
    row_count = fields.shape[0]
    identity = jnp.eye(8, dtype=jnp.float32)
    slope_y_table = jnp.kron(derivative.T, identity)
    slope_z_table = jnp.kron(identity, derivative.T)
    cube = fields.reshape(row_count, 8, 64)
    slope_x = jnp.einsum("xa,rab->rxb", derivative, cube, precision=HIGHEST).reshape(row_count, 512)
    flat = fields.reshape(row_count * 8, 64)
    slope_y = jnp.dot(flat, slope_y_table, precision=HIGHEST).reshape(row_count, 512)
    slope_z = jnp.dot(flat, slope_z_table, precision=HIGHEST).reshape(row_count, 512)
    return (slope_x, slope_y, slope_z)


def extract(state_now):
    element_count = state_now.shape[0]
    cube = state_now.reshape(element_count, 4, 8, 8, 8)
    surfaces = [
        cube[:, :, 0],
        cube[:, :, 7],
        cube[:, :, :, 0],
        cube[:, :, :, 7],
        cube[:, :, :, :, 0],
        cube[:, :, :, :, 7],
    ]
    return jnp.concatenate([surface.reshape(element_count, 4, 64) for surface in surfaces], 2)


def lift_faces(jumps):
    element_count = jumps.shape[0]
    faces = jumps.reshape(element_count, 4, 6, 8, 8)
    gap_x = jnp.zeros((element_count, 4, 6, 8, 8), jnp.float32)
    gap_y = jnp.zeros((element_count, 4, 8, 6, 8), jnp.float32)
    gap_z = jnp.zeros((element_count, 4, 8, 8, 6), jnp.float32)
    lifted_x = jnp.concatenate([faces[:, :, 0][:, :, None], gap_x, faces[:, :, 1][:, :, None]], 2)
    lifted_y = jnp.concatenate(
        [faces[:, :, 2][:, :, :, None], gap_y, faces[:, :, 3][:, :, :, None]], 3
    )
    lifted_z = jnp.concatenate([faces[:, :, 4][..., None], gap_z, faces[:, :, 5][..., None]], 4)
    return (lifted_x + lifted_y + lifted_z).reshape(element_count, 4, 512)


def face_jumps(own_faces, face_table, neighbour_rows):
    pieces = []
    for facet_index in range(6):
        opposite = facet_index ^ 1
        remote = face_table[:, :, opposite * 64 : (opposite + 1) * 64][
            neighbour_rows[:, facet_index]
        ]
        pieces.append(remote - own_faces[:, :, facet_index * 64 : (facet_index + 1) * 64])
    return jnp.concatenate(pieces, 2)


def acoustic_rate(state_now, jumps, source, sound_speed, derivative):
    element_count = state_now.shape[0]
    slope_x, slope_y, slope_z = nodal_slopes(state_now.reshape(element_count * 4, 512), derivative)
    slope_x = slope_x.reshape(element_count, 4, 512)
    slope_y = slope_y.reshape(element_count, 4, 512)
    slope_z = slope_z.reshape(element_count, 4, 512)
    pressure_gradient = jnp.stack([slope_x[:, 0], slope_y[:, 0], slope_z[:, 0]], 1)
    divergence = slope_x[:, 1] + slope_y[:, 2] + slope_z[:, 3]
    lifted = lift_faces(jumps)
    rate_pressure = -(sound_speed * sound_speed)[:, None] * divergence + PENALTY * lifted[:, 0]
    rate_velocity = -pressure_gradient + source + PENALTY * lifted[:, 1:4]
    return jnp.concatenate([rate_pressure[:, None], rate_velocity], 1)


def project_local(lamb_vector, mode_basis, pair_table):
    cells_x, cells_y, cells_z = (lamb_vector.shape[1], lamb_vector.shape[2], lamb_vector.shape[3])
    blocks = lamb_vector.reshape(3, cells_x // 8, 8, cells_y // 8, 8, cells_z // 8, 8)
    blocks = blocks.transpose(1, 3, 5, 0, 2, 4, 6).reshape(-1, 512)
    return apply_cube(blocks, mode_basis, pair_table).reshape(-1, 1536)


def route(projected, owners, elements_of, element_count):
    peers = lax.axis_size("fy")
    blocks_here = owners.shape[0]
    capacity = max(2, 2 * blocks_here // peers)
    matches = (owners[:, None] == jnp.arange(peers, dtype=jnp.int32)[None, :]).astype(jnp.int32)
    position = jnp.sum((jnp.cumsum(matches, 0) - 1) * matches, 1)
    slot_index = owners * capacity + position
    chooser = jnp.arange(peers * capacity, dtype=jnp.int32)[:, None] == slot_index[None, :]
    packed = jnp.dot(chooser.astype(jnp.float32), projected, precision=HIGHEST).reshape(
        peers, capacity, 1536
    )
    labels = (jnp.sum(jnp.where(chooser, elements_of[None, :] + 1, 0), 1) - 1).reshape(
        peers, capacity
    )
    arrived, arrived_labels = (
        lax.all_to_all(packed, "fy", split_axis=0, concat_axis=0, tiled=True),
        lax.all_to_all(labels, "fy", split_axis=0, concat_axis=0, tiled=True),
    )
    placer = (
        jnp.arange(element_count, dtype=jnp.int32)[:, None] == arrived_labels.reshape(-1)[None, :]
    ).astype(jnp.float32)
    summed = jnp.dot(placer, arrived.reshape(peers * capacity, 1536), precision=HIGHEST)
    return summed.reshape(element_count, 3, 512)


def per_device(
    density,
    velocity,
    pressure,
    acoustic,
    sound_speed,
    derivative,
    mode_basis,
    neighbours,
    block_owner,
    block_element,
):
    pair_table = jnp.kron(mode_basis, mode_basis).T
    element_count = acoustic.shape[0]
    device = lax.axis_index(("fx", "fy", "fz"))
    neighbour_rows = neighbours - (device - 1) * element_count
    owners = block_owner.reshape(-1)
    elements_of = block_element.reshape(-1)

    def section(flow_now, sound_now):
        padded = padded_2(flow_now, (("fx", 1), ("fy", 2), ("fz", 3)), 1, True)
        flow_rate, lamb_vector = flow_section(padded)
        source = route(
            project_local(lamb_vector, mode_basis, pair_table), owners, elements_of, element_count
        )
        wide_state = padded_2(sound_now, ((("fx", "fy", "fz"), 0),), element_count, False)
        face_table = extract(wide_state)
        own_faces = face_table[element_count : 2 * element_count]
        jumps = face_jumps(own_faces, face_table, neighbour_rows)
        return (flow_rate, acoustic_rate(sound_now, jumps, source, sound_speed, derivative))

    flow_start = conserved(density, velocity, pressure)
    rate_one, sound_rate = section(flow_start, acoustic)
    flow_one = flow_start + TIME_STEP * rate_one
    sound_one = acoustic + TIME_STEP * sound_rate
    rate_two, sound_rate = section(flow_one, sound_one)
    flow_two = 0.75 * flow_start + 0.25 * (flow_one + TIME_STEP * rate_two)
    sound_two = 0.75 * acoustic + 0.25 * (sound_one + TIME_STEP * sound_rate)
    rate_three, sound_rate = section(flow_two, sound_two)
    flow_state = 1.0 / 3.0 * flow_start + 2.0 / 3.0 * (flow_two + TIME_STEP * rate_three)
    sound_state = 1.0 / 3.0 * acoustic + 2.0 / 3.0 * (sound_two + TIME_STEP * sound_rate)
    return (flow_state, sound_state)


def solution(mesh):
    placed = (
        P("fx", "fy", "fz"),
        P(None, "fx", "fy", "fz"),
        P("fx", "fy", "fz"),
        P(("fx", "fy", "fz"), None, None),
        P(("fx", "fy", "fz")),
        P(),
        P(),
        P(("fx", "fy", "fz"), None),
        P("fx", "fy", "fz", None, None),
        P("fx", "fy", "fz", None),
    )
    return jax.shard_map(
        per_device,
        mesh=mesh,
        in_specs=placed,
        out_specs=(P(None, "fx", "fy", "fz"), P(("fx", "fy", "fz"), None, None)),
        check_vma=False,
    )
```

profile of v0, /device:TPU:2, one launch (start us, length us, event | category | flops | bytes accessed | tf_op | source)
XLA Modules:
  0.0 192.7 jit_solution(9799342283420970901)
XLA Ops:
  0.7 1.7 copy.253
  2.3 5.9 %collective-permute-start.19 = (f32[16,4,512]{2,0,1:T(8,128)}, f32[16,4,512]{2,0,1:T(8,128)}, u32[]{:S(2)}, u32[]{:S(2)}) collective-permute-start(f32[16,4,512]{2,0,1:T(8,128)} %copy.253), channel_id=1, source_target_pairs={{1,0},{2,1},{3,2},{4,3},{5,4},{6,5},{7,6},{8,7},{9,8},{10,9},{11,1... | collective-permute-start | bytes 393224 | tf_op jit(solution)/shard_map/ppermute | solution.py:23
  8.2 1.9 collective-permute-start.18
  12.7 2.0 %collective-permute-start = (f32[5,1,8,128]{3,2,1,0:T(8,128)S(1)}, f32[5,1,8,128]{3,2,1,0:T(8,128)S(1)}, u32[]{:S(2)}, u32[]{:S(2)}) collective-permute-start(f32[5,1,8,128]{3,2,1,0:T(8,128)S(1)} %get-tuple-element.132), channel_id=1, source_target_pairs={{0,16},{16,0},{1,17},{17,1},{2,18},{18,2},{3,19},{19,3},{4,20},{20... | collective-permute-start | bytes 61448 | tf_op jit(solution)/shard_map/ppermute | solution.py:21
  18.4 3.2 %all-to-all-start = ((s32[4,1,8]{2,1,0:T(1,128)}), s32[4,1,8]{2,1,0:T(1,128)S(1)}, u32[]{:S(2)}, u32[]{:S(2)}) async-start(s32[4,1,8]{2,1,0:T(1,128)} %bitcast.80), calls=%async_computation | async-start | bytes 4096 | tf_op jit(solution)/shard_map/all_to_all | solution.py:212
  34.0 3.8 %collective-permute-start.3 = (f32[5,10,1,128]{3,2,1,0:T(1,128)S(1)}, f32[5,10,1,128]{3,2,1,0:T(1,128)S(1)}, u32[]{:S(2)}, u32[]{:S(2)}) collective-permute-start(f32[5,10,1,128]{3,2,1,0:T(1,128)S(1)} %get-tuple-element.118), channel_id=1, source_target_pairs={{4,0},{8,4},{12,8},{0,12},{5,1},{9,5},{13,9},{1,13},{6,2},{10,6},{... | collective-permute-start | bytes 76808 | tf_op jit(solution)/shard_map/ppermute | solution.py:23
  38.2 1.2 collective-permute-done.3
  39.4 4.1 %collective-permute-done.2 = f32[5,10,1,128]{3,2,1,0:T(1,128)S(1)} collective-permute-done((f32[5,10,1,128]{3,2,1,0:T(1,128)S(1)}, f32[5,10,1,128]{3,2,1,0:T(1,128)S(1)}, u32[]{:S(2)}, u32[]{:S(2)}) %collective-permute-start.2) | collective-permute-done | bytes 25632 | tf_op jit(solution)/shard_map/ppermute | solution.py:21
  44.9 8.7 %collective-permute-done.5 = f32[5,10,10,1]{3,2,1,0:T(8,128)S(1)} collective-permute-done((f32[5,10,10,1]{3,2,1,0:T(8,128)S(1)}, f32[5,10,10,1]{3,2,1,0:T(8,128)S(1)}, u32[]{:S(2)}, u32[]{:S(2)}) %collective-permute-start.5) | collective-permute-done | bytes 2032 | tf_op jit(solution)/shard_map/ppermute | solution.py:23
  57.9 1.9 %collective-permute-start.6 = (f32[5,1,8,128]{3,2,1,0:T(8,128)S(1)}, f32[5,1,8,128]{3,2,1,0:T(8,128)S(1)}, u32[]{:S(2)}, u32[]{:S(2)}) collective-permute-start(f32[5,1,8,128]{3,2,1,0:T(8,128)S(1)} %get-tuple-element.130), channel_id=1, source_target_pairs={{0,16},{16,0},{1,17},{17,1},{2,18},{18,2},{3,19},{19,3},{4,20},{20... | collective-permute-start | bytes 61448 | tf_op jit(solution)/shard_map/ppermute | solution.py:21
  64.4 4.0 %all-to-all-start.1 = ((f32[4,8,1536]{2,1,0:T(8,128)}), f32[4,8,1536]{2,1,0:T(8,128)}, u32[]{:S(2)}, u32[]{:S(2)}) async-start(f32[4,8,1536]{2,1,0:T(8,128)} %fusion.168), calls=%async_computation.1 | async-start | bytes 393216 | tf_op jit(solution)/shard_map/all_to_all | solution.py:211
  68.5 3.8 %collective-permute-start.9 = (f32[5,10,1,128]{3,2,1,0:T(1,128)S(1)}, f32[5,10,1,128]{3,2,1,0:T(1,128)S(1)}, u32[]{:S(2)}, u32[]{:S(2)}) collective-permute-start(f32[5,10,1,128]{3,2,1,0:T(1,128)S(1)} %get-tuple-element.113), channel_id=1, source_target_pairs={{4,0},{8,4},{12,8},{0,12},{5,1},{9,5},{13,9},{1,13},{6,2},{10,6},{... | collective-permute-start | bytes 76808 | tf_op jit(solution)/shard_map/ppermute | solution.py:23
  72.6 1.2 collective-permute-done.9
  73.9 4.1 %collective-permute-done.8 = f32[5,10,1,128]{3,2,1,0:T(1,128)S(1)} collective-permute-done((f32[5,10,1,128]{3,2,1,0:T(1,128)S(1)}, f32[5,10,1,128]{3,2,1,0:T(1,128)S(1)}, u32[]{:S(2)}, u32[]{:S(2)}) %collective-permute-start.8) | collective-permute-done | bytes 25632 | tf_op jit(solution)/shard_map/ppermute | solution.py:21
  78.3 1.7 collective-permute-start.11
  80.6 8.0 %collective-permute-done.10 = f32[5,10,10,1]{3,2,1,0:T(8,128)S(1)} collective-permute-done((f32[5,10,10,1]{3,2,1,0:T(8,128)S(1)}, f32[5,10,10,1]{3,2,1,0:T(8,128)S(1)}, u32[]{:S(2)}, u32[]{:S(2)}) %collective-permute-start.10) | collective-permute-done | bytes 2032 | tf_op jit(solution)/shard_map/ppermute | solution.py:21
  90.7 1.9 %collective-permute-start.12 = (f32[5,1,8,128]{3,2,1,0:T(8,128)S(1)}, f32[5,1,8,128]{3,2,1,0:T(8,128)S(1)}, u32[]{:S(2)}, u32[]{:S(2)}) collective-permute-start(f32[5,1,8,128]{3,2,1,0:T(8,128)S(1)} %get-tuple-element.128), channel_id=1, source_target_pairs={{0,16},{16,0},{1,17},{17,1},{2,18},{18,2},{3,19},{19,3},{4,20},{20... | collective-permute-start | bytes 61448 | tf_op jit(solution)/shard_map/ppermute | solution.py:21
  97.8 1.9 collective-permute-start.14
  100.0 2.2 %copy.266 = f32[16,4,512]{0,2,1:T(8,128)} copy(f32[16,4,512]{2,0,1:T(8,128)} %collective-permute-done.19) | data formatting | bytes 262144 | tf_op jit(solution)/shard_map/ppermute | solution.py:23
  102.3 2.2 %copy.264 = f32[16,4,512]{0,2,1:T(8,128)} copy(f32[16,4,512]{2,0,1:T(8,128)} %collective-permute-done.18) | data formatting | bytes 262144 | tf_op jit(solution)/shard_map/ppermute | solution.py:21
  104.5 2.1 %pad_maximum_fusion = f32[48,4,512]{0,2,1:T(8,128)S(1)} fusion(f32[16,4,512]{0,2,1:T(8,128)} %copy.266, f32[16,4,512]{0,2,1:T(8,128)S(1)} %copy.265, f32[16,4,512]{0,2,1:T(8,128)} %copy.264), kind=kLoop, calls=%fused_computation.35 | loop fusion | flops 196608 | bytes 786432 | tf_op jit(solution)/shard_map/concatenate | solution.py:19
  115.5 1.7 collective-permute-start.17
  118.4 7.2 %collective-permute-done.16 = f32[5,10,10,1]{3,2,1,0:T(8,128)S(1)} collective-permute-done((f32[5,10,10,1]{3,2,1,0:T(8,128)S(1)}, f32[5,10,10,1]{3,2,1,0:T(8,128)S(1)}, u32[]{:S(2)}, u32[]{:S(2)}) %collective-permute-start.16) | collective-permute-done | bytes 2032 | tf_op jit(solution)/shard_map/ppermute | solution.py:21
  131.2 1.2 convolution_bitcast_fusion.3
  136.7 3.4 %all-to-all-start.2 = ((f32[4,8,1536]{2,1,0:T(8,128)}), f32[4,8,1536]{2,1,0:T(8,128)S(1)}, u32[]{:S(2)}, u32[]{:S(2)}) async-start(f32[4,8,1536]{2,1,0:T(8,128)} %fusion.166), calls=%async_computation.2 | async-start | bytes 393216 | tf_op jit(solution)/shard_map/all_to_all | solution.py:211
  142.4 6.3 %collective-permute-start.21 = (f32[16,4,512]{2,0,1:T(8,128)S(1)}, f32[16,4,512]{2,0,1:T(8,128)S(1)}, u32[]{:S(2)}, u32[]{:S(2)}) collective-permute-start(f32[16,4,512]{2,0,1:T(8,128)S(1)} %fusion.92), channel_id=1, source_target_pairs={{1,0},{2,1},{3,2},{4,3},{5,4},{6,5},{7,6},{8,7},{9,8},{10,9},{11,1... | collective-permute-start | bytes 393224 | tf_op jit(solution)/shard_map/ppermute | solution.py:23
  148.7 1.9 collective-permute-start.20
  151.6 7.0 %collective-permute-done.20 = f32[16,4,512]{2,0,1:T(8,128)S(1)} collective-permute-done((f32[16,4,512]{2,0,1:T(8,128)S(1)}, f32[16,4,512]{2,0,1:T(8,128)S(1)}, u32[]{:S(2)}, u32[]{:S(2)}) %collective-permute-start.20) | collective-permute-done | bytes 131104 | tf_op jit(solution)/shard_map/ppermute | solution.py:21
  166.7 3.4 %all-to-all-start.3 = ((f32[4,8,1536]{2,1,0:T(8,128)}), f32[4,8,1536]{2,1,0:T(8,128)S(1)}, u32[]{:S(2)}, u32[]{:S(2)}) async-start(f32[4,8,1536]{2,1,0:T(8,128)} %fusion.164), calls=%async_computation.3 | async-start | bytes 393216 | tf_op jit(solution)/shard_map/all_to_all | solution.py:211
  171.5 2.4 %collective-permute-start.23 = (f32[16,4,512]{2,0,1:T(8,128)S(1)}, f32[16,4,512]{2,0,1:T(8,128)S(1)}, u32[]{:S(2)}, u32[]{:S(2)}) collective-permute-start(f32[16,4,512]{2,0,1:T(8,128)S(1)} %fusion.95), channel_id=1, source_target_pairs={{1,0},{2,1},{3,2},{4,3},{5,4},{6,5},{7,6},{8,7},{9,8},{10,9},{11,1... | collective-permute-start | bytes 393224 | tf_op jit(solution)/shard_map/ppermute | solution.py:23
  173.9 2.2 %collective-permute-start.22 = (f32[16,4,512]{2,0,1:T(8,128)S(1)}, f32[16,4,512]{2,0,1:T(8,128)S(1)}, u32[]{:S(2)}, u32[]{:S(2)}) collective-permute-start(f32[16,4,512]{2,0,1:T(8,128)S(1)} %fusion.95), channel_id=1, source_target_pairs={{0,1},{1,2},{2,3},{3,4},{4,5},{5,6},{6,7},{7,8},{8,9},{9,10},{10,1... | collective-permute-start | bytes 393224 | tf_op jit(solution)/shard_map/ppermute | solution.py:21
  177.1 6.7 %collective-permute-done.22 = f32[16,4,512]{2,0,1:T(8,128)S(1)} collective-permute-done((f32[16,4,512]{2,0,1:T(8,128)S(1)}, f32[16,4,512]{2,0,1:T(8,128)S(1)}, u32[]{:S(2)}, u32[]{:S(2)}) %collective-permute-start.22) | collective-permute-done | bytes 131104 | tf_op jit(solution)/shard_map/ppermute | solution.py:21
  (412 shorter events, 78.8 us)
Async XLA Ops:
  0.6 22.3 %copy-start.15 = (f32[8,8]{1,0:T(8,128)S(1)}, f32[8,8]{1,0:T(8,128)}, u32[]{:S(2)}) copy-start(f32[8,8]{1,0:T(8,128)} %param.16) | copy-start | bytes 772
  0.7 22.4 %copy-start.16 = (f32[8,8]{1,0:T(8,128)S(1)}, f32[8,8]{1,0:T(8,128)}, u32[]{:S(2)}) copy-start(f32[8,8]{1,0:T(8,128)} %param.15) | copy-start | bytes 772
  2.3 97.7 %collective-permute-start.19 = (f32[16,4,512]{2,0,1:T(8,128)}, f32[16,4,512]{2,0,1:T(8,128)}, u32[]{:S(2)}, u32[]{:S(2)}) collective-permute-start(f32[16,4,512]{2,0,1:T(8,128)} %copy.253), channel_id=1, source_target_pairs={{1,0},{2,1},{3,2},{4,3},{5,4},{6,5},{7,6},{8,7},{9,8},{10,9},{11,1... | collective-permute-start | bytes 393224 | tf_op jit(solution)/shard_map/ppermute | solution.py:23
  8.2 94.1 %collective-permute-start.18 = (f32[16,4,512]{2,0,1:T(8,128)}, f32[16,4,512]{2,0,1:T(8,128)}, u32[]{:S(2)}, u32[]{:S(2)}) collective-permute-start(f32[16,4,512]{2,0,1:T(8,128)} %copy.253), channel_id=1, source_target_pairs={{0,1},{1,2},{2,3},{3,4},{4,5},{5,6},{6,7},{7,8},{8,9},{9,10},{10,1... | collective-permute-start | bytes 393224 | tf_op jit(solution)/shard_map/ppermute | solution.py:21
  12.6 21.3 %collective-permute-start.1 = (f32[5,1,8,128]{3,2,1,0:T(8,128)S(1)}, f32[5,1,8,128]{3,2,1,0:T(8,128)S(1)}, u32[]{:S(2)}, u32[]{:S(2)}) collective-permute-start(f32[5,1,8,128]{3,2,1,0:T(8,128)S(1)} %get-tuple-element.133), channel_id=1, source_target_pairs={{16,0},{0,16},{17,1},{1,17},{18,2},{2,18},{19,3},{3,19},{20,4},{4,... | collective-permute-start | bytes 61448 | tf_op jit(solution)/shard_map/ppermute | solution.py:23
  12.7 21.3 %collective-permute-start = (f32[5,1,8,128]{3,2,1,0:T(8,128)S(1)}, f32[5,1,8,128]{3,2,1,0:T(8,128)S(1)}, u32[]{:S(2)}, u32[]{:S(2)}) collective-permute-start(f32[5,1,8,128]{3,2,1,0:T(8,128)S(1)} %get-tuple-element.132), channel_id=1, source_target_pairs={{0,16},{16,0},{1,17},{17,1},{2,18},{18,2},{3,19},{19,3},{4,20},{20... | collective-permute-start | bytes 61448 | tf_op jit(solution)/shard_map/ppermute | solution.py:21
  18.4 13.8 %all-to-all-start = ((s32[4,1,8]{2,1,0:T(1,128)}), s32[4,1,8]{2,1,0:T(1,128)S(1)}, u32[]{:S(2)}, u32[]{:S(2)}) async-start(s32[4,1,8]{2,1,0:T(1,128)} %bitcast.80), calls=%async_computation | async-start | bytes 4096 | tf_op jit(solution)/shard_map/all_to_all | solution.py:212
  21.7 33.7 %copy-start.23 = (f32[3]{0:T(128)}, f32[3]{0:T(128)S(1)}, u32[]{:S(2)}) copy-start(f32[3]{0:T(128)S(1)} %compare_convert_fusion) | copy-start | bytes 40
  21.7 22.8 %copy-start.26 = (f32[3]{0:T(128)}, f32[3]{0:T(128)S(1)}, u32[]{:S(2)}) copy-start(f32[3]{0:T(128)S(1)} %compare_convert_fusion.1) | copy-start | bytes 40
  34.0 5.4 %collective-permute-start.3 = (f32[5,10,1,128]{3,2,1,0:T(1,128)S(1)}, f32[5,10,1,128]{3,2,1,0:T(1,128)S(1)}, u32[]{:S(2)}, u32[]{:S(2)}) collective-permute-start(f32[5,10,1,128]{3,2,1,0:T(1,128)S(1)} %get-tuple-element.118), channel_id=1, source_target_pairs={{4,0},{8,4},{12,8},{0,12},{5,1},{9,5},{13,9},{1,13},{6,2},{10,6},{... | collective-permute-start | bytes 76808 | tf_op jit(solution)/shard_map/ppermute | solution.py:23
  37.9 5.6 %collective-permute-start.2 = (f32[5,10,1,128]{3,2,1,0:T(1,128)S(1)}, f32[5,10,1,128]{3,2,1,0:T(1,128)S(1)}, u32[]{:S(2)}, u32[]{:S(2)}) collective-permute-start(f32[5,10,1,128]{3,2,1,0:T(1,128)S(1)} %get-tuple-element.117), channel_id=1, source_target_pairs={{0,4},{4,8},{8,12},{12,0},{1,5},{5,9},{9,13},{13,1},{2,6},{6,10},{... | collective-permute-start | bytes 76808 | tf_op jit(solution)/shard_map/ppermute | solution.py:21
  43.8 9.8 %collective-permute-start.5 = (f32[5,10,10,1]{3,2,1,0:T(8,128)S(1)}, f32[5,10,10,1]{3,2,1,0:T(8,128)S(1)}, u32[]{:S(2)}, u32[]{:S(2)}) collective-permute-start(f32[5,10,10,1]{3,2,1,0:T(8,128)S(1)} %get-tuple-element.82), channel_id=1, source_target_pairs={{1,0},{2,1},{3,2},{0,3},{5,4},{6,5},{7,6},{4,7},{9,8},{10,9},{11,1... | collective-permute-start | bytes 6008 | tf_op jit(solution)/shard_map/ppermute | solution.py:23
  44.1 10.4 %collective-permute-start.4 = (f32[5,10,10,1]{3,2,1,0:T(8,128)S(1)}, f32[5,10,10,1]{3,2,1,0:T(8,128)S(1)}, u32[]{:S(2)}, u32[]{:S(2)}) collective-permute-start(f32[5,10,10,1]{3,2,1,0:T(8,128)S(1)} %get-tuple-element.83), channel_id=1, source_target_pairs={{0,1},{1,2},{2,3},{3,0},{4,5},{5,6},{6,7},{7,4},{8,9},{9,10},{10,1... | collective-permute-start | bytes 6008 | tf_op jit(solution)/shard_map/ppermute | solution.py:21
  57.8 10.7 %collective-permute-start.7 = (f32[5,1,8,128]{3,2,1,0:T(8,128)}, f32[5,1,8,128]{3,2,1,0:T(8,128)S(1)}, u32[]{:S(2)}, u32[]{:S(2)}) collective-permute-start(f32[5,1,8,128]{3,2,1,0:T(8,128)} %get-tuple-element.131), channel_id=1, source_target_pairs={{16,0},{0,16},{17,1},{1,17},{18,2},{2,18},{19,3},{3,19},{20,4},{4,... | collective-permute-start | bytes 61448 | tf_op jit(solution)/shard_map/ppermute | solution.py:23
  57.9 10.5 %collective-permute-start.6 = (f32[5,1,8,128]{3,2,1,0:T(8,128)S(1)}, f32[5,1,8,128]{3,2,1,0:T(8,128)S(1)}, u32[]{:S(2)}, u32[]{:S(2)}) collective-permute-start(f32[5,1,8,128]{3,2,1,0:T(8,128)S(1)} %get-tuple-element.130), channel_id=1, source_target_pairs={{0,16},{16,0},{1,17},{17,1},{2,18},{18,2},{3,19},{19,3},{4,20},{20... | collective-permute-start | bytes 61448 | tf_op jit(solution)/shard_map/ppermute | solution.py:21
  64.4 72.3 %all-to-all-start.1 = ((f32[4,8,1536]{2,1,0:T(8,128)}), f32[4,8,1536]{2,1,0:T(8,128)}, u32[]{:S(2)}, u32[]{:S(2)}) async-start(f32[4,8,1536]{2,1,0:T(8,128)} %fusion.168), calls=%async_computation.1 | async-start | bytes 393216 | tf_op jit(solution)/shard_map/all_to_all | solution.py:211
  68.5 5.3 %collective-permute-start.9 = (f32[5,10,1,128]{3,2,1,0:T(1,128)S(1)}, f32[5,10,1,128]{3,2,1,0:T(1,128)S(1)}, u32[]{:S(2)}, u32[]{:S(2)}) collective-permute-start(f32[5,10,1,128]{3,2,1,0:T(1,128)S(1)} %get-tuple-element.113), channel_id=1, source_target_pairs={{4,0},{8,4},{12,8},{0,12},{5,1},{9,5},{13,9},{1,13},{6,2},{10,6},{... | collective-permute-start | bytes 76808 | tf_op jit(solution)/shard_map/ppermute | solution.py:23
  72.3 5.6 %collective-permute-start.8 = (f32[5,10,1,128]{3,2,1,0:T(1,128)S(1)}, f32[5,10,1,128]{3,2,1,0:T(1,128)S(1)}, u32[]{:S(2)}, u32[]{:S(2)}) collective-permute-start(f32[5,10,1,128]{3,2,1,0:T(1,128)S(1)} %get-tuple-element.112), channel_id=1, source_target_pairs={{0,4},{4,8},{8,12},{12,0},{1,5},{5,9},{9,13},{13,1},{2,6},{6,10},{... | collective-permute-start | bytes 76808 | tf_op jit(solution)/shard_map/ppermute | solution.py:21
  78.2 10.4 %collective-permute-start.10 = (f32[5,10,10,1]{3,2,1,0:T(8,128)S(1)}, f32[5,10,10,1]{3,2,1,0:T(8,128)S(1)}, u32[]{:S(2)}, u32[]{:S(2)}) collective-permute-start(f32[5,10,10,1]{3,2,1,0:T(8,128)S(1)} %get-tuple-element.81), channel_id=1, source_target_pairs={{0,1},{1,2},{2,3},{3,0},{4,5},{5,6},{6,7},{7,4},{8,9},{9,10},{10,1... | collective-permute-start | bytes 6008 | tf_op jit(solution)/shard_map/ppermute | solution.py:21
  78.3 10.4 %collective-permute-start.11 = (f32[5,10,10,1]{3,2,1,0:T(8,128)S(1)}, f32[5,10,10,1]{3,2,1,0:T(8,128)S(1)}, u32[]{:S(2)}, u32[]{:S(2)}) collective-permute-start(f32[5,10,10,1]{3,2,1,0:T(8,128)S(1)} %get-tuple-element.80), channel_id=1, source_target_pairs={{1,0},{2,1},{3,2},{0,3},{5,4},{6,5},{7,6},{4,7},{9,8},{10,9},{11,1... | collective-permute-start | bytes 6008 | tf_op jit(solution)/shard_map/ppermute | solution.py:23
  90.6 6.5 %collective-permute-start.13 = (f32[5,1,8,128]{3,2,1,0:T(8,128)S(1)}, f32[5,1,8,128]{3,2,1,0:T(8,128)S(1)}, u32[]{:S(2)}, u32[]{:S(2)}) collective-permute-start(f32[5,1,8,128]{3,2,1,0:T(8,128)S(1)} %get-tuple-element.129), channel_id=1, source_target_pairs={{16,0},{0,16},{17,1},{1,17},{18,2},{2,18},{19,3},{3,19},{20,4},{4,... | collective-permute-start | bytes 61448 | tf_op jit(solution)/shard_map/ppermute | solution.py:23
  90.7 6.4 %collective-permute-start.12 = (f32[5,1,8,128]{3,2,1,0:T(8,128)S(1)}, f32[5,1,8,128]{3,2,1,0:T(8,128)S(1)}, u32[]{:S(2)}, u32[]{:S(2)}) collective-permute-start(f32[5,1,8,128]{3,2,1,0:T(8,128)S(1)} %get-tuple-element.128), channel_id=1, source_target_pairs={{0,16},{16,0},{1,17},{17,1},{2,18},{18,2},{3,19},{19,3},{4,20},{20... | collective-permute-start | bytes 61448 | tf_op jit(solution)/shard_map/ppermute | solution.py:21
  97.7 17.4 %collective-permute-start.15 = (f32[5,10,1,128]{3,2,1,0:T(1,128)}, f32[5,10,1,128]{3,2,1,0:T(1,128)S(1)}, u32[]{:S(2)}, u32[]{:S(2)}) collective-permute-start(f32[5,10,1,128]{3,2,1,0:T(1,128)} %get-tuple-element.108), channel_id=1, source_target_pairs={{4,0},{8,4},{12,8},{0,12},{5,1},{9,5},{13,9},{1,13},{6,2},{10,6},{... | collective-permute-start | bytes 76808 | tf_op jit(solution)/shard_map/ppermute | solution.py:23
  97.8 17.3 %collective-permute-start.14 = (f32[5,10,1,128]{3,2,1,0:T(1,128)}, f32[5,10,1,128]{3,2,1,0:T(1,128)S(1)}, u32[]{:S(2)}, u32[]{:S(2)}) collective-permute-start(f32[5,10,1,128]{3,2,1,0:T(1,128)} %get-tuple-element.107), channel_id=1, source_target_pairs={{0,4},{4,8},{8,12},{12,0},{1,5},{5,9},{9,13},{13,1},{2,6},{6,10},{... | collective-permute-start | bytes 76808 | tf_op jit(solution)/shard_map/ppermute | solution.py:21
  115.4 10.2 %collective-permute-start.16 = (f32[5,10,10,1]{3,2,1,0:T(8,128)S(1)}, f32[5,10,10,1]{3,2,1,0:T(8,128)S(1)}, u32[]{:S(2)}, u32[]{:S(2)}) collective-permute-start(f32[5,10,10,1]{3,2,1,0:T(8,128)S(1)} %get-tuple-element.79), channel_id=1, source_target_pairs={{0,1},{1,2},{2,3},{3,0},{4,5},{5,6},{6,7},{7,4},{8,9},{9,10},{10,1... | collective-permute-start | bytes 6008 | tf_op jit(solution)/shard_map/ppermute | solution.py:21
  115.5 10.5 %collective-permute-start.17 = (f32[5,10,10,1]{3,2,1,0:T(8,128)S(1)}, f32[5,10,10,1]{3,2,1,0:T(8,128)S(1)}, u32[]{:S(2)}, u32[]{:S(2)}) collective-permute-start(f32[5,10,10,1]{3,2,1,0:T(8,128)S(1)} %get-tuple-element.78), channel_id=1, source_target_pairs={{1,0},{2,1},{3,2},{0,3},{5,4},{6,5},{7,6},{4,7},{9,8},{10,9},{11,1... | collective-permute-start | bytes 6008 | tf_op jit(solution)/shard_map/ppermute | solution.py:23
  136.7 30.0 %all-to-all-start.2 = ((f32[4,8,1536]{2,1,0:T(8,128)}), f32[4,8,1536]{2,1,0:T(8,128)S(1)}, u32[]{:S(2)}, u32[]{:S(2)}) async-start(f32[4,8,1536]{2,1,0:T(8,128)} %fusion.166), calls=%async_computation.2 | async-start | bytes 393216 | tf_op jit(solution)/shard_map/all_to_all | solution.py:211
  142.4 9.2 %collective-permute-start.21 = (f32[16,4,512]{2,0,1:T(8,128)S(1)}, f32[16,4,512]{2,0,1:T(8,128)S(1)}, u32[]{:S(2)}, u32[]{:S(2)}) collective-permute-start(f32[16,4,512]{2,0,1:T(8,128)S(1)} %fusion.92), channel_id=1, source_target_pairs={{1,0},{2,1},{3,2},{4,3},{5,4},{6,5},{7,6},{8,7},{9,8},{10,9},{11,1... | collective-permute-start | bytes 393224 | tf_op jit(solution)/shard_map/ppermute | solution.py:23
  148.7 9.9 %collective-permute-start.20 = (f32[16,4,512]{2,0,1:T(8,128)S(1)}, f32[16,4,512]{2,0,1:T(8,128)S(1)}, u32[]{:S(2)}, u32[]{:S(2)}) collective-permute-start(f32[16,4,512]{2,0,1:T(8,128)S(1)} %fusion.92), channel_id=1, source_target_pairs={{0,1},{1,2},{2,3},{3,4},{4,5},{5,6},{6,7},{7,8},{8,9},{9,10},{10,1... | collective-permute-start | bytes 393224 | tf_op jit(solution)/shard_map/ppermute | solution.py:21
  166.7 24.9 %all-to-all-start.3 = ((f32[4,8,1536]{2,1,0:T(8,128)}), f32[4,8,1536]{2,1,0:T(8,128)S(1)}, u32[]{:S(2)}, u32[]{:S(2)}) async-start(f32[4,8,1536]{2,1,0:T(8,128)} %fusion.164), calls=%async_computation.3 | async-start | bytes 393216 | tf_op jit(solution)/shard_map/all_to_all | solution.py:211
  171.5 5.6 %collective-permute-start.23 = (f32[16,4,512]{2,0,1:T(8,128)S(1)}, f32[16,4,512]{2,0,1:T(8,128)S(1)}, u32[]{:S(2)}, u32[]{:S(2)}) collective-permute-start(f32[16,4,512]{2,0,1:T(8,128)S(1)} %fusion.95), channel_id=1, source_target_pairs={{1,0},{2,1},{3,2},{4,3},{5,4},{6,5},{7,6},{8,7},{9,8},{10,9},{11,1... | collective-permute-start | bytes 393224 | tf_op jit(solution)/shard_map/ppermute | solution.py:23
  173.9 9.9 %collective-permute-start.22 = (f32[16,4,512]{2,0,1:T(8,128)S(1)}, f32[16,4,512]{2,0,1:T(8,128)S(1)}, u32[]{:S(2)}, u32[]{:S(2)}) collective-permute-start(f32[16,4,512]{2,0,1:T(8,128)S(1)} %fusion.95), channel_id=1, source_target_pairs={{0,1},{1,2},{2,3},{3,4},{4,5},{5,6},{6,7},{7,8},{8,9},{9,10},{10,1... | collective-permute-start | bytes 393224 | tf_op jit(solution)/shard_map/ppermute | solution.py:21
  (28 other events, 106.6 us)
where the time goes:
time: 194 us; the launch traced here: 193 us
  starting transfers between devices  54.6 us (28%)
  waiting for transfers between devices  49.7 us (26%)
  local copies, waits for them, and re-layouts  45.9 us (24%)
  other arithmetic  29.3 us (15%)
  matrix products  10.5 us (5%)
  between operations  2.77 us (1%)
    ppermute x12, waiting for transfers between devices, padded_2(): lax.ppermute(tail, axis, [(i, (i + 1) % count) for i in range(ends)])  38.1 us
    ppermute x12, starting transfers between devices, padded_2(): lax.ppermute(head, axis, [((i + 1) % count, i) for i in range(ends)])  26.4 us
    gather x36, local copies, waits for them, and re-layouts, face_jumps(): face_table[:, :, opposite * 64:(opposite + 1) * 64]  14.5 us
    ppermute x12, starting transfers between devices, padded_2(): lax.ppermute(tail, axis, [(i, (i + 1) % count) for i in range(ends)])  14.3 us
    ppermute x12, waiting for transfers between devices, padded_2(): lax.ppermute(head, axis, [((i + 1) % count, i) for i in range(ends)])  11.6 us
    all_to_all x3, starting transfers between devices, route(): lax.all_to_all(packed, 'fy', split_axis=0, concat_axis=0, tiled=True)  10.7 us
    unnamed x82, local copies, waits for them, and re-layouts  7.42 us
    concatenate x15, other arithmetic, padded_2(): jnp.concatenate([lax.ppermute(tail, axis, [(i, (i + 1) % count) for i in...  3.9 us
  transfers between devices with their start and end apart: 28, of which 12 were waited for; matrix products, arithmetic and copies ran while one was open for 42% of the time, Pallas kernels for 0%

commit v1 on v0

v1 whole, which is shorter than its diff:
```python
import functools

import jax
import jax.numpy as jnp
import numpy as np
from jax import lax
from jax.experimental import pallas as pl
from jax.experimental.pallas import tpu as pltpu
from jax.sharding import PartitionSpec as P

HEAT_RATIO = 1.4
TIME_STEP = 0.1
VISCOSITY = 0.05
PENALTY = 0.5
HALO = 3
F32 = jnp.float32
BF16 = jnp.bfloat16
PARAMS = pltpu.CompilerParams(vmem_limit_bytes=24 * 1024 * 1024)
MIXES = ((0.0, 1.0), (0.75, 0.25), (1.0 / 3.0, 2.0 / 3.0))


def parts(values):
    high = values.astype(BF16)
    return high, (values - high.astype(F32)).astype(BF16)


def dot(left, right):
    return lax.dot_general(left, right, (((1,), (0,)), ((), ())), preferred_element_type=F32)


def dot_three(left, right):
    left_high, left_low = parts(left)
    right_high, right_low = parts(right)
    return dot(left_high, right_high) + dot(left_high, right_low) + dot(left_low, right_high)


def dot_exact_right(left, right):
    left_high, left_low = parts(left)
    return dot(left_high, right) + dot(left_low, right)


def call(body, outs, *operands, scratch=()):
    return pl.pallas_call(
        body,
        out_shape=[jax.ShapeDtypeStruct(shape, F32) for shape in outs],
        in_specs=[pl.BlockSpec(memory_space=pltpu.VMEM)] * len(operands),
        out_specs=[pl.BlockSpec(memory_space=pltpu.VMEM)] * len(outs),
        scratch_shapes=list(scratch),
        compiler_params=PARAMS,
    )(*operands)


def pack_start_body(density, velocity, pressure, state, low, high):
    rho = density[...]
    vel = velocity[...]
    state[0] = rho
    for k in range(3):
        state[1 + k] = rho * vel[k]
    square = vel[0] * vel[0] + vel[1] * vel[1] + vel[2] * vel[2]
    state[4] = pressure[...] / (HEAT_RATIO - 1.0) + 0.5 * rho * square
    rows = state[...].reshape(-1, 128)
    count = rows.shape[0]
    for tile in range(low.shape[0] // 8):
        piece = rows[tile * 128 : min(count, tile * 128 + 128)]
        if piece.shape[0] < 128:
            piece = jnp.concatenate([piece, jnp.zeros((128 - piece.shape[0], 128), F32)], 0)
        turned = piece.T
        low[tile * 8 : tile * 8 + 8] = turned[0:8]
        high[tile * 8 : tile * 8 + 8] = turned[120:128]


def pack_next_body(state, above, below, edge, along_x, y_low, y_high, xy_low, xy_high):
    cells_x = state.shape[1]
    row = lax.broadcasted_iota(jnp.int32, edge.shape, 0) % 8
    both = jnp.where(row < 4, above[...], below[...])
    edge[...] = both
    planes = [cells_x - HALO + i for i in range(HALO)] + list(range(HALO))
    for f in range(5):
        for s, x in enumerate(planes):
            at = (f * len(planes) + s) * 8
            along_x[at : at + 8] = state[f, x]
            at = (f * len(planes) + s) * HALO
            xy_low[at : at + HALO] = state[f, x, 0:HALO]
            xy_high[at : at + HALO] = state[f, x, 8 - HALO : 8]
        for x in range(cells_x):
            at = (f * cells_x + x) * HALO
            y_low[at : at + HALO] = state[f, x, 0:HALO]
            y_high[at : at + HALO] = state[f, x, 8 - HALO : 8]
    for message in (along_x, y_low, y_high, xy_low, xy_high):
        size = message.shape[0]
        message[size - edge.shape[0] : size] = both


def turned_edges(message):
    size = message.shape[0]
    rows = []
    for tile in range(3):
        piece = message[size - 24 + tile * 8 : size - 16 + tile * 8]
        rows.append(jnp.concatenate([piece, jnp.zeros((112, 128), F32), piece], 0).T)
    return rows


def assemble(wide, state, edge, beside, cells_x):
    six = 2 * HALO
    for dx, dy, message in [(0, 0, edge)] + beside:
        turned = turned_edges(message)
        if dx == 0:
            columns = [(HALO + x, x, x) for x in range(cells_x)]
        elif dx < 0:
            columns = [(i, cells_x - HALO + i, i) for i in range(HALO)]
        else:
            columns = [(HALO + cells_x + i, i, HALO + i) for i in range(HALO)]
        slots = cells_x if dx == 0 else six
        target = {0: (0, 8), 1: (8, 8 + HALO), -1: (16 - HALO, 16)}[dy]
        source = {0: (0, 8), 1: (0, HALO), -1: (8 - HALO, 8)}[dy]
        height = target[1] - target[0]
        for f in range(5):
            for plane, x, slot in columns:
                if dx == 0 and dy == 0:
                    wide[f, plane, 0:8, 0:128] = state[f, x]
                else:
                    at = (f * slots + slot) * height
                    wide[f, plane, target[0] : target[1], 0:128] = message[at : at + height]
                group = f * cells_x + x
                block = turned[group // 16][(group % 16) * 8 : (group % 16) * 8 + 8]
                wide[f, plane, target[0] : target[1], 128:256] = block[source[0] : source[1]]


def flow_rate_section(wide, derived, start, offset, mix, write):
    depth = wide.shape[1]

    def derive(i, _):
        rho, mx, my, mz, energy = [wide[f, i] for f in range(5)]
        inverse = 1.0 / rho
        u, v, w = mx * inverse, my * inverse, mz * inverse
        p = (HEAT_RATIO - 1.0) * (energy - 0.5 * (mx * u + my * v + mz * w))
        derived[0, i] = u
        derived[1, i] = v
        derived[2, i] = w
        derived[3, i] = p
        derived[4, i] = jnp.sqrt(HEAT_RATIO * jnp.abs(p) * inverse)
        return 0

    lax.fori_loop(0, depth, derive, 0)

    def flux(fields, other, along):
        speed, p = other[along], other[3]
        out = [fields[1 + along]]
        for k in range(3):
            value = fields[1 + k] * speed
            out.append(value + p if k == along else value)
        out.append((fields[4] + p) * speed)
        return out, jnp.abs(speed) + other[4]

    def face(left, right):
        (fields_l, flux_l, speed_l), (fields_r, flux_r, speed_r) = left, right
        speed = jnp.maximum(speed_l, speed_r)
        viscous = speed + 2.0 * VISCOSITY
        return [
            (flux_l[f] + flux_r[f])
            - (viscous if 1 <= f <= 3 else speed) * (fields_r[f] - fields_l[f])
            for f in range(5)
        ]

    def plane(i, along):
        fields = [wide[f, i] for f in range(5)]
        other = [derived[f, i] for f in range(5)]
        return (fields,) + flux(fields, other, along)

    def section(i, before):
        here = plane(i, 0)
        ahead = face(here, plane(i + 1, 0))
        total = [ahead[f] - before[f] for f in range(5)]
        for along, axis, size in ((1, 0, 16), (2, 1, 256)):
            here = plane(i, along)
            moved = (
                [pltpu.roll(a, size - 1, axis) for a in here[0]],
                [pltpu.roll(a, size - 1, axis) for a in here[1]],
                pltpu.roll(here[2], size - 1, axis),
            )
            faces = face(here, moved)
            for f in range(5):
                total[f] = total[f] + (faces[f] - pltpu.roll(faces[f], 1, axis))
        for f in range(5):
            value = wide[f, i] - (0.5 * TIME_STEP) * total[f]
            if mix[0] != 0.0:
                value = mix[0] * start[f, i + offset] + mix[1] * value
            write(i - 1, f, value)
        return tuple(ahead)

    lax.fori_loop(1, depth - 1, section, tuple(face(plane(0, 0), plane(1, 0))))


def lamb(derived, first, cells_x, lamb_rows):
    def one(x, _):
        i = first + x
        slopes = []
        slopes.append([derived[c, i + 1, 0:8, 0:128] - derived[c, i - 1, 0:8, 0:128] for c in range(3)])
        columns = [derived[c, i, :, 0:128] for c in range(3)]
        slopes.append([(pltpu.roll(a, 15, 0) - pltpu.roll(a, 1, 0))[0:8] for a in columns])
        rows = [derived[c, i, 0:8, :] for c in range(3)]
        slopes.append([(pltpu.roll(a, 255, 1) - pltpu.roll(a, 1, 1))[:, 0:128] for a in rows])
        vel = [derived[c, i, 0:8, 0:128] for c in range(3)]
        curl = [
            0.5 * (slopes[1][2] - slopes[2][1]),
            0.5 * (slopes[2][0] - slopes[0][2]),
            0.5 * (slopes[0][1] - slopes[1][0]),
        ]
        at = pl.multiple_of(x * 8, 8)
        lamb_rows[0, pl.ds(at, 8), :] = curl[1] * vel[2] - curl[2] * vel[1]
        lamb_rows[1, pl.ds(at, 8), :] = curl[2] * vel[0] - curl[0] * vel[2]
        lamb_rows[2, pl.ds(at, 8), :] = curl[0] * vel[1] - curl[1] * vel[0]
        return 0

    lax.fori_loop(0, cells_x, one, 0)


def project(lamb_rows, pair, spread, labels, send):
    peers = send.shape[0]
    fold = send.shape[1] // 24 - 0
    fold = 192 // (send.shape[1] - 8)
    group = lax.broadcasted_iota(jnp.int32, (64 // fold, 128), 1) // (128 // fold)
    height = 64 // fold
    for c in range(3):
        modes = dot_three(pair[...], lamb_rows[c])
        sent = dot_three(modes, spread[...])
        for peer in range(peers):
            mine = sent[:, peer * 128 : peer * 128 + 128]
            folded = mine[0:height]
            for g in range(1, fold):
                folded = jnp.where(group == g, mine[g * height : g * height + height], folded)
            send[peer, c * height : c * height + height] = folded
    send[:, 3 * height : 3 * height + 8] = labels[...]


def flow_first_body(places, *refs):
    state, edge = refs[0:2]
    messages = refs[2 : 2 + len(places)]
    pair, spread, labels = refs[2 + len(places) : 5 + len(places)]
    wide, out, send, derived, lamb_rows = refs[5 + len(places) :]
    cells_x = state.shape[1]
    beside = []
    for message, spots in zip(messages, places):
        beside.extend((dx, dy, message) for dx, dy in spots)
    assemble(wide, state, edge, beside, cells_x)

    def write(i, f, value):
        out[f, i] = value

    flow_rate_section(wide, derived, wide, 0, MIXES[0], write)
    lamb(derived, HALO, cells_x, lamb_rows)
    project(lamb_rows, pair, spread, labels, send)


def flow_second_body(wide, start, pair, spread, labels, out, send, derived, lamb_rows):
    def write(i, f, value):
        out[f, i] = value

    flow_rate_section(wide, derived, start, 1, MIXES[1], write)
    lamb(derived, HALO - 1, wide.shape[1] - 2 * (HALO - 1), lamb_rows)
    project(lamb_rows, pair, spread, labels, send)


def flow_third_body(wide, start, pair, spread, labels, out, send, derived, lamb_rows):
    def write(i, f, value):
        out[f, i] = value[0:8, 0:128]

    flow_rate_section(wide, derived, start, 2, MIXES[2], write)
    lamb(derived, HALO - 2, wide.shape[1] - 2 * (HALO - 2), lamb_rows)
    project(lamb_rows, pair, spread, labels, send)


def faces_out(state, rear, front):
    lane = lax.broadcasted_iota(jnp.int32, (32, 128), 1) // 16
    for c in range(4):
        front[c * 8 : c * 8 + 8] = state[c, 56:64]
        rear[c * 8 : c * 8 + 8] = state[c, 0:8]
        front[32 + c * 8 : 40 + c * 8] = state[c, pl.ds(7, 8, stride=8), :]
        rear[32 + c * 8 : 40 + c * 8] = state[c, pl.ds(0, 8, stride=8), :]
    rows = state[...].reshape(256, 128)
    last = jnp.zeros((32, 128), F32)
    first = jnp.zeros((32, 128), F32)
    for j in range(8):
        piece = rows[j * 32 : j * 32 + 32]
        last = jnp.where(lane == j, pltpu.roll(piece, (j * 16 + 16) % 128, 1), last)
        first = jnp.where(lane == j, pltpu.roll(piece, j * 16, 1) if j else piece, first)
    front[64:96] = last
    rear[64:96] = first


def lift(total, before, after, sides, factor):
    def place(face, rows, target):
        value = factor * dot_exact_right(rows, sides[face])
        for c in range(4):
            total[c, target, :] += value[c * 8 : c * 8 + 8]

    place(0, before[0:32], pl.ds(0, 8))
    place(1, after[0:32], pl.ds(56, 8))
    place(2, before[32:64], pl.ds(0, 8, stride=8))
    place(3, after[32:64], pl.ds(7, 8, stride=8))


def rate_local(state, deriv_rows, deriv_lanes, speed, sides):
    fields = [state[c] for c in range(4)]
    by_rows = dot_three(deriv_rows[...], jnp.concatenate(fields[0:3], 1))
    by_lanes = dot_three(jnp.concatenate([fields[0], fields[3]], 0), deriv_lanes[...])
    divergence = by_rows[0:64, 128:256] + by_rows[64:128, 256:384] + by_lanes[64:128]
    rates = [
        -(speed[...] * speed[...]) * divergence,
        -by_rows[0:64, 0:128],
        -by_rows[64:128, 0:128],
        -by_lanes[0:64],
    ]
    row = lax.broadcasted_iota(jnp.int32, (64, 128), 0)
    lane = lax.broadcasted_iota(jnp.int32, (64, 128), 1)
    count = jnp.zeros((64, 128), F32)
    for value in (row // 8, row % 8, lane // 16):
        count = count + jnp.where((value == 0) | (value == 7), PENALTY, 0.0)
    side = PENALTY * dot_exact_right(state[...].reshape(256, 128), sides[4])
    return [rates[c] - count * fields[c] + side[c * 64 : c * 64 + 64] for c in range(4)]


def acoustic_local_body(mix, has_source, *refs):
    if has_source:
        state, start, source, deriv_rows, deriv_lanes, speed, sides, out, front, rear = refs
    else:
        state, deriv_rows, deriv_lanes, speed, sides, out, front, rear = refs
    rates = rate_local(state, deriv_rows, deriv_lanes, speed, sides)
    for c in range(4):
        rate = rates[c]
        if has_source and c > 0:
            rate = rate + source[c - 1]
        value = state[c] + TIME_STEP * rate
        if mix[0] != 0.0:
            value = mix[0] * start[c] + mix[1] * value
        out[c] = value
    faces_out(state, rear, front)
    lift(out, front, rear, sides, TIME_STEP * mix[1] * PENALTY)


def acoustic_first_body(state, deriv_rows, deriv_lanes, speed, sides, out, front, rear):
    acoustic_local_body(MIXES[0], False, state, deriv_rows, deriv_lanes, speed, sides, out, front, rear)


def remote_part(out, before, after, sides_far, factor):
    lift(out, before, after, sides_far, factor)
    lane = lax.broadcasted_iota(jnp.int32, (32, 128), 1) // 16
    last, first = before[64:96], after[64:96]
    pieces = []
    for j in range(8):
        left = pltpu.roll(last, 128 - j * 16, 1) if j else last
        right = pltpu.roll(first, (144 - j * 16) % 128, 1) if j != 1 else first
        pieces.append(jnp.where(lane == 0, left, jnp.where(lane == 1, right, 0.0)))
    value = factor * dot_exact_right(jnp.concatenate(pieces, 0), sides_far[4])
    for c in range(4):
        out[c] += value[c * 64 : c * 64 + 64]


def acoustic_far_body(factor, has_source, last, *refs):
    refs = list(refs)
    partial, before, after, sides_far = refs[0:4]
    refs = refs[4:]
    if has_source:
        source = refs.pop(0)
    out = refs[0]
    out[...] = partial[...]
    remote_part(out, before, after, sides_far, factor)
    if has_source:
        for c in range(3):
            out[1 + c] += TIME_STEP * source[c]
    if not last:
        faces_out(out, refs[2], refs[1])


def place_body(received, out):
    peers, size = received.shape[0], received.shape[1]
    fold = 192 // (size - 8)
    height = 64 // fold
    target = lax.broadcasted_iota(jnp.int32, (128, 128), 0)
    lane = lax.broadcasted_iota(jnp.int32, (128, 128), 1)
    total = None
    for peer in range(peers):
        label = received[peer, size - 8 : size - 7, :]
        label = jnp.broadcast_to(label, (128, 128)).astype(jnp.int32)
        hit = (label == target % 16) & (lane % 8 == target // 16)
        chosen = [jnp.where(hit & (lane // (128 // fold) == g), 1.0, 0.0) for g in range(fold)]
        chosen = jnp.concatenate(chosen, 0).astype(BF16)
        high, low = parts(received[peer, 0 : size - 8])
        dims = (((1,), (1,)), ((), ()))
        value = lax.dot_general(high, chosen, dims, preferred_element_type=F32)
        value = value + lax.dot_general(low, chosen, dims, preferred_element_type=F32)
        total = value if total is None else total + value
    for c in range(3):
        for g in range(fold):
            out[c, g * height : g * height + height] = total[
                c * height : c * height + height, g * 128 : g * 128 + 128
            ]


def routing_tables(mode_basis, owners, elements, peers):
    blocks = owners.shape[0]
    capacity = max(2, 2 * blocks // peers)
    matches = (owners[:, None] == jnp.arange(peers, dtype=jnp.int32)[None, :]).astype(jnp.int32)
    order = jnp.tril(jnp.ones((blocks, blocks), jnp.int32), -1)
    before = jnp.sum(order[:, :, None] * matches[None, :, :], 1)
    position = jnp.sum(before * matches, 1)
    slot = owners * capacity + position
    chooser = jnp.arange(peers * capacity, dtype=jnp.int32)[None, :] == slot[:, None]
    labels = (jnp.sum(jnp.where(chooser, elements[:, None] + 1, 0), 0) - 1).reshape(peers, capacity)
    fold = 128 // (8 * capacity)
    spread = chooser.astype(F32)[:, None, :, None] * mode_basis.T[None, :, None, :]
    spread = spread.reshape(blocks * 8, peers, 1, capacity * 8)
    spread = jnp.broadcast_to(spread, (blocks * 8, peers, fold, capacity * 8))
    spread = spread.reshape(blocks * 8, peers * 128)
    lanes = jnp.broadcast_to(labels[:, None, :, None], (peers, fold, capacity, 8)).reshape(peers, 1, 128)
    return spread, jnp.broadcast_to(lanes, (peers, 8, 128)).astype(F32), fold


def side_tables(local):
    count = local.shape[0]
    element = jnp.arange(count, dtype=jnp.int32)
    eye = jnp.eye(8, dtype=jnp.int32)
    near, far = [], []
    for facet in range(6):
        wanted = local[:, facet][None, :]
        shift = -count if facet % 2 == 0 else count
        near.append((element[:, None] == wanted).astype(jnp.int32))
        far.append((element[:, None] + shift == wanted).astype(jnp.int32))
    first, last = np.zeros((8, 8), np.int32), np.zeros((8, 8), np.int32)
    first[7, 0] = 1
    last[0, 7] = 1

    def cross(levels, chooser):
        return (levels[:, None, :, None] * chooser[None, :, None, :]).reshape(8 * count, 8 * count)

    near_out = [cross(eye, near[f]) for f in range(4)]
    near_out.append(cross(jnp.asarray(first), near[4]) + cross(jnp.asarray(last), near[5]))
    far_out = [cross(eye, far[f]) for f in range(4)]
    put_first, put_last = np.zeros((8, 8), np.int32), np.zeros((8, 8), np.int32)
    put_first[0, 0] = 1
    put_last[1, 7] = 1
    far_out.append(cross(jnp.asarray(put_first), far[4]) + cross(jnp.asarray(put_last), far[5]))
    return jnp.stack(near_out).astype(BF16), jnp.stack(far_out).astype(BF16)


def shifted(sizes, shifts):
    pairs = []
    for index in np.ndindex(*sizes):
        source = [(i + s) % n for i, s, n in zip(index, shifts, sizes)]
        pairs.append((int(np.ravel_multi_index(source, sizes)), int(np.ravel_multi_index(index, sizes))))
    return pairs


def per_device(
    density,
    velocity,
    pressure,
    acoustic,
    sound_speed,
    derivative,
    mode_basis,
    neighbours,
    block_owner,
    block_element,
):
    size_x, size_y, size_z = lax.axis_size("fx"), lax.axis_size("fy"), lax.axis_size("fz")
    devices = size_x * size_y * size_z
    cells_x = density.shape[0]
    elements = acoustic.shape[0]
    device = lax.axis_index(("fx", "fy", "fz"))

    rows = 5 * cells_x * 8
    tiles = -(-rows // 128)
    state, low, high = call(
        pack_start_body,
        [(5, cells_x, 8, 128), (tiles * 8, 128), (tiles * 8, 128)],
        density,
        velocity,
        pressure,
    )
    above = lax.ppermute(low, "fz", shifted((size_z,), (1,)))
    below = lax.ppermute(high, "fz", shifted((size_z,), (-1,)))

    sound = acoustic.reshape(elements, 4, 64, 8).transpose(1, 2, 3, 0).reshape(4, 64, 8 * elements)
    local = neighbours - device * elements
    near, far = side_tables(local)
    eye = jnp.eye(8, dtype=F32)
    deriv_rows = jnp.concatenate([jnp.kron(derivative, eye), jnp.kron(eye, derivative)], 0)
    deriv_lanes = jnp.kron(derivative.T, jnp.eye(elements, dtype=F32))
    speed = jnp.tile(sound_speed, 8)[None, :]
    forward = [(i, i + 1) for i in range(devices - 1)]
    backward = [(i + 1, i) for i in range(devices - 1)]
    names = ("fx", "fy", "fz")

    def traces(front, rear):
        return lax.ppermute(front, names, forward), lax.ppermute(rear, names, backward)

    partial, front, rear = call(
        acoustic_first_body,
        [(4, 64, 128), (96, 128), (96, 128)],
        sound,
        deriv_rows,
        deriv_lanes,
        speed,
        near,
    )
    before, after = traces(front, rear)

    six = 2 * HALO
    tall = 5 * six * HALO
    tall = -(-tall // 8) * 8
    edge_rows = tiles * 8
    edge, along_x, y_low, y_high, xy_low, xy_high = call(
        pack_next_body,
        [
            (edge_rows, 128),
            (5 * six * 8 + edge_rows, 128),
            (5 * cells_x * HALO + edge_rows, 128),
            (5 * cells_x * HALO + edge_rows, 128),
            (tall + edge_rows, 128),
            (tall + edge_rows, 128),
        ],
        state,
        above,
        below,
    )
    flat = (size_x, size_y)
    steps = [[(1, 0), (-1, 0)]] if size_x == 2 else [[(1, 0)], [(-1, 0)]]
    places, messages = [], []
    for spots in steps:
        messages.append(lax.ppermute(along_x, ("fx", "fy"), shifted(flat, spots[0])))
        places.append(tuple(spots))
    for dy, kept in ((1, y_low), (-1, y_high)):
        messages.append(lax.ppermute(kept, ("fx", "fy"), shifted(flat, (0, dy))))
        places.append(((0, dy),))
    for dy, kept in ((1, xy_low), (-1, xy_high)):
        for spots in steps:
            messages.append(lax.ppermute(kept, ("fx", "fy"), shifted(flat, (spots[0][0], dy))))
            places.append(tuple((dx, dy) for dx, _ in spots))

    spread, labels, fold = routing_tables(
        mode_basis, block_owner.reshape(-1), block_element.reshape(-1), size_y
    )
    pair = jnp.kron(mode_basis, mode_basis)
    sent_shape = (size_y, 192 // fold + 8, 128)

    def scratch(planes):
        return [pltpu.VMEM((5, planes, 16, 256), F32), pltpu.VMEM((3, 64, 128), F32)]

    def route(send):
        got = lax.all_to_all(send, "fy", split_axis=0, concat_axis=0, tiled=True)
        return call(place_body, [(3, 64, 128)], got)[0]

    wide = cells_x + 2 * HALO
    start, flow_one, send = call(
        functools.partial(flow_first_body, tuple(places)),
        [(5, wide, 16, 256), (5, wide - 2, 16, 256), sent_shape],
        state,
        edge,
        *messages,
        pair,
        spread,
        labels,
        scratch=scratch(wide),
    )
    source = route(send)

    factors = [TIME_STEP * mix[1] * PENALTY for mix in MIXES]
    sound_one, front, rear = call(
        functools.partial(acoustic_far_body, factors[0], True, False),
        [(4, 64, 128), (96, 128), (96, 128)],
        partial,
        before,
        after,
        far,
        source,
    )
    before, after = traces(front, rear)

    flow_two, send = call(
        flow_second_body,
        [(5, wide - 4, 16, 256), sent_shape],
        flow_one,
        start,
        pair,
        spread,
        labels,
        scratch=scratch(wide - 2),
    )
    source = route(send)
    partial, _, _ = call(
        functools.partial(acoustic_local_body, MIXES[1], True),
        [(4, 64, 128), (96, 128), (96, 128)],
        sound_one,
        sound,
        source,
        deriv_rows,
        deriv_lanes,
        speed,
        near,
    )
    sound_two, front, rear = call(
        functools.partial(acoustic_far_body, factors[1], False, False),
        [(4, 64, 128), (96, 128), (96, 128)],
        partial,
        before,
        after,
        far,
    )
    before, after = traces(front, rear)

    flow_state, send = call(
        flow_third_body,
        [(5, cells_x, 8, 128), sent_shape],
        flow_two,
        start,
        pair,
        spread,
        labels,
        scratch=scratch(wide - 4),
    )
    source = route(send)
    partial, _, _ = call(
        functools.partial(acoustic_local_body, MIXES[2], True),
        [(4, 64, 128), (96, 128), (96, 128)],
        sound_two,
        sound,
        source,
        deriv_rows,
        deriv_lanes,
        speed,
        near,
    )
    sound_three = call(
        functools.partial(acoustic_far_body, factors[2], False, True),
        [(4, 64, 128)],
        partial,
        before,
        after,
        far,
    )[0]
    sound_state = sound_three.reshape(4, 64, 8, elements).transpose(3, 0, 1, 2).reshape(elements, 4, 512)
    return (flow_state, sound_state)


def solution(mesh):
    placed = (
        P("fx", "fy", "fz"),
        P(None, "fx", "fy", "fz"),
        P("fx", "fy", "fz"),
        P(("fx", "fy", "fz"), None, None),
        P(("fx", "fy", "fz")),
        P(),
        P(),
        P(("fx", "fy", "fz"), None),
        P("fx", "fy", "fz", None, None),
        P("fx", "fy", "fz", None),
    )
    return jax.shard_map(
        per_device,
        mesh=mesh,
        in_specs=placed,
        out_specs=(P(None, "fx", "fy", "fz"), P(("fx", "fy", "fz"), None, None)),
        check_vma=False,
    )
```

time: 194 us -> 116 us (0.60)
  the two profiles are of different devices: /device:TPU:2 before, /device:TPU:29 now
where the time goes in v1:
time: 116 us; the launch traced here: 114 us
  starting transfers between devices  46 us (40%)
  local copies, waits for them, and re-layouts  26.2 us (23%)
  Pallas kernels  17.8 us (15%)
  waiting for transfers between devices  12.9 us (11%)
  other arithmetic  10.3 us (9%)
    pallas_call x14, Pallas kernels, call(): pl.pallas_call(body, out_shape=[jax.ShapeDtypeStruct(shape, F32) for shap...  17.8 us
    all_to_all x3, starting transfers between devices, route(): got = lax.all_to_all(send, 'fy', split_axis=0, concat_axis=0, tiled=True)  15.8 us
    ppermute x3, starting transfers between devices, traces(): lax.ppermute(front, names, forward)  13.4 us
    ppermute x3, waiting for transfers between devices, traces(): lax.ppermute(rear, names, backward)  11.3 us
    unnamed x39, local copies, waits for them, and re-layouts  8.13 us
    mul x8, local copies, waits for them, and re-layouts, cross(): levels[:, None, :, None] * chooser[None, :, None, :]  7.93 us
    ppermute x3, starting transfers between devices, traces(): lax.ppermute(rear, names, backward)  6.25 us
    ppermute x2, starting transfers between devices, per_device(): lax.ppermute(kept, ('fx', 'fy'), shifted(flat, (spots[0][0], dy)))  4.16 us
  transfers between devices with their start and end apart: 16, of which 3 were waited for; matrix products, arithmetic and copies ran while one was open for 27% of the time, Pallas kernels for 11%

profile of v1, /device:TPU:29, one launch (start us, length us, event | category | flops | bytes accessed | tf_op | source)
XLA Modules:
  0.0 114.2 jit_solution(15379227813144067665)
XLA Ops:
  3.9 1.1 collective-permute-start.1
  11.6 1.4 %multiply_convert_fusion = (bf16[8,16,8,16]{3,2,1,0:T(8,128)(2,1)}, bf16[8,16,8,16]{3,2,1,0:T(8,128)(2,1)S(1)}, bf16[8,16,8,16]{3,2,1,0:T(8,128)(2,1)S(1)}, bf16...) fusion(s32[16,16]{1,0:T(8,128)S(1)} %get-tuple-element.83, ...), kind=kLoop, calls=%fused_computation.2 | loop fusion | flops 262144 | bytes 270592 | tf_op jit(solution)/shard_map/convert.6
  13.4 1.6 %broadcast_multiply_fusion = f32[16,8,32,8]{1,0,3,2:T(8,128)} fusion(f32[8,8]{0,1:T(8,128)S(1)} %bitcast.67, f32[16,32]{0,1:T(8,128)S(1)} %fusion), kind=kLoop, calls=%fused_computation | loop fusion | flops 32768 | bytes 133376 | tf_op jit(solution)/shard_map/mul | solution.py:411
  16.2 1.3 %collective-permute-start.2 = (f32[264,128]{1,0:T(8,128)S(1)}, f32[264,128]{1,0:T(8,128)S(1)}, u32[]{:S(2)}, u32[]{:S(2)}) collective-permute-start(f32[264,128]{1,0:T(8,128)S(1)} %get-tuple-element.33), channel_id=1, source_target_pairs={{16,0},{20,4},{24,8},{28,12},{0,16},{4,20},{8,24},{12,28},{17,1},{... | collective-permute-start | bytes 405512 | tf_op jit(solution)/shard_map/ppermute | solution.py:531
  17.6 2.7 %mul.418 = f32[128,4,64]{0,2,1:T(8,128)S(1)} reshape(f32[16,8,32,8]{1,0,3,2:T(8,128)} %broadcast_multiply_fusion) | data formatting | bytes 262144 | tf_op jit(solution)/shard_map/mul | solution.py:411
  21.1 1.0 copy.36
  22.1 1.1 copy.38.state.refs_1_
  23.7 1.2 %add.101 = bf16[1,128,128]{2,1,0:T(8,128)(2,1)S(1)} reshape(bf16[8,16,8,16]{3,2,1,0:T(8,128)(2,1)} %add_convert_fusion.1) | data formatting | bytes 65536 | tf_op jit(solution)/shard_map/add | solution.py:437
  25.1 3.1 %collective-permute-start.4 = (f32[144,128]{1,0:T(8,128)S(1)}, f32[144,128]{1,0:T(8,128)S(1)}, u32[]{:S(2)}, u32[]{:S(2)}) collective-permute-start(f32[144,128]{1,0:T(8,128)S(1)} %get-tuple-element.35), channel_id=1, source_target_pairs={{12,0},{0,4},{4,8},{8,12},{28,16},{16,20},{20,24},{24,28},{13,1},{... | collective-permute-start | bytes 221192 | tf_op jit(solution)/shard_map/ppermute | solution.py:534
  28.2 4.2 %collective-permute-start.6 = (f32[120,128]{1,0:T(8,128)S(1)}, f32[120,128]{1,0:T(8,128)S(1)}, u32[]{:S(2)}, u32[]{:S(2)}) collective-permute-start(f32[120,128]{1,0:T(8,128)S(1)} %get-tuple-element.37), channel_id=1, source_target_pairs={{28,0},{16,4},{20,8},{24,12},{12,16},{0,20},{4,24},{8,28},{29,1},{... | collective-permute-start | bytes 184328 | tf_op jit(solution)/shard_map/ppermute | solution.py:538
  32.4 1.6 %collective-permute-done.5.refs_5_ = f32[120,128]{1,0:T(8,128)S(1)} collective-permute-done((f32[120,128]{1,0:T(8,128)S(1)}, f32[120,128]{1,0:T(8,128)S(1)}, u32[]{:S(2)}, u32[]{:S(2)}) %collective-permute-start.5) | collective-permute-done | bytes 61472 | tf_op jit(solution)/shard_map/ppermute | solution.py:538
  34.0 5.3 %shard_map.151 = (f32[5,14,16,256]{3,2,1,0:T(8,128)S(1)}, f32[5,12,16,256]{3,2,1,0:T(8,128)S(1)}, f32[4,104,128]{2,1,0:T(8,128)}) custom-call(f32[5,8,8,128]{3,2,1,0:T(8,128)S(1)} %get-tuple-element.29.state.refs_0_, f32[24,128]{1,0:T(8,128)S(1)} %get-tuple-element.32.refs_1_, f32[264,128]{1,0:T(8,128)S(1)} %collective-permute-done.2.refs_2_, ...), custom_call_target="tpu_custom_call" | custom-call | tf_op jit(solution)/shard_map/pallas_call | solution.py:43
  39.3 6.6 %all-to-all-start = ((f32[4,104,128]{2,1,0:T(8,128)}), f32[4,104,128]{2,1,0:T(8,128)S(1)}, u32[]{:S(2)}, u32[]{:S(2)}) async-start(f32[4,104,128]{2,1,0:T(8,128)} %get-tuple-element.45), calls=%async_computation | async-start | bytes 425984 | tf_op jit(solution)/shard_map/all_to_all | solution.py:551
  46.8 4.9 %collective-permute-start.7 = (f32[96,128]{1,0:T(8,128)}, f32[96,128]{1,0:T(8,128)S(1)}, u32[]{:S(2)}, u32[]{:S(2)}) collective-permute-start(f32[96,128]{1,0:T(8,128)} %get-tuple-element.43), channel_id=1, source_target_pairs={{0,1},{1,2},{2,3},{3,4},{4,5},{5,6},{6,7},{7,8},{8,9},{9,10},{10,1... | collective-permute-start | bytes 147464 | tf_op jit(solution)/shard_map/ppermute | solution.py:496
  51.6 1.9 %collective-permute-start.8 = (f32[96,128]{1,0:T(8,128)S(1)}, f32[96,128]{1,0:T(8,128)S(1)}, u32[]{:S(2)}, u32[]{:S(2)}) collective-permute-start(f32[96,128]{1,0:T(8,128)S(1)} %get-tuple-element.44), channel_id=1, source_target_pairs={{1,0},{2,1},{3,2},{4,3},{5,4},{6,5},{7,6},{8,7},{9,8},{10,9},{11,1... | collective-permute-start | bytes 147464 | tf_op jit(solution)/shard_map/ppermute | solution.py:496
  53.6 1.8 %mul.455 = bf16[1,128,128]{2,1,0:T(8,128)(2,1)} reshape(bf16[8,16,8,16]{3,2,1,0:T(8,128)(2,1)} %get-tuple-element.66) | data formatting | bytes 65536 | tf_op jit(solution)/shard_map/mul | solution.py:434
  55.4 1.8 %mul.458 = bf16[1,128,128]{2,1,0:T(8,128)(2,1)} reshape(bf16[8,16,8,16]{3,2,1,0:T(8,128)(2,1)} %get-tuple-element.67) | data formatting | bytes 65536 | tf_op jit(solution)/shard_map/mul | solution.py:434
  57.2 1.8 %mul.461 = bf16[1,128,128]{2,1,0:T(8,128)(2,1)} reshape(bf16[8,16,8,16]{3,2,1,0:T(8,128)(2,1)} %get-tuple-element.68) | data formatting | bytes 65536 | tf_op jit(solution)/shard_map/mul | solution.py:434
  59.0 1.8 %mul.464 = bf16[1,128,128]{2,1,0:T(8,128)(2,1)} reshape(bf16[8,16,8,16]{3,2,1,0:T(8,128)(2,1)} %get-tuple-element.62) | data formatting | bytes 65536 | tf_op jit(solution)/shard_map/mul | solution.py:434
  61.6 1.8 %add.105 = bf16[1,128,128]{2,1,0:T(8,128)(2,1)} reshape(bf16[8,16,8,16]{3,2,1,0:T(8,128)(2,1)} %add_convert_fusion) | data formatting | bytes 65536 | tf_op jit(solution)/shard_map/add | solution.py:442
  63.4 4.3 %shard_map.152 = (f32[5,10,16,256]{3,2,1,0:T(8,128)S(1)}, f32[4,104,128]{2,1,0:T(8,128)}) custom-call(f32[5,12,16,256]{3,2,1,0:T(8,128)S(1)} %get-tuple-element.38.wide, f32[5,14,16,256]{3,2,1,0:T(8,128)S(1)} %get-tuple-element.39.start, f32[64,64]{1,0:T(8,128)S(1)} %mul.409.refs_7_.pair, f32[128,512]{1,0:T(8,128)S(1)} %copy.32.refs_8_.spread, ...), custom_call_target="tpu_custom_call" | custom-call | tf_op jit(solution)/shard_map/pallas_call | solution.py:43
  68.7 4.7 %all-to-all-start.1 = ((f32[4,104,128]{2,1,0:T(8,128)}), f32[4,104,128]{2,1,0:T(8,128)S(1)}, u32[]{:S(2)}, u32[]{:S(2)}) async-start(f32[4,104,128]{2,1,0:T(8,128)} %get-tuple-element.47), calls=%async_computation.1 | async-start | bytes 425984 | tf_op jit(solution)/shard_map/all_to_all | solution.py:551
  75.6 1.1 %copy-done.1 = f32[5,10,16,256]{3,2,1,0:T(8,128)S(1)} copy-done((f32[5,10,16,256]{3,2,1,0:T(8,128)S(1)}, f32[5,10,16,256]{3,2,1,0:T(8,128)}, u32[]{:S(2)}) %copy-start.1) | copy-done | bytes 819224
  76.8 3.5 %shard_map.153 = (f32[5,8,8,128]{3,2,1,0:T(8,128)}, f32[4,104,128]{2,1,0:T(8,128)}) custom-call(f32[5,10,16,256]{3,2,1,0:T(8,128)S(1)} %copy-done.1, f32[5,14,16,256]{3,2,1,0:T(8,128)S(1)} %get-tuple-element.39.start, f32[64,64]{1,0:T(8,128)S(1)} %mul.409.refs_7_.pair, f32[128,512]{1,0:T(8,128)S(1)} %copy.32.refs_8_.spread, ...), custom_call_target="tpu_custom_call" | custom-call | tf_op jit(solution)/shard_map/pallas_call | solution.py:43
  80.3 4.5 %all-to-all-start.2 = ((f32[4,104,128]{2,1,0:T(8,128)}), f32[4,104,128]{2,1,0:T(8,128)S(1)}, u32[]{:S(2)}, u32[]{:S(2)}) async-start(f32[4,104,128]{2,1,0:T(8,128)} %get-tuple-element.52), calls=%async_computation.2 | async-start | bytes 425984 | tf_op jit(solution)/shard_map/all_to_all | solution.py:551
  85.6 6.6 %collective-permute-start.9 = (f32[96,128]{1,0:T(8,128)S(1)}, f32[96,128]{1,0:T(8,128)S(1)}, u32[]{:S(2)}, u32[]{:S(2)}) collective-permute-start(f32[96,128]{1,0:T(8,128)S(1)} %get-tuple-element.49), channel_id=1, source_target_pairs={{0,1},{1,2},{2,3},{3,4},{4,5},{5,6},{6,7},{7,8},{8,9},{9,10},{10,1... | collective-permute-start | bytes 147464 | tf_op jit(solution)/shard_map/ppermute | solution.py:496
  92.2 1.9 %collective-permute-start.10 = (f32[96,128]{1,0:T(8,128)S(1)}, f32[96,128]{1,0:T(8,128)S(1)}, u32[]{:S(2)}, u32[]{:S(2)}) collective-permute-start(f32[96,128]{1,0:T(8,128)S(1)} %get-tuple-element.50), channel_id=1, source_target_pairs={{1,0},{2,1},{3,2},{4,3},{5,4},{6,5},{7,6},{8,7},{9,8},{10,9},{11,1... | collective-permute-start | bytes 147464 | tf_op jit(solution)/shard_map/ppermute | solution.py:496
  95.3 5.9 %collective-permute-done.10.refs_2_ = f32[96,128]{1,0:T(8,128)S(1)} collective-permute-done((f32[96,128]{1,0:T(8,128)S(1)}, f32[96,128]{1,0:T(8,128)S(1)}, u32[]{:S(2)}, u32[]{:S(2)}) %collective-permute-start.10) | collective-permute-done | bytes 49184 | tf_op jit(solution)/shard_map/ppermute | solution.py:496
  101.5 1.9 %collective-permute-start.11 = (f32[96,128]{1,0:T(8,128)S(1)}, f32[96,128]{1,0:T(8,128)S(1)}, u32[]{:S(2)}, u32[]{:S(2)}) collective-permute-start(f32[96,128]{1,0:T(8,128)S(1)} %get-tuple-element.54), channel_id=1, source_target_pairs={{0,1},{1,2},{2,3},{3,4},{4,5},{5,6},{6,7},{7,8},{8,9},{9,10},{10,1... | collective-permute-start | bytes 147464 | tf_op jit(solution)/shard_map/ppermute | solution.py:496
  103.5 2.4 %collective-permute-start.12 = (f32[96,128]{1,0:T(8,128)S(1)}, f32[96,128]{1,0:T(8,128)S(1)}, u32[]{:S(2)}, u32[]{:S(2)}) collective-permute-start(f32[96,128]{1,0:T(8,128)S(1)} %get-tuple-element.55), channel_id=1, source_target_pairs={{1,0},{2,1},{3,2},{4,3},{5,4},{6,5},{7,6},{8,7},{9,8},{10,9},{11,1... | collective-permute-start | bytes 147464 | tf_op jit(solution)/shard_map/ppermute | solution.py:496
  107.1 5.4 %collective-permute-done.12.refs_2_ = f32[96,128]{1,0:T(8,128)S(1)} collective-permute-done((f32[96,128]{1,0:T(8,128)S(1)}, f32[96,128]{1,0:T(8,128)S(1)}, u32[]{:S(2)}, u32[]{:S(2)}) %collective-permute-start.12) | collective-permute-done | bytes 49184 | tf_op jit(solution)/shard_map/ppermute | solution.py:496
  113.3 1.0 copy.43
  (109 shorter events, 22.1 us)
Async XLA Ops:
  0.6 0.9 copy-start.2
  1.5 0.8 copy-start.3
  2.3 0.8 copy-start.4
  3.2 13.0 %collective-permute-start = (f32[24,128]{1,0:T(8,128)S(1)}, f32[24,128]{1,0:T(8,128)S(1)}, u32[]{:S(2)}, u32[]{:S(2)}) collective-permute-start(f32[24,128]{1,0:T(8,128)S(1)} %get-tuple-element.30), channel_id=1, source_target_pairs={{1,0},{2,1},{3,2},{0,3},{5,4},{6,5},{7,6},{4,7},{9,8},{10,9},{11,1... | collective-permute-start | bytes 36872 | tf_op jit(solution)/shard_map/ppermute | solution.py:481
  3.9 12.3 %collective-permute-start.1 = (f32[24,128]{1,0:T(8,128)S(1)}, f32[24,128]{1,0:T(8,128)S(1)}, u32[]{:S(2)}, u32[]{:S(2)}) collective-permute-start(f32[24,128]{1,0:T(8,128)S(1)} %get-tuple-element.31), channel_id=1, source_target_pairs={{3,0},{0,1},{1,2},{2,3},{7,4},{4,5},{5,6},{6,7},{11,8},{8,9},{9,10... | collective-permute-start | bytes 36872 | tf_op jit(solution)/shard_map/ppermute | solution.py:482
  8.9 4.5 %copy-start.8 = (f32[8,8]{1,0:T(8,128)S(1)}, f32[8,8]{1,0:T(8,128)}, u32[]{:S(2)}) copy-start(f32[8,8]{1,0:T(8,128)} %param.20) | copy-start | bytes 772
  13.0 2.1 %copy-start.11 = (s32[8,8]{1,0:T(8,128)S(1)}, s32[8,8]{1,0:T(8,128)}, u32[]{:S(2)}) copy-start(s32[8,8]{1,0:T(8,128)} %constant.44.clone) | copy-start | bytes 772
  13.0 2.1 %copy-start.12 = (s32[8,8]{1,0:T(8,128)S(1)}, s32[8,8]{1,0:T(8,128)}, u32[]{:S(2)}) copy-start(s32[8,8]{1,0:T(8,128)} %constant.43.clone) | copy-start | bytes 772
  15.9 4.8 %copy-start.5 = (f32[16,4,512]{2,1,0:T(4,128)S(1)}, f32[16,4,512]{2,1,0:T(4,128)}, u32[]{:S(2)}) copy-start(f32[16,4,512]{2,1,0:T(4,128)} %param.17) | copy-start | bytes 393220
  16.2 17.8 %collective-permute-start.2 = (f32[264,128]{1,0:T(8,128)S(1)}, f32[264,128]{1,0:T(8,128)S(1)}, u32[]{:S(2)}, u32[]{:S(2)}) collective-permute-start(f32[264,128]{1,0:T(8,128)S(1)} %get-tuple-element.33), channel_id=1, source_target_pairs={{16,0},{20,4},{24,8},{28,12},{0,16},{4,20},{8,24},{12,28},{17,1},{... | collective-permute-start | bytes 405512 | tf_op jit(solution)/shard_map/ppermute | solution.py:531
  20.3 3.1 %copy-start.13 = (f32[16]{0:T(128)S(1)}, f32[16]{0:T(128)}, u32[]{:S(2)}) copy-start(f32[16]{0:T(128)} %param.18) | copy-start | bytes 196
  23.2 37.5 %copy-start.9 = (s32[8,8]{1,0:T(8,128)S(1)}, s32[8,8]{1,0:T(8,128)}, u32[]{:S(2)}) copy-start(s32[8,8]{1,0:T(8,128)} %constant.46.clone) | copy-start | bytes 772
  23.2 37.5 %copy-start.10 = (s32[8,8]{1,0:T(8,128)S(1)}, s32[8,8]{1,0:T(8,128)}, u32[]{:S(2)}) copy-start(s32[8,8]{1,0:T(8,128)} %constant.45.clone) | copy-start | bytes 772
  24.9 9.1 %collective-permute-start.3 = (f32[144,128]{1,0:T(8,128)S(1)}, f32[144,128]{1,0:T(8,128)S(1)}, u32[]{:S(2)}, u32[]{:S(2)}) collective-permute-start(f32[144,128]{1,0:T(8,128)S(1)} %get-tuple-element.34), channel_id=1, source_target_pairs={{4,0},{8,4},{12,8},{0,12},{20,16},{24,20},{28,24},{16,28},{5,1},{9... | collective-permute-start | bytes 221192 | tf_op jit(solution)/shard_map/ppermute | solution.py:534
  25.1 8.9 %collective-permute-start.4 = (f32[144,128]{1,0:T(8,128)S(1)}, f32[144,128]{1,0:T(8,128)S(1)}, u32[]{:S(2)}, u32[]{:S(2)}) collective-permute-start(f32[144,128]{1,0:T(8,128)S(1)} %get-tuple-element.35), channel_id=1, source_target_pairs={{12,0},{0,4},{4,8},{8,12},{28,16},{16,20},{20,24},{24,28},{13,1},{... | collective-permute-start | bytes 221192 | tf_op jit(solution)/shard_map/ppermute | solution.py:534
  28.2 5.8 %collective-permute-start.5 = (f32[120,128]{1,0:T(8,128)S(1)}, f32[120,128]{1,0:T(8,128)S(1)}, u32[]{:S(2)}, u32[]{:S(2)}) collective-permute-start(f32[120,128]{1,0:T(8,128)S(1)} %get-tuple-element.36), channel_id=1, source_target_pairs={{20,0},{24,4},{28,8},{16,12},{4,16},{8,20},{12,24},{0,28},{21,1},{... | collective-permute-start | bytes 184328 | tf_op jit(solution)/shard_map/ppermute | solution.py:538
  28.2 5.8 %collective-permute-start.6 = (f32[120,128]{1,0:T(8,128)S(1)}, f32[120,128]{1,0:T(8,128)S(1)}, u32[]{:S(2)}, u32[]{:S(2)}) collective-permute-start(f32[120,128]{1,0:T(8,128)S(1)} %get-tuple-element.37), channel_id=1, source_target_pairs={{28,0},{16,4},{20,8},{24,12},{12,16},{0,20},{4,24},{8,28},{29,1},{... | collective-permute-start | bytes 184328 | tf_op jit(solution)/shard_map/ppermute | solution.py:538
  39.3 29.3 %all-to-all-start = ((f32[4,104,128]{2,1,0:T(8,128)}), f32[4,104,128]{2,1,0:T(8,128)S(1)}, u32[]{:S(2)}, u32[]{:S(2)}) async-start(f32[4,104,128]{2,1,0:T(8,128)} %get-tuple-element.45), calls=%async_computation | async-start | bytes 425984 | tf_op jit(solution)/shard_map/all_to_all | solution.py:551
  46.8 38.4 %collective-permute-start.7 = (f32[96,128]{1,0:T(8,128)}, f32[96,128]{1,0:T(8,128)S(1)}, u32[]{:S(2)}, u32[]{:S(2)}) collective-permute-start(f32[96,128]{1,0:T(8,128)} %get-tuple-element.43), channel_id=1, source_target_pairs={{0,1},{1,2},{2,3},{3,4},{4,5},{5,6},{6,7},{7,8},{8,9},{9,10},{10,1... | collective-permute-start | bytes 147464 | tf_op jit(solution)/shard_map/ppermute | solution.py:496
  51.6 33.6 %collective-permute-start.8 = (f32[96,128]{1,0:T(8,128)S(1)}, f32[96,128]{1,0:T(8,128)S(1)}, u32[]{:S(2)}, u32[]{:S(2)}) collective-permute-start(f32[96,128]{1,0:T(8,128)S(1)} %get-tuple-element.44), channel_id=1, source_target_pairs={{1,0},{2,1},{3,2},{4,3},{5,4},{6,5},{7,6},{8,7},{9,8},{10,9},{11,1... | collective-permute-start | bytes 147464 | tf_op jit(solution)/shard_map/ppermute | solution.py:496
  67.8 0.9 copy-start
  68.7 16.2 %copy-start.6 = (bf16[1,128,128]{2,1,0:T(8,128)(2,1)S(1)}, bf16[1,128,128]{2,1,0:T(8,128)(2,1)}, u32[]{:S(2)}) copy-start(bf16[1,128,128]{2,1,0:T(8,128)(2,1)} %mul.464) | copy-start | bytes 98308
  68.7 16.2 %copy-start.7 = (bf16[1,128,128]{2,1,0:T(8,128)(2,1)S(1)}, bf16[1,128,128]{2,1,0:T(8,128)(2,1)}, u32[]{:S(2)}) copy-start(bf16[1,128,128]{2,1,0:T(8,128)(2,1)} %add.105) | copy-start | bytes 98308
  68.7 11.6 %all-to-all-start.1 = ((f32[4,104,128]{2,1,0:T(8,128)}), f32[4,104,128]{2,1,0:T(8,128)S(1)}, u32[]{:S(2)}, u32[]{:S(2)}) async-start(f32[4,104,128]{2,1,0:T(8,128)} %get-tuple-element.47), calls=%async_computation.1 | async-start | bytes 425984 | tf_op jit(solution)/shard_map/all_to_all | solution.py:551
  75.6 1.1 %copy-start.1 = (f32[5,10,16,256]{3,2,1,0:T(8,128)S(1)}, f32[5,10,16,256]{3,2,1,0:T(8,128)}, u32[]{:S(2)}) copy-start(f32[5,10,16,256]{3,2,1,0:T(8,128)} %copy-done) | copy-start | bytes 2457604
  80.3 25.6 %all-to-all-start.2 = ((f32[4,104,128]{2,1,0:T(8,128)}), f32[4,104,128]{2,1,0:T(8,128)S(1)}, u32[]{:S(2)}, u32[]{:S(2)}) async-start(f32[4,104,128]{2,1,0:T(8,128)} %get-tuple-element.52), calls=%async_computation.2 | async-start | bytes 425984 | tf_op jit(solution)/shard_map/all_to_all | solution.py:551
  85.6 9.7 %collective-permute-start.9 = (f32[96,128]{1,0:T(8,128)S(1)}, f32[96,128]{1,0:T(8,128)S(1)}, u32[]{:S(2)}, u32[]{:S(2)}) collective-permute-start(f32[96,128]{1,0:T(8,128)S(1)} %get-tuple-element.49), channel_id=1, source_target_pairs={{0,1},{1,2},{2,3},{3,4},{4,5},{5,6},{6,7},{7,8},{8,9},{9,10},{10,1... | collective-permute-start | bytes 147464 | tf_op jit(solution)/shard_map/ppermute | solution.py:496
  92.2 9.0 %collective-permute-start.10 = (f32[96,128]{1,0:T(8,128)S(1)}, f32[96,128]{1,0:T(8,128)S(1)}, u32[]{:S(2)}, u32[]{:S(2)}) collective-permute-start(f32[96,128]{1,0:T(8,128)S(1)} %get-tuple-element.50), channel_id=1, source_target_pairs={{1,0},{2,1},{3,2},{4,3},{5,4},{6,5},{7,6},{8,7},{9,8},{10,9},{11,1... | collective-permute-start | bytes 147464 | tf_op jit(solution)/shard_map/ppermute | solution.py:496
  101.5 5.5 %collective-permute-start.11 = (f32[96,128]{1,0:T(8,128)S(1)}, f32[96,128]{1,0:T(8,128)S(1)}, u32[]{:S(2)}, u32[]{:S(2)}) collective-permute-start(f32[96,128]{1,0:T(8,128)S(1)} %get-tuple-element.54), channel_id=1, source_target_pairs={{0,1},{1,2},{2,3},{3,4},{4,5},{5,6},{6,7},{7,8},{8,9},{9,10},{10,1... | collective-permute-start | bytes 147464 | tf_op jit(solution)/shard_map/ppermute | solution.py:496
  103.5 9.0 %collective-permute-start.12 = (f32[96,128]{1,0:T(8,128)S(1)}, f32[96,128]{1,0:T(8,128)S(1)}, u32[]{:S(2)}, u32[]{:S(2)}) collective-permute-start(f32[96,128]{1,0:T(8,128)S(1)} %get-tuple-element.55), channel_id=1, source_target_pairs={{1,0},{2,1},{3,2},{4,3},{5,4},{6,5},{7,6},{8,7},{9,8},{10,9},{11,1... | collective-permute-start | bytes 147464 | tf_op jit(solution)/shard_map/ppermute | solution.py:496

commit v2 on v1

--- a/solution.py
+++ b/solution.py
@@ -34,16 +34,24 @@
     return dot(left_high, right_high) + dot(left_high, right_low) + dot(left_low, right_high)
 
 
+def dot_full(left, right, dims=((1,), (0,))):
+    return lax.dot_general(
+        left, right, (dims, ((), ())), precision=lax.Precision.HIGHEST, preferred_element_type=F32
+    )
+
+
 def dot_exact_right(left, right):
     left_high, left_low = parts(left)
     return dot(left_high, right) + dot(left_low, right)
 
 
-def call(body, outs, *operands, scratch=()):
+def call(body, outs, *operands, scratch=(), fetch=False):
+    spec = pl.BlockSpec() if fetch else pl.BlockSpec(memory_space=pltpu.VMEM)
+    outs = [out if isinstance(out, jax.ShapeDtypeStruct) else jax.ShapeDtypeStruct(out, F32) for out in outs]
     return pl.pallas_call(
         body,
-        out_shape=[jax.ShapeDtypeStruct(shape, F32) for shape in outs],
-        in_specs=[pl.BlockSpec(memory_space=pltpu.VMEM)] * len(operands),
+        out_shape=outs,
+        in_specs=[spec] * len(operands),
         out_specs=[pl.BlockSpec(memory_space=pltpu.VMEM)] * len(outs),
         scratch_shapes=list(scratch),
         compiler_params=PARAMS,
@@ -126,9 +134,7 @@
                 wide[f, plane, target[0] : target[1], 128:256] = block[source[0] : source[1]]
 
 
-def flow_rate_section(wide, derived, start, offset, mix, write):
-    depth = wide.shape[1]
-
+def derive_planes(wide, derived, first, last):
     def derive(i, _):
         rho, mx, my, mz, energy = [wide[f, i] for f in range(5)]
         inverse = 1.0 / rho
@@ -141,7 +147,25 @@
         derived[4, i] = jnp.sqrt(HEAT_RATIO * jnp.abs(p) * inverse)
         return 0
 
-    lax.fori_loop(0, depth, derive, 0)
+    lax.fori_loop(first, last, derive, 0)
+
+
+def derive_speeds(wide, derived, first, last):
+    def derive(i, _):
+        inverse = 1.0 / wide[0, i]
+        for k in range(3):
+            derived[k, i] = wide[1 + k, i] * inverse
+        return 0
+
+    lax.fori_loop(first, last, derive, 0)
+
+
+def flow_rate_section(wide, derived, start, offset, mix, write, inner=False):
+    depth = wide.shape[1]
+    near, lanes = slice(0, 8), slice(0, 128)
+    every = (slice(None), slice(None))
+    windows = [(near, lanes), (slice(None), lanes), (near, slice(None))] if inner else [every] * 3
+    kept = windows[0]
 
     def flux(fields, other, along):
         speed, p = other[along], other[3]
@@ -163,8 +187,9 @@
         ]
 
     def plane(i, along):
-        fields = [wide[f, i] for f in range(5)]
-        other = [derived[f, i] for f in range(5)]
+        rows, columns = windows[along]
+        fields = [wide[f, i, rows, columns] for f in range(5)]
+        other = [derived[f, i, rows, columns] for f in range(5)]
         return (fields,) + flux(fields, other, along)
 
     def section(i, before):
@@ -180,11 +205,12 @@
             )
             faces = face(here, moved)
             for f in range(5):
-                total[f] = total[f] + (faces[f] - pltpu.roll(faces[f], 1, axis))
+                change = faces[f] - pltpu.roll(faces[f], 1, axis)
+                total[f] = total[f] + (change[0:8, 0:128] if inner else change)
         for f in range(5):
-            value = wide[f, i] - (0.5 * TIME_STEP) * total[f]
+            value = wide[f, i, kept[0], kept[1]] - (0.5 * TIME_STEP) * total[f]
             if mix[0] != 0.0:
-                value = mix[0] * start[f, i + offset] + mix[1] * value
+                value = mix[0] * start[f, i + offset, kept[0], kept[1]] + mix[1] * value
             write(i - 1, f, value)
         return tuple(ahead)
 
@@ -217,7 +243,6 @@
 
 def project(lamb_rows, pair, spread, labels, send):
     peers = send.shape[0]
-    fold = send.shape[1] // 24 - 0
     fold = 192 // (send.shape[1] - 8)
     group = lax.broadcasted_iota(jnp.int32, (64 // fold, 128), 1) // (128 // fold)
     height = 64 // fold
@@ -233,41 +258,49 @@
     send[:, 3 * height : 3 * height + 8] = labels[...]
 
 
-def flow_first_body(places, *refs):
+def flow_sources_body(places, *refs):
     state, edge = refs[0:2]
     messages = refs[2 : 2 + len(places)]
     pair, spread, labels = refs[2 + len(places) : 5 + len(places)]
-    wide, out, send, derived, lamb_rows = refs[5 + len(places) :]
+    wide, send, derived, lamb_rows = refs[5 + len(places) :]
     cells_x = state.shape[1]
     beside = []
     for message, spots in zip(messages, places):
         beside.extend((dx, dy, message) for dx, dy in spots)
     assemble(wide, state, edge, beside, cells_x)
-
+    derive_speeds(wide, derived, HALO - 1, HALO + cells_x + 1)
+    lamb(derived, HALO, cells_x, lamb_rows)
+    project(lamb_rows, pair, spread, labels, send)
+
+
+def flow_first_body(wide, pair, spread, labels, out, send, derived, lamb_rows):
     def write(i, f, value):
         out[f, i] = value
 
+    planes = wide.shape[1]
+    cells_x = planes - 2 * HALO
+    derive_planes(wide, derived, 0, planes)
     flow_rate_section(wide, derived, wide, 0, MIXES[0], write)
-    lamb(derived, HALO, cells_x, lamb_rows)
+    derive_speeds(out, derived, HALO - 2, HALO + cells_x)
+    lamb(derived, HALO - 1, cells_x, lamb_rows)
     project(lamb_rows, pair, spread, labels, send)
 
 
-def flow_second_body(wide, start, pair, spread, labels, out, send, derived, lamb_rows):
+def flow_last_body(wide, start, pair, spread, labels, out, send, derived, lamb_rows, second):
+    def write_second(i, f, value):
+        second[f, i] = value
+
     def write(i, f, value):
         out[f, i] = value
 
-    flow_rate_section(wide, derived, start, 1, MIXES[1], write)
-    lamb(derived, HALO - 1, wide.shape[1] - 2 * (HALO - 1), lamb_rows)
+    planes = wide.shape[1]
+    cells_x = out.shape[1]
+    derive_planes(wide, derived, 0, planes)
+    flow_rate_section(wide, derived, start, 1, MIXES[1], write_second)
+    derive_planes(second, derived, 0, planes - 2)
+    lamb(derived, 1, cells_x, lamb_rows)
     project(lamb_rows, pair, spread, labels, send)
-
-
-def flow_third_body(wide, start, pair, spread, labels, out, send, derived, lamb_rows):
-    def write(i, f, value):
-        out[f, i] = value[0:8, 0:128]
-
-    flow_rate_section(wide, derived, start, 2, MIXES[2], write)
-    lamb(derived, HALO - 2, wide.shape[1] - 2 * (HALO - 2), lamb_rows)
-    project(lamb_rows, pair, spread, labels, send)
+    flow_rate_section(second, derived, start, 2, MIXES[2], write, inner=True)
 
 
 def faces_out(state, rear, front):
@@ -320,17 +353,10 @@
     return [rates[c] - count * fields[c] + side[c * 64 : c * 64 + 64] for c in range(4)]
 
 
-def acoustic_local_body(mix, has_source, *refs):
-    if has_source:
-        state, start, source, deriv_rows, deriv_lanes, speed, sides, out, front, rear = refs
-    else:
-        state, deriv_rows, deriv_lanes, speed, sides, out, front, rear = refs
+def local_update(mix, state, start, deriv_rows, deriv_lanes, speed, sides, out, front, rear):
     rates = rate_local(state, deriv_rows, deriv_lanes, speed, sides)
     for c in range(4):
-        rate = rates[c]
-        if has_source and c > 0:
-            rate = rate + source[c - 1]
-        value = state[c] + TIME_STEP * rate
+        value = state[c] + TIME_STEP * rates[c]
         if mix[0] != 0.0:
             value = mix[0] * start[c] + mix[1] * value
         out[c] = value
@@ -338,8 +364,48 @@
     lift(out, front, rear, sides, TIME_STEP * mix[1] * PENALTY)
 
 
-def acoustic_first_body(state, deriv_rows, deriv_lanes, speed, sides, out, front, rear):
-    acoustic_local_body(MIXES[0], False, state, deriv_rows, deriv_lanes, speed, sides, out, front, rear)
+def acoustic_local_body(mix, state, start, deriv_rows, deriv_lanes, speed, sides, out, front, rear):
+    local_update(mix, state, start, deriv_rows, deriv_lanes, speed, sides, out, front, rear)
+
+
+def order_table(count, turned):
+    row = lax.broadcasted_iota(jnp.int32, (4 * count, 4 * count), 0)
+    column = lax.broadcasted_iota(jnp.int32, (4 * count, 4 * count), 1)
+    if turned:
+        row, column = column, row
+    return (column == (row % count) * 4 + row // count).astype(F32)
+
+
+def acoustic_first_body(given, deriv_rows, deriv_lanes, speed, sides, state, out, front, rear, turned):
+    count = given.shape[0]
+    rows = jnp.concatenate([given[e] for e in range(count)], 0)
+    rows = dot_full(order_table(count, False), rows)
+    rows = jnp.concatenate([rows, jnp.zeros((128 - 4 * count, rows.shape[1]), F32)], 0)
+    turned[...] = rows.T
+    lane = lax.broadcasted_iota(jnp.int32, (64, 128), 1) // count
+    fields = [jnp.zeros((64, 128), F32)] * 4
+    for z in range(8):
+        piece = turned[pl.ds(z, 64, stride=8), :]
+        for c in range(4):
+            move = (z - c) * count % 128
+            fields[c] = jnp.where(lane == z, pltpu.roll(piece, move, 1) if move else piece, fields[c])
+    for c in range(4):
+        state[c] = fields[c]
+    local_update(MIXES[0], state, state, deriv_rows, deriv_lanes, speed, sides, out, front, rear)
+
+
+def natural_order(state, out, turned):
+    count = out.shape[0]
+    lane = lax.broadcasted_iota(jnp.int32, (64, 128), 1) // count
+    for z in range(8):
+        value = jnp.zeros((64, 128), F32)
+        for c in range(4):
+            move = (c - z) * count % 128
+            value = jnp.where(lane == c, pltpu.roll(state[c], move, 1) if move else state[c], value)
+        turned[pl.ds(z, 64, stride=8), :] = value
+    rows = dot_full(order_table(count, True), turned[...].T[0 : 4 * count])
+    for e in range(count):
+        out[e] = rows[4 * e : 4 * e + 4]
 
 
 def remote_part(out, before, after, sides_far, factor):
@@ -356,23 +422,22 @@
         out[c] += value[c * 64 : c * 64 + 64]
 
 
-def acoustic_far_body(factor, has_source, last, *refs):
-    refs = list(refs)
-    partial, before, after, sides_far = refs[0:4]
-    refs = refs[4:]
-    if has_source:
-        source = refs.pop(0)
-    out = refs[0]
+def acoustic_far_body(mix, last, *refs):
+    partial, before, after, sides_far, received = refs[0:5]
+    if last:
+        given_out, out, turned = refs[5:]
+    else:
+        out, front, rear = refs[5:]
     out[...] = partial[...]
-    remote_part(out, before, after, sides_far, factor)
-    if has_source:
-        for c in range(3):
-            out[1 + c] += TIME_STEP * source[c]
-    if not last:
-        faces_out(out, refs[2], refs[1])
-
-
-def place_body(received, out):
+    place(received, out, TIME_STEP * mix[1])
+    remote_part(out, before, after, sides_far, TIME_STEP * mix[1] * PENALTY)
+    if last:
+        natural_order(out, given_out, turned)
+    else:
+        faces_out(out, rear, front)
+
+
+def place(received, out, factor):
     peers, size = received.shape[0], received.shape[1]
     fold = 192 // (size - 8)
     height = 64 // fold
@@ -392,55 +457,97 @@
         total = value if total is None else total + value
     for c in range(3):
         for g in range(fold):
-            out[c, g * height : g * height + height] = total[
-                c * height : c * height + height, g * 128 : g * 128 + 128
-            ]
-
-
-def routing_tables(mode_basis, owners, elements, peers):
-    blocks = owners.shape[0]
+            rows = slice(g * height, g * height + height)
+            out[1 + c, rows] = out[1 + c, rows] + factor * (
+                total[c * height : c * height + height, g * 128 : g * 128 + 128]
+            )
+
+
+def kron_part(matrix, shape, rows_by, columns_by):
+    row = lax.broadcasted_iota(jnp.int32, (shape[0], 8), 0)
+    level = lax.broadcasted_iota(jnp.int32, (shape[0], 8), 1)
+    left = (row // rows_by % 8 == level).astype(F32)
+    level = lax.broadcasted_iota(jnp.int32, (8, shape[1]), 0)
+    column = lax.broadcasted_iota(jnp.int32, (8, shape[1]), 1)
+    right = (column // columns_by % 8 == level).astype(F32)
+    return dot_full(dot_full(left, matrix), right)
+
+
+def tables_body(
+    derivative,
+    basis,
+    local,
+    owner_column,
+    owner_row,
+    element_column,
+    sound_speed,
+    near,
+    far,
+    deriv_rows,
+    deriv_lanes,
+    pair,
+    spread,
+    labels,
+    speed,
+):
+    count = local.shape[0]
+    size = 8 * count
+
+    def place_of(shape):
+        return (lax.broadcasted_iota(jnp.int32, shape, 0), lax.broadcasted_iota(jnp.int32, shape, 1))
+
+    row, column = place_of((count, size))
+    repeat = (column % count == row).astype(F32)
+    speed[...] = dot_full(sound_speed[...], repeat)
+    wanted = dot_full(local[...].astype(F32), repeat, ((0,), (0,))).astype(jnp.int32)
+    row, column = place_of((size, size))
+    level, element = row // count, row % count
+    level_out = column // count
+    for facet in range(4):
+        shift = -count if facet % 2 == 0 else count
+        choice = jnp.broadcast_to(wanted[facet : facet + 1], (size, size))
+        near[facet] = jnp.where((level == level_out) & (element == choice), 1.0, 0.0).astype(BF16)
+        far[facet] = jnp.where((level == level_out) & (element + shift == choice), 1.0, 0.0).astype(BF16)
+    lower = jnp.broadcast_to(wanted[4:5], (size, size))
+    upper = jnp.broadcast_to(wanted[5:6], (size, size))
+    hit = (level == 7) & (level_out == 0) & (element == lower)
+    hit = hit | ((level == 0) & (level_out == 7) & (element == upper))
+    near[4] = jnp.where(hit, 1.0, 0.0).astype(BF16)
+    hit = (level == 0) & (level_out == 0) & (element - count == lower)
+    hit = hit | ((level == 1) & (level_out == 7) & (element + count == upper))
+    far[4] = jnp.where(hit, 1.0, 0.0).astype(BF16)
+
+    row, column = place_of((64, 64))
+    slopes, modes = derivative[...], basis[...]
+    outer = kron_part(slopes, (64, 64), 8, 8)
+    inner = kron_part(slopes, (64, 64), 1, 1)
+    deriv_rows[0:64] = jnp.where(row % 8 == column % 8, outer, 0.0)
+    deriv_rows[64:128] = jnp.where(row // 8 == column // 8, inner, 0.0)
+    row, column = place_of((size, size))
+    lanes = kron_part(slopes.T, (size, size), count, count)
+    deriv_lanes[...] = jnp.where(row % count == column % count, lanes, 0.0)
+    pair[...] = kron_part(modes, (64, 64), 8, 8) * kron_part(modes, (64, 64), 1, 1)
+
+    blocks = owner_column.shape[0]
+    peers = labels.shape[0]
     capacity = max(2, 2 * blocks // peers)
-    matches = (owners[:, None] == jnp.arange(peers, dtype=jnp.int32)[None, :]).astype(jnp.int32)
-    order = jnp.tril(jnp.ones((blocks, blocks), jnp.int32), -1)
-    before = jnp.sum(order[:, :, None] * matches[None, :, :], 1)
-    position = jnp.sum(before * matches, 1)
-    slot = owners * capacity + position
-    chooser = jnp.arange(peers * capacity, dtype=jnp.int32)[None, :] == slot[:, None]
-    labels = (jnp.sum(jnp.where(chooser, elements[:, None] + 1, 0), 0) - 1).reshape(peers, capacity)
-    fold = 128 // (8 * capacity)
-    spread = chooser.astype(F32)[:, None, :, None] * mode_basis.T[None, :, None, :]
-    spread = spread.reshape(blocks * 8, peers, 1, capacity * 8)
-    spread = jnp.broadcast_to(spread, (blocks * 8, peers, fold, capacity * 8))
-    spread = spread.reshape(blocks * 8, peers * 128)
-    lanes = jnp.broadcast_to(labels[:, None, :, None], (peers, fold, capacity, 8)).reshape(peers, 1, 128)
-    return spread, jnp.broadcast_to(lanes, (peers, 8, 128)).astype(F32), fold
-
-
-def side_tables(local):
-    count = local.shape[0]
-    element = jnp.arange(count, dtype=jnp.int32)
-    eye = jnp.eye(8, dtype=jnp.int32)
-    near, far = [], []
-    for facet in range(6):
-        wanted = local[:, facet][None, :]
-        shift = -count if facet % 2 == 0 else count
-        near.append((element[:, None] == wanted).astype(jnp.int32))
-        far.append((element[:, None] + shift == wanted).astype(jnp.int32))
-    first, last = np.zeros((8, 8), np.int32), np.zeros((8, 8), np.int32)
-    first[7, 0] = 1
-    last[0, 7] = 1
-
-    def cross(levels, chooser):
-        return (levels[:, None, :, None] * chooser[None, :, None, :]).reshape(8 * count, 8 * count)
-
-    near_out = [cross(eye, near[f]) for f in range(4)]
-    near_out.append(cross(jnp.asarray(first), near[4]) + cross(jnp.asarray(last), near[5]))
-    far_out = [cross(eye, far[f]) for f in range(4)]
-    put_first, put_last = np.zeros((8, 8), np.int32), np.zeros((8, 8), np.int32)
-    put_first[0, 0] = 1
-    put_last[1, 7] = 1
-    far_out.append(cross(jnp.asarray(put_first), far[4]) + cross(jnp.asarray(put_last), far[5]))
-    return jnp.stack(near_out).astype(BF16), jnp.stack(far_out).astype(BF16)
+    row, column = place_of((blocks, blocks))
+    earlier = (owner_column[...] == owner_row[...]) & (column < row)
+    position = jnp.sum(jnp.where(earlier, 1.0, 0.0), 1, keepdims=True)
+    slot = owner_column[...].astype(F32) * capacity + position
+    wide = (8 * blocks, peers * 128)
+    row, column = place_of((8 * blocks, blocks))
+    repeat = (row // 8 == column).astype(F32)
+    slot = dot_full(repeat, jnp.broadcast_to(slot, (blocks, 128)))
+    element = dot_full(repeat, jnp.broadcast_to(element_column[...].astype(F32), (blocks, 128)))
+    row, column = place_of((8 * blocks, 128))
+    values = kron_part(modes.T, (8 * blocks, 128), 1, 1)
+    inside = column % (8 * capacity) // 8
+    for peer in range(peers):
+        chosen = slot == (inside + peer * capacity).astype(F32)
+        spread[:, peer * 128 : peer * 128 + 128] = jnp.where(chosen, values, 0.0)
+        named = jnp.where(chosen & (row % 8 == 0), element + 1.0, 0.0)
+        labels[peer] = jnp.broadcast_to(jnp.sum(named, 0, keepdims=True) - 1.0, (8, 128))
 
 
 def shifted(sizes, shifts):
@@ -477,17 +584,39 @@
         density,
         velocity,
         pressure,
+        fetch=True,
     )
     above = lax.ppermute(low, "fz", shifted((size_z,), (1,)))
     below = lax.ppermute(high, "fz", shifted((size_z,), (-1,)))
 
-    sound = acoustic.reshape(elements, 4, 64, 8).transpose(1, 2, 3, 0).reshape(4, 64, 8 * elements)
     local = neighbours - device * elements
-    near, far = side_tables(local)
-    eye = jnp.eye(8, dtype=F32)
-    deriv_rows = jnp.concatenate([jnp.kron(derivative, eye), jnp.kron(eye, derivative)], 0)
-    deriv_lanes = jnp.kron(derivative.T, jnp.eye(elements, dtype=F32))
-    speed = jnp.tile(sound_speed, 8)[None, :]
+    size = 8 * elements
+    blocks = block_owner.size
+    capacity = max(2, 2 * blocks // size_y)
+    fold = 128 // (8 * capacity)
+    table = jax.ShapeDtypeStruct((5, size, size), BF16)
+    near, far, deriv_rows, deriv_lanes, pair, spread, labels, speed = call(
+        tables_body,
+        [
+            table,
+            table,
+            (128, 64),
+            (size, size),
+            (64, 64),
+            (8 * blocks, size_y * 128),
+            (size_y, 8, 128),
+            (1, size),
+        ],
+        derivative,
+        mode_basis,
+        local,
+        block_owner.reshape(blocks, 1),
+        block_owner.reshape(1, blocks),
+        block_element.reshape(blocks, 1),
+        sound_speed.reshape(1, elements),
+        fetch=True,
+    )
+
     forward = [(i, i + 1) for i in range(devices - 1)]
     backward = [(i + 1, i) for i in range(devices - 1)]
     names = ("fx", "fy", "fz")
@@ -495,14 +624,17 @@
     def traces(front, rear):
         return lax.ppermute(front, names, forward), lax.ppermute(rear, names, backward)
 
-    partial, front, rear = call(
+    held = (4, 64, size)
+    faces = (96, size)
+    sound, partial, front, rear = call(
         acoustic_first_body,
-        [(4, 64, 128), (96, 128), (96, 128)],
-        sound,
+        [held, held, faces, faces],
+        acoustic,
         deriv_rows,
         deriv_lanes,
         speed,
         near,
+        scratch=[pltpu.VMEM((512, 128), F32)],
     )
     before, after = traces(front, rear)
 
@@ -538,108 +670,94 @@
             messages.append(lax.ppermute(kept, ("fx", "fy"), shifted(flat, (spots[0][0], dy))))
             places.append(tuple((dx, dy) for dx, _ in spots))
 
-    spread, labels, fold = routing_tables(
-        mode_basis, block_owner.reshape(-1), block_element.reshape(-1), size_y
-    )
-    pair = jnp.kron(mode_basis, mode_basis)
-    sent_shape = (size_y, 192 // fold + 8, 128)
-
-    def scratch(planes):
-        return [pltpu.VMEM((5, planes, 16, 256), F32), pltpu.VMEM((3, 64, 128), F32)]
+    sent = (size_y, 192 // fold + 8, 128)
+    wide = cells_x + 2 * HALO
+    rows_scratch = pltpu.VMEM((3, 64, 128), F32)
+
+    def planes(count):
+        return (5, count, 16, 256)
 
     def route(send):
-        got = lax.all_to_all(send, "fy", split_axis=0, concat_axis=0, tiled=True)
-        return call(place_body, [(3, 64, 128)], got)[0]
-
-    wide = cells_x + 2 * HALO
-    start, flow_one, send = call(
-        functools.partial(flow_first_body, tuple(places)),
-        [(5, wide, 16, 256), (5, wide - 2, 16, 256), sent_shape],
+        return lax.all_to_all(send, "fy", split_axis=0, concat_axis=0, tiled=True)
+
+    start, send = call(
+        functools.partial(flow_sources_body, tuple(places)),
+        [planes(wide), sent],
         state,
         edge,
         *messages,
         pair,
         spread,
         labels,
-        scratch=scratch(wide),
-    )
-    source = route(send)
-
-    factors = [TIME_STEP * mix[1] * PENALTY for mix in MIXES]
+        scratch=[pltpu.VMEM((3, wide, 16, 256), F32), rows_scratch],
+    )
+    received = route(send)
+    flow_one, send_next = call(
+        flow_first_body,
+        [planes(wide - 2), sent],
+        start,
+        pair,
+        spread,
+        labels,
+        scratch=[pltpu.VMEM(planes(wide), F32), rows_scratch],
+    )
     sound_one, front, rear = call(
-        functools.partial(acoustic_far_body, factors[0], True, False),
-        [(4, 64, 128), (96, 128), (96, 128)],
+        functools.partial(acoustic_far_body, MIXES[0], False),
+        [held, faces, faces],
         partial,
         before,
         after,
         far,
-        source,
+        received,
     )
     before, after = traces(front, rear)
-
-    flow_two, send = call(
-        flow_second_body,
-        [(5, wide - 4, 16, 256), sent_shape],
+    received = route(send_next)
+    flow_state, send_next = call(
+        flow_last_body,
+        [(5, cells_x, 8, 128), sent],
         flow_one,
         start,
         pair,
         spread,
         labels,
-        scratch=scratch(wide - 2),
-    )
-    source = route(send)
-    partial, _, _ = call(
-        functools.partial(acoustic_local_body, MIXES[1], True),
-        [(4, 64, 128), (96, 128), (96, 128)],
-        sound_one,
-        sound,
-        source,
-        deriv_rows,
-        deriv_lanes,
-        speed,
-        near,
-    )
+        scratch=[pltpu.VMEM(planes(wide - 2), F32), rows_scratch, pltpu.VMEM(planes(wide - 4), F32)],
+    )
+
+    def local_part(mix, now):
+        return call(
+            functools.partial(acoustic_local_body, mix),
+            [held, faces, faces],
+            now,
+            sound,
+            deriv_rows,
+            deriv_lanes,
+            speed,
+            near,
+        )[0]
+
+    partial = local_part(MIXES[1], sound_one)
     sound_two, front, rear = call(
-        functools.partial(acoustic_far_body, factors[1], False, False),
-        [(4, 64, 128), (96, 128), (96, 128)],
+        functools.partial(acoustic_far_body, MIXES[1], False),
+        [held, faces, faces],
         partial,
         before,
         after,
         far,
+        received,
     )
     before, after = traces(front, rear)
-
-    flow_state, send = call(
-        flow_third_body,
-        [(5, cells_x, 8, 128), sent_shape],
-        flow_two,
-        start,
-        pair,
-        spread,
-        labels,
-        scratch=scratch(wide - 4),
-    )
-    source = route(send)
-    partial, _, _ = call(
-        functools.partial(acoustic_local_body, MIXES[2], True),
-        [(4, 64, 128), (96, 128), (96, 128)],
-        sound_two,
-        sound,
-        source,
-        deriv_rows,
-        deriv_lanes,
-        speed,
-        near,
-    )
-    sound_three = call(
-        functools.partial(acoustic_far_body, factors[2], False, True),
-        [(4, 64, 128)],
+    received = route(send_next)
+    partial = local_part(MIXES[2], sound_two)
+    sound_state, _ = call(
+        functools.partial(acoustic_far_body, MIXES[2], True),
+        [(elements, 4, 512), held],
         partial,
         before,
         after,
         far,
-    )[0]
-    sound_state = sound_three.reshape(4, 64, 8, elements).transpose(3, 0, 1, 2).reshape(elements, 4, 512)
+        received,
+        scratch=[pltpu.VMEM((512, 128), F32)],
+    )
     return (flow_state, sound_state)
 
 

time: 116 us -> 94.2 us (0.81)
  local copies, waits for them, and re-layouts: 26.2 us -> 7.31 us
  other arithmetic: 10.3 us -> 0.01 us
  starting transfers between devices: 46 us -> 50.7 us
  Pallas kernels: 17.8 us -> 20 us
  waiting for transfers between devices: 12.9 us -> 14.6 us
    mul x13 -> x0, local copies, waits for them, and re-layouts: 11.1 us -> none  [the longest x8 7.93 us: cross(): levels[:, None, :, None] * chooser[None, :, None, :]]
    ppermute x3, starting transfers between devices: 13.4 us -> 20.9 us  [traces(): lax.ppermute(front, names, forward)]
    mul x4 -> x0, other arithmetic: 3.38 us -> none  [the longest x1 1.57 us: routing_tables(): chooser.astype(F32)[:, None, :, None] * mode_basis.T[None, :, None, :]]
    another operation x3 -> x0, other arithmetic: 3.15 us -> none
    add x2 -> x0, local copies, waits for them, and re-layouts: 2.99 us -> none  [the longest x1 1.8 us: side_tables(): cross(jnp.asarray(put_first), far[4]) + cross(jnp.asarray(put_last), far[5])]
    unnamed x39 -> x17, local copies, waits for them, and re-layouts: 8.13 us -> 5.85 us
    transpose x3 -> x0, local copies, waits for them, and re-layouts: 2.19 us -> none  [the longest x1 1.04 us: per_device(): acoustic.reshape(elements, 4, 64, 8).transpose(1, 2, 3, 0)]
    pallas_call x14 -> x12, Pallas kernels: 17.8 us -> 20 us  [call(): pl.pallas_call(body, out_shape=outs, in_specs=[spec] * len(operands), out...]
  transfers between devices with their start and end apart: 16 -> 16, of which waited for: 3 -> 4; matrix products, arithmetic and copies ran while one was open for 27% -> 2% of each run, Pallas kernels for 11% -> 17%
where the time goes in v2:
time: 94.2 us; the launch traced here: 93.4 us
  starting transfers between devices  50.7 us (54%)
  Pallas kernels  20 us (21%)
  waiting for transfers between devices  14.6 us (15%)
  local copies, waits for them, and re-layouts  7.31 us (8%)
    ppermute x3, starting transfers between devices, traces(): lax.ppermute(front, names, forward)  20.9 us
    pallas_call x12, Pallas kernels, call(): pl.pallas_call(body, out_shape=outs, in_specs=[spec] * len(operands), out...  20 us
    all_to_all x3, starting transfers between devices, route(): return lax.all_to_all(send, 'fy', split_axis=0, concat_axis=0, tiled=True)  13.6 us
    ppermute x3, waiting for transfers between devices, traces(): lax.ppermute(rear, names, backward)  13.3 us
    unnamed x17, local copies, waits for them, and re-layouts  5.85 us
    ppermute x3, starting transfers between devices, traces(): lax.ppermute(rear, names, backward)  5.76 us
    ppermute x2, starting transfers between devices, per_device(): lax.ppermute(kept, ('fx', 'fy'), shifted(flat, (spots[0][0], dy)))  4.16 us
    ppermute x2, starting transfers between devices, per_device(): messages.append(lax.ppermute(kept, ('fx', 'fy'), shifted(flat, (0, dy))))  3.26 us
  transfers between devices with their start and end apart: 16, of which 4 were waited for; matrix products, arithmetic and copies ran while one was open for 2% of the time, Pallas kernels for 17%

profile of v2, /device:TPU:29, one launch (start us, length us, event | category | flops | bytes accessed | tf_op | source)
XLA Modules:
  0.0 93.4 jit_solution(5928399050805139692)
XLA Ops:
  0.6 0.9 copy-done.1
  1.5 0.8 copy-done.2
  2.3 0.8 copy-done.3
  3.2 0.7 collective-permute-start
  3.9 1.1 %collective-permute-start.1 = (f32[24,128]{1,0:T(8,128)S(1)}, f32[24,128]{1,0:T(8,128)S(1)}, u32[]{:S(2)}, u32[]{:S(2)}) collective-permute-start(f32[24,128]{1,0:T(8,128)S(1)} %get-tuple-element.40), channel_id=1, source_target_pairs={{3,0},{0,1},{1,2},{2,3},{7,4},{4,5},{5,6},{6,7},{11,8},{8,9},{9,10... | collective-permute-start | bytes 36872 | tf_op jit(solution)/shard_map/ppermute | solution.py:590
  5.0 0.8 copy.15
  5.7 1.0 %collective-permute-done.above = f32[24,128]{1,0:T(8,128)S(1)} collective-permute-done((f32[24,128]{1,0:T(8,128)S(1)}, f32[24,128]{1,0:T(8,128)S(1)}, u32[]{:S(2)}, u32[]{:S(2)}) %collective-permute-start) | collective-permute-done | bytes 12320 | tf_op jit(solution)/shard_map/ppermute | solution.py:589
  6.8 1.3 %collective-permute-start.2 = (f32[264,128]{1,0:T(8,128)S(1)}, f32[264,128]{1,0:T(8,128)S(1)}, u32[]{:S(2)}, u32[]{:S(2)}) collective-permute-start(f32[264,128]{1,0:T(8,128)S(1)} %get-tuple-element.42), channel_id=1, source_target_pairs={{16,0},{20,4},{24,8},{28,12},{0,16},{4,20},{8,24},{12,28},{17,1},{... | collective-permute-start | bytes 405512 | tf_op jit(solution)/shard_map/ppermute | solution.py:663
  8.2 3.1 %collective-permute-start.4 = (f32[144,128]{1,0:T(8,128)S(1)}, f32[144,128]{1,0:T(8,128)S(1)}, u32[]{:S(2)}, u32[]{:S(2)}) collective-permute-start(f32[144,128]{1,0:T(8,128)S(1)} %get-tuple-element.44), channel_id=1, source_target_pairs={{12,0},{0,4},{4,8},{8,12},{28,16},{16,20},{20,24},{24,28},{13,1},{... | collective-permute-start | bytes 221192 | tf_op jit(solution)/shard_map/ppermute | solution.py:666
  11.3 4.2 %collective-permute-start.6 = (f32[120,128]{1,0:T(8,128)S(1)}, f32[120,128]{1,0:T(8,128)S(1)}, u32[]{:S(2)}, u32[]{:S(2)}) collective-permute-start(f32[120,128]{1,0:T(8,128)S(1)} %get-tuple-element.46), channel_id=1, source_target_pairs={{28,0},{16,4},{20,8},{24,12},{12,16},{0,20},{4,24},{8,28},{29,1},{... | collective-permute-start | bytes 184328 | tf_op jit(solution)/shard_map/ppermute | solution.py:670
  15.5 0.7 copy.17.owner_column
  16.2 0.7 copy.18.element_column
  17.6 0.7 copy-done.5
  19.6 1.0 %shard_map.115 = (bf16[5,128,128]{2,1,0:T(8,128)(2,1)S(1)}, bf16[5,128,128]{2,1,0:T(8,128)(2,1)S(1)}, f32[128,64]{1,0:T(8,128)S(1)}, f32[128,128]{1,0:T(8,128)S(...) custom-call(f32[8,8]{1,0:T(8,128)S(1)} %copy-done.4, ...), custom_call_target="tpu_custom_call" | custom-call | tf_op jit(solution)/shard_map/pallas_call | solution.py:51
  20.7 2.5 %shard_map.116 = (f32[5,14,16,256]{3,2,1,0:T(8,128)S(1)}, f32[4,104,128]{2,1,0:T(8,128)}) custom-call(f32[5,8,8,128]{3,2,1,0:T(8,128)S(1)} %get-tuple-element.38.state.refs_0_, f32[24,128]{1,0:T(8,128)S(1)} %get-tuple-element.41.refs_1_, f32[264,128]{1,0:T(8,128)S(1)} %collective-permute-done.2.refs_2_, f32[144,128]{1,0:T(8,128)S(1)} %collective-permute-done.3.refs_3_, ...), custom_call_target="tpu_custom_call" | custom-call | tf_op jit(solution)/shard_map/pallas_call | solution.py:51
  23.2 4.5 %all-to-all-start = ((f32[4,104,128]{2,1,0:T(8,128)}), f32[4,104,128]{2,1,0:T(8,128)S(1)}, u32[]{:S(2)}, u32[]{:S(2)}) async-start(f32[4,104,128]{2,1,0:T(8,128)} %get-tuple-element.61), calls=%async_computation | async-start | bytes 425984 | tf_op jit(solution)/shard_map/all_to_all | solution.py:681
  27.7 4.9 %shard_map.117 = (f32[5,12,16,256]{3,2,1,0:T(8,128)S(1)}, f32[4,104,128]{2,1,0:T(8,128)}) custom-call(f32[5,14,16,256]{3,2,1,0:T(8,128)S(1)} %get-tuple-element.50.wide.start, f32[64,64]{1,0:T(8,128)S(1)} %get-tuple-element.47.refs_7_.pair, f32[128,512]{1,0:T(8,128)S(1)} %get-tuple-element.48.refs_8_.spread, f32[4,8,128]{2,1,0:T(8,128)S(1)} %get-tuple-element.49.refs_9_.labels), custom_call_target="tpu_custom_call" | custom-call | tf_op jit(solution)/shard_map/pallas_call | solution.py:51
  32.6 4.5 %all-to-all-start.1 = ((f32[4,104,128]{2,1,0:T(8,128)}), f32[4,104,128]{2,1,0:T(8,128)S(1)}, u32[]{:S(2)}, u32[]{:S(2)}) async-start(f32[4,104,128]{2,1,0:T(8,128)} %get-tuple-element.67), calls=%async_computation.1 | async-start | bytes 425984 | tf_op jit(solution)/shard_map/all_to_all | solution.py:681
  37.1 5.9 %shard_map.118 = (f32[5,8,8,128]{3,2,1,0:T(8,128)}, f32[4,104,128]{2,1,0:T(8,128)}) custom-call(f32[5,12,16,256]{3,2,1,0:T(8,128)S(1)} %get-tuple-element.51.wide, f32[5,14,16,256]{3,2,1,0:T(8,128)S(1)} %get-tuple-element.50.wide.start, f32[64,64]{1,0:T(8,128)S(1)} %get-tuple-element.47.refs_7_.pair, f32[128,512]{1,0:T(8,128)S(1)} %get-tuple-element.48.refs_8_.spread, ...), custom_call_target="tpu_custom_call" | custom-call | tf_op jit(solution)/shard_map/pallas_call | solution.py:51
  43.1 4.5 %all-to-all-start.2 = ((f32[4,104,128]{2,1,0:T(8,128)}), f32[4,104,128]{2,1,0:T(8,128)S(1)}, u32[]{:S(2)}, u32[]{:S(2)}) async-start(f32[4,104,128]{2,1,0:T(8,128)} %get-tuple-element.72), calls=%async_computation.2 | async-start | bytes 425984 | tf_op jit(solution)/shard_map/all_to_all | solution.py:681
  47.6 1.0 %shard_map.119 = (f32[4,64,128]{2,1,0:T(8,128)S(1)}, f32[4,64,128]{2,1,0:T(8,128)S(1)}, f32[96,128]{1,0:T(8,128)S(1)}, f32[96,128]{1,0:T(8,128)S(1)}) custom-call(f32[16,4,512]{2,1,0:T(4,128)S(1)} %copy-done, f32[128,64]{1,0:T(8,128)S(1)} %get-tuple-element.53.deriv_rows, f32[128,128]{1,0:T(8,128)S(1)} %get-tuple-element.54.deriv_lanes, ...), custom_call_target="tpu_custom_call" | custom-call | tf_op jit(solution)/shard_map/pallas_call | solution.py:51
  48.6 5.8 %collective-permute-start.7 = (f32[96,128]{1,0:T(8,128)S(1)}, f32[96,128]{1,0:T(8,128)S(1)}, u32[]{:S(2)}, u32[]{:S(2)}) collective-permute-start(f32[96,128]{1,0:T(8,128)S(1)} %get-tuple-element.58), channel_id=1, source_target_pairs={{0,1},{1,2},{2,3},{3,4},{4,5},{5,6},{6,7},{7,8},{8,9},{9,10},{10,1... | collective-permute-start | bytes 147464 | tf_op jit(solution)/shard_map/ppermute | solution.py:625
  54.4 1.9 %collective-permute-start.8 = (f32[96,128]{1,0:T(8,128)S(1)}, f32[96,128]{1,0:T(8,128)S(1)}, u32[]{:S(2)}, u32[]{:S(2)}) collective-permute-start(f32[96,128]{1,0:T(8,128)S(1)} %get-tuple-element.59), channel_id=1, source_target_pairs={{1,0},{2,1},{3,2},{4,3},{5,4},{6,5},{7,6},{8,7},{9,8},{10,9},{11,1... | collective-permute-start | bytes 147464 | tf_op jit(solution)/shard_map/ppermute | solution.py:625
  56.3 7.1 %collective-permute-done.8.refs_2_ = f32[96,128]{1,0:T(8,128)S(1)} collective-permute-done((f32[96,128]{1,0:T(8,128)S(1)}, f32[96,128]{1,0:T(8,128)S(1)}, u32[]{:S(2)}, u32[]{:S(2)}) %collective-permute-start.8) | collective-permute-done | bytes 49184 | tf_op jit(solution)/shard_map/ppermute | solution.py:625
  63.9 1.9 %collective-permute-start.10 = (f32[96,128]{1,0:T(8,128)S(1)}, f32[96,128]{1,0:T(8,128)S(1)}, u32[]{:S(2)}, u32[]{:S(2)}) collective-permute-start(f32[96,128]{1,0:T(8,128)S(1)} %get-tuple-element.66), channel_id=1, source_target_pairs={{1,0},{2,1},{3,2},{4,3},{5,4},{6,5},{7,6},{8,7},{9,8},{10,9},{11,1... | collective-permute-start | bytes 147464 | tf_op jit(solution)/shard_map/ppermute | solution.py:625
  65.8 7.2 %collective-permute-start.9 = (f32[96,128]{1,0:T(8,128)S(1)}, f32[96,128]{1,0:T(8,128)S(1)}, u32[]{:S(2)}, u32[]{:S(2)}) collective-permute-start(f32[96,128]{1,0:T(8,128)S(1)} %get-tuple-element.65), channel_id=1, source_target_pairs={{0,1},{1,2},{2,3},{3,4},{4,5},{5,6},{6,7},{7,8},{8,9},{9,10},{10,1... | collective-permute-start | bytes 147464 | tf_op jit(solution)/shard_map/ppermute | solution.py:625
  73.1 0.9 shard_map.121
  74.8 7.8 %collective-permute-start.11 = (f32[96,128]{1,0:T(8,128)S(1)}, f32[96,128]{1,0:T(8,128)S(1)}, u32[]{:S(2)}, u32[]{:S(2)}) collective-permute-start(f32[96,128]{1,0:T(8,128)S(1)} %get-tuple-element.70), channel_id=1, source_target_pairs={{0,1},{1,2},{2,3},{3,4},{4,5},{5,6},{6,7},{7,8},{8,9},{9,10},{10,1... | collective-permute-start | bytes 147464 | tf_op jit(solution)/shard_map/ppermute | solution.py:625
  82.6 1.9 %collective-permute-start.12 = (f32[96,128]{1,0:T(8,128)S(1)}, f32[96,128]{1,0:T(8,128)S(1)}, u32[]{:S(2)}, u32[]{:S(2)}) collective-permute-start(f32[96,128]{1,0:T(8,128)S(1)} %get-tuple-element.71), channel_id=1, source_target_pairs={{1,0},{2,1},{3,2},{4,3},{5,4},{6,5},{7,6},{8,7},{9,8},{10,9},{11,1... | collective-permute-start | bytes 147464 | tf_op jit(solution)/shard_map/ppermute | solution.py:625
  84.6 0.9 shard_map.123
  85.4 6.2 %collective-permute-done.12.refs_2_ = f32[96,128]{1,0:T(8,128)S(1)} collective-permute-done((f32[96,128]{1,0:T(8,128)S(1)}, f32[96,128]{1,0:T(8,128)S(1)}, u32[]{:S(2)}, u32[]{:S(2)}) %collective-permute-start.12) | collective-permute-done | bytes 49184 | tf_op jit(solution)/shard_map/ppermute | solution.py:625
  91.6 1.7 %shard_map.124 = (f32[16,4,512]{2,1,0:T(4,128)}, f32[4,64,128]{2,1,0:T(8,128)}) custom-call(f32[4,64,128]{2,1,0:T(8,128)S(1)} %get-tuple-element.69.refs_0_, f32[96,128]{1,0:T(8,128)S(1)} %collective-permute-done.11.refs_1_, f32[96,128]{1,0:T(8,128)S(1)} %collective-permute-done.12.refs_2_, bf16[5,128,128]{2,1,0:T(8,128)(2,1)S(1)} %get-tuple-element.60.refs_3_, ...), custom_call_target="tpu_custom_call" | custom-call | tf_op jit(solution)/shard_map/pallas_call | solution.py:51
  (32 shorter events, 3.7 us)
Async XLA Ops:
  0.6 0.9 copy-start.1
  1.5 0.8 copy-start.2
  2.3 0.8 copy-start.3
  3.2 3.5 %collective-permute-start = (f32[24,128]{1,0:T(8,128)S(1)}, f32[24,128]{1,0:T(8,128)S(1)}, u32[]{:S(2)}, u32[]{:S(2)}) collective-permute-start(f32[24,128]{1,0:T(8,128)S(1)} %get-tuple-element.39), channel_id=1, source_target_pairs={{1,0},{2,1},{3,2},{0,3},{5,4},{6,5},{7,6},{4,7},{9,8},{10,9},{11,1... | collective-permute-start | bytes 36872 | tf_op jit(solution)/shard_map/ppermute | solution.py:589
  3.9 2.8 %collective-permute-start.1 = (f32[24,128]{1,0:T(8,128)S(1)}, f32[24,128]{1,0:T(8,128)S(1)}, u32[]{:S(2)}, u32[]{:S(2)}) collective-permute-start(f32[24,128]{1,0:T(8,128)S(1)} %get-tuple-element.40), channel_id=1, source_target_pairs={{3,0},{0,1},{1,2},{2,3},{7,4},{4,5},{5,6},{6,7},{11,8},{8,9},{9,10... | collective-permute-start | bytes 36872 | tf_op jit(solution)/shard_map/ppermute | solution.py:590
  6.8 13.9 %collective-permute-start.2 = (f32[264,128]{1,0:T(8,128)S(1)}, f32[264,128]{1,0:T(8,128)S(1)}, u32[]{:S(2)}, u32[]{:S(2)}) collective-permute-start(f32[264,128]{1,0:T(8,128)S(1)} %get-tuple-element.42), channel_id=1, source_target_pairs={{16,0},{20,4},{24,8},{28,12},{0,16},{4,20},{8,24},{12,28},{17,1},{... | collective-permute-start | bytes 405512 | tf_op jit(solution)/shard_map/ppermute | solution.py:663
  8.0 12.6 %collective-permute-start.3 = (f32[144,128]{1,0:T(8,128)S(1)}, f32[144,128]{1,0:T(8,128)S(1)}, u32[]{:S(2)}, u32[]{:S(2)}) collective-permute-start(f32[144,128]{1,0:T(8,128)S(1)} %get-tuple-element.43), channel_id=1, source_target_pairs={{4,0},{8,4},{12,8},{0,12},{20,16},{24,20},{28,24},{16,28},{5,1},{9... | collective-permute-start | bytes 221192 | tf_op jit(solution)/shard_map/ppermute | solution.py:666
  8.2 12.4 %collective-permute-start.4 = (f32[144,128]{1,0:T(8,128)S(1)}, f32[144,128]{1,0:T(8,128)S(1)}, u32[]{:S(2)}, u32[]{:S(2)}) collective-permute-start(f32[144,128]{1,0:T(8,128)S(1)} %get-tuple-element.44), channel_id=1, source_target_pairs={{12,0},{0,4},{4,8},{8,12},{28,16},{16,20},{20,24},{24,28},{13,1},{... | collective-permute-start | bytes 221192 | tf_op jit(solution)/shard_map/ppermute | solution.py:666
  11.3 9.3 %collective-permute-start.5 = (f32[120,128]{1,0:T(8,128)S(1)}, f32[120,128]{1,0:T(8,128)S(1)}, u32[]{:S(2)}, u32[]{:S(2)}) collective-permute-start(f32[120,128]{1,0:T(8,128)S(1)} %get-tuple-element.45), channel_id=1, source_target_pairs={{20,0},{24,4},{28,8},{16,12},{4,16},{8,20},{12,24},{0,28},{21,1},{... | collective-permute-start | bytes 184328 | tf_op jit(solution)/shard_map/ppermute | solution.py:670
  11.3 9.3 %collective-permute-start.6 = (f32[120,128]{1,0:T(8,128)S(1)}, f32[120,128]{1,0:T(8,128)S(1)}, u32[]{:S(2)}, u32[]{:S(2)}) collective-permute-start(f32[120,128]{1,0:T(8,128)S(1)} %get-tuple-element.46), channel_id=1, source_target_pairs={{28,0},{16,4},{20,8},{24,12},{12,16},{0,20},{4,24},{8,28},{29,1},{... | collective-permute-start | bytes 184328 | tf_op jit(solution)/shard_map/ppermute | solution.py:670
  16.9 0.7 copy-start.4
  17.6 0.7 copy-start.5
  18.3 0.7 copy-start.6
  19.0 0.7 copy-start.7
  23.2 9.4 %all-to-all-start = ((f32[4,104,128]{2,1,0:T(8,128)}), f32[4,104,128]{2,1,0:T(8,128)S(1)}, u32[]{:S(2)}, u32[]{:S(2)}) async-start(f32[4,104,128]{2,1,0:T(8,128)} %get-tuple-element.61), calls=%async_computation | async-start | bytes 425984 | tf_op jit(solution)/shard_map/all_to_all | solution.py:681
  32.6 10.5 %all-to-all-start.1 = ((f32[4,104,128]{2,1,0:T(8,128)}), f32[4,104,128]{2,1,0:T(8,128)S(1)}, u32[]{:S(2)}, u32[]{:S(2)}) async-start(f32[4,104,128]{2,1,0:T(8,128)} %get-tuple-element.67), calls=%async_computation.1 | async-start | bytes 425984 | tf_op jit(solution)/shard_map/all_to_all | solution.py:681
  37.1 10.5 %copy-start = (f32[16,4,512]{2,1,0:T(4,128)S(1)}, f32[16,4,512]{2,1,0:T(4,128)}, u32[]{:S(2)}) copy-start(f32[16,4,512]{2,1,0:T(4,128)} %given.1) | copy-start | bytes 393220
  43.1 42.3 %all-to-all-start.2 = ((f32[4,104,128]{2,1,0:T(8,128)}), f32[4,104,128]{2,1,0:T(8,128)S(1)}, u32[]{:S(2)}, u32[]{:S(2)}) async-start(f32[4,104,128]{2,1,0:T(8,128)} %get-tuple-element.72), calls=%async_computation.2 | async-start | bytes 425984 | tf_op jit(solution)/shard_map/all_to_all | solution.py:681
  48.6 7.7 %collective-permute-start.7 = (f32[96,128]{1,0:T(8,128)S(1)}, f32[96,128]{1,0:T(8,128)S(1)}, u32[]{:S(2)}, u32[]{:S(2)}) collective-permute-start(f32[96,128]{1,0:T(8,128)S(1)} %get-tuple-element.58), channel_id=1, source_target_pairs={{0,1},{1,2},{2,3},{3,4},{4,5},{5,6},{6,7},{7,8},{8,9},{9,10},{10,1... | collective-permute-start | bytes 147464 | tf_op jit(solution)/shard_map/ppermute | solution.py:625
  54.4 9.0 %collective-permute-start.8 = (f32[96,128]{1,0:T(8,128)S(1)}, f32[96,128]{1,0:T(8,128)S(1)}, u32[]{:S(2)}, u32[]{:S(2)}) collective-permute-start(f32[96,128]{1,0:T(8,128)S(1)} %get-tuple-element.59), channel_id=1, source_target_pairs={{1,0},{2,1},{3,2},{4,3},{5,4},{6,5},{7,6},{8,7},{9,8},{10,9},{11,1... | collective-permute-start | bytes 147464 | tf_op jit(solution)/shard_map/ppermute | solution.py:625
  63.9 10.0 %collective-permute-start.10 = (f32[96,128]{1,0:T(8,128)S(1)}, f32[96,128]{1,0:T(8,128)S(1)}, u32[]{:S(2)}, u32[]{:S(2)}) collective-permute-start(f32[96,128]{1,0:T(8,128)S(1)} %get-tuple-element.66), channel_id=1, source_target_pairs={{1,0},{2,1},{3,2},{4,3},{5,4},{6,5},{7,6},{8,7},{9,8},{10,9},{11,1... | collective-permute-start | bytes 147464 | tf_op jit(solution)/shard_map/ppermute | solution.py:625
  65.8 8.4 %collective-permute-start.9 = (f32[96,128]{1,0:T(8,128)S(1)}, f32[96,128]{1,0:T(8,128)S(1)}, u32[]{:S(2)}, u32[]{:S(2)}) collective-permute-start(f32[96,128]{1,0:T(8,128)S(1)} %get-tuple-element.65), channel_id=1, source_target_pairs={{0,1},{1,2},{2,3},{3,4},{4,5},{5,6},{6,7},{7,8},{8,9},{9,10},{10,1... | collective-permute-start | bytes 147464 | tf_op jit(solution)/shard_map/ppermute | solution.py:625
  74.8 10.7 %collective-permute-start.11 = (f32[96,128]{1,0:T(8,128)S(1)}, f32[96,128]{1,0:T(8,128)S(1)}, u32[]{:S(2)}, u32[]{:S(2)}) collective-permute-start(f32[96,128]{1,0:T(8,128)S(1)} %get-tuple-element.70), channel_id=1, source_target_pairs={{0,1},{1,2},{2,3},{3,4},{4,5},{5,6},{6,7},{7,8},{8,9},{9,10},{10,1... | collective-permute-start | bytes 147464 | tf_op jit(solution)/shard_map/ppermute | solution.py:625
  82.6 9.0 %collective-permute-start.12 = (f32[96,128]{1,0:T(8,128)S(1)}, f32[96,128]{1,0:T(8,128)S(1)}, u32[]{:S(2)}, u32[]{:S(2)}) collective-permute-start(f32[96,128]{1,0:T(8,128)S(1)} %get-tuple-element.71), channel_id=1, source_target_pairs={{1,0},{2,1},{3,2},{4,3},{5,4},{6,5},{7,6},{8,7},{9,8},{10,9},{11,1... | collective-permute-start | bytes 147464 | tf_op jit(solution)/shard_map/ppermute | solution.py:625

commit v3 on v2

--- a/solution.py
+++ b/solution.py
@@ -45,20 +45,50 @@
     return dot(left_high, right) + dot(left_low, right)
 
 
-def call(body, outs, *operands, scratch=(), fetch=False):
-    spec = pl.BlockSpec() if fetch else pl.BlockSpec(memory_space=pltpu.VMEM)
+def call(body, outs, *operands, scratch=(), fetch=False, flags=None):
+    whole = pl.BlockSpec(memory_space=pltpu.VMEM)
     outs = [out if isinstance(out, jax.ShapeDtypeStruct) else jax.ShapeDtypeStruct(out, F32) for out in outs]
+    scratch = list(scratch)
+    specs = [pl.BlockSpec(memory_space=pl.ANY) if fetch else whole] * len(operands)
+    params = PARAMS
+    kernel = body
+    if fetch:
+        count = len(operands)
+        params = pltpu.CompilerParams(vmem_limit_bytes=60 * 1024 * 1024)
+        first = 1 if flags is not None else 0
+        total = first + count + len(outs)
+
+        def kernel(*refs):
+            held, sems = refs[total : total + count], refs[total + count]
+            copies = [
+                pltpu.make_async_copy(refs[first + i], held[i], sems.at[i]) for i in range(count)
+            ]
+            for copy in copies:
+                copy.start()
+            for copy in copies:
+                copy.wait()
+            body(*refs[:first], *held, *refs[first + count : total], *refs[total + count + 1 :])
+
+        scratch = [pltpu.VMEM(o.shape, o.dtype) for o in operands] + [pltpu.SemaphoreType.DMA((count,))] + scratch
+    if flags is not None:
+        specs = [pl.BlockSpec(memory_space=pltpu.SMEM)] + specs
+        operands = (flags,) + operands
     return pl.pallas_call(
-        body,
+        kernel,
         out_shape=outs,
-        in_specs=[spec] * len(operands),
-        out_specs=[pl.BlockSpec(memory_space=pltpu.VMEM)] * len(outs),
-        scratch_shapes=list(scratch),
-        compiler_params=PARAMS,
+        in_specs=specs,
+        out_specs=[whole] * len(outs),
+        scratch_shapes=scratch,
+        compiler_params=params,
     )(*operands)
 
 
-def pack_start_body(density, velocity, pressure, state, low, high):
+def paired(odd, to_next, to_last):
+    return jnp.where(odd, to_last, to_next), jnp.where(odd, to_next, to_last)
+
+
+def pack_start_body(flags, density, velocity, pressure, state, message_a, message_b):
+    odd = flags[0] == 1
     rho = density[...]
     vel = velocity[...]
     state[0] = rho
@@ -68,33 +98,41 @@
     state[4] = pressure[...] / (HEAT_RATIO - 1.0) + 0.5 * rho * square
     rows = state[...].reshape(-1, 128)
     count = rows.shape[0]
-    for tile in range(low.shape[0] // 8):
+    for tile in range(message_a.shape[0] // 8):
         piece = rows[tile * 128 : min(count, tile * 128 + 128)]
         if piece.shape[0] < 128:
             piece = jnp.concatenate([piece, jnp.zeros((128 - piece.shape[0], 128), F32)], 0)
         turned = piece.T
-        low[tile * 8 : tile * 8 + 8] = turned[0:8]
-        high[tile * 8 : tile * 8 + 8] = turned[120:128]
-
-
-def pack_next_body(state, above, below, edge, along_x, y_low, y_high, xy_low, xy_high):
+        first, second = paired(odd, turned[120:128], turned[0:8])
+        message_a[tile * 8 : tile * 8 + 8] = first
+        message_b[tile * 8 : tile * 8 + 8] = second
+
+
+def pack_next_body(flags, state, got_a, got_b, edge, along_x, y_a, y_b, xy_a, xy_b):
     cells_x = state.shape[1]
+    odd_z, odd = flags[0] == 1, flags[1] == 1
     row = lax.broadcasted_iota(jnp.int32, edge.shape, 0) % 8
-    both = jnp.where(row < 4, above[...], below[...])
+    above, below = paired(odd_z, got_a[...], got_b[...])
+    both = jnp.where(row < 4, above, below)
     edge[...] = both
     planes = [cells_x - HALO + i for i in range(HALO)] + list(range(HALO))
     for f in range(5):
         for s, x in enumerate(planes):
             at = (f * len(planes) + s) * 8
             along_x[at : at + 8] = state[f, x]
-            at = (f * len(planes) + s) * HALO
-            xy_low[at : at + HALO] = state[f, x, 0:HALO]
-            xy_high[at : at + HALO] = state[f, x, 8 - HALO : 8]
         for x in range(cells_x):
             at = (f * cells_x + x) * HALO
-            y_low[at : at + HALO] = state[f, x, 0:HALO]
-            y_high[at : at + HALO] = state[f, x, 8 - HALO : 8]
-    for message in (along_x, y_low, y_high, xy_low, xy_high):
+            first, second = paired(odd, state[f, x, 8 - HALO : 8], state[f, x, 0:HALO])
+            y_a[at : at + HALO] = first
+            y_b[at : at + HALO] = second
+        at = f * 6
+        for slot, height in ((1, 1), (2, 2), (3, 2), (4, 1)):
+            x = planes[slot]
+            first, second = paired(odd, state[f, x, 8 - height : 8], state[f, x, 0:height])
+            xy_a[at : at + height] = first
+            xy_b[at : at + height] = second
+            at += height
+    for message in (along_x, y_a, y_b, xy_a, xy_b):
         size = message.shape[0]
         message[size - edge.shape[0] : size] = both
 
@@ -109,7 +147,6 @@
 
 
 def assemble(wide, state, edge, beside, cells_x):
-    six = 2 * HALO
     for dx, dy, message in [(0, 0, edge)] + beside:
         turned = turned_edges(message)
         if dx == 0:
@@ -118,20 +155,24 @@
             columns = [(i, cells_x - HALO + i, i) for i in range(HALO)]
         else:
             columns = [(HALO + cells_x + i, i, HALO + i) for i in range(HALO)]
-        slots = cells_x if dx == 0 else six
-        target = {0: (0, 8), 1: (8, 8 + HALO), -1: (16 - HALO, 16)}[dy]
-        source = {0: (0, 8), 1: (0, HALO), -1: (8 - HALO, 8)}[dy]
-        height = target[1] - target[0]
         for f in range(5):
             for plane, x, slot in columns:
+                height = 8 if dy == 0 else HALO
+                at = (f * (cells_x if dx == 0 else 2 * HALO) + slot) * height
+                if dx != 0 and dy != 0:
+                    if slot in (0, 5):
+                        continue
+                    height = (0, 1, 2, 2, 1)[slot]
+                    at = f * 6 + (0, 0, 1, 3, 5)[slot]
+                low, high = {0: (0, 8), 1: (8, 8 + height), -1: (16 - height, 16)}[dy]
                 if dx == 0 and dy == 0:
                     wide[f, plane, 0:8, 0:128] = state[f, x]
                 else:
-                    at = (f * slots + slot) * height
-                    wide[f, plane, target[0] : target[1], 0:128] = message[at : at + height]
+                    wide[f, plane, low:high, 0:128] = message[at : at + height]
                 group = f * cells_x + x
                 block = turned[group // 16][(group % 16) * 8 : (group % 16) * 8 + 8]
-                wide[f, plane, target[0] : target[1], 128:256] = block[source[0] : source[1]]
+                first = 8 - height if dy < 0 else 0
+                wide[f, plane, low:high, 128:256] = block[first : first + height]
 
 
 def derive_planes(wide, derived, first, last):
@@ -258,22 +299,33 @@
     send[:, 3 * height : 3 * height + 8] = labels[...]
 
 
-def flow_sources_body(places, *refs):
+def flow_sources_body(places, flags, *refs):
     state, edge = refs[0:2]
     messages = refs[2 : 2 + len(places)]
     pair, spread, labels = refs[2 + len(places) : 5 + len(places)]
-    wide, send, derived, lamb_rows = refs[5 + len(places) :]
+    wide, send, derived, lamb_rows = refs[5 + len(places) : 9 + len(places)]
+    spare = refs[9 + len(places) :]
     cells_x = state.shape[1]
-    beside = []
-    for message, spots in zip(messages, places):
-        beside.extend((dx, dy, message) for dx, dy in spots)
+    odd = flags[1] == 1
+    beside, k = [], 0
+    while k < len(places):
+        if places[k][0][1] == 0:
+            beside.extend((dx, 0, messages[k]) for dx, _ in places[k])
+            k += 1
+            continue
+        above, below = spare[:2]
+        spare = spare[2:]
+        above[...], below[...] = paired(odd, messages[k][...], messages[k + 1][...])
+        beside.extend((dx, 1, above) for dx, _ in places[k])
+        beside.extend((dx, -1, below) for dx, _ in places[k])
+        k += 2
     assemble(wide, state, edge, beside, cells_x)
     derive_speeds(wide, derived, HALO - 1, HALO + cells_x + 1)
     lamb(derived, HALO, cells_x, lamb_rows)
     project(lamb_rows, pair, spread, labels, send)
 
 
-def flow_first_body(wide, pair, spread, labels, out, send, derived, lamb_rows):
+def flow_first_body(wide, out, lamb_rows, derived):
     def write(i, f, value):
         out[f, i] = value
 
@@ -283,7 +335,6 @@
     flow_rate_section(wide, derived, wide, 0, MIXES[0], write)
     derive_speeds(out, derived, HALO - 2, HALO + cells_x)
     lamb(derived, HALO - 1, cells_x, lamb_rows)
-    project(lamb_rows, pair, spread, labels, send)
 
 
 def flow_last_body(wide, start, pair, spread, labels, out, send, derived, lamb_rows, second):
@@ -319,6 +370,11 @@
         first = jnp.where(lane == j, pltpu.roll(piece, j * 16, 1) if j else piece, first)
     front[64:96] = last
     rear[64:96] = first
+
+
+def faces_sent(odd, state, message_a, message_b):
+    faces_out(state, message_b, message_a)
+    message_a[...], message_b[...] = paired(odd, message_a[...], message_b[...])
 
 
 def lift(total, before, after, sides, factor):
@@ -376,7 +432,9 @@
     return (column == (row % count) * 4 + row // count).astype(F32)
 
 
-def acoustic_first_body(given, deriv_rows, deriv_lanes, speed, sides, state, out, front, rear, turned):
+def acoustic_first_body(
+    flags, given, deriv_rows, deriv_lanes, speed, sides, state, out, message_a, message_b, turned, front, rear
+):
     count = given.shape[0]
     rows = jnp.concatenate([given[e] for e in range(count)], 0)
     rows = dot_full(order_table(count, False), rows)
@@ -392,6 +450,7 @@
     for c in range(4):
         state[c] = fields[c]
     local_update(MIXES[0], state, state, deriv_rows, deriv_lanes, speed, sides, out, front, rear)
+    message_a[...], message_b[...] = paired(flags[0] == 1, front[...], rear[...])
 
 
 def natural_order(state, out, turned):
@@ -422,19 +481,24 @@
         out[c] += value[c * 64 : c * 64 + 64]
 
 
-def acoustic_far_body(mix, last, *refs):
-    partial, before, after, sides_far, received = refs[0:5]
-    if last:
-        given_out, out, turned = refs[5:]
+def acoustic_far_body(mix, kind, flags, partial, got_a, got_b, sides_far, received, *refs):
+    odd = flags[0] == 1
+    if kind == "last":
+        given_out, out, turned, before, after = refs
+    elif kind == "first":
+        lamb_rows, pair, spread, labels, out, message_a, message_b, send, before, after = refs
     else:
-        out, front, rear = refs[5:]
+        out, message_a, message_b, before, after = refs
+    after[...], before[...] = paired(odd, got_a[...], got_b[...])
     out[...] = partial[...]
+    remote_part(out, before, after, sides_far, TIME_STEP * mix[1] * PENALTY)
     place(received, out, TIME_STEP * mix[1])
-    remote_part(out, before, after, sides_far, TIME_STEP * mix[1] * PENALTY)
-    if last:
+    if kind == "last":
         natural_order(out, given_out, turned)
-    else:
-        faces_out(out, rear, front)
+        return
+    faces_sent(odd, out, message_a, message_b)
+    if kind == "first":
+        project(lamb_rows, pair, spread, labels, send)
 
 
 def place(received, out, factor):
@@ -474,13 +538,7 @@
 
 
 def tables_body(
-    derivative,
-    basis,
-    local,
-    owner_column,
-    owner_row,
-    element_column,
-    sound_speed,
+    packed,
     near,
     far,
     deriv_rows,
@@ -490,16 +548,17 @@
     labels,
     speed,
 ):
-    count = local.shape[0]
-    size = 8 * count
+    size = near.shape[1]
+    count = size // 8
+    blocks = spread.shape[0] // 8
 
     def place_of(shape):
         return (lax.broadcasted_iota(jnp.int32, shape, 0), lax.broadcasted_iota(jnp.int32, shape, 1))
 
     row, column = place_of((count, size))
     repeat = (column % count == row).astype(F32)
-    speed[...] = dot_full(sound_speed[...], repeat)
-    wanted = dot_full(local[...].astype(F32), repeat, ((0,), (0,))).astype(jnp.int32)
+    speed[...] = dot_full(packed[24:25, 0:count], repeat)
+    wanted = dot_full(packed[16:24, 0:count], repeat).astype(jnp.int32)
     row, column = place_of((size, size))
     level, element = row // count, row % count
     level_out = column // count
@@ -518,7 +577,7 @@
     far[4] = jnp.where(hit, 1.0, 0.0).astype(BF16)
 
     row, column = place_of((64, 64))
-    slopes, modes = derivative[...], basis[...]
+    slopes, modes = packed[0:8, 0:8], packed[8:16, 0:8]
     outer = kron_part(slopes, (64, 64), 8, 8)
     inner = kron_part(slopes, (64, 64), 1, 1)
     deriv_rows[0:64] = jnp.where(row % 8 == column % 8, outer, 0.0)
@@ -528,18 +587,24 @@
     deriv_lanes[...] = jnp.where(row % count == column % count, lanes, 0.0)
     pair[...] = kron_part(modes, (64, 64), 8, 8) * kron_part(modes, (64, 64), 1, 1)
 
-    blocks = owner_column.shape[0]
     peers = labels.shape[0]
     capacity = max(2, 2 * blocks // peers)
     row, column = place_of((blocks, blocks))
-    earlier = (owner_column[...] == owner_row[...]) & (column < row)
+
+    def upright(values):
+        return jnp.sum(jnp.where(row == column, values, 0.0), 1, keepdims=True)
+
+    owner_row = packed[25:26, 0:blocks]
+    owner_column = upright(owner_row)
+    earlier = (owner_column == owner_row) & (column < row)
     position = jnp.sum(jnp.where(earlier, 1.0, 0.0), 1, keepdims=True)
-    slot = owner_column[...].astype(F32) * capacity + position
+    slot = owner_column * capacity + position
+    element_column = upright(packed[26:27, 0:blocks])
     wide = (8 * blocks, peers * 128)
     row, column = place_of((8 * blocks, blocks))
     repeat = (row // 8 == column).astype(F32)
     slot = dot_full(repeat, jnp.broadcast_to(slot, (blocks, 128)))
-    element = dot_full(repeat, jnp.broadcast_to(element_column[...].astype(F32), (blocks, 128)))
+    element = dot_full(repeat, jnp.broadcast_to(element_column, (blocks, 128)))
     row, column = place_of((8 * blocks, 128))
     values = kron_part(modes.T, (8 * blocks, 128), 1, 1)
     inside = column % (8 * capacity) // 8
@@ -554,6 +619,18 @@
     pairs = []
     for index in np.ndindex(*sizes):
         source = [(i + s) % n for i, s, n in zip(index, shifts, sizes)]
+        pairs.append((int(np.ravel_multi_index(source, sizes)), int(np.ravel_multi_index(index, sizes))))
+    return pairs
+
+
+def partners(sizes, axis, second, shift_x=0):
+    pairs = []
+    for index in np.ndindex(*sizes):
+        source = list(index)
+        step = 1 if (index[axis] % 2 == 0) != second else -1
+        source[axis] = (index[axis] + step) % sizes[axis]
+        if shift_x:
+            source[0] = (index[0] + shift_x) % sizes[0]
         pairs.append((int(np.ravel_multi_index(source, sizes)), int(np.ravel_multi_index(index, sizes))))
     return pairs
 
@@ -576,24 +653,40 @@
     elements = acoustic.shape[0]
     device = lax.axis_index(("fx", "fy", "fz"))
 
+    names = ("fx", "fy", "fz")
+    flags = jnp.stack([lax.axis_index("fz") % 2, lax.axis_index("fy") % 2]).astype(jnp.int32)
+
     rows = 5 * cells_x * 8
     tiles = -(-rows // 128)
-    state, low, high = call(
+    state, to_a, to_b = call(
         pack_start_body,
         [(5, cells_x, 8, 128), (tiles * 8, 128), (tiles * 8, 128)],
         density,
         velocity,
         pressure,
         fetch=True,
-    )
-    above = lax.ppermute(low, "fz", shifted((size_z,), (1,)))
-    below = lax.ppermute(high, "fz", shifted((size_z,), (-1,)))
-
-    local = neighbours - device * elements
+        flags=flags,
+    )
+    edge_a = lax.ppermute(to_a, "fz", partners((size_z,), 0, False))
+    edge_b = lax.ppermute(to_b, "fz", partners((size_z,), 0, True))
+
+    local = (neighbours - device * elements).T.astype(F32)
     size = 8 * elements
     blocks = block_owner.size
     capacity = max(2, 2 * blocks // size_y)
     fold = 128 // (8 * capacity)
+    width = max(elements, blocks)
+    packed = jnp.concatenate(
+        [
+            jnp.pad(derivative, ((0, 0), (0, width - 8))),
+            jnp.pad(mode_basis, ((0, 0), (0, width - 8))),
+            jnp.pad(local, ((0, 2), (0, width - elements))),
+            jnp.pad(sound_speed.reshape(1, elements), ((0, 0), (0, width - elements))),
+            jnp.pad(block_owner.reshape(1, blocks).astype(F32), ((0, 0), (0, width - blocks))),
+            jnp.pad(block_element.reshape(1, blocks).astype(F32), ((0, 5), (0, width - blocks))),
+        ],
+        0,
+    )
     table = jax.ShapeDtypeStruct((5, size, size), BF16)
     near, far, deriv_rows, deriv_lanes, pair, spread, labels, speed = call(
         tables_body,
@@ -607,26 +700,20 @@
             (size_y, 8, 128),
             (1, size),
         ],
-        derivative,
-        mode_basis,
-        local,
-        block_owner.reshape(blocks, 1),
-        block_owner.reshape(1, blocks),
-        block_element.reshape(blocks, 1),
-        sound_speed.reshape(1, elements),
-        fetch=True,
-    )
-
-    forward = [(i, i + 1) for i in range(devices - 1)]
-    backward = [(i + 1, i) for i in range(devices - 1)]
-    names = ("fx", "fy", "fz")
-
-    def traces(front, rear):
-        return lax.ppermute(front, names, forward), lax.ppermute(rear, names, backward)
+        packed,
+    )
+
+    near_pairs = [(i ^ 1, i) for i in range(devices)]
+    far_pairs = [pair for i in range(1, devices - 1, 2) for pair in ((i, i + 1), (i + 1, i))]
+
+    def traces(to_a, to_b):
+        far_got = lax.ppermute(to_b, names, far_pairs)
+        return lax.ppermute(to_a, names, near_pairs), far_got
 
     held = (4, 64, size)
     faces = (96, size)
-    sound, partial, front, rear = call(
+    sides = [pltpu.VMEM(faces, F32)] * 2
+    sound, partial, to_a, to_b = call(
         acoustic_first_body,
         [held, held, faces, faces],
         acoustic,
@@ -634,45 +721,38 @@
         deriv_lanes,
         speed,
         near,
-        scratch=[pltpu.VMEM((512, 128), F32)],
-    )
-    before, after = traces(front, rear)
+        scratch=[pltpu.VMEM((512, 128), F32)] + sides,
+        flags=flags,
+    )
+    got_a, got_b = traces(to_a, to_b)
 
     six = 2 * HALO
-    tall = 5 * six * HALO
-    tall = -(-tall // 8) * 8
     edge_rows = tiles * 8
-    edge, along_x, y_low, y_high, xy_low, xy_high = call(
-        pack_next_body,
-        [
-            (edge_rows, 128),
-            (5 * six * 8 + edge_rows, 128),
-            (5 * cells_x * HALO + edge_rows, 128),
-            (5 * cells_x * HALO + edge_rows, 128),
-            (tall + edge_rows, 128),
-            (tall + edge_rows, 128),
-        ],
-        state,
-        above,
-        below,
-    )
+    shapes = [
+        (edge_rows, 128),
+        (5 * six * 8 + edge_rows, 128),
+        (5 * cells_x * HALO + edge_rows, 128),
+        (5 * cells_x * HALO + edge_rows, 128),
+        (32 + edge_rows, 128),
+        (32 + edge_rows, 128),
+    ]
+    edge, along_x, y_a, y_b, xy_a, xy_b = call(pack_next_body, shapes, state, edge_a, edge_b, flags=flags)
     flat = (size_x, size_y)
     steps = [[(1, 0), (-1, 0)]] if size_x == 2 else [[(1, 0)], [(-1, 0)]]
     places, messages = [], []
+    for first, second, spots in [(y_a, y_b, [(0, 0)])] + [(xy_a, xy_b, spots) for spots in steps]:
+        shift = spots[0][0]
+        for kept, side in ((first, False), (second, True)):
+            messages.append(lax.ppermute(kept, ("fx", "fy"), partners(flat, 1, side, shift)))
+            places.append(tuple((dx, 1) for dx, _ in spots))
     for spots in steps:
         messages.append(lax.ppermute(along_x, ("fx", "fy"), shifted(flat, spots[0])))
         places.append(tuple(spots))
-    for dy, kept in ((1, y_low), (-1, y_high)):
-        messages.append(lax.ppermute(kept, ("fx", "fy"), shifted(flat, (0, dy))))
-        places.append(((0, dy),))
-    for dy, kept in ((1, xy_low), (-1, xy_high)):
-        for spots in steps:
-            messages.append(lax.ppermute(kept, ("fx", "fy"), shifted(flat, (spots[0][0], dy))))
-            places.append(tuple((dx, dy) for dx, _ in spots))
 
     sent = (size_y, 192 // fold + 8, 128)
     wide = cells_x + 2 * HALO
-    rows_scratch = pltpu.VMEM((3, 64, 128), F32)
+    rows_shape = (3, 64, 128)
+    rows_scratch = pltpu.VMEM(rows_shape, F32)
 
     def planes(count):
         return (5, count, 16, 256)
@@ -680,6 +760,7 @@
     def route(send):
         return lax.all_to_all(send, "fy", split_axis=0, concat_axis=0, tiled=True)
 
+    spare = [pltpu.VMEM(shapes[2], F32)] * 2 + [pltpu.VMEM(shapes[4], F32)] * (2 * len(steps))
     start, send = call(
         functools.partial(flow_sources_body, tuple(places)),
         [planes(wide), sent],
@@ -689,39 +770,33 @@
         pair,
         spread,
         labels,
-        scratch=[pltpu.VMEM((3, wide, 16, 256), F32), rows_scratch],
+        scratch=[pltpu.VMEM((3, wide, 16, 256), F32), rows_scratch] + spare,
+        flags=flags,
     )
     received = route(send)
-    flow_one, send_next = call(
+    flow_one, lamb_rows = call(
         flow_first_body,
-        [planes(wide - 2), sent],
+        [planes(wide - 2), rows_shape],
         start,
+        scratch=[pltpu.VMEM(planes(wide), F32)],
+    )
+    sound_one, to_a, to_b, send = call(
+        functools.partial(acoustic_far_body, MIXES[0], "first"),
+        [held, faces, faces, sent],
+        partial,
+        got_a,
+        got_b,
+        far,
+        received,
+        lamb_rows,
         pair,
         spread,
         labels,
-        scratch=[pltpu.VMEM(planes(wide), F32), rows_scratch],
-    )
-    sound_one, front, rear = call(
-        functools.partial(acoustic_far_body, MIXES[0], False),
-        [held, faces, faces],
-        partial,
-        before,
-        after,
-        far,
-        received,
-    )
-    before, after = traces(front, rear)
-    received = route(send_next)
-    flow_state, send_next = call(
-        flow_last_body,
-        [(5, cells_x, 8, 128), sent],
-        flow_one,
-        start,
-        pair,
-        spread,
-        labels,
-        scratch=[pltpu.VMEM(planes(wide - 2), F32), rows_scratch, pltpu.VMEM(planes(wide - 4), F32)],
-    )
+        scratch=sides,
+        flags=flags,
+    )
+    got_a, got_b = traces(to_a, to_b)
+    received = route(send)
 
     def local_part(mix, now):
         return call(
@@ -736,27 +811,40 @@
         )[0]
 
     partial = local_part(MIXES[1], sound_one)
-    sound_two, front, rear = call(
-        functools.partial(acoustic_far_body, MIXES[1], False),
+    flow_state, send = call(
+        flow_last_body,
+        [(5, cells_x, 8, 128), sent],
+        flow_one,
+        start,
+        pair,
+        spread,
+        labels,
+        scratch=[pltpu.VMEM(planes(wide - 2), F32), rows_scratch, pltpu.VMEM(planes(wide - 4), F32)],
+    )
+    sound_two, to_a, to_b = call(
+        functools.partial(acoustic_far_body, MIXES[1], "second"),
         [held, faces, faces],
         partial,
-        before,
-        after,
+        got_a,
+        got_b,
         far,
         received,
-    )
-    before, after = traces(front, rear)
-    received = route(send_next)
+        scratch=sides,
+        flags=flags,
+    )
+    got_a, got_b = traces(to_a, to_b)
+    received = route(send)
     partial = local_part(MIXES[2], sound_two)
     sound_state, _ = call(
-        functools.partial(acoustic_far_body, MIXES[2], True),
+        functools.partial(acoustic_far_body, MIXES[2], "last"),
         [(elements, 4, 512), held],
         partial,
-        before,
-        after,
+        got_a,
+        got_b,
         far,
         received,
-        scratch=[pltpu.VMEM((512, 128), F32)],
+        scratch=[pltpu.VMEM((512, 128), F32)] + sides,
+        flags=flags,
     )
     return (flow_state, sound_state)
 

time: 94.2 us -> 85.9 us (0.912)
  the two profiles are of different devices: /device:TPU:29 before, /device:TPU:2 now
where the time goes in v3:
time: 85.9 us; the launch traced here: 85.1 us
  starting transfers between devices  38.2 us (44%)
  Pallas kernels  25.6 us (30%)
  local copies, waits for them, and re-layouts  9.9 us (12%)
  waiting for transfers between devices  7.97 us (9%)
  other arithmetic  2.58 us (3%)
  between operations  0.86 us (1%)
    pallas_call x12, Pallas kernels, call(): pl.pallas_call(kernel, out_shape=outs, in_specs=specs, out_specs=[whole]...  25.6 us
    ppermute x3, starting transfers between devices, traces(): far_got = lax.ppermute(to_b, names, far_pairs)  17.8 us
    all_to_all x3, starting transfers between devices, route(): return lax.all_to_all(send, 'fy', split_axis=0, concat_axis=0, tiled=True)  11.5 us
    unnamed x36, local copies, waits for them, and re-layouts  7.83 us
    ppermute x4, starting transfers between devices, per_device(): lax.ppermute(kept, ('fx', 'fy'), partners(flat, 1, side, shift))  6.59 us
    ppermute x3, waiting for transfers between devices, traces(): far_got = lax.ppermute(to_b, names, far_pairs)  5.57 us
  transfers between devices with their start and end apart: 16, of which 6 were waited for; matrix products, arithmetic and copies ran while one was open for 5% of the time, Pallas kernels for 17%

profile of v3, /device:TPU:2, one launch (start us, length us, event | category | flops | bytes accessed | tf_op | source)
XLA Modules:
  0.0 85.1 jit_solution(9318960119045750424)
XLA Ops:
  1.2 2.5 %shard_map.113 = (f32[5,8,8,128]{3,2,1,0:T(8,128)}, f32[24,128]{1,0:T(8,128)}, f32[24,128]{1,0:T(8,128)}) custom-call(s32[2]{0:T(128)} %pad_add_fusion.refs_0_.flags, f32[8,8,128]{2,1,0:T(8,128)} %refs_1_.1, f32[3,8,8,128]{3,2,1,0:T(8,128)} %refs_2_.1, f32[8,8,128]{2,1,0:T(8,128)} %refs_3_.1), custom_call_target="tpu_custom_call" | custom-call | tf_op jit(solution)/shard_map/pallas_call | solution.py:76
  3.8 1.6 %collective-permute-start.1 = (f32[24,128]{1,0:T(8,128)}, f32[24,128]{1,0:T(8,128)S(1)}, u32[]{:S(2)}, u32[]{:S(2)}) collective-permute-start(f32[24,128]{1,0:T(8,128)} %get-tuple-element.41), channel_id=1, source_target_pairs={{3,0},{2,1},{1,2},{0,3},{7,4},{6,5},{5,6},{4,7},{11,8},{10,9},{9,1... | collective-permute-start | bytes 36872 | tf_op jit(solution)/shard_map/ppermute | solution.py:671
  5.4 0.7 convert_bitcast_fusion
  7.2 0.9 %copy-done = f32[5,8,8,128]{3,2,1,0:T(8,128)S(1)} copy-done((f32[5,8,8,128]{3,2,1,0:T(8,128)S(1)}, f32[5,8,8,128]{3,2,1,0:T(8,128)}, u32[]{:S(2)}) %copy-start) | copy-done | bytes 163864
  9.3 1.6 %collective-permute-start.2 = (f32[144,128]{1,0:T(8,128)S(1)}, f32[144,128]{1,0:T(8,128)S(1)}, u32[]{:S(2)}, u32[]{:S(2)}) collective-permute-start(f32[144,128]{1,0:T(8,128)S(1)} %get-tuple-element.43), channel_id=1, source_target_pairs={{4,0},{0,4},{12,8},{8,12},{20,16},{16,20},{28,24},{24,28},{5,1},{1... | collective-permute-start | bytes 221192 | tf_op jit(solution)/shard_map/ppermute | solution.py:746
  10.9 2.5 %collective-permute-start.3 = (f32[144,128]{1,0:T(8,128)S(1)}, f32[144,128]{1,0:T(8,128)S(1)}, u32[]{:S(2)}, u32[]{:S(2)}) collective-permute-start(f32[144,128]{1,0:T(8,128)S(1)} %get-tuple-element.44), channel_id=1, source_target_pairs={{12,0},{8,4},{4,8},{0,12},{28,16},{24,20},{20,24},{16,28},{13,1},{... | collective-permute-start | bytes 221192 | tf_op jit(solution)/shard_map/ppermute | solution.py:746
  14.1 1.8 %collective-permute-start.5 = (f32[56,128]{1,0:T(8,128)S(1)}, f32[56,128]{1,0:T(8,128)S(1)}, u32[]{:S(2)}, u32[]{:S(2)}) collective-permute-start(f32[56,128]{1,0:T(8,128)S(1)} %get-tuple-element.46), channel_id=1, source_target_pairs={{28,0},{24,4},{20,8},{16,12},{12,16},{8,20},{4,24},{0,28},{29,1},{... | collective-permute-start | bytes 86024 | tf_op jit(solution)/shard_map/ppermute | solution.py:746
  17.1 0.7 pad.15
  17.8 0.7 pad.16
  18.5 0.7 concatenate.3.packed
  19.2 1.0 %shard_map.115 = (bf16[5,128,128]{2,1,0:T(8,128)(2,1)S(1)}, bf16[5,128,128]{2,1,0:T(8,128)(2,1)S(1)}, f32[128,64]{1,0:T(8,128)S(1)}, f32[128,128]{1,0:T(8,128)S(...) custom-call(f32[32,16]{1,0:T(8,128)S(1)} %concatenate.3.packed), custom_call_target="tpu_custom_call" | custom-call | tf_op jit(solution)/shard_map/pallas_call | solution.py:76
  20.7 1.0 %collective-permute-done.6.refs_6_ = f32[264,128]{1,0:T(8,128)S(1)} collective-permute-done((f32[264,128]{1,0:T(8,128)S(1)}, f32[264,128]{1,0:T(8,128)S(1)}, u32[]{:S(2)}, u32[]{:S(2)}) %collective-permute-start.6) | collective-permute-done | bytes 135200 | tf_op jit(solution)/shard_map/ppermute | solution.py:749
  21.8 0.9 %copy-done.1 = f32[5,8,8,128]{3,2,1,0:T(8,128)S(1)} copy-done((f32[5,8,8,128]{3,2,1,0:T(8,128)S(1)}, f32[5,8,8,128]{3,2,1,0:T(8,128)}, u32[]{:S(2)}) %copy-start.1) | copy-done | bytes 163864
  23.3 3.1 %shard_map.116 = (f32[5,14,16,256]{3,2,1,0:T(8,128)S(1)}, f32[4,104,128]{2,1,0:T(8,128)}) custom-call(s32[2]{0:T(128)S(1)} %copy-done.8, f32[5,8,8,128]{3,2,1,0:T(8,128)S(1)} %copy-done.1, f32[24,128]{1,0:T(8,128)S(1)} %get-tuple-element.42.refs_1_, f32[144,128]{1,0:T(8,128)S(1)} %collective-permute-done.2.refs_2_, ...), custom_call_target="tpu_custom_call" | custom-call | tf_op jit(solution)/shard_map/pallas_call | solution.py:76
  26.4 3.4 %all-to-all-start = ((f32[4,104,128]{2,1,0:T(8,128)}), f32[4,104,128]{2,1,0:T(8,128)S(1)}, u32[]{:S(2)}, u32[]{:S(2)}) async-start(f32[4,104,128]{2,1,0:T(8,128)} %get-tuple-element.62), calls=%async_computation | async-start | bytes 425984 | tf_op jit(solution)/shard_map/all_to_all | solution.py:761
  29.9 1.5 %shard_map.119 = (f32[4,64,128]{2,1,0:T(8,128)S(1)}, f32[4,64,128]{2,1,0:T(8,128)S(1)}, f32[96,128]{1,0:T(8,128)S(1)}, f32[96,128]{1,0:T(8,128)S(1)}) custom-call(s32[2]{0:T(128)S(1)} %copy-done.9, f32[16,4,512]{2,1,0:T(4,128)S(1)} %copy-done.2, f32[128,64]{1,0:T(8,128)S(1)} %get-tuple-element.54.deriv_rows, f32[128,128]{1,0:T(8,128)S(1)} %get-tuple-element.55.deriv_lanes, ...), custom_call_target="tpu_custom_call" | custom-call | tf_op jit(solution)/shard_map/pallas_call | solution.py:76
  31.5 7.1 %collective-permute-start.8 = (f32[96,128]{1,0:T(8,128)S(1)}, f32[96,128]{1,0:T(8,128)S(1)}, u32[]{:S(2)}, u32[]{:S(2)}) collective-permute-start(f32[96,128]{1,0:T(8,128)S(1)} %get-tuple-element.60), channel_id=1, source_target_pairs={{1,2},{2,1},{3,4},{4,3},{5,6},{6,5},{7,8},{8,7},{9,10},{10,9},{11,... | collective-permute-start | bytes 147464 | tf_op jit(solution)/shard_map/ppermute | solution.py:710
  38.5 3.6 %shard_map.117 = (f32[5,12,16,256]{3,2,1,0:T(8,128)S(1)}, f32[3,64,128]{2,1,0:T(8,128)S(1)}) custom-call(f32[5,14,16,256]{3,2,1,0:T(8,128)S(1)} %get-tuple-element.51.wide.start), custom_call_target="tpu_custom_call" | custom-call | tf_op jit(solution)/shard_map/pallas_call | solution.py:76
  43.4 0.9 %copy-done.4 = f32[3,64,128]{2,1,0:T(8,128)S(1)} copy-done((f32[3,64,128]{2,1,0:T(8,128)S(1)}, f32[3,64,128]{2,1,0:T(8,128)}, u32[]{:S(2)}) %copy-start.4) | copy-done | bytes 98328
  44.3 0.8 copy-done.6
  45.7 2.2 %shard_map.120 = (f32[4,64,128]{2,1,0:T(8,128)S(1)}, f32[96,128]{1,0:T(8,128)S(1)}, f32[96,128]{1,0:T(8,128)S(1)}, f32[4,104,128]{2,1,0:T(8,128)}) custom-call(s32[2]{0:T(128)S(1)} %copy-done.10, f32[4,64,128]{2,1,0:T(8,128)S(1)} %get-tuple-element.58.partial, f32[96,128]{1,0:T(8,128)S(1)} %collective-permute-done.7.got_a, f32[96,128]{1,0:T(8,128)S(1)} %copy-done.6, ...), custom_call_target="tpu_custom_call" | custom-call | tf_op jit(solution)/shard_map/pallas_call | solution.py:76
  49.2 3.4 %all-to-all-start.1 = ((f32[4,104,128]{2,1,0:T(8,128)}), f32[4,104,128]{2,1,0:T(8,128)S(1)}, u32[]{:S(2)}, u32[]{:S(2)}) async-start(f32[4,104,128]{2,1,0:T(8,128)} %get-tuple-element.69), calls=%async_computation.1 | async-start | bytes 425984 | tf_op jit(solution)/shard_map/all_to_all | solution.py:761
  52.6 5.9 %shard_map.118 = (f32[5,8,8,128]{3,2,1,0:T(8,128)}, f32[4,104,128]{2,1,0:T(8,128)}) custom-call(f32[5,12,16,256]{3,2,1,0:T(8,128)S(1)} %get-tuple-element.52.wide, f32[5,14,16,256]{3,2,1,0:T(8,128)S(1)} %get-tuple-element.51.wide.start, f32[64,64]{1,0:T(8,128)S(1)} %get-tuple-element.48.refs_7_.pair.refs_1_, ...), custom_call_target="tpu_custom_call" | custom-call | tf_op jit(solution)/shard_map/pallas_call | solution.py:76
  58.9 4.7 %all-to-all-start.2 = ((f32[4,104,128]{2,1,0:T(8,128)}), f32[4,104,128]{2,1,0:T(8,128)S(1)}, u32[]{:S(2)}, u32[]{:S(2)}) async-start(f32[4,104,128]{2,1,0:T(8,128)} %get-tuple-element.74), calls=%async_computation.2 | async-start | bytes 425984 | tf_op jit(solution)/shard_map/all_to_all | solution.py:761
  63.6 5.3 %collective-permute-start.10 = (f32[96,128]{1,0:T(8,128)S(1)}, f32[96,128]{1,0:T(8,128)S(1)}, u32[]{:S(2)}, u32[]{:S(2)}) collective-permute-start(f32[96,128]{1,0:T(8,128)S(1)} %copy-done.15), channel_id=1, source_target_pairs={{1,2},{2,1},{3,4},{4,3},{5,6},{6,5},{7,8},{8,7},{9,10},{10,9},{11,... | collective-permute-start | bytes 147464 | tf_op jit(solution)/shard_map/ppermute | solution.py:710
  69.0 0.9 %shard_map.121 = (f32[4,64,128]{2,1,0:T(8,128)S(1)}, f32[96,128]{1,0:T(8,128)}, f32[96,128]{1,0:T(8,128)}) custom-call(f32[4,64,128]{2,1,0:T(8,128)S(1)} %get-tuple-element.64.state, f32[4,64,128]{2,1,0:T(8,128)S(1)} %get-tuple-element.65.start, f32[128,64]{1,0:T(8,128)S(1)} %get-tuple-element.54.deriv_rows, f32[128,128]{1,0:T(8,128)S(1)} %get-tuple-element.55.deriv_lanes, ...), custom_call_target="tpu_custom_call" | custom-call | tf_op jit(solution)/shard_map/pallas_call | solution.py:76
  69.8 2.8 %collective-permute-done.10.got_b = f32[96,128]{1,0:T(8,128)S(1)} collective-permute-done((f32[96,128]{1,0:T(8,128)S(1)}, f32[96,128]{1,0:T(8,128)S(1)}, u32[]{:S(2)}, u32[]{:S(2)}) %collective-permute-start.10) | collective-permute-done | bytes 49184 | tf_op jit(solution)/shard_map/ppermute | solution.py:710
  72.6 1.0 %shard_map.122 = (f32[4,64,128]{2,1,0:T(8,128)S(1)}, f32[96,128]{1,0:T(8,128)S(1)}, f32[96,128]{1,0:T(8,128)S(1)}) custom-call(s32[2]{0:T(128)S(1)} %copy-done.11, f32[4,64,128]{2,1,0:T(8,128)S(1)} %get-tuple-element.66.partial, f32[96,128]{1,0:T(8,128)S(1)} %collective-permute-done.9.got_a, f32[96,128]{1,0:T(8,128)S(1)} %collective-permute-done.10.got_b, ...), custom_call_target="tpu_custom_call" | custom-call | tf_op jit(solution)/shard_map/pallas_call | solution.py:76
  73.8 5.3 %collective-permute-start.12 = (f32[96,128]{1,0:T(8,128)S(1)}, f32[96,128]{1,0:T(8,128)S(1)}, u32[]{:S(2)}, u32[]{:S(2)}) collective-permute-start(f32[96,128]{1,0:T(8,128)S(1)} %get-tuple-element.73), channel_id=1, source_target_pairs={{1,2},{2,1},{3,4},{4,3},{5,6},{6,5},{7,8},{8,7},{9,10},{10,9},{11,... | collective-permute-start | bytes 147464 | tf_op jit(solution)/shard_map/ppermute | solution.py:710
  79.1 0.9 %shard_map.123 = (f32[4,64,128]{2,1,0:T(8,128)S(1)}, f32[96,128]{1,0:T(8,128)}, f32[96,128]{1,0:T(8,128)}) custom-call(f32[4,64,128]{2,1,0:T(8,128)S(1)} %get-tuple-element.70.state, f32[4,64,128]{2,1,0:T(8,128)S(1)} %get-tuple-element.65.start, f32[128,64]{1,0:T(8,128)S(1)} %get-tuple-element.54.deriv_rows, f32[128,128]{1,0:T(8,128)S(1)} %get-tuple-element.55.deriv_lanes, ...), custom_call_target="tpu_custom_call" | custom-call | tf_op jit(solution)/shard_map/pallas_call | solution.py:76
  80.0 2.8 %collective-permute-done.12.got_b = f32[96,128]{1,0:T(8,128)S(1)} collective-permute-done((f32[96,128]{1,0:T(8,128)S(1)}, f32[96,128]{1,0:T(8,128)S(1)}, u32[]{:S(2)}, u32[]{:S(2)}) %collective-permute-start.12) | collective-permute-done | bytes 49184 | tf_op jit(solution)/shard_map/ppermute | solution.py:710
  82.8 2.3 %shard_map.124 = (f32[16,4,512]{2,1,0:T(4,128)}, f32[4,64,128]{2,1,0:T(8,128)}) custom-call(s32[2]{0:T(128)S(1)} %copy-done.11, f32[4,64,128]{2,1,0:T(8,128)S(1)} %get-tuple-element.71.partial, f32[96,128]{1,0:T(8,128)S(1)} %collective-permute-done.11.got_a, f32[96,128]{1,0:T(8,128)S(1)} %collective-permute-done.12.got_b, ...), custom_call_target="tpu_custom_call" | custom-call | tf_op jit(solution)/shard_map/pallas_call | solution.py:76
  (57 shorter events, 9.6 us)
Async XLA Ops:
  0.6 29.2 %copy-start.2 = (f32[16,4,512]{2,1,0:T(4,128)S(1)}, f32[16,4,512]{2,1,0:T(4,128)}, u32[]{:S(2)}) copy-start(f32[16,4,512]{2,1,0:T(4,128)} %given.1) | copy-start | bytes 393220
  1.2 28.6 %copy-start.9 = (s32[2]{0:T(128)S(1)}, s32[2]{0:T(128)}, u32[]{:S(2)}) copy-start(s32[2]{0:T(128)} %pad_add_fusion.refs_0_.flags) | copy-start | bytes 28
  3.7 3.1 %collective-permute-start = (f32[24,128]{1,0:T(8,128)}, f32[24,128]{1,0:T(8,128)S(1)}, u32[]{:S(2)}, u32[]{:S(2)}) collective-permute-start(f32[24,128]{1,0:T(8,128)} %get-tuple-element.40), channel_id=1, source_target_pairs={{1,0},{0,1},{3,2},{2,3},{5,4},{4,5},{7,6},{6,7},{9,8},{8,9},{11,10... | collective-permute-start | bytes 36872 | tf_op jit(solution)/shard_map/ppermute | solution.py:670
  3.8 3.4 %collective-permute-start.1 = (f32[24,128]{1,0:T(8,128)}, f32[24,128]{1,0:T(8,128)S(1)}, u32[]{:S(2)}, u32[]{:S(2)}) collective-permute-start(f32[24,128]{1,0:T(8,128)} %get-tuple-element.41), channel_id=1, source_target_pairs={{3,0},{2,1},{1,2},{0,3},{7,4},{6,5},{5,6},{4,7},{11,8},{10,9},{9,1... | collective-permute-start | bytes 36872 | tf_op jit(solution)/shard_map/ppermute | solution.py:671
  7.2 0.9 %copy-start = (f32[5,8,8,128]{3,2,1,0:T(8,128)S(1)}, f32[5,8,8,128]{3,2,1,0:T(8,128)}, u32[]{:S(2)}) copy-start(f32[5,8,8,128]{3,2,1,0:T(8,128)} %get-tuple-element.39.state.refs_0_) | copy-start | bytes 491524
  8.1 0.6 copy-start.7
  9.3 11.4 %collective-permute-start.2 = (f32[144,128]{1,0:T(8,128)S(1)}, f32[144,128]{1,0:T(8,128)S(1)}, u32[]{:S(2)}, u32[]{:S(2)}) collective-permute-start(f32[144,128]{1,0:T(8,128)S(1)} %get-tuple-element.43), channel_id=1, source_target_pairs={{4,0},{0,4},{12,8},{8,12},{20,16},{16,20},{28,24},{24,28},{5,1},{1... | collective-permute-start | bytes 221192 | tf_op jit(solution)/shard_map/ppermute | solution.py:746
  10.9 9.8 %collective-permute-start.3 = (f32[144,128]{1,0:T(8,128)S(1)}, f32[144,128]{1,0:T(8,128)S(1)}, u32[]{:S(2)}, u32[]{:S(2)}) collective-permute-start(f32[144,128]{1,0:T(8,128)S(1)} %get-tuple-element.44), channel_id=1, source_target_pairs={{12,0},{8,4},{4,8},{0,12},{28,16},{24,20},{20,24},{16,28},{13,1},{... | collective-permute-start | bytes 221192 | tf_op jit(solution)/shard_map/ppermute | solution.py:746
  13.4 6.7 %collective-permute-start.4 = (f32[56,128]{1,0:T(8,128)S(1)}, f32[56,128]{1,0:T(8,128)S(1)}, u32[]{:S(2)}, u32[]{:S(2)}) collective-permute-start(f32[56,128]{1,0:T(8,128)S(1)} %get-tuple-element.45), channel_id=1, source_target_pairs={{20,0},{16,4},{28,8},{24,12},{4,16},{0,20},{12,24},{8,28},{21,1},{... | collective-permute-start | bytes 86024 | tf_op jit(solution)/shard_map/ppermute | solution.py:746
  14.1 6.7 %collective-permute-start.5 = (f32[56,128]{1,0:T(8,128)S(1)}, f32[56,128]{1,0:T(8,128)S(1)}, u32[]{:S(2)}, u32[]{:S(2)}) collective-permute-start(f32[56,128]{1,0:T(8,128)S(1)} %get-tuple-element.46), channel_id=1, source_target_pairs={{28,0},{24,4},{20,8},{16,12},{12,16},{8,20},{4,24},{0,28},{29,1},{... | collective-permute-start | bytes 86024 | tf_op jit(solution)/shard_map/ppermute | solution.py:746
  15.9 5.9 %collective-permute-start.6 = (f32[264,128]{1,0:T(8,128)S(1)}, f32[264,128]{1,0:T(8,128)S(1)}, u32[]{:S(2)}, u32[]{:S(2)}) collective-permute-start(f32[264,128]{1,0:T(8,128)S(1)} %get-tuple-element.47), channel_id=1, source_target_pairs={{16,0},{20,4},{24,8},{28,12},{0,16},{4,20},{8,24},{12,28},{17,1},{... | collective-permute-start | bytes 405512 | tf_op jit(solution)/shard_map/ppermute | solution.py:749
  20.2 18.4 %copy-start.12 = (f32[1,128]{1,0:T(1,128)}, f32[1,128]{1,0:T(1,128)S(1)}, u32[]{:S(2)}) copy-start(f32[1,128]{1,0:T(1,128)S(1)} %get-tuple-element.56.speed) | copy-start | bytes 1540
  21.8 0.9 %copy-start.1 = (f32[5,8,8,128]{3,2,1,0:T(8,128)S(1)}, f32[5,8,8,128]{3,2,1,0:T(8,128)}, u32[]{:S(2)}) copy-start(f32[5,8,8,128]{3,2,1,0:T(8,128)} %get-tuple-element.39.state.refs_0_) | copy-start | bytes 491524
  26.4 17.0 %all-to-all-start = ((f32[4,104,128]{2,1,0:T(8,128)}), f32[4,104,128]{2,1,0:T(8,128)S(1)}, u32[]{:S(2)}, u32[]{:S(2)}) async-start(f32[4,104,128]{2,1,0:T(8,128)} %get-tuple-element.62), calls=%async_computation | async-start | bytes 425984 | tf_op jit(solution)/shard_map/all_to_all | solution.py:761
  31.4 11.4 %collective-permute-start.7 = (f32[96,128]{1,0:T(8,128)S(1)}, f32[96,128]{1,0:T(8,128)S(1)}, u32[]{:S(2)}, u32[]{:S(2)}) collective-permute-start(f32[96,128]{1,0:T(8,128)S(1)} %get-tuple-element.59), channel_id=1, source_target_pairs={{1,0},{0,1},{3,2},{2,3},{5,4},{4,5},{7,6},{6,7},{9,8},{8,9},{11,10... | collective-permute-start | bytes 147464 | tf_op jit(solution)/shard_map/ppermute | solution.py:711
  31.5 11.3 %collective-permute-start.8 = (f32[96,128]{1,0:T(8,128)S(1)}, f32[96,128]{1,0:T(8,128)S(1)}, u32[]{:S(2)}, u32[]{:S(2)}) collective-permute-start(f32[96,128]{1,0:T(8,128)S(1)} %get-tuple-element.60), channel_id=1, source_target_pairs={{1,2},{2,1},{3,4},{4,3},{5,6},{6,5},{7,8},{8,7},{9,10},{10,9},{11,... | collective-permute-start | bytes 147464 | tf_op jit(solution)/shard_map/ppermute | solution.py:710
  42.1 0.7 copy-start.3
  42.8 0.6 copy-start.5
  43.4 0.9 %copy-start.4 = (f32[3,64,128]{2,1,0:T(8,128)S(1)}, f32[3,64,128]{2,1,0:T(8,128)}, u32[]{:S(2)}) copy-start(f32[3,64,128]{2,1,0:T(8,128)} %copy-done.3) | copy-start | bytes 294916
  44.3 0.8 copy-start.6
  48.0 0.6 copy-start.14
  48.6 0.6 copy-start.16
  49.2 9.7 %all-to-all-start.1 = ((f32[4,104,128]{2,1,0:T(8,128)}), f32[4,104,128]{2,1,0:T(8,128)S(1)}, u32[]{:S(2)}, u32[]{:S(2)}) async-start(f32[4,104,128]{2,1,0:T(8,128)} %get-tuple-element.69), calls=%async_computation.1 | async-start | bytes 425984 | tf_op jit(solution)/shard_map/all_to_all | solution.py:761
  52.6 11.0 %copy-start.17 = (f32[96,128]{1,0:T(8,128)S(1)}, f32[96,128]{1,0:T(8,128)}, u32[]{:S(2)}) copy-start(f32[96,128]{1,0:T(8,128)} %copy-done.16) | copy-start | bytes 147460
  52.6 11.0 %copy-start.15 = (f32[96,128]{1,0:T(8,128)S(1)}, f32[96,128]{1,0:T(8,128)}, u32[]{:S(2)}) copy-start(f32[96,128]{1,0:T(8,128)} %copy-done.14) | copy-start | bytes 147460
  52.6 16.4 %copy-start.13 = (f32[1,128]{1,0:T(1,128)S(1)}, f32[1,128]{1,0:T(1,128)}, u32[]{:S(2)}) copy-start(f32[1,128]{1,0:T(1,128)} %copy-done.12) | copy-start | bytes 1540
  52.6 20.0 %copy-start.11 = (s32[2]{0:T(128)S(1)}, s32[2]{0:T(128)}, u32[]{:S(2)}) copy-start(s32[2]{0:T(128)} %pad_add_fusion.refs_0_.flags) | copy-start | bytes 28
  58.9 21.0 %all-to-all-start.2 = ((f32[4,104,128]{2,1,0:T(8,128)}), f32[4,104,128]{2,1,0:T(8,128)S(1)}, u32[]{:S(2)}, u32[]{:S(2)}) async-start(f32[4,104,128]{2,1,0:T(8,128)} %get-tuple-element.74), calls=%async_computation.2 | async-start | bytes 425984 | tf_op jit(solution)/shard_map/all_to_all | solution.py:761
  63.6 6.2 %collective-permute-start.9 = (f32[96,128]{1,0:T(8,128)S(1)}, f32[96,128]{1,0:T(8,128)S(1)}, u32[]{:S(2)}, u32[]{:S(2)}) collective-permute-start(f32[96,128]{1,0:T(8,128)S(1)} %copy-done.17), channel_id=1, source_target_pairs={{1,0},{0,1},{3,2},{2,3},{5,4},{4,5},{7,6},{6,7},{9,8},{8,9},{11,10... | collective-permute-start | bytes 147464 | tf_op jit(solution)/shard_map/ppermute | solution.py:711
  63.6 9.0 %collective-permute-start.10 = (f32[96,128]{1,0:T(8,128)S(1)}, f32[96,128]{1,0:T(8,128)S(1)}, u32[]{:S(2)}, u32[]{:S(2)}) collective-permute-start(f32[96,128]{1,0:T(8,128)S(1)} %copy-done.15), channel_id=1, source_target_pairs={{1,2},{2,1},{3,4},{4,3},{5,6},{6,5},{7,8},{8,7},{9,10},{10,9},{11,... | collective-permute-start | bytes 147464 | tf_op jit(solution)/shard_map/ppermute | solution.py:710
  73.7 6.3 %collective-permute-start.11 = (f32[96,128]{1,0:T(8,128)S(1)}, f32[96,128]{1,0:T(8,128)S(1)}, u32[]{:S(2)}, u32[]{:S(2)}) collective-permute-start(f32[96,128]{1,0:T(8,128)S(1)} %get-tuple-element.72), channel_id=1, source_target_pairs={{1,0},{0,1},{3,2},{2,3},{5,4},{4,5},{7,6},{6,7},{9,8},{8,9},{11,10... | collective-permute-start | bytes 147464 | tf_op jit(solution)/shard_map/ppermute | solution.py:711
  73.8 9.0 %collective-permute-start.12 = (f32[96,128]{1,0:T(8,128)S(1)}, f32[96,128]{1,0:T(8,128)S(1)}, u32[]{:S(2)}, u32[]{:S(2)}) collective-permute-start(f32[96,128]{1,0:T(8,128)S(1)} %get-tuple-element.73), channel_id=1, source_target_pairs={{1,2},{2,1},{3,4},{4,3},{5,6},{6,5},{7,8},{8,7},{9,10},{10,9},{11,... | collective-permute-start | bytes 147464 | tf_op jit(solution)/shard_map/ppermute | solution.py:710
  (2 other events, 1.2 us)

commit v4 on v3

--- a/solution.py
+++ b/solution.py
@@ -45,50 +45,49 @@
     return dot(left_high, right) + dot(left_low, right)
 
 
-def call(body, outs, *operands, scratch=(), fetch=False, flags=None):
+def call(body, outs, *operands, scratch=(), fetch=False, last=0):
     whole = pl.BlockSpec(memory_space=pltpu.VMEM)
     outs = [out if isinstance(out, jax.ShapeDtypeStruct) else jax.ShapeDtypeStruct(out, F32) for out in outs]
     scratch = list(scratch)
-    specs = [pl.BlockSpec(memory_space=pl.ANY) if fetch else whole] * len(operands)
-    params = PARAMS
+    anywhere = pl.BlockSpec(memory_space=pltpu.HBM)
+    specs = [anywhere if fetch else whole] * (len(operands) - last) + [anywhere] * last
     kernel = body
     if fetch:
         count = len(operands)
-        params = pltpu.CompilerParams(vmem_limit_bytes=60 * 1024 * 1024)
-        first = 1 if flags is not None else 0
-        total = first + count + len(outs)
+        total = count + len(outs)
 
         def kernel(*refs):
             held, sems = refs[total : total + count], refs[total + count]
             copies = [
-                pltpu.make_async_copy(refs[first + i], held[i], sems.at[i]) for i in range(count)
+                pltpu.make_async_copy(refs[i], held[i], sems.at[i]) for i in range(count)
             ]
             for copy in copies:
                 copy.start()
             for copy in copies:
                 copy.wait()
-            body(*refs[:first], *held, *refs[first + count : total], *refs[total + count + 1 :])
+            body(*held, *refs[count:total], *refs[total + count + 1 :])
 
         scratch = [pltpu.VMEM(o.shape, o.dtype) for o in operands] + [pltpu.SemaphoreType.DMA((count,))] + scratch
-    if flags is not None:
-        specs = [pl.BlockSpec(memory_space=pltpu.SMEM)] + specs
-        operands = (flags,) + operands
     return pl.pallas_call(
         kernel,
         out_shape=outs,
         in_specs=specs,
         out_specs=[whole] * len(outs),
         scratch_shapes=scratch,
-        compiler_params=params,
+        compiler_params=PARAMS,
     )(*operands)
+
+
+def is_odd(axis):
+    return lax.axis_index(axis) % 2 == 1
 
 
 def paired(odd, to_next, to_last):
     return jnp.where(odd, to_last, to_next), jnp.where(odd, to_next, to_last)
 
 
-def pack_start_body(flags, density, velocity, pressure, state, message_a, message_b):
-    odd = flags[0] == 1
+def pack_start_body(density, velocity, pressure, state, message_a, message_b):
+    odd = is_odd("fz")
     rho = density[...]
     vel = velocity[...]
     state[0] = rho
@@ -108,9 +107,9 @@
         message_b[tile * 8 : tile * 8 + 8] = second
 
 
-def pack_next_body(flags, state, got_a, got_b, edge, along_x, y_a, y_b, xy_a, xy_b):
+def pack_next_body(state, got_a, got_b, _, edge, along_x, y_a, y_b, xy_a, xy_b):
     cells_x = state.shape[1]
-    odd_z, odd = flags[0] == 1, flags[1] == 1
+    odd_z, odd = is_odd("fz"), is_odd("fy")
     row = lax.broadcasted_iota(jnp.int32, edge.shape, 0) % 8
     above, below = paired(odd_z, got_a[...], got_b[...])
     both = jnp.where(row < 4, above, below)
@@ -282,31 +281,22 @@
     lax.fori_loop(0, cells_x, one, 0)
 
 
-def project(lamb_rows, pair, spread, labels, send):
+def project(lamb_rows, pair, spread, send):
     peers = send.shape[0]
-    fold = 192 // (send.shape[1] - 8)
-    group = lax.broadcasted_iota(jnp.int32, (64 // fold, 128), 1) // (128 // fold)
-    height = 64 // fold
     for c in range(3):
-        modes = dot_three(pair[...], lamb_rows[c])
-        sent = dot_three(modes, spread[...])
+        sent = dot_three(dot_three(pair[...], lamb_rows[c]), spread[...])
         for peer in range(peers):
-            mine = sent[:, peer * 128 : peer * 128 + 128]
-            folded = mine[0:height]
-            for g in range(1, fold):
-                folded = jnp.where(group == g, mine[g * height : g * height + height], folded)
-            send[peer, c * height : c * height + height] = folded
-    send[:, 3 * height : 3 * height + 8] = labels[...]
-
-
-def flow_sources_body(places, flags, *refs):
+            send[peer, c] = sent[:, peer * 128 : peer * 128 + 128]
+
+
+def flow_sources_body(places, *refs):
     state, edge = refs[0:2]
     messages = refs[2 : 2 + len(places)]
-    pair, spread, labels = refs[2 + len(places) : 5 + len(places)]
+    pair, spread, _ = refs[2 + len(places) : 5 + len(places)]
     wide, send, derived, lamb_rows = refs[5 + len(places) : 9 + len(places)]
     spare = refs[9 + len(places) :]
     cells_x = state.shape[1]
-    odd = flags[1] == 1
+    odd = is_odd("fy")
     beside, k = [], 0
     while k < len(places):
         if places[k][0][1] == 0:
@@ -322,10 +312,10 @@
     assemble(wide, state, edge, beside, cells_x)
     derive_speeds(wide, derived, HALO - 1, HALO + cells_x + 1)
     lamb(derived, HALO, cells_x, lamb_rows)
-    project(lamb_rows, pair, spread, labels, send)
-
-
-def flow_first_body(wide, out, lamb_rows, derived):
+    project(lamb_rows, pair, spread, send)
+
+
+def flow_first_body(wide, pair, spread, out, send, derived, lamb_rows):
     def write(i, f, value):
         out[f, i] = value
 
@@ -335,9 +325,10 @@
     flow_rate_section(wide, derived, wide, 0, MIXES[0], write)
     derive_speeds(out, derived, HALO - 2, HALO + cells_x)
     lamb(derived, HALO - 1, cells_x, lamb_rows)
-
-
-def flow_last_body(wide, start, pair, spread, labels, out, send, derived, lamb_rows, second):
+    project(lamb_rows, pair, spread, send)
+
+
+def flow_last_body(wide, start, pair, spread, out, send, derived, lamb_rows, second):
     def write_second(i, f, value):
         second[f, i] = value
 
@@ -350,7 +341,7 @@
     flow_rate_section(wide, derived, start, 1, MIXES[1], write_second)
     derive_planes(second, derived, 0, planes - 2)
     lamb(derived, 1, cells_x, lamb_rows)
-    project(lamb_rows, pair, spread, labels, send)
+    project(lamb_rows, pair, spread, send)
     flow_rate_section(second, derived, start, 2, MIXES[2], write, inner=True)
 
 
@@ -409,7 +400,7 @@
     return [rates[c] - count * fields[c] + side[c * 64 : c * 64 + 64] for c in range(4)]
 
 
-def local_update(mix, state, start, deriv_rows, deriv_lanes, speed, sides, out, front, rear):
+def acoustic_local_body(mix, state, start, deriv_rows, deriv_lanes, speed, sides, out, front, rear):
     rates = rate_local(state, deriv_rows, deriv_lanes, speed, sides)
     for c in range(4):
         value = state[c] + TIME_STEP * rates[c]
@@ -420,10 +411,6 @@
     lift(out, front, rear, sides, TIME_STEP * mix[1] * PENALTY)
 
 
-def acoustic_local_body(mix, state, start, deriv_rows, deriv_lanes, speed, sides, out, front, rear):
-    local_update(mix, state, start, deriv_rows, deriv_lanes, speed, sides, out, front, rear)
-
-
 def order_table(count, turned):
     row = lax.broadcasted_iota(jnp.int32, (4 * count, 4 * count), 0)
     column = lax.broadcasted_iota(jnp.int32, (4 * count, 4 * count), 1)
@@ -432,9 +419,7 @@
     return (column == (row % count) * 4 + row // count).astype(F32)
 
 
-def acoustic_first_body(
-    flags, given, deriv_rows, deriv_lanes, speed, sides, state, out, message_a, message_b, turned, front, rear
-):
+def acoustic_start_body(given, _, state, message_a, message_b, turned):
     count = given.shape[0]
     rows = jnp.concatenate([given[e] for e in range(count)], 0)
     rows = dot_full(order_table(count, False), rows)
@@ -449,8 +434,7 @@
             fields[c] = jnp.where(lane == z, pltpu.roll(piece, move, 1) if move else piece, fields[c])
     for c in range(4):
         state[c] = fields[c]
-    local_update(MIXES[0], state, state, deriv_rows, deriv_lanes, speed, sides, out, front, rear)
-    message_a[...], message_b[...] = paired(flags[0] == 1, front[...], rear[...])
+    faces_sent(is_odd("fz"), state, message_a, message_b)
 
 
 def natural_order(state, out, turned):
@@ -481,50 +465,24 @@
         out[c] += value[c * 64 : c * 64 + 64]
 
 
-def acoustic_far_body(mix, kind, flags, partial, got_a, got_b, sides_far, received, *refs):
-    odd = flags[0] == 1
-    if kind == "last":
-        given_out, out, turned, before, after = refs
-    elif kind == "first":
-        lamb_rows, pair, spread, labels, out, message_a, message_b, send, before, after = refs
+def acoustic_far_body(mix, last, partial, got_a, got_b, sides_far, received, *refs):
+    if last:
+        given_out, before, after, source, sem, out, turned = refs
     else:
-        out, message_a, message_b, before, after = refs
+        out, message_a, message_b, before, after, source, sem = refs
+    copy = pltpu.make_async_copy(received, source, sem)
+    copy.start()
+    odd = is_odd("fz")
     after[...], before[...] = paired(odd, got_a[...], got_b[...])
     out[...] = partial[...]
     remote_part(out, before, after, sides_far, TIME_STEP * mix[1] * PENALTY)
-    place(received, out, TIME_STEP * mix[1])
-    if kind == "last":
+    copy.wait()
+    for c in range(3):
+        out[1 + c] += (TIME_STEP * mix[1]) * source[0, c]
+    if last:
         natural_order(out, given_out, turned)
-        return
-    faces_sent(odd, out, message_a, message_b)
-    if kind == "first":
-        project(lamb_rows, pair, spread, labels, send)
-
-
-def place(received, out, factor):
-    peers, size = received.shape[0], received.shape[1]
-    fold = 192 // (size - 8)
-    height = 64 // fold
-    target = lax.broadcasted_iota(jnp.int32, (128, 128), 0)
-    lane = lax.broadcasted_iota(jnp.int32, (128, 128), 1)
-    total = None
-    for peer in range(peers):
-        label = received[peer, size - 8 : size - 7, :]
-        label = jnp.broadcast_to(label, (128, 128)).astype(jnp.int32)
-        hit = (label == target % 16) & (lane % 8 == target // 16)
-        chosen = [jnp.where(hit & (lane // (128 // fold) == g), 1.0, 0.0) for g in range(fold)]
-        chosen = jnp.concatenate(chosen, 0).astype(BF16)
-        high, low = parts(received[peer, 0 : size - 8])
-        dims = (((1,), (1,)), ((), ()))
-        value = lax.dot_general(high, chosen, dims, preferred_element_type=F32)
-        value = value + lax.dot_general(low, chosen, dims, preferred_element_type=F32)
-        total = value if total is None else total + value
-    for c in range(3):
-        for g in range(fold):
-            rows = slice(g * height, g * height + height)
-            out[1 + c, rows] = out[1 + c, rows] + factor * (
-                total[c * height : c * height + height, g * 128 : g * 128 + 128]
-            )
+    else:
+        faces_sent(odd, out, message_a, message_b)
 
 
 def kron_part(matrix, shape, rows_by, columns_by):
@@ -545,7 +503,6 @@
     deriv_lanes,
     pair,
     spread,
-    labels,
     speed,
 ):
     size = near.shape[1]
@@ -587,32 +544,21 @@
     deriv_lanes[...] = jnp.where(row % count == column % count, lanes, 0.0)
     pair[...] = kron_part(modes, (64, 64), 8, 8) * kron_part(modes, (64, 64), 1, 1)
 
-    peers = labels.shape[0]
-    capacity = max(2, 2 * blocks // peers)
     row, column = place_of((blocks, blocks))
 
     def upright(values):
-        return jnp.sum(jnp.where(row == column, values, 0.0), 1, keepdims=True)
-
-    owner_row = packed[25:26, 0:blocks]
-    owner_column = upright(owner_row)
-    earlier = (owner_column == owner_row) & (column < row)
-    position = jnp.sum(jnp.where(earlier, 1.0, 0.0), 1, keepdims=True)
-    slot = owner_column * capacity + position
-    element_column = upright(packed[26:27, 0:blocks])
-    wide = (8 * blocks, peers * 128)
-    row, column = place_of((8 * blocks, blocks))
-    repeat = (row // 8 == column).astype(F32)
-    slot = dot_full(repeat, jnp.broadcast_to(slot, (blocks, 128)))
-    element = dot_full(repeat, jnp.broadcast_to(element_column, (blocks, 128)))
-    row, column = place_of((8 * blocks, 128))
-    values = kron_part(modes.T, (8 * blocks, 128), 1, 1)
-    inside = column % (8 * capacity) // 8
-    for peer in range(peers):
-        chosen = slot == (inside + peer * capacity).astype(F32)
-        spread[:, peer * 128 : peer * 128 + 128] = jnp.where(chosen, values, 0.0)
-        named = jnp.where(chosen & (row % 8 == 0), element + 1.0, 0.0)
-        labels[peer] = jnp.broadcast_to(jnp.sum(named, 0, keepdims=True) - 1.0, (8, 128))
+        values = jnp.sum(jnp.where(row == column, values, 0.0), 1, keepdims=True)
+        return dot_full(repeat, jnp.broadcast_to(values, (blocks, size)))
+
+    row_wide, column_wide = place_of((8 * blocks, blocks))
+    repeat = (row_wide // 8 == column_wide).astype(F32)
+    owner = upright(packed[25:26, 0:blocks])
+    element = upright(packed[26:27, 0:blocks])
+    _, column_wide = place_of((8 * blocks, size))
+    values = kron_part(modes.T, (8 * blocks, size), 1, count)
+    values = jnp.where(element == (column_wide % count).astype(F32), values, 0.0)
+    for peer in range(spread.shape[1] // size):
+        spread[:, peer * size : peer * size + size] = jnp.where(owner == float(peer), values, 0.0)
 
 
 def shifted(sizes, shifts):
@@ -654,7 +600,6 @@
     device = lax.axis_index(("fx", "fy", "fz"))
 
     names = ("fx", "fy", "fz")
-    flags = jnp.stack([lax.axis_index("fz") % 2, lax.axis_index("fy") % 2]).astype(jnp.int32)
 
     rows = 5 * cells_x * 8
     tiles = -(-rows // 128)
@@ -665,16 +610,57 @@
         velocity,
         pressure,
         fetch=True,
-        flags=flags,
     )
     edge_a = lax.ppermute(to_a, "fz", partners((size_z,), 0, False))
     edge_b = lax.ppermute(to_b, "fz", partners((size_z,), 0, True))
 
+    near_pairs = [(i ^ 1, i) for i in range(devices)]
+    far_pairs = [pair for i in range(1, devices - 1, 2) for pair in ((i, i + 1), (i + 1, i))]
+
+    def traces(to_a, to_b):
+        far_got = lax.ppermute(to_b, names, far_pairs)
+        return lax.ppermute(to_a, names, near_pairs), far_got
+
+    size = 8 * elements
+    held = (4, 64, size)
+    faces = (96, size)
+    sides = [pltpu.VMEM(faces, F32)] * 2
+    far_scratch = sides + [pltpu.VMEM((1, 3, 64, size), F32), pltpu.SemaphoreType.DMA]
+    sound, to_a, to_b = call(
+        acoustic_start_body,
+        [held, faces, faces],
+        acoustic,
+        to_a,
+        scratch=[pltpu.VMEM((512, 128), F32)],
+        last=1,
+    )
+    got_a, got_b = traces(to_a, to_b)
+
+    six = 2 * HALO
+    edge_rows = tiles * 8
+    shapes = [
+        (edge_rows, 128),
+        (5 * six * 8 + edge_rows, 128),
+        (5 * cells_x * HALO + edge_rows, 128),
+        (5 * cells_x * HALO + edge_rows, 128),
+        (32 + edge_rows, 128),
+        (32 + edge_rows, 128),
+    ]
+    edge, along_x, y_a, y_b, xy_a, xy_b = call(pack_next_body, shapes, state, edge_a, edge_b, got_a, last=1)
+    flat = (size_x, size_y)
+    steps = [[(1, 0), (-1, 0)]] if size_x == 2 else [[(1, 0)], [(-1, 0)]]
+    places, messages = [], []
+    for first, second, spots in [(y_a, y_b, [(0, 0)])] + [(xy_a, xy_b, spots) for spots in steps]:
+        shift = spots[0][0]
+        for kept, side in ((first, False), (second, True)):
+            messages.append(lax.ppermute(kept, ("fx", "fy"), partners(flat, 1, side, shift)))
+            places.append(tuple((dx, 1) for dx, _ in spots))
+    for spots in steps:
+        messages.append(lax.ppermute(along_x, ("fx", "fy"), shifted(flat, spots[0])))
+        places.append(tuple(spots))
+
     local = (neighbours - device * elements).T.astype(F32)
-    size = 8 * elements
     blocks = block_owner.size
-    capacity = max(2, 2 * blocks // size_y)
-    fold = 128 // (8 * capacity)
     width = max(elements, blocks)
     packed = jnp.concatenate(
         [
@@ -688,7 +674,7 @@
         0,
     )
     table = jax.ShapeDtypeStruct((5, size, size), BF16)
-    near, far, deriv_rows, deriv_lanes, pair, spread, labels, speed = call(
+    near, far, deriv_rows, deriv_lanes, pair, spread, speed = call(
         tables_body,
         [
             table,
@@ -696,69 +682,21 @@
             (128, 64),
             (size, size),
             (64, 64),
-            (8 * blocks, size_y * 128),
-            (size_y, 8, 128),
+            (8 * blocks, size_y * size),
             (1, size),
         ],
         packed,
     )
 
-    near_pairs = [(i ^ 1, i) for i in range(devices)]
-    far_pairs = [pair for i in range(1, devices - 1, 2) for pair in ((i, i + 1), (i + 1, i))]
-
-    def traces(to_a, to_b):
-        far_got = lax.ppermute(to_b, names, far_pairs)
-        return lax.ppermute(to_a, names, near_pairs), far_got
-
-    held = (4, 64, size)
-    faces = (96, size)
-    sides = [pltpu.VMEM(faces, F32)] * 2
-    sound, partial, to_a, to_b = call(
-        acoustic_first_body,
-        [held, held, faces, faces],
-        acoustic,
-        deriv_rows,
-        deriv_lanes,
-        speed,
-        near,
-        scratch=[pltpu.VMEM((512, 128), F32)] + sides,
-        flags=flags,
-    )
-    got_a, got_b = traces(to_a, to_b)
-
-    six = 2 * HALO
-    edge_rows = tiles * 8
-    shapes = [
-        (edge_rows, 128),
-        (5 * six * 8 + edge_rows, 128),
-        (5 * cells_x * HALO + edge_rows, 128),
-        (5 * cells_x * HALO + edge_rows, 128),
-        (32 + edge_rows, 128),
-        (32 + edge_rows, 128),
-    ]
-    edge, along_x, y_a, y_b, xy_a, xy_b = call(pack_next_body, shapes, state, edge_a, edge_b, flags=flags)
-    flat = (size_x, size_y)
-    steps = [[(1, 0), (-1, 0)]] if size_x == 2 else [[(1, 0)], [(-1, 0)]]
-    places, messages = [], []
-    for first, second, spots in [(y_a, y_b, [(0, 0)])] + [(xy_a, xy_b, spots) for spots in steps]:
-        shift = spots[0][0]
-        for kept, side in ((first, False), (second, True)):
-            messages.append(lax.ppermute(kept, ("fx", "fy"), partners(flat, 1, side, shift)))
-            places.append(tuple((dx, 1) for dx, _ in spots))
-    for spots in steps:
-        messages.append(lax.ppermute(along_x, ("fx", "fy"), shifted(flat, spots[0])))
-        places.append(tuple(spots))
-
-    sent = (size_y, 192 // fold + 8, 128)
+    sent = (size_y, 3, 64, size)
     wide = cells_x + 2 * HALO
-    rows_shape = (3, 64, 128)
-    rows_scratch = pltpu.VMEM(rows_shape, F32)
+    rows_scratch = pltpu.VMEM((3, 64, 128), F32)
 
     def planes(count):
         return (5, count, 16, 256)
 
     def route(send):
-        return lax.all_to_all(send, "fy", split_axis=0, concat_axis=0, tiled=True)
+        return lax.psum_scatter(send, "fy", scatter_dimension=0, tiled=True)
 
     spare = [pltpu.VMEM(shapes[2], F32)] * 2 + [pltpu.VMEM(shapes[4], F32)] * (2 * len(steps))
     start, send = call(
@@ -769,46 +707,47 @@
         *messages,
         pair,
         spread,
-        labels,
+        got_b,
         scratch=[pltpu.VMEM((3, wide, 16, 256), F32), rows_scratch] + spare,
-        flags=flags,
+        last=1,
     )
     received = route(send)
-    flow_one, lamb_rows = call(
+    flow_one, send = call(
         flow_first_body,
-        [planes(wide - 2), rows_shape],
+        [planes(wide - 2), sent],
         start,
-        scratch=[pltpu.VMEM(planes(wide), F32)],
-    )
-    sound_one, to_a, to_b, send = call(
-        functools.partial(acoustic_far_body, MIXES[0], "first"),
-        [held, faces, faces, sent],
-        partial,
-        got_a,
-        got_b,
-        far,
-        received,
-        lamb_rows,
         pair,
         spread,
-        labels,
-        scratch=sides,
-        flags=flags,
-    )
-    got_a, got_b = traces(to_a, to_b)
-    received = route(send)
-
+        scratch=[pltpu.VMEM(planes(wide), F32), rows_scratch],
+    )
+    received_next = route(send)
     def local_part(mix, now):
         return call(
             functools.partial(acoustic_local_body, mix),
-            [held, faces, faces],
+            [held],
             now,
             sound,
             deriv_rows,
             deriv_lanes,
             speed,
             near,
+            scratch=sides,
         )[0]
+
+    partial = local_part(MIXES[0], sound)
+    sound_one, to_a, to_b = call(
+        functools.partial(acoustic_far_body, MIXES[0], False),
+        [held, faces, faces],
+        partial,
+        got_a,
+        got_b,
+        far,
+        received,
+        scratch=far_scratch,
+        last=1,
+    )
+    got_a, got_b = traces(to_a, to_b)
+    received = received_next
 
     partial = local_part(MIXES[1], sound_one)
     flow_state, send = call(
@@ -818,34 +757,33 @@
         start,
         pair,
         spread,
-        labels,
         scratch=[pltpu.VMEM(planes(wide - 2), F32), rows_scratch, pltpu.VMEM(planes(wide - 4), F32)],
     )
     sound_two, to_a, to_b = call(
-        functools.partial(acoustic_far_body, MIXES[1], "second"),
+        functools.partial(acoustic_far_body, MIXES[1], False),
         [held, faces, faces],
         partial,
         got_a,
         got_b,
         far,
         received,
-        scratch=sides,
-        flags=flags,
+        scratch=far_scratch,
+        last=1,
     )
     got_a, got_b = traces(to_a, to_b)
     received = route(send)
     partial = local_part(MIXES[2], sound_two)
-    sound_state, _ = call(
-        functools.partial(acoustic_far_body, MIXES[2], "last"),
-        [(elements, 4, 512), held],
+    sound_state = call(
+        functools.partial(acoustic_far_body, MIXES[2], True),
+        [(elements, 4, 512)],
         partial,
         got_a,
         got_b,
         far,
         received,
-        scratch=[pltpu.VMEM((512, 128), F32)] + sides,
-        flags=flags,
-    )
+        scratch=far_scratch + [pltpu.VMEM(held, F32), pltpu.VMEM((512, 128), F32)],
+        last=1,
+    )[0]
     return (flow_state, sound_state)
 
 

time: 85.9 us -> 107 us (1.25)
  waiting for transfers between devices: 7.97 us -> 41.6 us
  starting transfers between devices: 38.2 us -> 20.3 us
  between operations: 0.86 us -> 13.9 us
  Pallas kernels: 25.6 us -> 19.4 us
  local copies, waits for them, and re-layouts: 9.9 us -> 8.05 us
    reduce_scatter x0 -> x3, waiting for transfers between devices: none -> 41 us  [route(): return lax.psum_scatter(send, 'fy', scatter_dimension=0, tiled=True)]
    all_to_all x3 -> x0, starting transfers between devices: 11.5 us -> none  [route(): return lax.all_to_all(send, 'fy', split_axis=0, concat_axis=0, tiled=True)]
    ppermute x3, starting transfers between devices: 17.8 us -> 10.7 us  [traces(): far_got = lax.ppermute(to_b, names, far_pairs)]
    pallas_call x12 -> x13, Pallas kernels: 25.6 us -> 19.4 us  [call(): pl.pallas_call(kernel, out_shape=outs, in_specs=specs, out_specs=[whole]...]
    ppermute x3, waiting for transfers between devices: 5.57 us -> 0.01 us  [traces(): far_got = lax.ppermute(to_b, names, far_pairs)]
    ppermute x3, starting transfers between devices: 0.14 us -> 2.29 us  [traces(): return (lax.ppermute(to_a, names, near_pairs), far_got)]
    unnamed x36 -> x14, local copies, waits for them, and re-layouts: 7.83 us -> 5.98 us
  transfers between devices with their start and end apart: 16 -> 16, of which waited for: 6 -> 4; matrix products, arithmetic and copies ran while one was open for 5% -> 4% of each run, Pallas kernels for 17% -> 14%
where the time goes in v4:
time: 107 us; the launch traced here: 105 us
  waiting for transfers between devices  41.6 us (39%)
  starting transfers between devices  20.3 us (19%)
  Pallas kernels  19.4 us (18%)
  between operations  13.9 us (13%)
  local copies, waits for them, and re-layouts  8.05 us (8%)
  other arithmetic  2.01 us (2%)
    reduce_scatter x3, waiting for transfers between devices, route(): return lax.psum_scatter(send, 'fy', scatter_dimension=0, tiled=True)  41 us
    pallas_call x13, Pallas kernels, call(): pl.pallas_call(kernel, out_shape=outs, in_specs=specs, out_specs=[whole]...  19.4 us
    ppermute x3, starting transfers between devices, traces(): far_got = lax.ppermute(to_b, names, far_pairs)  10.7 us
    unnamed x14, local copies, waits for them, and re-layouts  5.98 us
    ppermute x4, starting transfers between devices, per_device(): lax.ppermute(kept, ('fx', 'fy'), partners(flat, 1, side, shift))  5.91 us
    ppermute x3, starting transfers between devices, traces(): return (lax.ppermute(to_a, names, near_pairs), far_got)  2.29 us
  transfers between devices with their start and end apart: 16, of which 4 were waited for; matrix products, arithmetic and copies ran while one was open for 4% of the time, Pallas kernels for 14%

profile of v4, /device:TPU:2, one launch (start us, length us, event | category | flops | bytes accessed | tf_op | source)
XLA Modules:
  0.0 105.3 jit_solution(15395430365902179863)
XLA Ops:
  7.2 0.9 copy-done.2
  8.1 0.8 copy-done.5
  8.9 0.8 copy-done.6
  10.1 0.9 copy-done
  11.0 0.8 shard_map.114
  11.8 0.6 collective-permute-start.2
  12.3 1.2 %collective-permute-start.1 = (f32[24,128]{1,0:T(8,128)S(1)}, f32[24,128]{1,0:T(8,128)S(1)}, u32[]{:S(2)}, u32[]{:S(2)}) collective-permute-start(f32[24,128]{1,0:T(8,128)S(1)} %get-tuple-element.35), channel_id=1, source_target_pairs={{3,0},{2,1},{1,2},{0,3},{7,4},{6,5},{5,6},{4,7},{11,8},{10,9},{9,1... | collective-permute-start | bytes 36872 | tf_op jit(solution)/shard_map/ppermute | solution.py:615
  13.5 5.4 %collective-permute-start.8 = (f32[96,128]{1,0:T(8,128)S(1)}, f32[96,128]{1,0:T(8,128)S(1)}, u32[]{:S(2)}, u32[]{:S(2)}) collective-permute-start(f32[96,128]{1,0:T(8,128)S(1)} %get-tuple-element.45), channel_id=1, source_target_pairs={{1,2},{2,1},{3,4},{4,3},{5,6},{6,5},{7,8},{8,7},{9,10},{10,9},{11,... | collective-permute-start | bytes 147464 | tf_op jit(solution)/shard_map/ppermute | solution.py:621
  19.0 0.7 convert_bitcast_fusion
  19.7 0.7 convert_bitcast_fusion.1
  20.6 1.4 %collective-permute-start.4 = (f32[144,128]{1,0:T(8,128)S(1)}, f32[144,128]{1,0:T(8,128)S(1)}, u32[]{:S(2)}, u32[]{:S(2)}) collective-permute-start(f32[144,128]{1,0:T(8,128)S(1)} %get-tuple-element.39), channel_id=1, source_target_pairs={{12,0},{8,4},{4,8},{0,12},{28,16},{24,20},{20,24},{16,28},{13,1},{... | collective-permute-start | bytes 221192 | tf_op jit(solution)/shard_map/ppermute | solution.py:656
  21.9 2.0 %collective-permute-start.5 = (f32[56,128]{1,0:T(8,128)S(1)}, f32[56,128]{1,0:T(8,128)S(1)}, u32[]{:S(2)}, u32[]{:S(2)}) collective-permute-start(f32[56,128]{1,0:T(8,128)S(1)} %get-tuple-element.40), channel_id=1, source_target_pairs={{20,0},{16,4},{28,8},{24,12},{4,16},{0,20},{12,24},{8,28},{21,1},{... | collective-permute-start | bytes 86024 | tf_op jit(solution)/shard_map/ppermute | solution.py:656
  24.0 2.4 %collective-permute-start.6 = (f32[56,128]{1,0:T(8,128)S(1)}, f32[56,128]{1,0:T(8,128)S(1)}, u32[]{:S(2)}, u32[]{:S(2)}) collective-permute-start(f32[56,128]{1,0:T(8,128)S(1)} %get-tuple-element.41), channel_id=1, source_target_pairs={{28,0},{24,4},{20,8},{16,12},{12,16},{8,20},{4,24},{0,28},{29,1},{... | collective-permute-start | bytes 86024 | tf_op jit(solution)/shard_map/ppermute | solution.py:656
  26.4 0.7 convert_bitcast_fusion.2
  27.1 0.7 pad.15
  27.8 0.7 pad.16
  28.5 0.7 concatenate.3.packed
  29.1 0.9 shard_map.116
  30.6 2.7 %shard_map.117 = (f32[5,14,16,256]{3,2,1,0:T(8,128)S(1)}, f32[4,3,64,128]{3,2,1,0:T(8,128)}) custom-call(f32[5,8,8,128]{3,2,1,0:T(8,128)S(1)} %get-tuple-element.33.state.refs_0_, f32[24,128]{1,0:T(8,128)S(1)} %get-tuple-element.37.refs_1_, f32[144,128]{1,0:T(8,128)S(1)} %collective-permute-done.3.refs_2_, f32[144,128]{1,0:T(8,128)S(1)} %collective-permute-done.4.refs_3_, ...), custom_call_target="tpu_custom_call" | custom-call | tf_op jit(solution)/shard_map/pallas_call | solution.py:71
  33.3 4.9 %shard_map.118 = (f32[5,12,16,256]{3,2,1,0:T(8,128)S(1)}, f32[4,3,64,128]{3,2,1,0:T(8,128)}) custom-call(f32[5,14,16,256]{3,2,1,0:T(8,128)S(1)} %get-tuple-element.46.wide.start, f32[64,64]{1,0:T(8,128)S(1)} %get-tuple-element.43.refs_7_.pair, f32[128,512]{1,0:T(8,128)S(1)} %get-tuple-element.44.refs_8_.spread), custom_call_target="tpu_custom_call" | custom-call | tf_op jit(solution)/shard_map/pallas_call | solution.py:71
  38.3 5.9 %shard_map.119 = (f32[5,8,8,128]{3,2,1,0:T(8,128)}, f32[4,3,64,128]{3,2,1,0:T(8,128)}) custom-call(f32[5,12,16,256]{3,2,1,0:T(8,128)S(1)} %get-tuple-element.47.wide, f32[5,14,16,256]{3,2,1,0:T(8,128)S(1)} %get-tuple-element.46.wide.start, f32[64,64]{1,0:T(8,128)S(1)} %get-tuple-element.43.refs_7_.pair, f32[128,512]{1,0:T(8,128)S(1)} %get-tuple-element.44.refs_8_.spread), custom_call_target="tpu_custom_call" | custom-call | tf_op jit(solution)/shard_map/pallas_call | solution.py:71
  44.6 9.0 %reduce-scatter.4.cloned.1.call-done.received = f32[1,3,64,128]{3,2,1,0:T(8,128)} async-done(((f32[4,3,64,128]{3,2,1,0:T(8,128)}), f32[1,3,64,128]{3,2,1,0:T(8,128)}) %reduce-scatter.4.cloned.1.call-update) | async-done | bytes 98320 | tf_op jit(solution)/shard_map/reduce_scatter | solution.py:699
  53.6 0.9 copy-done.4
  54.5 0.5 shard_map.121
  55.0 1.9 %collective-permute-start.10 = (f32[96,128]{1,0:T(8,128)S(1)}, f32[96,128]{1,0:T(8,128)S(1)}, u32[]{:S(2)}, u32[]{:S(2)}) collective-permute-start(f32[96,128]{1,0:T(8,128)S(1)} %get-tuple-element.58), channel_id=1, source_target_pairs={{1,2},{2,1},{3,4},{4,3},{5,6},{6,5},{7,8},{8,7},{9,10},{10,9},{11,... | collective-permute-start | bytes 147464 | tf_op jit(solution)/shard_map/ppermute | solution.py:621
  57.0 1.7 %collective-permute-start.9 = (f32[96,128]{1,0:T(8,128)S(1)}, f32[96,128]{1,0:T(8,128)S(1)}, u32[]{:S(2)}, u32[]{:S(2)}) collective-permute-start(f32[96,128]{1,0:T(8,128)S(1)} %get-tuple-element.57), channel_id=1, source_target_pairs={{1,0},{0,1},{3,2},{2,3},{5,4},{4,5},{7,6},{6,7},{9,8},{8,9},{11,10... | collective-permute-start | bytes 147464 | tf_op jit(solution)/shard_map/ppermute | solution.py:622
  59.0 16.0 %reduce-scatter.6.cloned.1.call-done.received = f32[1,3,64,128]{3,2,1,0:T(8,128)} async-done(((f32[4,3,64,128]{3,2,1,0:T(8,128)}), f32[1,3,64,128]{3,2,1,0:T(8,128)}) %reduce-scatter.6.cloned.1.call-update) | async-done | bytes 98320 | tf_op jit(solution)/shard_map/reduce_scatter | solution.py:699
  75.0 0.9 copy-done.3
  76.4 3.3 %collective-permute-start.12 = (f32[96,128]{1,0:T(8,128)S(1)}, f32[96,128]{1,0:T(8,128)S(1)}, u32[]{:S(2)}, u32[]{:S(2)}) collective-permute-start(f32[96,128]{1,0:T(8,128)S(1)} %get-tuple-element.62), channel_id=1, source_target_pairs={{1,2},{2,1},{3,4},{4,3},{5,6},{6,5},{7,8},{8,7},{9,10},{10,9},{11,... | collective-permute-start | bytes 147464 | tf_op jit(solution)/shard_map/ppermute | solution.py:621
  80.1 16.0 %reduce-scatter.8.cloned.1.call-done.received = f32[1,3,64,128]{3,2,1,0:T(8,128)} async-done(((f32[4,3,64,128]{3,2,1,0:T(8,128)}), f32[1,3,64,128]{3,2,1,0:T(8,128)}) %reduce-scatter.8.cloned.1.call-update) | async-done | bytes 98320 | tf_op jit(solution)/shard_map/reduce_scatter | solution.py:699
  96.1 0.9 copy-done.1
  97.0 1.7 %shard_map.125 = f32[16,4,512]{2,1,0:T(4,128)} custom-call(f32[4,64,128]{2,1,0:T(8,128)S(1)} %shard_map.124.partial, f32[96,128]{1,0:T(8,128)S(1)} %collective-permute-done.11.got_a, f32[96,128]{1,0:T(8,128)S(1)} %collective-permute-done.12.got_b, bf16[5,128,128]{2,1,0:T(8,128)(2,1)S(1)} %get-tuple-element.54.sides_far, f32[1,3,64,128]{3,2,1,0:T(8,128)S(1)} %copy-done.1), custom_call_target="tpu_custom_call" | custom-call | tf_op jit(solution)/shard_map/pallas_call | solution.py:71
  (38 shorter events, 2.9 us)
Async XLA Ops:
  7.2 46.5 %reduce-scatter.4.cloned.1.call-start = ((), (), s32[]{:S(2)}) async-start(), calls=%async_computation.3 | async-start | bytes 491520 | tf_op jit(solution)/shard_map/reduce_scatter | solution.py:699
  7.2 0.9 copy-start.2
  8.1 0.8 copy-start.5
  8.9 0.8 copy-start.6
  10.0 10.4 %collective-permute-start = (f32[24,128]{1,0:T(8,128)S(1)}, f32[24,128]{1,0:T(8,128)S(1)}, u32[]{:S(2)}, u32[]{:S(2)}) collective-permute-start(f32[24,128]{1,0:T(8,128)S(1)} %get-tuple-element.34._), channel_id=1, source_target_pairs={{1,0},{0,1},{3,2},{2,3},{5,4},{4,5},{7,6},{6,7},{9,8},{8,9},{11,10... | collective-permute-start | bytes 36872 | tf_op jit(solution)/shard_map/ppermute | solution.py:614
  10.0 0.9 copy-start
  11.8 8.6 %collective-permute-start.2 = (f32[96,128]{1,0:T(8,128)S(1)}, f32[96,128]{1,0:T(8,128)S(1)}, u32[]{:S(2)}, u32[]{:S(2)}) collective-permute-start(f32[96,128]{1,0:T(8,128)S(1)} %get-tuple-element.36), channel_id=1, source_target_pairs={{1,0},{0,1},{3,2},{2,3},{5,4},{4,5},{7,6},{6,7},{9,8},{8,9},{11,10... | collective-permute-start | bytes 147464 | tf_op jit(solution)/shard_map/ppermute | solution.py:622
  12.3 8.0 %collective-permute-start.1 = (f32[24,128]{1,0:T(8,128)S(1)}, f32[24,128]{1,0:T(8,128)S(1)}, u32[]{:S(2)}, u32[]{:S(2)}) collective-permute-start(f32[24,128]{1,0:T(8,128)S(1)} %get-tuple-element.35), channel_id=1, source_target_pairs={{3,0},{2,1},{1,2},{0,3},{7,4},{6,5},{5,6},{4,7},{11,8},{10,9},{9,1... | collective-permute-start | bytes 36872 | tf_op jit(solution)/shard_map/ppermute | solution.py:615
  13.5 10.5 %collective-permute-start.8 = (f32[96,128]{1,0:T(8,128)S(1)}, f32[96,128]{1,0:T(8,128)S(1)}, u32[]{:S(2)}, u32[]{:S(2)}) collective-permute-start(f32[96,128]{1,0:T(8,128)S(1)} %get-tuple-element.45), channel_id=1, source_target_pairs={{1,2},{2,1},{3,4},{4,3},{5,6},{6,5},{7,8},{8,7},{9,10},{10,9},{11,... | collective-permute-start | bytes 147464 | tf_op jit(solution)/shard_map/ppermute | solution.py:621
  20.4 10.1 %collective-permute-start.7 = (f32[264,128]{1,0:T(8,128)S(1)}, f32[264,128]{1,0:T(8,128)S(1)}, u32[]{:S(2)}, u32[]{:S(2)}) collective-permute-start(f32[264,128]{1,0:T(8,128)S(1)} %get-tuple-element.42), channel_id=1, source_target_pairs={{16,0},{20,4},{24,8},{28,12},{0,16},{4,20},{8,24},{12,28},{17,1},{... | collective-permute-start | bytes 405512 | tf_op jit(solution)/shard_map/ppermute | solution.py:659
  20.5 10.1 %collective-permute-start.3 = (f32[144,128]{1,0:T(8,128)S(1)}, f32[144,128]{1,0:T(8,128)S(1)}, u32[]{:S(2)}, u32[]{:S(2)}) collective-permute-start(f32[144,128]{1,0:T(8,128)S(1)} %get-tuple-element.38), channel_id=1, source_target_pairs={{4,0},{0,4},{12,8},{8,12},{20,16},{16,20},{28,24},{24,28},{5,1},{1... | collective-permute-start | bytes 221192 | tf_op jit(solution)/shard_map/ppermute | solution.py:656
  20.6 10.0 %collective-permute-start.4 = (f32[144,128]{1,0:T(8,128)S(1)}, f32[144,128]{1,0:T(8,128)S(1)}, u32[]{:S(2)}, u32[]{:S(2)}) collective-permute-start(f32[144,128]{1,0:T(8,128)S(1)} %get-tuple-element.39), channel_id=1, source_target_pairs={{12,0},{8,4},{4,8},{0,12},{28,16},{24,20},{20,24},{16,28},{13,1},{... | collective-permute-start | bytes 221192 | tf_op jit(solution)/shard_map/ppermute | solution.py:656
  21.9 8.1 %collective-permute-start.5 = (f32[56,128]{1,0:T(8,128)S(1)}, f32[56,128]{1,0:T(8,128)S(1)}, u32[]{:S(2)}, u32[]{:S(2)}) collective-permute-start(f32[56,128]{1,0:T(8,128)S(1)} %get-tuple-element.40), channel_id=1, source_target_pairs={{20,0},{16,4},{28,8},{24,12},{4,16},{0,20},{12,24},{8,28},{21,1},{... | collective-permute-start | bytes 86024 | tf_op jit(solution)/shard_map/ppermute | solution.py:656
  24.0 6.6 %collective-permute-start.6 = (f32[56,128]{1,0:T(8,128)S(1)}, f32[56,128]{1,0:T(8,128)S(1)}, u32[]{:S(2)}, u32[]{:S(2)}) collective-permute-start(f32[56,128]{1,0:T(8,128)S(1)} %get-tuple-element.41), channel_id=1, source_target_pairs={{28,0},{24,4},{20,8},{16,12},{12,16},{8,20},{4,24},{0,28},{29,1},{... | collective-permute-start | bytes 86024 | tf_op jit(solution)/shard_map/ppermute | solution.py:656
  33.2 41.7 %reduce-scatter.6.cloned.1.call-start = ((), (), s32[]{:S(2)}) async-start(), calls=%async_computation.4 | async-start | bytes 491520 | tf_op jit(solution)/shard_map/reduce_scatter | solution.py:699
  38.3 57.9 %reduce-scatter.8.cloned.1.call-start = ((), (), s32[]{:S(2)}) async-start(), calls=%async_computation.5 | async-start | bytes 491520 | tf_op jit(solution)/shard_map/reduce_scatter | solution.py:699
  53.6 0.9 copy-start.4
  55.0 19.9 %collective-permute-start.10 = (f32[96,128]{1,0:T(8,128)S(1)}, f32[96,128]{1,0:T(8,128)S(1)}, u32[]{:S(2)}, u32[]{:S(2)}) collective-permute-start(f32[96,128]{1,0:T(8,128)S(1)} %get-tuple-element.58), channel_id=1, source_target_pairs={{1,2},{2,1},{3,4},{4,3},{5,6},{6,5},{7,8},{8,7},{9,10},{10,9},{11,... | collective-permute-start | bytes 147464 | tf_op jit(solution)/shard_map/ppermute | solution.py:621
  57.0 18.0 %collective-permute-start.9 = (f32[96,128]{1,0:T(8,128)S(1)}, f32[96,128]{1,0:T(8,128)S(1)}, u32[]{:S(2)}, u32[]{:S(2)}) collective-permute-start(f32[96,128]{1,0:T(8,128)S(1)} %get-tuple-element.57), channel_id=1, source_target_pairs={{1,0},{0,1},{3,2},{2,3},{5,4},{4,5},{7,6},{6,7},{9,8},{8,9},{11,10... | collective-permute-start | bytes 147464 | tf_op jit(solution)/shard_map/ppermute | solution.py:622
  75.0 0.9 copy-start.3
  76.4 19.8 %collective-permute-start.11 = (f32[96,128]{1,0:T(8,128)S(1)}, f32[96,128]{1,0:T(8,128)S(1)}, u32[]{:S(2)}, u32[]{:S(2)}) collective-permute-start(f32[96,128]{1,0:T(8,128)S(1)} %get-tuple-element.61), channel_id=1, source_target_pairs={{1,0},{0,1},{3,2},{2,3},{5,4},{4,5},{7,6},{6,7},{9,8},{8,9},{11,10... | collective-permute-start | bytes 147464 | tf_op jit(solution)/shard_map/ppermute | solution.py:622
  76.4 19.7 %collective-permute-start.12 = (f32[96,128]{1,0:T(8,128)S(1)}, f32[96,128]{1,0:T(8,128)S(1)}, u32[]{:S(2)}, u32[]{:S(2)}) collective-permute-start(f32[96,128]{1,0:T(8,128)S(1)} %get-tuple-element.62), channel_id=1, source_target_pairs={{1,2},{2,1},{3,4},{4,3},{5,6},{6,5},{7,8},{8,7},{9,10},{10,9},{11,... | collective-permute-start | bytes 147464 | tf_op jit(solution)/shard_map/ppermute | solution.py:621
  96.1 0.9 copy-start.1
Sparse Core Ops, SparseCore 0:
  33.4 20.2 reduce-scatter.3
  56.0 18.8 reduce-scatter.5
  77.2 18.8 reduce-scatter.7

commit v5 on v4

--- a/solution.py
+++ b/solution.py
@@ -78,6 +78,14 @@
     )(*operands)
 
 
+def capacity_of(peers, blocks):
+    return max(2, 2 * blocks // peers)
+
+
+def fold_of(peers, blocks):
+    return 128 // (8 * capacity_of(peers, blocks))
+
+
 def is_odd(axis):
     return lax.axis_index(axis) % 2 == 1
 
@@ -86,15 +94,8 @@
     return jnp.where(odd, to_last, to_next), jnp.where(odd, to_next, to_last)
 
 
-def pack_start_body(density, velocity, pressure, state, message_a, message_b):
+def pack_start_body(state, message_a, message_b):
     odd = is_odd("fz")
-    rho = density[...]
-    vel = velocity[...]
-    state[0] = rho
-    for k in range(3):
-        state[1 + k] = rho * vel[k]
-    square = vel[0] * vel[0] + vel[1] * vel[1] + vel[2] * vel[2]
-    state[4] = pressure[...] / (HEAT_RATIO - 1.0) + 0.5 * rho * square
     rows = state[...].reshape(-1, 128)
     count = rows.shape[0]
     for tile in range(message_a.shape[0] // 8):
@@ -281,20 +282,27 @@
     lax.fori_loop(0, cells_x, one, 0)
 
 
-def project(lamb_rows, pair, spread, send):
+def project(lamb_rows, pair, spread, send, base):
     peers = send.shape[0]
+    fold = fold_of(peers, spread.shape[0] // 8)
+    height = 64 // fold
+    group = lax.broadcasted_iota(jnp.int32, (height, 128), 1) // (128 // fold)
     for c in range(3):
         sent = dot_three(dot_three(pair[...], lamb_rows[c]), spread[...])
         for peer in range(peers):
-            send[peer, c] = sent[:, peer * 128 : peer * 128 + 128]
+            mine = sent[:, peer * 128 : peer * 128 + 128]
+            folded = mine[0:height]
+            for g in range(1, fold):
+                folded = jnp.where(group == g, mine[g * height : g * height + height], folded)
+            send[peer, base + c * height : base + c * height + height] = folded
 
 
 def flow_sources_body(places, *refs):
     state, edge = refs[0:2]
     messages = refs[2 : 2 + len(places)]
-    pair, spread, _ = refs[2 + len(places) : 5 + len(places)]
-    wide, send, derived, lamb_rows = refs[5 + len(places) : 9 + len(places)]
-    spare = refs[9 + len(places) :]
+    pair, spread, labels, _ = refs[2 + len(places) : 6 + len(places)]
+    wide, send, derived, lamb_rows = refs[6 + len(places) : 10 + len(places)]
+    spare = refs[10 + len(places) :]
     cells_x = state.shape[1]
     odd = is_odd("fy")
     beside, k = [], 0
@@ -312,37 +320,31 @@
     assemble(wide, state, edge, beside, cells_x)
     derive_speeds(wide, derived, HALO - 1, HALO + cells_x + 1)
     lamb(derived, HALO, cells_x, lamb_rows)
-    project(lamb_rows, pair, spread, send)
-
-
-def flow_first_body(wide, pair, spread, out, send, derived, lamb_rows):
-    def write(i, f, value):
-        out[f, i] = value
-
-    planes = wide.shape[1]
-    cells_x = planes - 2 * HALO
-    derive_planes(wide, derived, 0, planes)
-    flow_rate_section(wide, derived, wide, 0, MIXES[0], write)
-    derive_speeds(out, derived, HALO - 2, HALO + cells_x)
-    lamb(derived, HALO - 1, cells_x, lamb_rows)
-    project(lamb_rows, pair, spread, send)
-
-
-def flow_last_body(wide, start, pair, spread, out, send, derived, lamb_rows, second):
-    def write_second(i, f, value):
-        second[f, i] = value
-
-    def write(i, f, value):
-        out[f, i] = value
+    project(lamb_rows, pair, spread, send, 0)
+    send[:, send.shape[1] - 8 :] = labels[...]
+
+
+def flow_stages_body(wide, pair, spread, labels, out, send, derived, lamb_rows, first, second):
+    def writer(target):
+        def write(i, f, value):
+            target[f, i] = value
+
+        return write
 
     planes = wide.shape[1]
     cells_x = out.shape[1]
+    size = (send.shape[1] - 8) // 2
     derive_planes(wide, derived, 0, planes)
-    flow_rate_section(wide, derived, start, 1, MIXES[1], write_second)
-    derive_planes(second, derived, 0, planes - 2)
+    flow_rate_section(wide, derived, wide, 0, MIXES[0], writer(first))
+    derive_planes(first, derived, 0, planes - 2)
+    lamb(derived, 2, cells_x, lamb_rows)
+    project(lamb_rows, pair, spread, send, 0)
+    flow_rate_section(first, derived, wide, 1, MIXES[1], writer(second))
+    derive_planes(second, derived, 0, planes - 4)
     lamb(derived, 1, cells_x, lamb_rows)
-    project(lamb_rows, pair, spread, send)
-    flow_rate_section(second, derived, start, 2, MIXES[2], write, inner=True)
+    project(lamb_rows, pair, spread, send, size)
+    send[:, 2 * size :] = labels[...]
+    flow_rate_section(second, derived, wide, 2, MIXES[2], writer(out), inner=True)
 
 
 def faces_out(state, rear, front):
@@ -465,24 +467,50 @@
         out[c] += value[c * 64 : c * 64 + 64]
 
 
-def acoustic_far_body(mix, last, partial, got_a, got_b, sides_far, received, *refs):
-    if last:
-        given_out, before, after, source, sem, out, turned = refs
+def acoustic_far_body(mix, kind, partial, got_a, got_b, sides_far, received, *refs):
+    if kind == "last":
+        given_out, before, after, out, turned = refs
+    elif kind == "first":
+        _, out, message_a, message_b, before, after, source = refs
+        place_body(received, source)
+        received = source
     else:
-        out, message_a, message_b, before, after, source, sem = refs
-    copy = pltpu.make_async_copy(received, source, sem)
-    copy.start()
+        out, message_a, message_b, before, after = refs
     odd = is_odd("fz")
     after[...], before[...] = paired(odd, got_a[...], got_b[...])
-    out[...] = partial[...]
+    out[0] = partial[0]
+    for c in range(3):
+        out[1 + c] = partial[1 + c] + (TIME_STEP * mix[1]) * received[c]
     remote_part(out, before, after, sides_far, TIME_STEP * mix[1] * PENALTY)
-    copy.wait()
-    for c in range(3):
-        out[1 + c] += (TIME_STEP * mix[1]) * source[0, c]
-    if last:
+    if kind == "last":
         natural_order(out, given_out, turned)
     else:
         faces_sent(odd, out, message_a, message_b)
+
+
+def place_body(received, *outs):
+    peers, size = received.shape[0], received.shape[1]
+    fold = 192 * len(outs) // (size - 8)
+    height = 64 // fold
+    target = lax.broadcasted_iota(jnp.int32, (128, 128), 0)
+    lane = lax.broadcasted_iota(jnp.int32, (128, 128), 1)
+    total = None
+    for peer in range(peers):
+        label = received[peer, size - 8 : size - 7, :]
+        label = jnp.broadcast_to(label, (128, 128)).astype(jnp.int32)
+        hit = (label == target % 16) & (lane % 8 == target // 16)
+        chosen = [jnp.where(hit & (lane // (128 // fold) == g), 1.0, 0.0) for g in range(fold)]
+        chosen = jnp.concatenate(chosen, 0).astype(BF16)
+        high, low = parts(received[peer, 0 : size - 8])
+        dims = (((1,), (1,)), ((), ()))
+        value = lax.dot_general(high, chosen, dims, preferred_element_type=F32)
+        value = value + lax.dot_general(low, chosen, dims, preferred_element_type=F32)
+        total = value if total is None else total + value
+    for k, out in enumerate(outs):
+        for c in range(3):
+            for g in range(fold):
+                at = (k * 3 + c) * height
+                out[c, g * height : g * height + height] = total[at : at + height, g * 128 : g * 128 + 128]
 
 
 def kron_part(matrix, shape, rows_by, columns_by):
@@ -503,6 +531,7 @@
     deriv_lanes,
     pair,
     spread,
+    labels,
     speed,
 ):
     size = near.shape[1]
@@ -544,21 +573,31 @@
     deriv_lanes[...] = jnp.where(row % count == column % count, lanes, 0.0)
     pair[...] = kron_part(modes, (64, 64), 8, 8) * kron_part(modes, (64, 64), 1, 1)
 
+    peers = labels.shape[0]
+    capacity = capacity_of(peers, blocks)
     row, column = place_of((blocks, blocks))
 
     def upright(values):
-        values = jnp.sum(jnp.where(row == column, values, 0.0), 1, keepdims=True)
-        return dot_full(repeat, jnp.broadcast_to(values, (blocks, size)))
-
-    row_wide, column_wide = place_of((8 * blocks, blocks))
-    repeat = (row_wide // 8 == column_wide).astype(F32)
-    owner = upright(packed[25:26, 0:blocks])
-    element = upright(packed[26:27, 0:blocks])
-    _, column_wide = place_of((8 * blocks, size))
-    values = kron_part(modes.T, (8 * blocks, size), 1, count)
-    values = jnp.where(element == (column_wide % count).astype(F32), values, 0.0)
-    for peer in range(spread.shape[1] // size):
-        spread[:, peer * size : peer * size + size] = jnp.where(owner == float(peer), values, 0.0)
+        return jnp.sum(jnp.where(row == column, values, 0.0), 1, keepdims=True)
+
+    owner_row = packed[25:26, 0:blocks]
+    owner_column = upright(owner_row)
+    earlier = (owner_column == owner_row) & (column < row)
+    position = jnp.sum(jnp.where(earlier, 1.0, 0.0), 1, keepdims=True)
+    slot = owner_column * capacity + position
+    element_column = upright(packed[26:27, 0:blocks])
+    row, column = place_of((8 * blocks, blocks))
+    repeat = (row // 8 == column).astype(F32)
+    slot = dot_full(repeat, jnp.broadcast_to(slot, (blocks, 128)))
+    element = dot_full(repeat, jnp.broadcast_to(element_column, (blocks, 128)))
+    row, column = place_of((8 * blocks, 128))
+    values = kron_part(modes.T, (8 * blocks, 128), 1, 1)
+    inside = column % (8 * capacity) // 8
+    for peer in range(peers):
+        chosen = slot == (inside + peer * capacity).astype(F32)
+        spread[:, peer * 128 : peer * 128 + 128] = jnp.where(chosen, values, 0.0)
+        named = jnp.where(chosen & (row % 8 == 0), element + 1.0, 0.0)
+        labels[peer] = jnp.broadcast_to(jnp.sum(named, 0, keepdims=True) - 1.0, (8, 128))
 
 
 def shifted(sizes, shifts):
@@ -603,14 +642,12 @@
 
     rows = 5 * cells_x * 8
     tiles = -(-rows // 128)
-    state, to_a, to_b = call(
-        pack_start_body,
-        [(5, cells_x, 8, 128), (tiles * 8, 128), (tiles * 8, 128)],
-        density,
-        velocity,
-        pressure,
-        fetch=True,
-    )
+    square = velocity[0] * velocity[0] + velocity[1] * velocity[1] + velocity[2] * velocity[2]
+    energy = pressure / (HEAT_RATIO - 1.0) + 0.5 * density * square
+    rest = ((0, 0), (0, 0), (0, 0))
+    state = jnp.pad(density[None], ((0, 4),) + rest) + jnp.pad(density * velocity, ((1, 1),) + rest)
+    state = state + jnp.pad(energy[None], ((4, 0),) + rest)
+    to_a, to_b = call(pack_start_body, [(tiles * 8, 128), (tiles * 8, 128)], state)
     edge_a = lax.ppermute(to_a, "fz", partners((size_z,), 0, False))
     edge_b = lax.ppermute(to_b, "fz", partners((size_z,), 0, True))
 
@@ -625,7 +662,6 @@
     held = (4, 64, size)
     faces = (96, size)
     sides = [pltpu.VMEM(faces, F32)] * 2
-    far_scratch = sides + [pltpu.VMEM((1, 3, 64, size), F32), pltpu.SemaphoreType.DMA]
     sound, to_a, to_b = call(
         acoustic_start_body,
         [held, faces, faces],
@@ -659,22 +695,24 @@
         messages.append(lax.ppermute(along_x, ("fx", "fy"), shifted(flat, spots[0])))
         places.append(tuple(spots))
 
-    local = (neighbours - device * elements).T.astype(F32)
+    local = (neighbours - device * elements).T
     blocks = block_owner.size
     width = max(elements, blocks)
-    packed = jnp.concatenate(
-        [
-            jnp.pad(derivative, ((0, 0), (0, width - 8))),
-            jnp.pad(mode_basis, ((0, 0), (0, width - 8))),
-            jnp.pad(local, ((0, 2), (0, width - elements))),
-            jnp.pad(sound_speed.reshape(1, elements), ((0, 0), (0, width - elements))),
-            jnp.pad(block_owner.reshape(1, blocks).astype(F32), ((0, 0), (0, width - blocks))),
-            jnp.pad(block_element.reshape(1, blocks).astype(F32), ((0, 5), (0, width - blocks))),
-        ],
-        0,
+
+    def piece(values, first):
+        values = values.astype(F32)
+        return jnp.pad(values, ((first, 32 - first - values.shape[0]), (0, width - values.shape[1])))
+
+    packed = (
+        piece(derivative, 0)
+        + piece(mode_basis, 8)
+        + piece(local, 16)
+        + piece(sound_speed.reshape(1, elements), 24)
+        + piece(block_owner.reshape(1, blocks), 25)
+        + piece(block_element.reshape(1, blocks), 26)
     )
     table = jax.ShapeDtypeStruct((5, size, size), BF16)
-    near, far, deriv_rows, deriv_lanes, pair, spread, speed = call(
+    near, far, deriv_rows, deriv_lanes, pair, spread, labels, speed = call(
         tables_body,
         [
             table,
@@ -682,13 +720,14 @@
             (128, 64),
             (size, size),
             (64, 64),
-            (8 * blocks, size_y * size),
+            (8 * blocks, size_y * 128),
+            (size_y, 8, 128),
             (1, size),
         ],
         packed,
     )
 
-    sent = (size_y, 3, 64, size)
+    fold = fold_of(size_y, blocks)
     wide = cells_x + 2 * HALO
     rows_scratch = pltpu.VMEM((3, 64, 128), F32)
 
@@ -696,31 +735,38 @@
         return (5, count, 16, 256)
 
     def route(send):
-        return lax.psum_scatter(send, "fy", scatter_dimension=0, tiled=True)
+        return lax.all_to_all(send, "fy", split_axis=0, concat_axis=0, tiled=True)
 
     spare = [pltpu.VMEM(shapes[2], F32)] * 2 + [pltpu.VMEM(shapes[4], F32)] * (2 * len(steps))
     start, send = call(
         functools.partial(flow_sources_body, tuple(places)),
-        [planes(wide), sent],
+        [planes(wide), (size_y, 192 // fold + 8, 128)],
         state,
         edge,
         *messages,
         pair,
         spread,
+        labels,
         got_b,
         scratch=[pltpu.VMEM((3, wide, 16, 256), F32), rows_scratch] + spare,
         last=1,
     )
     received = route(send)
-    flow_one, send = call(
-        flow_first_body,
-        [planes(wide - 2), sent],
+    flow_state, send = call(
+        flow_stages_body,
+        [(5, cells_x, 8, 128), (size_y, 2 * 192 // fold + 8, 128)],
         start,
         pair,
         spread,
-        scratch=[pltpu.VMEM(planes(wide), F32), rows_scratch],
-    )
-    received_next = route(send)
+        labels,
+        scratch=[
+            pltpu.VMEM(planes(wide), F32),
+            rows_scratch,
+            pltpu.VMEM(planes(wide - 2), F32),
+            pltpu.VMEM(planes(wide - 4), F32),
+        ],
+    )
+
     def local_part(mix, now):
         return call(
             functools.partial(acoustic_local_body, mix),
@@ -736,53 +782,41 @@
 
     partial = local_part(MIXES[0], sound)
     sound_one, to_a, to_b = call(
-        functools.partial(acoustic_far_body, MIXES[0], False),
+        functools.partial(acoustic_far_body, MIXES[0], "first"),
         [held, faces, faces],
         partial,
         got_a,
         got_b,
         far,
         received,
-        scratch=far_scratch,
+        send,
+        scratch=sides + [rows_scratch],
         last=1,
     )
+    source_two, source_three = call(place_body, [(3, 64, 128)] * 2, route(send))
     got_a, got_b = traces(to_a, to_b)
-    received = received_next
-
     partial = local_part(MIXES[1], sound_one)
-    flow_state, send = call(
-        flow_last_body,
-        [(5, cells_x, 8, 128), sent],
-        flow_one,
-        start,
-        pair,
-        spread,
-        scratch=[pltpu.VMEM(planes(wide - 2), F32), rows_scratch, pltpu.VMEM(planes(wide - 4), F32)],
-    )
     sound_two, to_a, to_b = call(
-        functools.partial(acoustic_far_body, MIXES[1], False),
+        functools.partial(acoustic_far_body, MIXES[1], "second"),
         [held, faces, faces],
         partial,
         got_a,
         got_b,
         far,
-        received,
-        scratch=far_scratch,
-        last=1,
+        source_two,
+        scratch=sides,
     )
     got_a, got_b = traces(to_a, to_b)
-    received = route(send)
     partial = local_part(MIXES[2], sound_two)
     sound_state = call(
-        functools.partial(acoustic_far_body, MIXES[2], True),
+        functools.partial(acoustic_far_body, MIXES[2], "last"),
         [(elements, 4, 512)],
         partial,
         got_a,
         got_b,
         far,
-        received,
-        scratch=far_scratch + [pltpu.VMEM(held, F32), pltpu.VMEM((512, 128), F32)],
-        last=1,
+        source_three,
+        scratch=sides + [pltpu.VMEM(held, F32), pltpu.VMEM((512, 128), F32)],
     )[0]
     return (flow_state, sound_state)
 

time: 107 us -> 67.2 us (0.63); the launches traced: 105 us -> 66.7 us
  waiting for transfers between devices: 41.6 us -> 12 us
  between operations: 13.9 us -> 0.85 us
  starting transfers between devices: 20.3 us -> 30.7 us
  local copies, waits for them, and re-layouts: 8.05 us -> 0.92 us
  other arithmetic: 2.01 us -> 3.91 us
    reduce_scatter x3 -> x0, waiting for transfers between devices: 41 us -> none  [route(): return lax.psum_scatter(send, 'fy', scatter_dimension=0, tiled=True)]
    all_to_all x0 -> x2, starting transfers between devices: none -> 9.28 us  [route(): return lax.all_to_all(send, 'fy', split_axis=0, concat_axis=0, tiled=True)]
    unnamed x14 -> x10, local copies, waits for them, and re-layouts: 5.98 us -> 0.92 us
    all_to_all x0 -> x2, waiting for transfers between devices: none -> 4.74 us  [route(): return lax.all_to_all(send, 'fy', split_axis=0, concat_axis=0, tiled=True)]
    ppermute x3, waiting for transfers between devices: 0.01 us -> 4.1 us  [traces(): far_got = lax.ppermute(to_b, names, far_pairs)]
    ppermute x3, starting transfers between devices: 10.7 us -> 13.4 us  [traces(): far_got = lax.ppermute(to_b, names, far_pairs)]
    ppermute x4, waiting for transfers between devices: 0.51 us -> 3.1 us  [per_device(): lax.ppermute(kept, ('fx', 'fy'), partners(flat, 1, side, shift))]
    ppermute x3, starting transfers between devices: 2.29 us -> 0.7 us  [traces(): return (lax.ppermute(to_a, names, near_pairs), far_got)]
  transfers between devices with their start and end apart: 16 -> 15, of which waited for: 4 -> 4; matrix products, arithmetic and copies ran while one was open for 4% -> 2% of each run, Pallas kernels for 14% -> 21%
where the time goes in v5:
time: 67.2 us; the launch traced here: 66.7 us
  starting transfers between devices  30.7 us (46%)
  Pallas kernels  18.4 us (27%)
  waiting for transfers between devices  12 us (18%)
  other arithmetic  3.91 us (6%)
  local copies, waits for them, and re-layouts  0.92 us (1%)
  between operations  0.85 us (1%)
    pallas_call x13, Pallas kernels, call(): pl.pallas_call(kernel, out_shape=outs, in_specs=specs, out_specs=[whole]...  18.4 us
    ppermute x3, starting transfers between devices, traces(): far_got = lax.ppermute(to_b, names, far_pairs)  13.4 us
    all_to_all x2, starting transfers between devices, route(): return lax.all_to_all(send, 'fy', split_axis=0, concat_axis=0, tiled=True)  9.28 us
    ppermute x4, starting transfers between devices, per_device(): lax.ppermute(kept, ('fx', 'fy'), partners(flat, 1, side, shift))  5.91 us
    all_to_all x2, waiting for transfers between devices, route(): return lax.all_to_all(send, 'fy', split_axis=0, concat_axis=0, tiled=True)  4.74 us
    ppermute x3, waiting for transfers between devices, traces(): far_got = lax.ppermute(to_b, names, far_pairs)  4.1 us
    ppermute x4, waiting for transfers between devices, per_device(): lax.ppermute(kept, ('fx', 'fy'), partners(flat, 1, side, shift))  3.1 us
    convert_element_type x3, other arithmetic, piece(): values = values.astype(F32)  1.35 us
  transfers between devices with their start and end apart: 15, of which 4 were waited for; matrix products, arithmetic and copies ran while one was open for 2% of the time, Pallas kernels for 21%

profile of v5, /device:TPU:2, one launch (start us, length us, event | category | flops | bytes accessed | tf_op | source)
XLA Modules:
  0.0 66.7 jit_solution(3328133122245189554)
XLA Ops:
  0.7 0.9 %broadcast_multiply_fusion = f32[3,8,8,128]{3,2,1,0:T(8,128)S(1)} fusion(f32[3,8,8,128]{3,2,1,0:T(8,128)} %param.11, f32[8,8,128]{2,1,0:T(8,128)} %param.10), kind=kLoop, calls=%fused_computation.1 | loop fusion | flops 24576 | bytes 229376 | tf_op jit(solution)/shard_map/mul | solution.py:648
  1.6 0.8 %fusion.1 = f32[1,8,8,128]{3,2,1,0:T(8,128)S(1)} fusion(f32[3,8,8,128]{3,2,1,0:T(8,128)} %param.11, f32[8,8,128]{2,1,0:T(8,128)} %param.10, f32[8,8,128]{2,1,0:T(8,128)} %param.12), kind=kLoop, calls=%fused_computation.4 | loop fusion | flops 73728 | bytes 196608 | tf_op jit(solution)/shard_map/broadcast_in_dim | solution.py:649
  2.4 0.8 %pad_add_fusion.state.refs_0_ = f32[5,8,8,128]{3,2,1,0:T(8,128)S(1)} fusion(f32[1,8,8,128]{3,2,1,0:T(8,128)S(1)} %fusion.1, f32[3,8,8,128]{3,2,1,0:T(8,128)S(1)} %broadcast_multiply_fusion, f32[1,8,8,128]{3,2,1,0:T(8,128)} %bitcast.16), kind=kLoop, calls=%fused_computation | loop fusion | flops 81920 | bytes 327680 | tf_op jit(solution)/shard_map/add | solution.py:649
  3.2 0.1 shard_map.113
  3.4 0.9 %copy-done = f32[16,4,512]{2,1,0:T(4,128)S(1)} copy-done((f32[16,4,512]{2,1,0:T(4,128)S(1)}, f32[16,4,512]{2,1,0:T(4,128)}, u32[]{:S(2)}) %copy-start) | copy-done | bytes 131096
  4.3 0.8 %shard_map.114 = (f32[4,64,128]{2,1,0:T(8,128)S(1)}, f32[96,128]{1,0:T(8,128)S(1)}, f32[96,128]{1,0:T(8,128)S(1)}) custom-call(f32[16,4,512]{2,1,0:T(4,128)S(1)} %copy-done, f32[24,128]{1,0:T(8,128)S(1)} %get-tuple-element.33._), custom_call_target="tpu_custom_call" | custom-call | tf_op jit(solution)/shard_map/pallas_call | solution.py:71
  5.1 0.6 collective-permute-start.2
  5.7 1.2 %collective-permute-start.1 = (f32[24,128]{1,0:T(8,128)S(1)}, f32[24,128]{1,0:T(8,128)S(1)}, u32[]{:S(2)}, u32[]{:S(2)}) collective-permute-start(f32[24,128]{1,0:T(8,128)S(1)} %get-tuple-element.34), channel_id=1, source_target_pairs={{3,0},{2,1},{1,2},{0,3},{7,4},{6,5},{5,6},{4,7},{11,8},{10,9},{9,1... | collective-permute-start | bytes 36872 | tf_op jit(solution)/shard_map/ppermute | solution.py:652
  6.9 5.4 %collective-permute-start.8 = (f32[96,128]{1,0:T(8,128)S(1)}, f32[96,128]{1,0:T(8,128)S(1)}, u32[]{:S(2)}, u32[]{:S(2)}) collective-permute-start(f32[96,128]{1,0:T(8,128)S(1)} %get-tuple-element.45), channel_id=1, source_target_pairs={{1,2},{2,1},{3,4},{4,3},{5,6},{6,5},{7,8},{8,7},{9,10},{10,9},{11,... | collective-permute-start | bytes 147464 | tf_op jit(solution)/shard_map/ppermute | solution.py:658
  12.4 0.7 %convert_bitcast_fusion = f32[6,16]{1,0:T(8,128)S(1)} fusion(s32[16,6]{0,1:T(8,128)} %param.17, s32[]{:T(128)S(6)} %mul.48), kind=kLoop, calls=%fused_computation.6 | loop fusion | flops 192 | bytes 772 | tf_op jit(solution)/shard_map/convert_element_type | solution.py:703
  13.1 0.7 convert_bitcast_fusion.1
  14.0 1.4 %collective-permute-start.4 = (f32[144,128]{1,0:T(8,128)S(1)}, f32[144,128]{1,0:T(8,128)S(1)}, u32[]{:S(2)}, u32[]{:S(2)}) collective-permute-start(f32[144,128]{1,0:T(8,128)S(1)} %get-tuple-element.38), channel_id=1, source_target_pairs={{12,0},{8,4},{4,8},{0,12},{28,16},{24,20},{20,24},{16,28},{13,1},{... | collective-permute-start | bytes 221192 | tf_op jit(solution)/shard_map/ppermute | solution.py:692
  15.3 2.0 %collective-permute-start.5 = (f32[56,128]{1,0:T(8,128)S(1)}, f32[56,128]{1,0:T(8,128)S(1)}, u32[]{:S(2)}, u32[]{:S(2)}) collective-permute-start(f32[56,128]{1,0:T(8,128)S(1)} %get-tuple-element.39), channel_id=1, source_target_pairs={{20,0},{16,4},{28,8},{24,12},{4,16},{0,20},{12,24},{8,28},{21,1},{... | collective-permute-start | bytes 86024 | tf_op jit(solution)/shard_map/ppermute | solution.py:692
  17.4 2.5 %collective-permute-start.6 = (f32[56,128]{1,0:T(8,128)S(1)}, f32[56,128]{1,0:T(8,128)S(1)}, u32[]{:S(2)}, u32[]{:S(2)}) collective-permute-start(f32[56,128]{1,0:T(8,128)S(1)} %get-tuple-element.40), channel_id=1, source_target_pairs={{28,0},{24,4},{20,8},{16,12},{12,16},{8,20},{4,24},{0,28},{29,1},{... | collective-permute-start | bytes 86024 | tf_op jit(solution)/shard_map/ppermute | solution.py:692
  19.8 1.0 %shard_map.116 = (bf16[5,128,128]{2,1,0:T(8,128)(2,1)S(1)}, bf16[5,128,128]{2,1,0:T(8,128)(2,1)S(1)}, f32[128,64]{1,0:T(8,128)S(1)}, f32[128,128]{1,0:T(8,128)S(...) custom-call(f32[32,16]{1,0:T(8,128)S(1)} %pad_add_fusion.1.packed), custom_call_target="tpu_custom_call" | custom-call | tf_op jit(solution)/shard_map/pallas_call | solution.py:71
  20.8 3.1 %collective-permute-done.6.refs_5_ = f32[56,128]{1,0:T(8,128)S(1)} collective-permute-done((f32[56,128]{1,0:T(8,128)S(1)}, f32[56,128]{1,0:T(8,128)S(1)}, u32[]{:S(2)}, u32[]{:S(2)}) %collective-permute-start.6) | collective-permute-done | bytes 28704 | tf_op jit(solution)/shard_map/ppermute | solution.py:692
  23.9 2.6 %shard_map.117 = (f32[5,14,16,256]{3,2,1,0:T(8,128)S(1)}, f32[4,104,128]{2,1,0:T(8,128)}) custom-call(f32[5,8,8,128]{3,2,1,0:T(8,128)S(1)} %pad_add_fusion.state.refs_0_, f32[24,128]{1,0:T(8,128)S(1)} %get-tuple-element.36.refs_1_, f32[144,128]{1,0:T(8,128)S(1)} %collective-permute-done.3.refs_2_, f32[144,128]{1,0:T(8,128)S(1)} %collective-permute-done.4.refs_3_, ...), custom_call_target="tpu_custom_call" | custom-call | tf_op jit(solution)/shard_map/pallas_call | solution.py:71
  26.5 4.2 %all-to-all-start = ((f32[4,104,128]{2,1,0:T(8,128)}), f32[4,104,128]{2,1,0:T(8,128)S(1)}, u32[]{:S(2)}, u32[]{:S(2)}) async-start(f32[4,104,128]{2,1,0:T(8,128)} %get-tuple-element.54), calls=%async_computation | async-start | bytes 425984 | tf_op jit(solution)/shard_map/all_to_all | solution.py:738
  30.7 10.0 %shard_map.118 = (f32[5,8,8,128]{3,2,1,0:T(8,128)}, f32[4,200,128]{2,1,0:T(8,128)}) custom-call(f32[5,14,16,256]{3,2,1,0:T(8,128)S(1)} %get-tuple-element.46.wide, f32[64,64]{1,0:T(8,128)S(1)} %get-tuple-element.42.refs_7_.pair, f32[128,512]{1,0:T(8,128)S(1)} %get-tuple-element.43.refs_8_.spread, f32[4,8,128]{2,1,0:T(8,128)S(1)} %get-tuple-element.44.refs_9_.labels), custom_call_target="tpu_custom_call" | custom-call | tf_op jit(solution)/shard_map/pallas_call | solution.py:71
  40.7 5.1 %all-to-all-start.1 = ((f32[4,200,128]{2,1,0:T(8,128)}), f32[4,200,128]{2,1,0:T(8,128)S(1)}, u32[]{:S(2)}, u32[]{:S(2)}) async-start(f32[4,200,128]{2,1,0:T(8,128)} %get-tuple-element.55.refs_0_), calls=%async_computation.1 | async-start | bytes 819200 | tf_op jit(solution)/shard_map/all_to_all | solution.py:738
  45.8 0.3 shard_map.119.partial
  46.1 0.5 shard_map.120
  46.7 3.0 %collective-permute-start.10 = (f32[96,128]{1,0:T(8,128)S(1)}, f32[96,128]{1,0:T(8,128)S(1)}, u32[]{:S(2)}, u32[]{:S(2)}) collective-permute-start(f32[96,128]{1,0:T(8,128)S(1)} %get-tuple-element.58), channel_id=1, source_target_pairs={{1,2},{2,1},{3,4},{4,3},{5,6},{6,5},{7,8},{8,7},{9,10},{10,9},{11,... | collective-permute-start | bytes 147464 | tf_op jit(solution)/shard_map/ppermute | solution.py:658
  49.8 0.3 shard_map.121.partial
  50.1 4.7 %all-to-all-done.1.received = f32[4,200,128]{2,1,0:T(8,128)S(1)} async-done(((f32[4,200,128]{2,1,0:T(8,128)}), f32[4,200,128]{2,1,0:T(8,128)S(1)}, u32[]{:S(2)}, u32[]{:S(2)}) %all-to-all-start.1) | async-done | bytes 409632 | tf_op jit(solution)/shard_map/all_to_all | solution.py:738
  54.9 0.4 shard_map.122
  55.2 0.4 collective-permute-done.10.got_b
  55.7 0.3 shard_map.123
  56.1 5.0 %collective-permute-start.12 = (f32[96,128]{1,0:T(8,128)S(1)}, f32[96,128]{1,0:T(8,128)S(1)}, u32[]{:S(2)}, u32[]{:S(2)}) collective-permute-start(f32[96,128]{1,0:T(8,128)S(1)} %get-tuple-element.62), channel_id=1, source_target_pairs={{1,2},{2,1},{3,4},{4,3},{5,6},{6,5},{7,8},{8,7},{9,10},{10,9},{11,... | collective-permute-start | bytes 147464 | tf_op jit(solution)/shard_map/ppermute | solution.py:658
  61.1 0.3 shard_map.124.partial
  61.4 3.7 %collective-permute-done.12.got_b = f32[96,128]{1,0:T(8,128)S(1)} collective-permute-done((f32[96,128]{1,0:T(8,128)S(1)}, f32[96,128]{1,0:T(8,128)S(1)}, u32[]{:S(2)}, u32[]{:S(2)}) %collective-permute-start.12) | collective-permute-done | bytes 49184 | tf_op jit(solution)/shard_map/ppermute | solution.py:658
  65.1 1.6 %shard_map.125 = f32[16,4,512]{2,1,0:T(4,128)} custom-call(f32[4,64,128]{2,1,0:T(8,128)S(1)} %shard_map.124.partial, f32[96,128]{1,0:T(8,128)S(1)} %collective-permute-done.11.got_a, f32[96,128]{1,0:T(8,128)S(1)} %collective-permute-done.12.got_b, bf16[5,128,128]{2,1,0:T(8,128)(2,1)S(1)} %get-tuple-element.53.sides_far, ...), custom_call_target="tpu_custom_call" | custom-call | tf_op jit(solution)/shard_map/pallas_call | solution.py:71
  (28 shorter events, 0.5 us)
Async XLA Ops:
  0.6 13.2 %copy-start.4 = (s32[1,1,1,16,1]{3,4,2,1,0:T(1,128)S(1)}, s32[1,1,1,16,1]{3,4,2,1,0:T(1,128)}, u32[]{:S(2)}) copy-start(s32[1,1,1,16,1]{3,4,2,1,0:T(1,128)} %param.18) | copy-start | bytes 196
  0.6 19.2 %copy-start.3 = (f32[16]{0:T(128)S(1)}, f32[16]{0:T(128)}, u32[]{:S(2)}) copy-start(f32[16]{0:T(128)} %param.14) | copy-start | bytes 196
  0.7 19.2 %copy-start.2 = (f32[8,8]{1,0:T(8,128)S(1)}, f32[8,8]{1,0:T(8,128)}, u32[]{:S(2)}) copy-start(f32[8,8]{1,0:T(8,128)} %param.15) | copy-start | bytes 772
  0.7 19.2 %copy-start.1 = (f32[8,8]{1,0:T(8,128)S(1)}, f32[8,8]{1,0:T(8,128)}, u32[]{:S(2)}) copy-start(f32[8,8]{1,0:T(8,128)} %param.16) | copy-start | bytes 772
  3.3 10.4 %collective-permute-start = (f32[24,128]{1,0:T(8,128)S(1)}, f32[24,128]{1,0:T(8,128)S(1)}, u32[]{:S(2)}, u32[]{:S(2)}) collective-permute-start(f32[24,128]{1,0:T(8,128)S(1)} %get-tuple-element.33._), channel_id=1, source_target_pairs={{1,0},{0,1},{3,2},{2,3},{5,4},{4,5},{7,6},{6,7},{9,8},{8,9},{11,10... | collective-permute-start | bytes 36872 | tf_op jit(solution)/shard_map/ppermute | solution.py:651
  3.4 0.9 %copy-start = (f32[16,4,512]{2,1,0:T(4,128)S(1)}, f32[16,4,512]{2,1,0:T(4,128)}, u32[]{:S(2)}) copy-start(f32[16,4,512]{2,1,0:T(4,128)} %given.1) | copy-start | bytes 393220
  5.1 8.6 %collective-permute-start.2 = (f32[96,128]{1,0:T(8,128)S(1)}, f32[96,128]{1,0:T(8,128)S(1)}, u32[]{:S(2)}, u32[]{:S(2)}) collective-permute-start(f32[96,128]{1,0:T(8,128)S(1)} %get-tuple-element.35), channel_id=1, source_target_pairs={{1,0},{0,1},{3,2},{2,3},{5,4},{4,5},{7,6},{6,7},{9,8},{8,9},{11,10... | collective-permute-start | bytes 147464 | tf_op jit(solution)/shard_map/ppermute | solution.py:659
  5.7 8.0 %collective-permute-start.1 = (f32[24,128]{1,0:T(8,128)S(1)}, f32[24,128]{1,0:T(8,128)S(1)}, u32[]{:S(2)}, u32[]{:S(2)}) collective-permute-start(f32[24,128]{1,0:T(8,128)S(1)} %get-tuple-element.34), channel_id=1, source_target_pairs={{3,0},{2,1},{1,2},{0,3},{7,4},{6,5},{5,6},{4,7},{11,8},{10,9},{9,1... | collective-permute-start | bytes 36872 | tf_op jit(solution)/shard_map/ppermute | solution.py:652
  6.9 10.5 %collective-permute-start.8 = (f32[96,128]{1,0:T(8,128)S(1)}, f32[96,128]{1,0:T(8,128)S(1)}, u32[]{:S(2)}, u32[]{:S(2)}) collective-permute-start(f32[96,128]{1,0:T(8,128)S(1)} %get-tuple-element.45), channel_id=1, source_target_pairs={{1,2},{2,1},{3,4},{4,3},{5,6},{6,5},{7,8},{8,7},{9,10},{10,9},{11,... | collective-permute-start | bytes 147464 | tf_op jit(solution)/shard_map/ppermute | solution.py:658
  13.8 10.1 %collective-permute-start.7 = (f32[264,128]{1,0:T(8,128)S(1)}, f32[264,128]{1,0:T(8,128)S(1)}, u32[]{:S(2)}, u32[]{:S(2)}) collective-permute-start(f32[264,128]{1,0:T(8,128)S(1)} %get-tuple-element.41), channel_id=1, source_target_pairs={{16,0},{20,4},{24,8},{28,12},{0,16},{4,20},{8,24},{12,28},{17,1},{... | collective-permute-start | bytes 405512 | tf_op jit(solution)/shard_map/ppermute | solution.py:695
  13.9 10.0 %collective-permute-start.3 = (f32[144,128]{1,0:T(8,128)S(1)}, f32[144,128]{1,0:T(8,128)S(1)}, u32[]{:S(2)}, u32[]{:S(2)}) collective-permute-start(f32[144,128]{1,0:T(8,128)S(1)} %get-tuple-element.37), channel_id=1, source_target_pairs={{4,0},{0,4},{12,8},{8,12},{20,16},{16,20},{28,24},{24,28},{5,1},{1... | collective-permute-start | bytes 221192 | tf_op jit(solution)/shard_map/ppermute | solution.py:692
  14.0 10.0 %collective-permute-start.4 = (f32[144,128]{1,0:T(8,128)S(1)}, f32[144,128]{1,0:T(8,128)S(1)}, u32[]{:S(2)}, u32[]{:S(2)}) collective-permute-start(f32[144,128]{1,0:T(8,128)S(1)} %get-tuple-element.38), channel_id=1, source_target_pairs={{12,0},{8,4},{4,8},{0,12},{28,16},{24,20},{20,24},{16,28},{13,1},{... | collective-permute-start | bytes 221192 | tf_op jit(solution)/shard_map/ppermute | solution.py:692
  15.3 5.5 %collective-permute-start.5 = (f32[56,128]{1,0:T(8,128)S(1)}, f32[56,128]{1,0:T(8,128)S(1)}, u32[]{:S(2)}, u32[]{:S(2)}) collective-permute-start(f32[56,128]{1,0:T(8,128)S(1)} %get-tuple-element.39), channel_id=1, source_target_pairs={{20,0},{16,4},{28,8},{24,12},{4,16},{0,20},{12,24},{8,28},{21,1},{... | collective-permute-start | bytes 86024 | tf_op jit(solution)/shard_map/ppermute | solution.py:692
  17.4 6.6 %collective-permute-start.6 = (f32[56,128]{1,0:T(8,128)S(1)}, f32[56,128]{1,0:T(8,128)S(1)}, u32[]{:S(2)}, u32[]{:S(2)}) collective-permute-start(f32[56,128]{1,0:T(8,128)S(1)} %get-tuple-element.40), channel_id=1, source_target_pairs={{28,0},{24,4},{20,8},{16,12},{12,16},{8,20},{4,24},{0,28},{29,1},{... | collective-permute-start | bytes 86024 | tf_op jit(solution)/shard_map/ppermute | solution.py:692
  26.5 14.2 %all-to-all-start = ((f32[4,104,128]{2,1,0:T(8,128)}), f32[4,104,128]{2,1,0:T(8,128)S(1)}, u32[]{:S(2)}, u32[]{:S(2)}) async-start(f32[4,104,128]{2,1,0:T(8,128)} %get-tuple-element.54), calls=%async_computation | async-start | bytes 425984 | tf_op jit(solution)/shard_map/all_to_all | solution.py:738
  40.7 14.1 %all-to-all-start.1 = ((f32[4,200,128]{2,1,0:T(8,128)}), f32[4,200,128]{2,1,0:T(8,128)S(1)}, u32[]{:S(2)}, u32[]{:S(2)}) async-start(f32[4,200,128]{2,1,0:T(8,128)} %get-tuple-element.55.refs_0_), calls=%async_computation.1 | async-start | bytes 819200 | tf_op jit(solution)/shard_map/all_to_all | solution.py:738
  46.7 9.0 %collective-permute-start.10 = (f32[96,128]{1,0:T(8,128)S(1)}, f32[96,128]{1,0:T(8,128)S(1)}, u32[]{:S(2)}, u32[]{:S(2)}) collective-permute-start(f32[96,128]{1,0:T(8,128)S(1)} %get-tuple-element.58), channel_id=1, source_target_pairs={{1,2},{2,1},{3,4},{4,3},{5,6},{6,5},{7,8},{8,7},{9,10},{10,9},{11,... | collective-permute-start | bytes 147464 | tf_op jit(solution)/shard_map/ppermute | solution.py:658
  49.7 6.0 %collective-permute-start.9 = (f32[96,128]{1,0:T(8,128)S(1)}, f32[96,128]{1,0:T(8,128)S(1)}, u32[]{:S(2)}, u32[]{:S(2)}) collective-permute-start(f32[96,128]{1,0:T(8,128)S(1)} %get-tuple-element.57), channel_id=1, source_target_pairs={{1,0},{0,1},{3,2},{2,3},{5,4},{4,5},{7,6},{6,7},{9,8},{8,9},{11,10... | collective-permute-start | bytes 147464 | tf_op jit(solution)/shard_map/ppermute | solution.py:659
  56.0 5.4 %collective-permute-start.11 = (f32[96,128]{1,0:T(8,128)S(1)}, f32[96,128]{1,0:T(8,128)S(1)}, u32[]{:S(2)}, u32[]{:S(2)}) collective-permute-start(f32[96,128]{1,0:T(8,128)S(1)} %get-tuple-element.61), channel_id=1, source_target_pairs={{1,0},{0,1},{3,2},{2,3},{5,4},{4,5},{7,6},{6,7},{9,8},{8,9},{11,10... | collective-permute-start | bytes 147464 | tf_op jit(solution)/shard_map/ppermute | solution.py:659
  56.1 9.0 %collective-permute-start.12 = (f32[96,128]{1,0:T(8,128)S(1)}, f32[96,128]{1,0:T(8,128)S(1)}, u32[]{:S(2)}, u32[]{:S(2)}) collective-permute-start(f32[96,128]{1,0:T(8,128)S(1)} %get-tuple-element.62), channel_id=1, source_target_pairs={{1,2},{2,1},{3,4},{4,3},{5,6},{6,5},{7,8},{8,7},{9,10},{10,9},{11,... | collective-permute-start | bytes 147464 | tf_op jit(solution)/shard_map/ppermute | solution.py:658

commit v6 on v5

--- a/solution.py
+++ b/solution.py
@@ -108,13 +108,27 @@
         message_b[tile * 8 : tile * 8 + 8] = second
 
 
-def pack_next_body(state, got_a, got_b, _, edge, along_x, y_a, y_b, xy_a, xy_b):
+def pack_next_body(state, sent_a, sent_b, got_a, got_b, _, edge, along_x, y_a, y_b, xy_a, xy_b):
     cells_x = state.shape[1]
     odd_z, odd = is_odd("fz"), is_odd("fy")
-    row = lax.broadcasted_iota(jnp.int32, edge.shape, 0) % 8
+    high, low = paired(odd_z, sent_a[...], sent_b[...])
     above, below = paired(odd_z, got_a[...], got_b[...])
-    both = jnp.where(row < 4, above, below)
-    edge[...] = both
+    row = lax.broadcasted_iota(jnp.int32, (8, 128), 0)
+    x_of_lane = lax.broadcasted_iota(jnp.int32, (16, 128), 1) // 8 % cells_x
+    for tile in range(high.shape[0] // 8):
+        rows = slice(tile * 8, tile * 8 + 8)
+        upper = jnp.where(row < 3, pltpu.roll(high[rows], 3, 0), pltpu.roll(above[rows], 3, 0))
+        lower = jnp.where(row < 3, pltpu.roll(below[rows], 3, 0), pltpu.roll(low[rows], 3, 0))
+        slots = jnp.concatenate([upper, lower], 0)
+        spread = jnp.concatenate([jnp.where(x_of_lane == x, slots, 0.0) for x in range(8)], 0).T
+        for half in range(16 // cells_x):
+            f = tile * (16 // cells_x) + half
+            if f < 5:
+                at = half * cells_x * 8
+                total = spread[at : at + 8]
+                for x in range(1, cells_x):
+                    total = total + spread[at + x * 8 : at + x * 8 + 8]
+                edge[f * 8 : f * 8 + 8] = total
     planes = [cells_x - HALO + i for i in range(HALO)] + list(range(HALO))
     for f in range(5):
         for s, x in enumerate(planes):
@@ -134,29 +148,19 @@
             at += height
     for message in (along_x, y_a, y_b, xy_a, xy_b):
         size = message.shape[0]
-        message[size - edge.shape[0] : size] = both
-
-
-def turned_edges(message):
-    size = message.shape[0]
-    rows = []
-    for tile in range(3):
-        piece = message[size - 24 + tile * 8 : size - 16 + tile * 8]
-        rows.append(jnp.concatenate([piece, jnp.zeros((112, 128), F32), piece], 0).T)
-    return rows
-
-
-def assemble(wide, state, edge, beside, cells_x):
-    for dx, dy, message in [(0, 0, edge)] + beside:
-        turned = turned_edges(message)
+        message[size - 40 : size] = edge[...]
+
+
+def assemble(wide, rim, state, edge, beside, cells_x):
+    for dx, dy, message in beside:
         if dx == 0:
-            columns = [(HALO + x, x, x) for x in range(cells_x)]
+            columns = [(HALO + x, x) for x in range(cells_x)]
         elif dx < 0:
-            columns = [(i, cells_x - HALO + i, i) for i in range(HALO)]
+            columns = [(i, i) for i in range(HALO)]
         else:
-            columns = [(HALO + cells_x + i, i, HALO + i) for i in range(HALO)]
+            columns = [(HALO + cells_x + i, HALO + i) for i in range(HALO)]
         for f in range(5):
-            for plane, x, slot in columns:
+            for plane, slot in columns:
                 height = 8 if dy == 0 else HALO
                 at = (f * (cells_x if dx == 0 else 2 * HALO) + slot) * height
                 if dx != 0 and dy != 0:
@@ -165,27 +169,42 @@
                     height = (0, 1, 2, 2, 1)[slot]
                     at = f * 6 + (0, 0, 1, 3, 5)[slot]
                 low, high = {0: (0, 8), 1: (8, 8 + height), -1: (16 - height, 16)}[dy]
-                if dx == 0 and dy == 0:
-                    wide[f, plane, 0:8, 0:128] = state[f, x]
-                else:
-                    wide[f, plane, low:high, 0:128] = message[at : at + height]
-                group = f * cells_x + x
-                block = turned[group // 16][(group % 16) * 8 : (group % 16) * 8 + 8]
-                first = 8 - height if dy < 0 else 0
-                wide[f, plane, low:high, 128:256] = block[first : first + height]
+                wide[f, plane, low:high] = message[at : at + height]
+    edges = {(dx, dy): message for dx, dy, message in beside}
+    edges[0, 0] = edge
+    row = lax.broadcasted_iota(jnp.int32, (8, 128), 0)
+    lane = lax.broadcasted_iota(jnp.int32, (8, 128), 1)
+
+    def part(f, dx, dy):
+        message = edges[dx, dy]
+        at = message.shape[0] - 40 + f * 8
+        return message[at : at + 8]
+
+    def beyond(f, dy):
+        if edges[1, dy] is edges[-1, dy]:
+            return part(f, 1, dy)
+        return jnp.where(lane < 64, part(f, 1, dy), part(f, -1, dy))
+
+    for f in range(5):
+        for x in range(cells_x):
+            wide[f, HALO + x, 0:8] = state[f, x]
+        rim[f, 0:8, 0:128] = part(f, 0, 0)
+        rim[f, 0:8, 128:256] = beyond(f, 0)
+        rim[f, 8:16, 0:128] = jnp.where(row < 4, part(f, 0, 1), part(f, 0, -1))
+        rim[f, 8:16, 128:256] = jnp.where(row < 4, beyond(f, 1), beyond(f, -1))
+
+
+def primitive(rho, mx, my, mz, energy):
+    inverse = 1.0 / rho
+    u, v, w = mx * inverse, my * inverse, mz * inverse
+    p = (HEAT_RATIO - 1.0) * (energy - 0.5 * (mx * u + my * v + mz * w))
+    return u, v, w, p, jnp.sqrt(HEAT_RATIO * jnp.abs(p) * inverse)
 
 
 def derive_planes(wide, derived, first, last):
     def derive(i, _):
-        rho, mx, my, mz, energy = [wide[f, i] for f in range(5)]
-        inverse = 1.0 / rho
-        u, v, w = mx * inverse, my * inverse, mz * inverse
-        p = (HEAT_RATIO - 1.0) * (energy - 0.5 * (mx * u + my * v + mz * w))
-        derived[0, i] = u
-        derived[1, i] = v
-        derived[2, i] = w
-        derived[3, i] = p
-        derived[4, i] = jnp.sqrt(HEAT_RATIO * jnp.abs(p) * inverse)
+        for k, value in enumerate(primitive(*[wide[f, i] for f in range(5)])):
+            derived[k, i] = value
         return 0
 
     lax.fori_loop(first, last, derive, 0)
@@ -201,77 +220,118 @@
     lax.fori_loop(first, last, derive, 0)
 
 
-def flow_rate_section(wide, derived, start, offset, mix, write, inner=False):
+def with_flux(fields, other, along):
+    speed, p = other[along], other[3]
+    out = [fields[1 + along]]
+    for k in range(3):
+        value = fields[1 + k] * speed
+        out.append(value + p if k == along else value)
+    out.append((fields[4] + p) * speed)
+    return fields, out, jnp.abs(speed) + other[4]
+
+
+def face(left, right):
+    (fields_l, flux_l, speed_l), (fields_r, flux_r, speed_r) = left, right
+    speed = jnp.maximum(speed_l, speed_r)
+    viscous = speed + 2.0 * VISCOSITY
+    return [
+        (flux_l[f] + flux_r[f]) - (viscous if 1 <= f <= 3 else speed) * (fields_r[f] - fields_l[f])
+        for f in range(5)
+    ]
+
+
+def rolled(here, shift, axis):
+    fields, flux, speed = here
+    return (
+        [pltpu.roll(a, shift, axis) for a in fields],
+        [pltpu.roll(a, shift, axis) for a in flux],
+        pltpu.roll(speed, shift, axis),
+    )
+
+
+def rim_section(fields, start, mix):
+    other = primitive(*fields)
+    here = with_flux(fields, other, 2)
+    along_z = face(here, rolled(here, 255, 1))
+    if mix is None:
+        return other, along_z, None
+    total = [g - pltpu.roll(g, 1, 1) for g in along_z]
+    for along, step, axis, size in ((0, 16, 1, 256), (1, 1, 0, 16)):
+        here = with_flux(fields, other, along)
+        faces = face(here, rolled(here, size - step, axis))
+        total = [total[f] + (faces[f] - pltpu.roll(faces[f], step, axis)) for f in range(5)]
+    out = []
+    for f in range(5):
+        value = fields[f] - (0.5 * TIME_STEP) * total[f]
+        out.append(mix[0] * start[f] + mix[1] * value if mix[0] != 0.0 else value)
+    return other, along_z, out
+
+
+def to_ends(values, after, rows, first, last, ends):
+    slot = lax.broadcasted_iota(jnp.int32, (rows, 256), 1) % 16
+    for f, value in enumerate(values):
+        value = value[0:rows]
+        value = jnp.where(slot == 9, pltpu.roll(value, 9 - after, 1), value)
+        for x in range(first, last):
+            at = x % 16 // 8 * 128
+            move = (118 - x % 8 * 16) % 128
+            tile = value[:, at : at + 128]
+            ends[f, x - first, 0:rows] = pltpu.roll(tile, move, 1) if move else tile
+
+
+def flow_rate_section(wide, derived, ends, start, offset, mix, write, inner=False):
     depth = wide.shape[1]
-    near, lanes = slice(0, 8), slice(0, 128)
-    every = (slice(None), slice(None))
-    windows = [(near, lanes), (slice(None), lanes), (near, slice(None))] if inner else [every] * 3
-    kept = windows[0]
-
-    def flux(fields, other, along):
-        speed, p = other[along], other[3]
-        out = [fields[1 + along]]
-        for k in range(3):
-            value = fields[1 + k] * speed
-            out.append(value + p if k == along else value)
-        out.append((fields[4] + p) * speed)
-        return out, jnp.abs(speed) + other[4]
-
-    def face(left, right):
-        (fields_l, flux_l, speed_l), (fields_r, flux_r, speed_r) = left, right
-        speed = jnp.maximum(speed_l, speed_r)
-        viscous = speed + 2.0 * VISCOSITY
-        return [
-            (flux_l[f] + flux_r[f])
-            - (viscous if 1 <= f <= 3 else speed) * (fields_r[f] - fields_l[f])
-            for f in range(5)
-        ]
+    rows = slice(0, 8) if inner else slice(None)
+    windows = [rows, slice(None), rows]
+    lane = lax.broadcasted_iota(jnp.int32, (8 if inner else 16, 128), 1)
 
     def plane(i, along):
-        rows, columns = windows[along]
-        fields = [wide[f, i, rows, columns] for f in range(5)]
-        other = [derived[f, i, rows, columns] for f in range(5)]
-        return (fields,) + flux(fields, other, along)
+        kept = windows[along]
+        fields = [wide[f, i, kept] for f in range(5)]
+        return with_flux(fields, [derived[f, i, kept] for f in range(5)], along)
 
     def section(i, before):
-        here = plane(i, 0)
-        ahead = face(here, plane(i + 1, 0))
+        ahead = face(plane(i, 0), plane(i + 1, 0))
         total = [ahead[f] - before[f] for f in range(5)]
-        for along, axis, size in ((1, 0, 16), (2, 1, 256)):
-            here = plane(i, along)
-            moved = (
-                [pltpu.roll(a, size - 1, axis) for a in here[0]],
-                [pltpu.roll(a, size - 1, axis) for a in here[1]],
-                pltpu.roll(here[2], size - 1, axis),
-            )
-            faces = face(here, moved)
-            for f in range(5):
-                change = faces[f] - pltpu.roll(faces[f], 1, axis)
-                total[f] = total[f] + (change[0:8, 0:128] if inner else change)
+        here = plane(i, 1)
+        faces = face(here, rolled(here, 15, 0))
         for f in range(5):
-            value = wide[f, i, kept[0], kept[1]] - (0.5 * TIME_STEP) * total[f]
+            change = faces[f] - pltpu.roll(faces[f], 1, 0)
+            total[f] = total[f] + (change[0:8] if inner else change)
+        here = plane(i, 2)
+        faces = face(here, rolled(here, 127, 1))
+        for f in range(5):
+            end = ends[f, i - 1, rows]
+            value = jnp.where(lane == 127, end, faces[f])
+            total[f] = total[f] + (value - jnp.where(lane == 0, end, pltpu.roll(value, 1, 1)))
+        for f in range(5):
+            value = wide[f, i, rows] - (0.5 * TIME_STEP) * total[f]
             if mix[0] != 0.0:
-                value = mix[0] * start[f, i + offset, kept[0], kept[1]] + mix[1] * value
+                value = mix[0] * start[f, i + offset, rows] + mix[1] * value
             write(i - 1, f, value)
         return tuple(ahead)
 
     lax.fori_loop(1, depth - 1, section, tuple(face(plane(0, 0), plane(1, 0))))
 
 
-def lamb(derived, first, cells_x, lamb_rows):
+def lamb(derived, ends, first, cells_x, lamb_rows):
+    lane = lax.broadcasted_iota(jnp.int32, (8, 128), 1)
+
     def one(x, _):
         i = first + x
-        slopes = []
-        slopes.append([derived[c, i + 1, 0:8, 0:128] - derived[c, i - 1, 0:8, 0:128] for c in range(3)])
-        columns = [derived[c, i, :, 0:128] for c in range(3)]
-        slopes.append([(pltpu.roll(a, 15, 0) - pltpu.roll(a, 1, 0))[0:8] for a in columns])
-        rows = [derived[c, i, 0:8, :] for c in range(3)]
-        slopes.append([(pltpu.roll(a, 255, 1) - pltpu.roll(a, 1, 1))[:, 0:128] for a in rows])
-        vel = [derived[c, i, 0:8, 0:128] for c in range(3)]
+        vel = [derived[c, i, 0:8] for c in range(3)]
+        along_x = [derived[c, i + 1, 0:8] - derived[c, i - 1, 0:8] for c in range(3)]
+        columns = [derived[c, i] for c in range(3)]
+        along_y = [(pltpu.roll(a, 15, 0) - pltpu.roll(a, 1, 0))[0:8] for a in columns]
+        along_z = []
+        for c in range(2):
+            end = ends[c, x, 0:8]
+            after = jnp.where(lane == 127, end, pltpu.roll(vel[c], 127, 1))
+            along_z.append(after - jnp.where(lane == 0, end, pltpu.roll(vel[c], 1, 1)))
         curl = [
-            0.5 * (slopes[1][2] - slopes[2][1]),
-            0.5 * (slopes[2][0] - slopes[0][2]),
-            0.5 * (slopes[0][1] - slopes[1][0]),
+            0.5 * (along_y[2] - along_z[1]),
+            0.5 * (along_z[0] - along_x[2]),
+            0.5 * (along_x[1] - along_y[0]),
         ]
         at = pl.multiple_of(x * 8, 8)
         lamb_rows[0, pl.ds(at, 8), :] = curl[1] * vel[2] - curl[2] * vel[1]
@@ -301,8 +361,8 @@
     state, edge = refs[0:2]
     messages = refs[2 : 2 + len(places)]
     pair, spread, labels, _ = refs[2 + len(places) : 6 + len(places)]
-    wide, send, derived, lamb_rows = refs[6 + len(places) : 10 + len(places)]
-    spare = refs[10 + len(places) :]
+    wide, rim, send, derived, lamb_rows, ends = refs[6 + len(places) : 12 + len(places)]
+    spare = refs[12 + len(places) :]
     cells_x = state.shape[1]
     odd = is_odd("fy")
     beside, k = [], 0
@@ -317,14 +377,16 @@
         beside.extend((dx, 1, above) for dx, _ in places[k])
         beside.extend((dx, -1, below) for dx, _ in places[k])
         k += 2
-    assemble(wide, state, edge, beside, cells_x)
+    assemble(wide, rim, state, edge, beside, cells_x)
     derive_speeds(wide, derived, HALO - 1, HALO + cells_x + 1)
-    lamb(derived, HALO, cells_x, lamb_rows)
+    inverse = 1.0 / rim[0, 0:8]
+    to_ends([rim[1, 0:8] * inverse, rim[2, 0:8] * inverse], 3, 8, 0, cells_x, ends)
+    lamb(derived, ends, HALO, cells_x, lamb_rows)
     project(lamb_rows, pair, spread, send, 0)
     send[:, send.shape[1] - 8 :] = labels[...]
 
 
-def flow_stages_body(wide, pair, spread, labels, out, send, derived, lamb_rows, first, second):
+def flow_stages_body(wide, rim, pair, spread, labels, out, send, derived, lamb_rows, ends, first, second):
     def writer(target):
         def write(i, f, value):
             target[f, i] = value
@@ -334,17 +396,26 @@
     planes = wide.shape[1]
     cells_x = out.shape[1]
     size = (send.shape[1] - 8) // 2
+    rim_start = [rim[f] for f in range(5)]
     derive_planes(wide, derived, 0, planes)
-    flow_rate_section(wide, derived, wide, 0, MIXES[0], writer(first))
+    _, along_z, rim_first = rim_section(rim_start, None, MIXES[0])
+    to_ends(along_z, 2, 16, -2, cells_x + 2, ends)
+    flow_rate_section(wide, derived, ends, wide, 0, MIXES[0], writer(first))
     derive_planes(first, derived, 0, planes - 2)
-    lamb(derived, 2, cells_x, lamb_rows)
+    other, along_z, rim_second = rim_section(rim_first, [rim[f] for f in range(5)], MIXES[1])
+    to_ends(other[0:2], 3, 8, 0, cells_x, ends)
+    lamb(derived, ends, 2, cells_x, lamb_rows)
     project(lamb_rows, pair, spread, send, 0)
-    flow_rate_section(first, derived, wide, 1, MIXES[1], writer(second))
+    to_ends(along_z, 2, 16, -1, cells_x + 1, ends)
+    flow_rate_section(first, derived, ends, wide, 1, MIXES[1], writer(second))
     derive_planes(second, derived, 0, planes - 4)
-    lamb(derived, 1, cells_x, lamb_rows)
+    other, along_z, _ = rim_section(rim_second, None, None)
+    to_ends(other[0:2], 3, 8, 0, cells_x, ends)
+    lamb(derived, ends, 1, cells_x, lamb_rows)
     project(lamb_rows, pair, spread, send, size)
     send[:, 2 * size :] = labels[...]
-    flow_rate_section(second, derived, wide, 2, MIXES[2], writer(out), inner=True)
+    to_ends(along_z, 2, 8, 0, cells_x, ends)
+    flow_rate_section(second, derived, ends, wide, 2, MIXES[2], writer(out), inner=True)
 
 
 def faces_out(state, rear, front):
@@ -647,9 +718,9 @@
     rest = ((0, 0), (0, 0), (0, 0))
     state = jnp.pad(density[None], ((0, 4),) + rest) + jnp.pad(density * velocity, ((1, 1),) + rest)
     state = state + jnp.pad(energy[None], ((4, 0),) + rest)
-    to_a, to_b = call(pack_start_body, [(tiles * 8, 128), (tiles * 8, 128)], state)
-    edge_a = lax.ppermute(to_a, "fz", partners((size_z,), 0, False))
-    edge_b = lax.ppermute(to_b, "fz", partners((size_z,), 0, True))
+    flow_a, flow_b = call(pack_start_body, [(tiles * 8, 128), (tiles * 8, 128)], state)
+    edge_a = lax.ppermute(flow_a, "fz", partners((size_z,), 0, False))
+    edge_b = lax.ppermute(flow_b, "fz", partners((size_z,), 0, True))
 
     near_pairs = [(i ^ 1, i) for i in range(devices)]
     far_pairs = [pair for i in range(1, devices - 1, 2) for pair in ((i, i + 1), (i + 1, i))]
@@ -666,14 +737,14 @@
         acoustic_start_body,
         [held, faces, faces],
         acoustic,
-        to_a,
+        flow_a,
         scratch=[pltpu.VMEM((512, 128), F32)],
         last=1,
     )
     got_a, got_b = traces(to_a, to_b)
 
     six = 2 * HALO
-    edge_rows = tiles * 8
+    edge_rows = 5 * 8
     shapes = [
         (edge_rows, 128),
         (5 * six * 8 + edge_rows, 128),
@@ -682,7 +753,9 @@
         (32 + edge_rows, 128),
         (32 + edge_rows, 128),
     ]
-    edge, along_x, y_a, y_b, xy_a, xy_b = call(pack_next_body, shapes, state, edge_a, edge_b, got_a, last=1)
+    edge, along_x, y_a, y_b, xy_a, xy_b = call(
+        pack_next_body, shapes, state, flow_a, flow_b, edge_a, edge_b, got_a, last=1
+    )
     flat = (size_x, size_y)
     steps = [[(1, 0), (-1, 0)]] if size_x == 2 else [[(1, 0)], [(-1, 0)]]
     places, messages = [], []
@@ -732,15 +805,15 @@
     rows_scratch = pltpu.VMEM((3, 64, 128), F32)
 
     def planes(count):
-        return (5, count, 16, 256)
+        return (5, count, 16, 128)
 
     def route(send):
         return lax.all_to_all(send, "fy", split_axis=0, concat_axis=0, tiled=True)
 
     spare = [pltpu.VMEM(shapes[2], F32)] * 2 + [pltpu.VMEM(shapes[4], F32)] * (2 * len(steps))
-    start, send = call(
+    start, rim, send = call(
         functools.partial(flow_sources_body, tuple(places)),
-        [planes(wide), (size_y, 192 // fold + 8, 128)],
+        [planes(wide), (5, 16, 256), (size_y, 192 // fold + 8, 128)],
         state,
         edge,
         *messages,
@@ -748,7 +821,12 @@
         spread,
         labels,
         got_b,
-        scratch=[pltpu.VMEM((3, wide, 16, 256), F32), rows_scratch] + spare,
+        scratch=[
+            pltpu.VMEM((3, wide, 16, 128), F32),
+            rows_scratch,
+            pltpu.VMEM((2, cells_x, 8, 128), F32),
+        ]
+        + spare,
         last=1,
     )
     received = route(send)
@@ -756,12 +834,14 @@
         flow_stages_body,
         [(5, cells_x, 8, 128), (size_y, 2 * 192 // fold + 8, 128)],
         start,
+        rim,
         pair,
         spread,
         labels,
         scratch=[
             pltpu.VMEM(planes(wide), F32),
             rows_scratch,
+            pltpu.VMEM(planes(wide - 2), F32),
             pltpu.VMEM(planes(wide - 2), F32),
             pltpu.VMEM(planes(wide - 4), F32),
         ],

time: 67.2 us -> 65.1 us (0.969)
  other arithmetic: 3.91 us -> 1.01 us
  local copies, waits for them, and re-layouts: 0.92 us -> 2.63 us
    unnamed x10 -> x20, local copies, waits for them, and re-layouts: 0.92 us -> 2.63 us
    convert_element_type x3, other arithmetic: 1.35 us -> 0.01 us  [piece(): values = values.astype(F32)]
    broadcast_in_dim x1, other arithmetic: 0.84 us -> 0.02 us  [per_device(): state = state + jnp.pad(energy[None], ((4, 0),) + rest)]
    add x1, other arithmetic: 0.77 us -> 0.01 us  [per_device(): state = state + jnp.pad(energy[None], ((4, 0),) + rest)]
  transfers between devices with their start and end apart: 15 -> 15, of which waited for: 4 -> 5; matrix products, arithmetic and copies ran while one was open for 2% -> 0% of each run, Pallas kernels for 21% -> 21%
where the time goes in v6:
time: 65.1 us; the launch traced here: 64.7 us
  starting transfers between devices  30.6 us (47%)
  Pallas kernels  18 us (28%)
  waiting for transfers between devices  11.6 us (18%)
  local copies, waits for them, and re-layouts  2.63 us (4%)
  other arithmetic  1.01 us (2%)
  between operations  0.88 us (1%)
    pallas_call x13, Pallas kernels, call(): pl.pallas_call(kernel, out_shape=outs, in_specs=specs, out_specs=[whole]...  18 us
    ppermute x3, starting transfers between devices, traces(): far_got = lax.ppermute(to_b, names, far_pairs)  13.5 us
    all_to_all x2, starting transfers between devices, route(): return lax.all_to_all(send, 'fy', split_axis=0, concat_axis=0, tiled=True)  9.28 us
    ppermute x4, starting transfers between devices, per_device(): lax.ppermute(kept, ('fx', 'fy'), partners(flat, 1, side, shift))  5.84 us
    all_to_all x2, waiting for transfers between devices, route(): return lax.all_to_all(send, 'fy', split_axis=0, concat_axis=0, tiled=True)  4.55 us
    ppermute x3, waiting for transfers between devices, traces(): far_got = lax.ppermute(to_b, names, far_pairs)  4.26 us
    ppermute x4, waiting for transfers between devices, per_device(): lax.ppermute(kept, ('fx', 'fy'), partners(flat, 1, side, shift))  2.78 us
    unnamed x20, local copies, waits for them, and re-layouts  2.63 us
  transfers between devices with their start and end apart: 15, of which 5 were waited for; matrix products, arithmetic and copies ran while one was open for 0% of the time, Pallas kernels for 21%

profile of v6, /device:TPU:2, one launch (start us, length us, event | category | flops | bytes accessed | tf_op | source)
XLA Modules:
  0.0 64.7 jit_solution(4919127230001349084)
XLA Ops:
  0.7 1.0 %broadcast_multiply_fusion = f32[3,8,8,128]{3,2,1,0:T(8,128)S(1)} fusion(f32[3,8,8,128]{3,2,1,0:T(8,128)} %param.11, f32[8,8,128]{2,1,0:T(8,128)} %param.10), kind=kLoop, calls=%fused_computation.1 | loop fusion | flops 24576 | bytes 229376 | tf_op jit(solution)/shard_map/mul | solution.py:719
  1.7 0.1 shard_map.113
  1.9 0.7 %copy-done = f32[16,4,512]{2,1,0:T(4,128)S(1)} copy-done((f32[16,4,512]{2,1,0:T(4,128)S(1)}, f32[16,4,512]{2,1,0:T(4,128)}, u32[]{:S(2)}) %copy-start) | copy-done | bytes 131096
  2.6 0.8 %shard_map.114 = (f32[4,64,128]{2,1,0:T(8,128)S(1)}, f32[96,128]{1,0:T(8,128)S(1)}, f32[96,128]{1,0:T(8,128)S(1)}) custom-call(f32[16,4,512]{2,1,0:T(4,128)S(1)} %copy-done, f32[24,128]{1,0:T(8,128)S(1)} %get-tuple-element.34._.sent_a), custom_call_target="tpu_custom_call" | custom-call | tf_op jit(solution)/shard_map/pallas_call | solution.py:71
  3.5 1.6 %collective-permute-start.1 = (f32[24,128]{1,0:T(8,128)S(1)}, f32[24,128]{1,0:T(8,128)S(1)}, u32[]{:S(2)}, u32[]{:S(2)}) collective-permute-start(f32[24,128]{1,0:T(8,128)S(1)} %get-tuple-element.35.sent_b), channel_id=1, source_target_pairs={{3,0},{2,1},{1,2},{0,3},{7,4},{6,5},{5,6},{4,7},{11,8},{10,9},{9,1... | collective-permute-start | bytes 36872 | tf_op jit(solution)/shard_map/ppermute | solution.py:723
  5.1 5.1 %collective-permute-start.8 = (f32[96,128]{1,0:T(8,128)S(1)}, f32[96,128]{1,0:T(8,128)S(1)}, u32[]{:S(2)}, u32[]{:S(2)}) collective-permute-start(f32[96,128]{1,0:T(8,128)S(1)} %get-tuple-element.46), channel_id=1, source_target_pairs={{1,2},{2,1},{3,4},{4,3},{5,6},{6,5},{7,8},{8,7},{9,10},{10,9},{11,... | collective-permute-start | bytes 147464 | tf_op jit(solution)/shard_map/ppermute | solution.py:729
  10.2 0.7 %copy-done.4 = s32[16,6]{0,1:T(8,128)S(1)} copy-done((s32[16,6]{0,1:T(8,128)S(1)}, s32[16,6]{0,1:T(8,128)}, u32[]{:S(2)}) %copy-start.4) | copy-done | bytes 408
  10.9 0.6 %copy-done.8 = s32[1,1,1,16]{3,2,1,0:T(1,128)S(1)} copy-done((s32[1,1,1,16]{3,2,1,0:T(1,128)S(1)}, s32[1,1,1,16]{3,2,1,0:T(1,128)}, u32[]{:S(2)}) %copy-start.8) | copy-done | bytes 88
  11.6 0.1 shard_map.115
  11.8 0.6 copy-done.9
  12.4 1.0 %collective-permute-start.4 = (f32[160,128]{1,0:T(8,128)S(1)}, f32[160,128]{1,0:T(8,128)S(1)}, u32[]{:S(2)}, u32[]{:S(2)}) collective-permute-start(f32[160,128]{1,0:T(8,128)S(1)} %get-tuple-element.39), channel_id=1, source_target_pairs={{12,0},{8,4},{4,8},{0,12},{28,16},{24,20},{20,24},{16,28},{13,1},{... | collective-permute-start | bytes 245768 | tf_op jit(solution)/shard_map/ppermute | solution.py:765
  13.4 2.0 %collective-permute-start.5 = (f32[72,128]{1,0:T(8,128)S(1)}, f32[72,128]{1,0:T(8,128)S(1)}, u32[]{:S(2)}, u32[]{:S(2)}) collective-permute-start(f32[72,128]{1,0:T(8,128)S(1)} %get-tuple-element.40), channel_id=1, source_target_pairs={{20,0},{16,4},{28,8},{24,12},{4,16},{0,20},{12,24},{8,28},{21,1},{... | collective-permute-start | bytes 110600 | tf_op jit(solution)/shard_map/ppermute | solution.py:765
  15.4 2.9 %collective-permute-start.6 = (f32[72,128]{1,0:T(8,128)S(1)}, f32[72,128]{1,0:T(8,128)S(1)}, u32[]{:S(2)}, u32[]{:S(2)}) collective-permute-start(f32[72,128]{1,0:T(8,128)S(1)} %get-tuple-element.41), channel_id=1, source_target_pairs={{28,0},{24,4},{20,8},{16,12},{12,16},{8,20},{4,24},{0,28},{29,1},{... | collective-permute-start | bytes 110600 | tf_op jit(solution)/shard_map/ppermute | solution.py:765
  18.3 1.0 %shard_map.116 = (bf16[5,128,128]{2,1,0:T(8,128)(2,1)S(1)}, bf16[5,128,128]{2,1,0:T(8,128)(2,1)S(1)}, f32[128,64]{1,0:T(8,128)S(1)}, f32[128,128]{1,0:T(8,128)S(...) custom-call(f32[32,16]{1,0:T(8,128)S(1)} %pad_add_fusion.1.packed), custom_call_target="tpu_custom_call" | custom-call | tf_op jit(solution)/shard_map/pallas_call | solution.py:71
  19.3 1.0 %collective-permute-done.5.refs_4_ = f32[72,128]{1,0:T(8,128)S(1)} collective-permute-done((f32[72,128]{1,0:T(8,128)S(1)}, f32[72,128]{1,0:T(8,128)S(1)}, u32[]{:S(2)}, u32[]{:S(2)}) %collective-permute-start.5) | collective-permute-done | bytes 36896 | tf_op jit(solution)/shard_map/ppermute | solution.py:765
  20.3 1.8 %collective-permute-done.6.refs_5_ = f32[72,128]{1,0:T(8,128)S(1)} collective-permute-done((f32[72,128]{1,0:T(8,128)S(1)}, f32[72,128]{1,0:T(8,128)S(1)}, u32[]{:S(2)}, u32[]{:S(2)}) %collective-permute-start.6) | collective-permute-done | bytes 36896 | tf_op jit(solution)/shard_map/ppermute | solution.py:765
  22.1 2.2 %shard_map.117 = (f32[5,14,16,128]{3,2,1,0:T(8,128)S(1)}, f32[5,16,256]{2,1,0:T(8,128)S(1)}, f32[4,104,128]{2,1,0:T(8,128)}) custom-call(f32[5,8,8,128]{3,2,1,0:T(8,128)S(1)} %pad_add_fusion.state.refs_0_, f32[40,128]{1,0:T(8,128)S(1)} %get-tuple-element.37.refs_1_, f32[160,128]{1,0:T(8,128)S(1)} %collective-permute-done.3.refs_2_, ...), custom_call_target="tpu_custom_call" | custom-call | tf_op jit(solution)/shard_map/pallas_call | solution.py:71
  24.3 4.2 %all-to-all-start = ((f32[4,104,128]{2,1,0:T(8,128)}), f32[4,104,128]{2,1,0:T(8,128)S(1)}, u32[]{:S(2)}, u32[]{:S(2)}) async-start(f32[4,104,128]{2,1,0:T(8,128)} %get-tuple-element.56), calls=%async_computation | async-start | bytes 425984 | tf_op jit(solution)/shard_map/all_to_all | solution.py:811
  28.5 9.9 %shard_map.118 = (f32[5,8,8,128]{3,2,1,0:T(8,128)}, f32[4,200,128]{2,1,0:T(8,128)}) custom-call(f32[5,14,16,128]{3,2,1,0:T(8,128)S(1)} %get-tuple-element.47.wide, f32[5,16,256]{2,1,0:T(8,128)S(1)} %get-tuple-element.48.rim, f32[64,64]{1,0:T(8,128)S(1)} %get-tuple-element.43.refs_7_.pair, f32[128,512]{1,0:T(8,128)S(1)} %get-tuple-element.44.refs_8_.spread, ...), custom_call_target="tpu_custom_call" | custom-call | tf_op jit(solution)/shard_map/pallas_call | solution.py:71
  38.4 5.1 %all-to-all-start.1 = ((f32[4,200,128]{2,1,0:T(8,128)}), f32[4,200,128]{2,1,0:T(8,128)S(1)}, u32[]{:S(2)}, u32[]{:S(2)}) async-start(f32[4,200,128]{2,1,0:T(8,128)} %get-tuple-element.57.refs_0_), calls=%async_computation.1 | async-start | bytes 819200 | tf_op jit(solution)/shard_map/all_to_all | solution.py:811
  43.4 0.3 shard_map.119.partial
  43.8 0.5 shard_map.120
  44.3 3.4 %collective-permute-start.10 = (f32[96,128]{1,0:T(8,128)S(1)}, f32[96,128]{1,0:T(8,128)S(1)}, u32[]{:S(2)}, u32[]{:S(2)}) collective-permute-start(f32[96,128]{1,0:T(8,128)S(1)} %get-tuple-element.60), channel_id=1, source_target_pairs={{1,2},{2,1},{3,4},{4,3},{5,6},{6,5},{7,8},{8,7},{9,10},{10,9},{11,... | collective-permute-start | bytes 147464 | tf_op jit(solution)/shard_map/ppermute | solution.py:729
  47.8 0.3 shard_map.121.partial
  48.2 4.6 %all-to-all-done.1.received = f32[4,200,128]{2,1,0:T(8,128)S(1)} async-done(((f32[4,200,128]{2,1,0:T(8,128)}), f32[4,200,128]{2,1,0:T(8,128)S(1)}, u32[]{:S(2)}, u32[]{:S(2)}) %all-to-all-start.1) | async-done | bytes 409632 | tf_op jit(solution)/shard_map/all_to_all | solution.py:811
  52.7 0.4 shard_map.122
  53.1 0.6 collective-permute-done.10.got_b
  53.7 0.3 shard_map.123
  54.1 5.0 %collective-permute-start.12 = (f32[96,128]{1,0:T(8,128)S(1)}, f32[96,128]{1,0:T(8,128)S(1)}, u32[]{:S(2)}, u32[]{:S(2)}) collective-permute-start(f32[96,128]{1,0:T(8,128)S(1)} %get-tuple-element.64), channel_id=1, source_target_pairs={{1,2},{2,1},{3,4},{4,3},{5,6},{6,5},{7,8},{8,7},{9,10},{10,9},{11,... | collective-permute-start | bytes 147464 | tf_op jit(solution)/shard_map/ppermute | solution.py:729
  59.1 0.3 shard_map.124.partial
  59.5 3.7 %collective-permute-done.12.got_b = f32[96,128]{1,0:T(8,128)S(1)} collective-permute-done((f32[96,128]{1,0:T(8,128)S(1)}, f32[96,128]{1,0:T(8,128)S(1)}, u32[]{:S(2)}, u32[]{:S(2)}) %collective-permute-start.12) | collective-permute-done | bytes 49184 | tf_op jit(solution)/shard_map/ppermute | solution.py:729
  63.1 1.6 %shard_map.125 = f32[16,4,512]{2,1,0:T(4,128)} custom-call(f32[4,64,128]{2,1,0:T(8,128)S(1)} %shard_map.124.partial, f32[96,128]{1,0:T(8,128)S(1)} %collective-permute-done.11.got_a, f32[96,128]{1,0:T(8,128)S(1)} %collective-permute-done.12.got_b, bf16[5,128,128]{2,1,0:T(8,128)(2,1)S(1)} %get-tuple-element.55.sides_far, ...), custom_call_target="tpu_custom_call" | custom-call | tf_op jit(solution)/shard_map/pallas_call | solution.py:71
  (38 shorter events, 0.5 us)
Async XLA Ops:
  0.6 1.0 %copy-start.2 = (f32[8,8,128]{2,1,0:T(8,128)S(1)}, f32[8,8,128]{2,1,0:T(8,128)}, u32[]{:S(2)}) copy-start(f32[8,8,128]{2,1,0:T(8,128)} %param.10) | copy-start | bytes 98308
  0.6 1.0 %copy-start.1 = (f32[3,8,8,128]{3,2,1,0:T(8,128)S(1)}, f32[3,8,8,128]{3,2,1,0:T(8,128)}, u32[]{:S(2)}) copy-start(f32[3,8,8,128]{3,2,1,0:T(8,128)} %param.11) | copy-start | bytes 294916
  0.6 1.0 %copy-start.3 = (f32[8,8,128]{2,1,0:T(8,128)S(1)}, f32[8,8,128]{2,1,0:T(8,128)}, u32[]{:S(2)}) copy-start(f32[8,8,128]{2,1,0:T(8,128)} %param.12) | copy-start | bytes 98308
  1.7 0.9 %copy-start = (f32[16,4,512]{2,1,0:T(4,128)S(1)}, f32[16,4,512]{2,1,0:T(4,128)}, u32[]{:S(2)}) copy-start(f32[16,4,512]{2,1,0:T(4,128)} %given.1) | copy-start | bytes 393220
  1.8 9.7 %collective-permute-start = (f32[24,128]{1,0:T(8,128)S(1)}, f32[24,128]{1,0:T(8,128)S(1)}, u32[]{:S(2)}, u32[]{:S(2)}) collective-permute-start(f32[24,128]{1,0:T(8,128)S(1)} %get-tuple-element.34._.sent_a), channel_id=1, source_target_pairs={{1,0},{0,1},{3,2},{2,3},{5,4},{4,5},{7,6},{6,7},{9,8},{8,9},{11,10... | collective-permute-start | bytes 36872 | tf_op jit(solution)/shard_map/ppermute | solution.py:722
  3.4 8.2 %collective-permute-start.2 = (f32[96,128]{1,0:T(8,128)S(1)}, f32[96,128]{1,0:T(8,128)S(1)}, u32[]{:S(2)}, u32[]{:S(2)}) collective-permute-start(f32[96,128]{1,0:T(8,128)S(1)} %get-tuple-element.36), channel_id=1, source_target_pairs={{1,0},{0,1},{3,2},{2,3},{5,4},{4,5},{7,6},{6,7},{9,8},{8,9},{11,10... | collective-permute-start | bytes 147464 | tf_op jit(solution)/shard_map/ppermute | solution.py:730
  3.5 8.1 %collective-permute-start.1 = (f32[24,128]{1,0:T(8,128)S(1)}, f32[24,128]{1,0:T(8,128)S(1)}, u32[]{:S(2)}, u32[]{:S(2)}) collective-permute-start(f32[24,128]{1,0:T(8,128)S(1)} %get-tuple-element.35.sent_b), channel_id=1, source_target_pairs={{3,0},{2,1},{1,2},{0,3},{7,4},{6,5},{5,6},{4,7},{11,8},{10,9},{9,1... | collective-permute-start | bytes 36872 | tf_op jit(solution)/shard_map/ppermute | solution.py:723
  5.1 10.3 %collective-permute-start.8 = (f32[96,128]{1,0:T(8,128)S(1)}, f32[96,128]{1,0:T(8,128)S(1)}, u32[]{:S(2)}, u32[]{:S(2)}) collective-permute-start(f32[96,128]{1,0:T(8,128)S(1)} %get-tuple-element.46), channel_id=1, source_target_pairs={{1,2},{2,1},{3,4},{4,3},{5,6},{6,5},{7,8},{8,7},{9,10},{10,9},{11,... | collective-permute-start | bytes 147464 | tf_op jit(solution)/shard_map/ppermute | solution.py:729
  10.2 0.7 %copy-start.4 = (s32[16,6]{0,1:T(8,128)S(1)}, s32[16,6]{0,1:T(8,128)}, u32[]{:S(2)}) copy-start(s32[16,6]{0,1:T(8,128)} %param.17) | copy-start | bytes 1156
  10.9 0.7 %copy-start.8 = (s32[1,1,1,16]{3,2,1,0:T(1,128)S(1)}, s32[1,1,1,16]{3,2,1,0:T(1,128)}, u32[]{:S(2)}) copy-start(s32[1,1,1,16]{3,2,1,0:T(1,128)} %param.19) | copy-start | bytes 196
  11.7 0.7 %copy-start.9 = (s32[1,1,1,16,1]{3,4,2,1,0:T(1,128)S(1)}, s32[1,1,1,16,1]{3,4,2,1,0:T(1,128)}, u32[]{:S(2)}) copy-start(s32[1,1,1,16,1]{3,4,2,1,0:T(1,128)} %param.18) | copy-start | bytes 196
  11.7 10.3 %collective-permute-start.7 = (f32[280,128]{1,0:T(8,128)S(1)}, f32[280,128]{1,0:T(8,128)S(1)}, u32[]{:S(2)}, u32[]{:S(2)}) collective-permute-start(f32[280,128]{1,0:T(8,128)S(1)} %get-tuple-element.42), channel_id=1, source_target_pairs={{16,0},{20,4},{24,8},{28,12},{0,16},{4,20},{8,24},{12,28},{17,1},{... | collective-permute-start | bytes 430088 | tf_op jit(solution)/shard_map/ppermute | solution.py:768
  12.4 5.9 %copy-start.6 = (f32[8,8]{1,0:T(8,128)S(1)}, f32[8,8]{1,0:T(8,128)}, u32[]{:S(2)}) copy-start(f32[8,8]{1,0:T(8,128)} %param.15) | copy-start | bytes 772
  12.4 5.9 %copy-start.5 = (f32[8,8]{1,0:T(8,128)S(1)}, f32[8,8]{1,0:T(8,128)}, u32[]{:S(2)}) copy-start(f32[8,8]{1,0:T(8,128)} %param.16) | copy-start | bytes 772
  12.4 9.6 %collective-permute-start.3 = (f32[160,128]{1,0:T(8,128)S(1)}, f32[160,128]{1,0:T(8,128)S(1)}, u32[]{:S(2)}, u32[]{:S(2)}) collective-permute-start(f32[160,128]{1,0:T(8,128)S(1)} %get-tuple-element.38), channel_id=1, source_target_pairs={{4,0},{0,4},{12,8},{8,12},{20,16},{16,20},{28,24},{24,28},{5,1},{1... | collective-permute-start | bytes 245768 | tf_op jit(solution)/shard_map/ppermute | solution.py:765
  12.4 9.6 %collective-permute-start.4 = (f32[160,128]{1,0:T(8,128)S(1)}, f32[160,128]{1,0:T(8,128)S(1)}, u32[]{:S(2)}, u32[]{:S(2)}) collective-permute-start(f32[160,128]{1,0:T(8,128)S(1)} %get-tuple-element.39), channel_id=1, source_target_pairs={{12,0},{8,4},{4,8},{0,12},{28,16},{24,20},{20,24},{16,28},{13,1},{... | collective-permute-start | bytes 245768 | tf_op jit(solution)/shard_map/ppermute | solution.py:765
  13.4 6.9 %collective-permute-start.5 = (f32[72,128]{1,0:T(8,128)S(1)}, f32[72,128]{1,0:T(8,128)S(1)}, u32[]{:S(2)}, u32[]{:S(2)}) collective-permute-start(f32[72,128]{1,0:T(8,128)S(1)} %get-tuple-element.40), channel_id=1, source_target_pairs={{20,0},{16,4},{28,8},{24,12},{4,16},{0,20},{12,24},{8,28},{21,1},{... | collective-permute-start | bytes 110600 | tf_op jit(solution)/shard_map/ppermute | solution.py:765
  15.4 2.9 %copy-start.7 = (f32[16]{0:T(128)S(1)}, f32[16]{0:T(128)}, u32[]{:S(2)}) copy-start(f32[16]{0:T(128)} %param.14) | copy-start | bytes 196
  15.4 6.7 %collective-permute-start.6 = (f32[72,128]{1,0:T(8,128)S(1)}, f32[72,128]{1,0:T(8,128)S(1)}, u32[]{:S(2)}, u32[]{:S(2)}) collective-permute-start(f32[72,128]{1,0:T(8,128)S(1)} %get-tuple-element.41), channel_id=1, source_target_pairs={{28,0},{24,4},{20,8},{16,12},{12,16},{8,20},{4,24},{0,28},{29,1},{... | collective-permute-start | bytes 110600 | tf_op jit(solution)/shard_map/ppermute | solution.py:765
  24.3 14.1 %all-to-all-start = ((f32[4,104,128]{2,1,0:T(8,128)}), f32[4,104,128]{2,1,0:T(8,128)S(1)}, u32[]{:S(2)}, u32[]{:S(2)}) async-start(f32[4,104,128]{2,1,0:T(8,128)} %get-tuple-element.56), calls=%async_computation | async-start | bytes 425984 | tf_op jit(solution)/shard_map/all_to_all | solution.py:811
  38.4 14.4 %all-to-all-start.1 = ((f32[4,200,128]{2,1,0:T(8,128)}), f32[4,200,128]{2,1,0:T(8,128)S(1)}, u32[]{:S(2)}, u32[]{:S(2)}) async-start(f32[4,200,128]{2,1,0:T(8,128)} %get-tuple-element.57.refs_0_), calls=%async_computation.1 | async-start | bytes 819200 | tf_op jit(solution)/shard_map/all_to_all | solution.py:811
  44.3 9.4 %collective-permute-start.10 = (f32[96,128]{1,0:T(8,128)S(1)}, f32[96,128]{1,0:T(8,128)S(1)}, u32[]{:S(2)}, u32[]{:S(2)}) collective-permute-start(f32[96,128]{1,0:T(8,128)S(1)} %get-tuple-element.60), channel_id=1, source_target_pairs={{1,2},{2,1},{3,4},{4,3},{5,6},{6,5},{7,8},{8,7},{9,10},{10,9},{11,... | collective-permute-start | bytes 147464 | tf_op jit(solution)/shard_map/ppermute | solution.py:729
  47.7 6.0 %collective-permute-start.9 = (f32[96,128]{1,0:T(8,128)S(1)}, f32[96,128]{1,0:T(8,128)S(1)}, u32[]{:S(2)}, u32[]{:S(2)}) collective-permute-start(f32[96,128]{1,0:T(8,128)S(1)} %get-tuple-element.59), channel_id=1, source_target_pairs={{1,0},{0,1},{3,2},{2,3},{5,4},{4,5},{7,6},{6,7},{9,8},{8,9},{11,10... | collective-permute-start | bytes 147464 | tf_op jit(solution)/shard_map/ppermute | solution.py:730
  54.0 5.4 %collective-permute-start.11 = (f32[96,128]{1,0:T(8,128)S(1)}, f32[96,128]{1,0:T(8,128)S(1)}, u32[]{:S(2)}, u32[]{:S(2)}) collective-permute-start(f32[96,128]{1,0:T(8,128)S(1)} %get-tuple-element.63), channel_id=1, source_target_pairs={{1,0},{0,1},{3,2},{2,3},{5,4},{4,5},{7,6},{6,7},{9,8},{8,9},{11,10... | collective-permute-start | bytes 147464 | tf_op jit(solution)/shard_map/ppermute | solution.py:730
  54.1 9.0 %collective-permute-start.12 = (f32[96,128]{1,0:T(8,128)S(1)}, f32[96,128]{1,0:T(8,128)S(1)}, u32[]{:S(2)}, u32[]{:S(2)}) collective-permute-start(f32[96,128]{1,0:T(8,128)S(1)} %get-tuple-element.64), channel_id=1, source_target_pairs={{1,2},{2,1},{3,4},{4,3},{5,6},{6,5},{7,8},{8,7},{9,10},{10,9},{11,... | collective-permute-start | bytes 147464 | tf_op jit(solution)/shard_map/ppermute | solution.py:729

commit v7 on v6

--- a/solution.py
+++ b/solution.py
@@ -108,7 +108,9 @@
         message_b[tile * 8 : tile * 8 + 8] = second
 
 
-def pack_next_body(state, sent_a, sent_b, got_a, got_b, _, edge, along_x, y_a, y_b, xy_a, xy_b):
+def pack_next_body(
+    state, sent_a, sent_b, got_a, got_b, _, edge, along_x, y_a, y_b, xy_a, xy_b
+):
     cells_x = state.shape[1]
     odd_z, odd = is_odd("fz"), is_odd("fy")
     high, low = paired(odd_z, sent_a[...], sent_b[...])
@@ -201,23 +203,21 @@
     return u, v, w, p, jnp.sqrt(HEAT_RATIO * jnp.abs(p) * inverse)
 
 
+def chunks(first, last, size):
+    return [(i, min(i + size, last)) for i in range(first, last, size)]
+
+
 def derive_planes(wide, derived, first, last):
-    def derive(i, _):
-        for k, value in enumerate(primitive(*[wide[f, i] for f in range(5)])):
-            derived[k, i] = value
-        return 0
-
-    lax.fori_loop(first, last, derive, 0)
+    for i, j in chunks(first, last, 4):
+        for k, value in enumerate(primitive(*[wide[f, i:j] for f in range(5)])):
+            derived[k, i:j] = value
 
 
 def derive_speeds(wide, derived, first, last):
-    def derive(i, _):
-        inverse = 1.0 / wide[0, i]
+    for i, j in chunks(first, last, 5):
+        inverse = 1.0 / wide[0, i:j]
         for k in range(3):
-            derived[k, i] = wide[1 + k, i] * inverse
-        return 0
-
-    lax.fori_loop(first, last, derive, 0)
+            derived[k, i:j] = wide[1 + k, i:j] * inverse
 
 
 def with_flux(fields, other, along):
@@ -282,64 +282,63 @@
 def flow_rate_section(wide, derived, ends, start, offset, mix, write, inner=False):
     depth = wide.shape[1]
     rows = slice(0, 8) if inner else slice(None)
-    windows = [rows, slice(None), rows]
-    lane = lax.broadcasted_iota(jnp.int32, (8 if inner else 16, 128), 1)
-
-    def plane(i, along):
-        kept = windows[along]
-        fields = [wide[f, i, kept] for f in range(5)]
-        return with_flux(fields, [derived[f, i, kept] for f in range(5)], along)
-
-    def section(i, before):
-        ahead = face(plane(i, 0), plane(i + 1, 0))
-        total = [ahead[f] - before[f] for f in range(5)]
-        here = plane(i, 1)
-        faces = face(here, rolled(here, 15, 0))
+    size = 4 if inner else 2
+
+    def planes(i, j, kept, along):
+        fields = [wide[f, i:j, kept] for f in range(5)]
+        return with_flux(fields, [derived[f, i:j, kept] for f in range(5)], along)
+
+    def cut(here, i, j):
+        return [a[i:j] for a in here[0]], [a[i:j] for a in here[1]], here[2][i:j]
+
+    for i, j in chunks(1, depth - 1, size):
+        count = j - i
+        lane = lax.broadcasted_iota(jnp.int32, (count, 8 if inner else 16, 128), 2)
+        here = planes(i - 1, j + 1, rows, 0)
+        faces = face(cut(here, 0, count + 1), cut(here, 1, count + 2))
+        total = [g[1:] - g[:-1] for g in faces]
+        here = planes(i, j, slice(None), 1)
+        faces = face(here, rolled(here, 15, 1))
         for f in range(5):
-            change = faces[f] - pltpu.roll(faces[f], 1, 0)
-            total[f] = total[f] + (change[0:8] if inner else change)
-        here = plane(i, 2)
-        faces = face(here, rolled(here, 127, 1))
+            change = faces[f] - pltpu.roll(faces[f], 1, 1)
+            total[f] = total[f] + (change[:, 0:8] if inner else change)
+        here = planes(i, j, rows, 2)
+        faces = face(here, rolled(here, 127, 2))
         for f in range(5):
-            end = ends[f, i - 1, rows]
+            end = ends[f, i - 1 : j - 1, rows]
             value = jnp.where(lane == 127, end, faces[f])
-            total[f] = total[f] + (value - jnp.where(lane == 0, end, pltpu.roll(value, 1, 1)))
+            total[f] = total[f] + (value - jnp.where(lane == 0, end, pltpu.roll(value, 1, 2)))
         for f in range(5):
-            value = wide[f, i, rows] - (0.5 * TIME_STEP) * total[f]
+            value = wide[f, i:j, rows] - (0.5 * TIME_STEP) * total[f]
             if mix[0] != 0.0:
-                value = mix[0] * start[f, i + offset, rows] + mix[1] * value
-            write(i - 1, f, value)
-        return tuple(ahead)
-
-    lax.fori_loop(1, depth - 1, section, tuple(face(plane(0, 0), plane(1, 0))))
+                value = mix[0] * start[f, i + offset : j + offset, rows] + mix[1] * value
+            write(slice(i - 1, j - 1), f, value)
 
 
 def lamb(derived, ends, first, cells_x, lamb_rows):
-    lane = lax.broadcasted_iota(jnp.int32, (8, 128), 1)
-
-    def one(x, _):
-        i = first + x
-        vel = [derived[c, i, 0:8] for c in range(3)]
-        along_x = [derived[c, i + 1, 0:8] - derived[c, i - 1, 0:8] for c in range(3)]
-        columns = [derived[c, i] for c in range(3)]
-        along_y = [(pltpu.roll(a, 15, 0) - pltpu.roll(a, 1, 0))[0:8] for a in columns]
+    for i, j in chunks(first, first + cells_x, 4):
+        count = j - i
+        lane = lax.broadcasted_iota(jnp.int32, (count, 8, 128), 2)
+        vel = [derived[c, i:j, 0:8] for c in range(3)]
+        along_x = [derived[c, i + 1 : j + 1, 0:8] - derived[c, i - 1 : j - 1, 0:8] for c in range(3)]
+        along_y = []
+        for c in range(3):
+            column = derived[c, i:j]
+            along_y.append((pltpu.roll(column, 15, 1) - pltpu.roll(column, 1, 1))[:, 0:8])
         along_z = []
         for c in range(2):
-            end = ends[c, x, 0:8]
-            after = jnp.where(lane == 127, end, pltpu.roll(vel[c], 127, 1))
-            along_z.append(after - jnp.where(lane == 0, end, pltpu.roll(vel[c], 1, 1)))
+            end = ends[c, i - first : j - first, 0:8]
+            after = jnp.where(lane == 127, end, pltpu.roll(vel[c], 127, 2))
+            along_z.append(after - jnp.where(lane == 0, end, pltpu.roll(vel[c], 1, 2)))
         curl = [
             0.5 * (along_y[2] - along_z[1]),
             0.5 * (along_z[0] - along_x[2]),
             0.5 * (along_x[1] - along_y[0]),
         ]
-        at = pl.multiple_of(x * 8, 8)
-        lamb_rows[0, pl.ds(at, 8), :] = curl[1] * vel[2] - curl[2] * vel[1]
-        lamb_rows[1, pl.ds(at, 8), :] = curl[2] * vel[0] - curl[0] * vel[2]
-        lamb_rows[2, pl.ds(at, 8), :] = curl[0] * vel[1] - curl[1] * vel[0]
-        return 0
-
-    lax.fori_loop(0, cells_x, one, 0)
+        at = slice((i - first) * 8, (j - first) * 8)
+        lamb_rows[0, at] = (curl[1] * vel[2] - curl[2] * vel[1]).reshape(count * 8, 128)
+        lamb_rows[1, at] = (curl[2] * vel[0] - curl[0] * vel[2]).reshape(count * 8, 128)
+        lamb_rows[2, at] = (curl[0] * vel[1] - curl[1] * vel[0]).reshape(count * 8, 128)
 
 
 def project(lamb_rows, pair, spread, send, base):
@@ -347,10 +346,12 @@
     fold = fold_of(peers, spread.shape[0] // 8)
     height = 64 // fold
     group = lax.broadcasted_iota(jnp.int32, (height, 128), 1) // (128 // fold)
+    modes = dot_three(pair[...], jnp.concatenate([lamb_rows[c] for c in range(3)], 1))
+    modes = jnp.concatenate([modes[:, c * 128 : c * 128 + 128] for c in range(3)], 0)
+    sent = dot_three(modes, spread[...])
     for c in range(3):
-        sent = dot_three(dot_three(pair[...], lamb_rows[c]), spread[...])
         for peer in range(peers):
-            mine = sent[:, peer * 128 : peer * 128 + 128]
+            mine = sent[c * 64 : c * 64 + 64, peer * 128 : peer * 128 + 128]
             folded = mine[0:height]
             for g in range(1, fold):
                 folded = jnp.where(group == g, mine[g * height : g * height + height], folded)
@@ -360,9 +361,9 @@
 def flow_sources_body(places, *refs):
     state, edge = refs[0:2]
     messages = refs[2 : 2 + len(places)]
-    pair, spread, labels, _ = refs[2 + len(places) : 6 + len(places)]
-    wide, rim, send, derived, lamb_rows, ends = refs[6 + len(places) : 12 + len(places)]
-    spare = refs[12 + len(places) :]
+    pair, spread, labels = refs[2 + len(places) : 5 + len(places)]
+    wide, rim, send, derived, lamb_rows, ends = refs[5 + len(places) : 11 + len(places)]
+    spare = refs[11 + len(places) :]
     cells_x = state.shape[1]
     odd = is_odd("fy")
     beside, k = [], 0
@@ -386,7 +387,7 @@
     send[:, send.shape[1] - 8 :] = labels[...]
 
 
-def flow_stages_body(wide, rim, pair, spread, labels, out, send, derived, lamb_rows, ends, first, second):
+def flow_stages_body(wide, rim, pair, spread, labels, _, out, send, derived, lamb_rows, ends, first, second):
     def writer(target):
         def write(i, f, value):
             target[f, i] = value
@@ -484,20 +485,15 @@
     lift(out, front, rear, sides, TIME_STEP * mix[1] * PENALTY)
 
 
-def order_table(count, turned):
-    row = lax.broadcasted_iota(jnp.int32, (4 * count, 4 * count), 0)
-    column = lax.broadcasted_iota(jnp.int32, (4 * count, 4 * count), 1)
-    if turned:
-        row, column = column, row
-    return (column == (row % count) * 4 + row // count).astype(F32)
-
-
-def acoustic_start_body(given, _, state, message_a, message_b, turned):
+def acoustic_start_body(given, _, state, message_a, message_b, turned, stored):
     count = given.shape[0]
-    rows = jnp.concatenate([given[e] for e in range(count)], 0)
-    rows = dot_full(order_table(count, False), rows)
-    rows = jnp.concatenate([rows, jnp.zeros((128 - 4 * count, rows.shape[1]), F32)], 0)
-    turned[...] = rows.T
+    for e in range(count):
+        for t in range(4):
+            stored[t, 4 * e : 4 * e + 4] = given[e, :, t * 128 : t * 128 + 128]
+    for t in range(4):
+        rows = [stored[t, pl.ds(c, count, stride=4), :] for c in range(4)]
+        rows = jnp.concatenate(rows + [jnp.zeros((128 - 4 * count, 128), F32)], 0)
+        turned[t * 128 : t * 128 + 128] = rows.T
     lane = lax.broadcasted_iota(jnp.int32, (64, 128), 1) // count
     fields = [jnp.zeros((64, 128), F32)] * 4
     for z in range(8):
@@ -510,7 +506,7 @@
     faces_sent(is_odd("fz"), state, message_a, message_b)
 
 
-def natural_order(state, out, turned):
+def natural_order(state, out, turned, stored):
     count = out.shape[0]
     lane = lax.broadcasted_iota(jnp.int32, (64, 128), 1) // count
     for z in range(8):
@@ -519,9 +515,13 @@
             move = (c - z) * count % 128
             value = jnp.where(lane == c, pltpu.roll(state[c], move, 1) if move else state[c], value)
         turned[pl.ds(z, 64, stride=8), :] = value
-    rows = dot_full(order_table(count, True), turned[...].T[0 : 4 * count])
+    for t in range(4):
+        rows = turned[t * 128 : t * 128 + 128].T
+        for c in range(4):
+            stored[t, pl.ds(c, count, stride=4), :] = rows[c * count : c * count + count]
     for e in range(count):
-        out[e] = rows[4 * e : 4 * e + 4]
+        for t in range(4):
+            out[e, :, t * 128 : t * 128 + 128] = stored[t, 4 * e : 4 * e + 4]
 
 
 def remote_part(out, before, after, sides_far, factor):
@@ -540,7 +540,7 @@
 
 def acoustic_far_body(mix, kind, partial, got_a, got_b, sides_far, received, *refs):
     if kind == "last":
-        given_out, before, after, out, turned = refs
+        given_out, before, after, out, turned, stored = refs
     elif kind == "first":
         _, out, message_a, message_b, before, after, source = refs
         place_body(received, source)
@@ -554,7 +554,7 @@
         out[1 + c] = partial[1 + c] + (TIME_STEP * mix[1]) * received[c]
     remote_part(out, before, after, sides_far, TIME_STEP * mix[1] * PENALTY)
     if kind == "last":
-        natural_order(out, given_out, turned)
+        natural_order(out, given_out, turned, stored)
     else:
         faces_sent(odd, out, message_a, message_b)
 
@@ -596,6 +596,8 @@
 
 def tables_body(
     packed,
+    faces,
+    faces_out,
     near,
     far,
     deriv_rows,
@@ -605,6 +607,7 @@
     labels,
     speed,
 ):
+    faces_out[...] = faces[...]
     size = near.shape[1]
     count = size // 8
     blocks = spread.shape[0] // 8
@@ -733,15 +736,16 @@
     held = (4, 64, size)
     faces = (96, size)
     sides = [pltpu.VMEM(faces, F32)] * 2
+    turning = [pltpu.VMEM((512, 128), F32), pltpu.VMEM((4, 4 * elements, 128), F32)]
     sound, to_a, to_b = call(
         acoustic_start_body,
         [held, faces, faces],
         acoustic,
-        flow_a,
-        scratch=[pltpu.VMEM((512, 128), F32)],
+        edge_a,
+        scratch=turning,
         last=1,
     )
-    got_a, got_b = traces(to_a, to_b)
+    got_a = lax.ppermute(to_a, names, near_pairs)
 
     six = 2 * HALO
     edge_rows = 5 * 8
@@ -785,9 +789,10 @@
         + piece(block_element.reshape(1, blocks), 26)
     )
     table = jax.ShapeDtypeStruct((5, size, size), BF16)
-    near, far, deriv_rows, deriv_lanes, pair, spread, labels, speed = call(
+    to_b, near, far, deriv_rows, deriv_lanes, pair, spread, labels, speed = call(
         tables_body,
         [
+            faces,
             table,
             table,
             (128, 64),
@@ -798,7 +803,9 @@
             (1, size),
         ],
         packed,
-    )
+        to_b,
+    )
+    got_b = lax.ppermute(to_b, names, far_pairs)
 
     fold = fold_of(size_y, blocks)
     wide = cells_x + 2 * HALO
@@ -820,14 +827,12 @@
         pair,
         spread,
         labels,
-        got_b,
         scratch=[
             pltpu.VMEM((3, wide, 16, 128), F32),
             rows_scratch,
             pltpu.VMEM((2, cells_x, 8, 128), F32),
         ]
         + spare,
-        last=1,
     )
     received = route(send)
     flow_state, send = call(
@@ -838,6 +843,8 @@
         pair,
         spread,
         labels,
+        got_b,
+        last=1,
         scratch=[
             pltpu.VMEM(planes(wide), F32),
             rows_scratch,
@@ -896,7 +903,7 @@
         got_b,
         far,
         source_three,
-        scratch=sides + [pltpu.VMEM(held, F32), pltpu.VMEM((512, 128), F32)],
+        scratch=sides + [pltpu.VMEM(held, F32)] + turning,
     )[0]
     return (flow_state, sound_state)
 

time: 65.1 us -> 62.9 us (0.966)
  waiting for transfers between devices: 11.6 us -> 20.2 us
  Pallas kernels: 18 us -> 11.3 us
  starting transfers between devices: 30.6 us -> 27.9 us
  local copies, waits for them, and re-layouts: 2.63 us -> 1.29 us
    pallas_call x13, Pallas kernels: 18 us -> 11.3 us  [call(): pl.pallas_call(kernel, out_shape=outs, in_specs=specs, out_specs=[whole]...]
    ppermute x0 -> x2, waiting for transfers between devices: none -> 6.26 us  [the longest x1 5.61 us: per_device(): got_b = lax.ppermute(to_b, names, far_pairs)]
    ppermute x3 -> x2, starting transfers between devices: 13.5 us -> 8.5 us  [traces(): far_got = lax.ppermute(to_b, names, far_pairs)]
    ppermute x0 -> x2, starting transfers between devices: none -> 3.51 us  [the longest x1 3.38 us: per_device(): got_b = lax.ppermute(to_b, names, far_pairs)]
    all_to_all x2, starting transfers between devices: 9.28 us -> 6.84 us  [route(): return lax.all_to_all(send, 'fy', split_axis=0, concat_axis=0, tiled=True)]
    ppermute x4, waiting for transfers between devices: 2.78 us -> 4.76 us  [per_device(): lax.ppermute(kept, ('fx', 'fy'), partners(flat, 1, side, shift))]
    unnamed x20, local copies, waits for them, and re-layouts: 2.63 us -> 1.29 us
    ppermute x3 -> x2, waiting for transfers between devices: 4.26 us -> 5.56 us  [traces(): far_got = lax.ppermute(to_b, names, far_pairs)]
  transfers between devices with their start and end apart: 15 -> 15, of which waited for: 5 -> 7; matrix products, arithmetic and copies ran while one was open for 0% -> 0% of each run, Pallas kernels for 21% -> 13%
where the time goes in v7:
time: 62.9 us; the launch traced here: 62.5 us
  starting transfers between devices  27.9 us (44%)
  waiting for transfers between devices  20.2 us (32%)
  Pallas kernels  11.3 us (18%)
  local copies, waits for them, and re-layouts  1.29 us (2%)
  other arithmetic  1.01 us (2%)
  between operations  0.86 us (1%)
    pallas_call x13, Pallas kernels, call(): pl.pallas_call(kernel, out_shape=outs, in_specs=specs, out_specs=[whole]...  11.3 us
    ppermute x2, starting transfers between devices, traces(): far_got = lax.ppermute(to_b, names, far_pairs)  8.5 us
    all_to_all x2, starting transfers between devices, route(): return lax.all_to_all(send, 'fy', split_axis=0, concat_axis=0, tiled=True)  6.84 us
    ppermute x4, starting transfers between devices, per_device(): lax.ppermute(kept, ('fx', 'fy'), partners(flat, 1, side, shift))  6.57 us
    ppermute x1, waiting for transfers between devices, per_device(): got_b = lax.ppermute(to_b, names, far_pairs)  5.61 us
    ppermute x2, waiting for transfers between devices, traces(): far_got = lax.ppermute(to_b, names, far_pairs)  5.56 us
    ppermute x4, waiting for transfers between devices, per_device(): lax.ppermute(kept, ('fx', 'fy'), partners(flat, 1, side, shift))  4.76 us
    all_to_all x2, waiting for transfers between devices, route(): return lax.all_to_all(send, 'fy', split_axis=0, concat_axis=0, tiled=True)  3.61 us
  transfers between devices with their start and end apart: 15, of which 7 were waited for; matrix products, arithmetic and copies ran while one was open for 0% of the time, Pallas kernels for 13%

profile of v7, /device:TPU:2, one launch (start us, length us, event | category | flops | bytes accessed | tf_op | source)
XLA Modules:
  0.0 62.5 jit_solution(651121269577504172)
XLA Ops:
  0.7 1.0 %broadcast_multiply_fusion = f32[3,8,8,128]{3,2,1,0:T(8,128)S(1)} fusion(f32[3,8,8,128]{3,2,1,0:T(8,128)} %param.11, f32[8,8,128]{2,1,0:T(8,128)} %param.10), kind=kLoop, calls=%fused_computation.1 | loop fusion | flops 24576 | bytes 229376 | tf_op jit(solution)/shard_map/mul | solution.py:722
  1.9 1.6 %collective-permute-start.1 = (f32[24,128]{1,0:T(8,128)S(1)}, f32[24,128]{1,0:T(8,128)S(1)}, u32[]{:S(2)}, u32[]{:S(2)}) collective-permute-start(f32[24,128]{1,0:T(8,128)S(1)} %get-tuple-element.36.sent_b), channel_id=1, source_target_pairs={{3,0},{2,1},{1,2},{0,3},{7,4},{6,5},{5,6},{4,7},{11,8},{10,9},{9,1... | collective-permute-start | bytes 36872 | tf_op jit(solution)/shard_map/ppermute | solution.py:726
  3.5 0.7 %copy-done.4 = s32[16,6]{0,1:T(8,128)S(1)} copy-done((s32[16,6]{0,1:T(8,128)S(1)}, s32[16,6]{0,1:T(8,128)}, u32[]{:S(2)}) %copy-start.4) | copy-done | bytes 408
  4.2 0.6 shard_map.114
  5.0 0.5 copy-done.8
  5.5 0.6 %collective-permute-done.2._.got_a = f32[96,128]{1,0:T(8,128)S(1)} collective-permute-done((f32[96,128]{1,0:T(8,128)S(1)}, f32[96,128]{1,0:T(8,128)S(1)}, u32[]{:S(2)}, u32[]{:S(2)}) %collective-permute-start.2) | collective-permute-done | bytes 49184 | tf_op jit(solution)/shard_map/ppermute | solution.py:748
  6.3 0.6 collective-permute-start.7
  6.9 1.6 %collective-permute-start.3 = (f32[160,128]{1,0:T(8,128)S(1)}, f32[160,128]{1,0:T(8,128)S(1)}, u32[]{:S(2)}, u32[]{:S(2)}) collective-permute-start(f32[160,128]{1,0:T(8,128)S(1)} %get-tuple-element.39), channel_id=1, source_target_pairs={{4,0},{0,4},{12,8},{8,12},{20,16},{16,20},{28,24},{24,28},{5,1},{1... | collective-permute-start | bytes 245768 | tf_op jit(solution)/shard_map/ppermute | solution.py:769
  8.5 2.5 %collective-permute-start.4 = (f32[160,128]{1,0:T(8,128)S(1)}, f32[160,128]{1,0:T(8,128)S(1)}, u32[]{:S(2)}, u32[]{:S(2)}) collective-permute-start(f32[160,128]{1,0:T(8,128)S(1)} %get-tuple-element.40), channel_id=1, source_target_pairs={{12,0},{8,4},{4,8},{0,12},{28,16},{24,20},{20,24},{16,28},{13,1},{... | collective-permute-start | bytes 245768 | tf_op jit(solution)/shard_map/ppermute | solution.py:769
  11.0 1.6 %collective-permute-start.5 = (f32[72,128]{1,0:T(8,128)S(1)}, f32[72,128]{1,0:T(8,128)S(1)}, u32[]{:S(2)}, u32[]{:S(2)}) collective-permute-start(f32[72,128]{1,0:T(8,128)S(1)} %get-tuple-element.41), channel_id=1, source_target_pairs={{20,0},{16,4},{28,8},{24,12},{4,16},{0,20},{12,24},{8,28},{21,1},{... | collective-permute-start | bytes 110600 | tf_op jit(solution)/shard_map/ppermute | solution.py:769
  12.6 0.9 %collective-permute-start.6 = (f32[72,128]{1,0:T(8,128)S(1)}, f32[72,128]{1,0:T(8,128)S(1)}, u32[]{:S(2)}, u32[]{:S(2)}) collective-permute-start(f32[72,128]{1,0:T(8,128)S(1)} %get-tuple-element.42), channel_id=1, source_target_pairs={{28,0},{24,4},{20,8},{16,12},{12,16},{8,20},{4,24},{0,28},{29,1},{... | collective-permute-start | bytes 110600 | tf_op jit(solution)/shard_map/ppermute | solution.py:769
  13.5 1.0 %shard_map.116 = (f32[96,128]{1,0:T(8,128)S(1)}, bf16[5,128,128]{2,1,0:T(8,128)(2,1)S(1)}, bf16[5,128,128]{2,1,0:T(8,128)(2,1)S(1)}, f32[128,64]{1,0:T(8,128)S(1...) custom-call(f32[32,16]{1,0:T(8,128)S(1)} %pad_add_fusion.1.packed, ...), custom_call_target="tpu_custom_call" | custom-call | tf_op jit(solution)/shard_map/pallas_call | solution.py:71
  14.5 2.1 %collective-permute-done.5.refs_4_ = f32[72,128]{1,0:T(8,128)S(1)} collective-permute-done((f32[72,128]{1,0:T(8,128)S(1)}, f32[72,128]{1,0:T(8,128)S(1)}, u32[]{:S(2)}, u32[]{:S(2)}) %collective-permute-start.5) | collective-permute-done | bytes 36896 | tf_op jit(solution)/shard_map/ppermute | solution.py:769
  16.6 2.6 %collective-permute-done.6.refs_5_ = f32[72,128]{1,0:T(8,128)S(1)} collective-permute-done((f32[72,128]{1,0:T(8,128)S(1)}, f32[72,128]{1,0:T(8,128)S(1)}, u32[]{:S(2)}, u32[]{:S(2)}) %collective-permute-start.6) | collective-permute-done | bytes 36896 | tf_op jit(solution)/shard_map/ppermute | solution.py:769
  19.3 1.3 %shard_map.117 = (f32[5,14,16,128]{3,2,1,0:T(8,128)S(1)}, f32[5,16,256]{2,1,0:T(8,128)S(1)}, f32[4,104,128]{2,1,0:T(8,128)}) custom-call(f32[5,8,8,128]{3,2,1,0:T(8,128)S(1)} %pad_add_fusion.state.refs_0_, f32[40,128]{1,0:T(8,128)S(1)} %get-tuple-element.38.refs_1_, f32[160,128]{1,0:T(8,128)S(1)} %collective-permute-done.3.refs_2_, ...), custom_call_target="tpu_custom_call" | custom-call | tf_op jit(solution)/shard_map/pallas_call | solution.py:71
  20.6 3.4 %all-to-all-start = ((f32[4,104,128]{2,1,0:T(8,128)}), f32[4,104,128]{2,1,0:T(8,128)S(1)}, u32[]{:S(2)}, u32[]{:S(2)}) async-start(f32[4,104,128]{2,1,0:T(8,128)} %get-tuple-element.58), calls=%async_computation | async-start | bytes 425984 | tf_op jit(solution)/shard_map/all_to_all | solution.py:818
  24.0 3.4 %collective-permute-start.8 = (f32[96,128]{1,0:T(8,128)S(1)}, f32[96,128]{1,0:T(8,128)S(1)}, u32[]{:S(2)}, u32[]{:S(2)}) collective-permute-start(f32[96,128]{1,0:T(8,128)S(1)} %get-tuple-element.50), channel_id=1, source_target_pairs={{1,2},{2,1},{3,4},{4,3},{5,6},{6,5},{7,8},{8,7},{9,10},{10,9},{11,... | collective-permute-start | bytes 147464 | tf_op jit(solution)/shard_map/ppermute | solution.py:808
  27.4 5.6 %collective-permute-done.8._.got_b = f32[96,128]{1,0:T(8,128)S(1)} collective-permute-done((f32[96,128]{1,0:T(8,128)S(1)}, f32[96,128]{1,0:T(8,128)S(1)}, u32[]{:S(2)}, u32[]{:S(2)}) %collective-permute-start.8) | collective-permute-done | bytes 49184 | tf_op jit(solution)/shard_map/ppermute | solution.py:808
  33.0 4.6 %shard_map.118 = (f32[5,8,8,128]{3,2,1,0:T(8,128)}, f32[4,200,128]{2,1,0:T(8,128)}) custom-call(f32[5,14,16,128]{3,2,1,0:T(8,128)S(1)} %get-tuple-element.48.wide, f32[5,16,256]{2,1,0:T(8,128)S(1)} %get-tuple-element.49.rim, f32[64,64]{1,0:T(8,128)S(1)} %get-tuple-element.45.refs_7_.pair, f32[128,512]{1,0:T(8,128)S(1)} %get-tuple-element.46.refs_8_.spread, ...), custom_call_target="tpu_custom_call" | custom-call | tf_op jit(solution)/shard_map/pallas_call | solution.py:71
  37.6 3.5 %all-to-all-start.1 = ((f32[4,200,128]{2,1,0:T(8,128)}), f32[4,200,128]{2,1,0:T(8,128)S(1)}, u32[]{:S(2)}, u32[]{:S(2)}) async-start(f32[4,200,128]{2,1,0:T(8,128)} %get-tuple-element.59.refs_0_), calls=%async_computation.1 | async-start | bytes 819200 | tf_op jit(solution)/shard_map/all_to_all | solution.py:818
  41.0 0.3 shard_map.119.partial
  41.4 0.5 shard_map.120
  41.9 4.4 %collective-permute-start.10 = (f32[96,128]{1,0:T(8,128)S(1)}, f32[96,128]{1,0:T(8,128)S(1)}, u32[]{:S(2)}, u32[]{:S(2)}) collective-permute-start(f32[96,128]{1,0:T(8,128)S(1)} %get-tuple-element.62), channel_id=1, source_target_pairs={{1,2},{2,1},{3,4},{4,3},{5,6},{6,5},{7,8},{8,7},{9,10},{10,9},{11,... | collective-permute-start | bytes 147464 | tf_op jit(solution)/shard_map/ppermute | solution.py:732
  46.5 0.3 shard_map.121.partial
  46.8 3.6 %all-to-all-done.1.received = f32[4,200,128]{2,1,0:T(8,128)S(1)} async-done(((f32[4,200,128]{2,1,0:T(8,128)}), f32[4,200,128]{2,1,0:T(8,128)S(1)}, u32[]{:S(2)}, u32[]{:S(2)}) %all-to-all-start.1) | async-done | bytes 409632 | tf_op jit(solution)/shard_map/all_to_all | solution.py:818
  50.4 0.4 shard_map.122
  50.8 1.0 %collective-permute-done.10.got_b = f32[96,128]{1,0:T(8,128)S(1)} collective-permute-done((f32[96,128]{1,0:T(8,128)S(1)}, f32[96,128]{1,0:T(8,128)S(1)}, u32[]{:S(2)}, u32[]{:S(2)}) %collective-permute-start.10) | collective-permute-done | bytes 49184 | tf_op jit(solution)/shard_map/ppermute | solution.py:732
  51.8 0.3 shard_map.123
  52.2 4.1 %collective-permute-start.12 = (f32[96,128]{1,0:T(8,128)S(1)}, f32[96,128]{1,0:T(8,128)S(1)}, u32[]{:S(2)}, u32[]{:S(2)}) collective-permute-start(f32[96,128]{1,0:T(8,128)S(1)} %get-tuple-element.66), channel_id=1, source_target_pairs={{1,2},{2,1},{3,4},{4,3},{5,6},{6,5},{7,8},{8,7},{9,10},{10,9},{11,... | collective-permute-start | bytes 147464 | tf_op jit(solution)/shard_map/ppermute | solution.py:732
  56.3 0.3 shard_map.124.partial
  56.6 4.6 %collective-permute-done.12.got_b = f32[96,128]{1,0:T(8,128)S(1)} collective-permute-done((f32[96,128]{1,0:T(8,128)S(1)}, f32[96,128]{1,0:T(8,128)S(1)}, u32[]{:S(2)}, u32[]{:S(2)}) %collective-permute-start.12) | collective-permute-done | bytes 49184 | tf_op jit(solution)/shard_map/ppermute | solution.py:732
  61.2 1.3 %shard_map.125 = f32[16,4,512]{2,1,0:T(4,128)} custom-call(f32[4,64,128]{2,1,0:T(8,128)S(1)} %shard_map.124.partial, f32[96,128]{1,0:T(8,128)S(1)} %collective-permute-done.11.got_a, f32[96,128]{1,0:T(8,128)S(1)} %collective-permute-done.12.got_b, bf16[5,128,128]{2,1,0:T(8,128)(2,1)S(1)} %get-tuple-element.57.sides_far, ...), custom_call_target="tpu_custom_call" | custom-call | tf_op jit(solution)/shard_map/pallas_call | solution.py:71
  (38 shorter events, 0.8 us)
Async XLA Ops:
  0.6 1.0 %copy-start.2 = (f32[8,8,128]{2,1,0:T(8,128)S(1)}, f32[8,8,128]{2,1,0:T(8,128)}, u32[]{:S(2)}) copy-start(f32[8,8,128]{2,1,0:T(8,128)} %param.10) | copy-start | bytes 98308
  0.6 1.0 %copy-start.1 = (f32[3,8,8,128]{3,2,1,0:T(8,128)S(1)}, f32[3,8,8,128]{3,2,1,0:T(8,128)}, u32[]{:S(2)}) copy-start(f32[3,8,8,128]{3,2,1,0:T(8,128)} %param.11) | copy-start | bytes 294916
  0.6 1.0 %copy-start.3 = (f32[8,8,128]{2,1,0:T(8,128)S(1)}, f32[8,8,128]{2,1,0:T(8,128)}, u32[]{:S(2)}) copy-start(f32[8,8,128]{2,1,0:T(8,128)} %param.12) | copy-start | bytes 98308
  1.7 2.5 %copy-start = (f32[16,4,512]{2,1,0:T(4,128)S(1)}, f32[16,4,512]{2,1,0:T(4,128)}, u32[]{:S(2)}) copy-start(f32[16,4,512]{2,1,0:T(4,128)} %given.1) | copy-start | bytes 393220
  1.8 2.4 %collective-permute-start = (f32[24,128]{1,0:T(8,128)S(1)}, f32[24,128]{1,0:T(8,128)S(1)}, u32[]{:S(2)}, u32[]{:S(2)}) collective-permute-start(f32[24,128]{1,0:T(8,128)S(1)} %get-tuple-element.35.sent_a), channel_id=1, source_target_pairs={{1,0},{0,1},{3,2},{2,3},{5,4},{4,5},{7,6},{6,7},{9,8},{8,9},{11,10... | collective-permute-start | bytes 36872 | tf_op jit(solution)/shard_map/ppermute | solution.py:725
  1.9 3.6 %collective-permute-start.1 = (f32[24,128]{1,0:T(8,128)S(1)}, f32[24,128]{1,0:T(8,128)S(1)}, u32[]{:S(2)}, u32[]{:S(2)}) collective-permute-start(f32[24,128]{1,0:T(8,128)S(1)} %get-tuple-element.36.sent_b), channel_id=1, source_target_pairs={{3,0},{2,1},{1,2},{0,3},{7,4},{6,5},{5,6},{4,7},{11,8},{10,9},{9,1... | collective-permute-start | bytes 36872 | tf_op jit(solution)/shard_map/ppermute | solution.py:726
  3.5 0.7 %copy-start.4 = (s32[16,6]{0,1:T(8,128)S(1)}, s32[16,6]{0,1:T(8,128)}, u32[]{:S(2)}) copy-start(s32[16,6]{0,1:T(8,128)} %param.17) | copy-start | bytes 1156
  4.8 0.7 %copy-start.8 = (s32[1,1,1,16]{3,2,1,0:T(1,128)S(1)}, s32[1,1,1,16]{3,2,1,0:T(1,128)}, u32[]{:S(2)}) copy-start(s32[1,1,1,16]{3,2,1,0:T(1,128)} %param.19) | copy-start | bytes 196
  4.8 1.3 %collective-permute-start.2 = (f32[96,128]{1,0:T(8,128)S(1)}, f32[96,128]{1,0:T(8,128)S(1)}, u32[]{:S(2)}, u32[]{:S(2)}) collective-permute-start(f32[96,128]{1,0:T(8,128)S(1)} %get-tuple-element.37), channel_id=1, source_target_pairs={{1,0},{0,1},{3,2},{2,3},{5,4},{4,5},{7,6},{6,7},{9,8},{8,9},{11,10... | collective-permute-start | bytes 147464 | tf_op jit(solution)/shard_map/ppermute | solution.py:748
  6.3 0.7 %copy-start.9 = (s32[1,1,1,16,1]{3,4,2,1,0:T(1,128)S(1)}, s32[1,1,1,16,1]{3,4,2,1,0:T(1,128)}, u32[]{:S(2)}) copy-start(s32[1,1,1,16,1]{3,4,2,1,0:T(1,128)} %param.18) | copy-start | bytes 196
  6.3 13.0 %collective-permute-start.7 = (f32[280,128]{1,0:T(8,128)S(1)}, f32[280,128]{1,0:T(8,128)S(1)}, u32[]{:S(2)}, u32[]{:S(2)}) collective-permute-start(f32[280,128]{1,0:T(8,128)S(1)} %get-tuple-element.43), channel_id=1, source_target_pairs={{16,0},{20,4},{24,8},{28,12},{0,16},{4,20},{8,24},{12,28},{17,1},{... | collective-permute-start | bytes 430088 | tf_op jit(solution)/shard_map/ppermute | solution.py:772
  6.9 6.6 %copy-start.6 = (f32[8,8]{1,0:T(8,128)S(1)}, f32[8,8]{1,0:T(8,128)}, u32[]{:S(2)}) copy-start(f32[8,8]{1,0:T(8,128)} %param.15) | copy-start | bytes 772
  6.9 6.6 %copy-start.5 = (f32[8,8]{1,0:T(8,128)S(1)}, f32[8,8]{1,0:T(8,128)}, u32[]{:S(2)}) copy-start(f32[8,8]{1,0:T(8,128)} %param.16) | copy-start | bytes 772
  6.9 12.3 %collective-permute-start.3 = (f32[160,128]{1,0:T(8,128)S(1)}, f32[160,128]{1,0:T(8,128)S(1)}, u32[]{:S(2)}, u32[]{:S(2)}) collective-permute-start(f32[160,128]{1,0:T(8,128)S(1)} %get-tuple-element.39), channel_id=1, source_target_pairs={{4,0},{0,4},{12,8},{8,12},{20,16},{16,20},{28,24},{24,28},{5,1},{1... | collective-permute-start | bytes 245768 | tf_op jit(solution)/shard_map/ppermute | solution.py:769
  8.5 10.7 %collective-permute-start.4 = (f32[160,128]{1,0:T(8,128)S(1)}, f32[160,128]{1,0:T(8,128)S(1)}, u32[]{:S(2)}, u32[]{:S(2)}) collective-permute-start(f32[160,128]{1,0:T(8,128)S(1)} %get-tuple-element.40), channel_id=1, source_target_pairs={{12,0},{8,4},{4,8},{0,12},{28,16},{24,20},{20,24},{16,28},{13,1},{... | collective-permute-start | bytes 245768 | tf_op jit(solution)/shard_map/ppermute | solution.py:769
  11.0 5.6 %collective-permute-start.5 = (f32[72,128]{1,0:T(8,128)S(1)}, f32[72,128]{1,0:T(8,128)S(1)}, u32[]{:S(2)}, u32[]{:S(2)}) collective-permute-start(f32[72,128]{1,0:T(8,128)S(1)} %get-tuple-element.41), channel_id=1, source_target_pairs={{20,0},{16,4},{28,8},{24,12},{4,16},{0,20},{12,24},{8,28},{21,1},{... | collective-permute-start | bytes 110600 | tf_op jit(solution)/shard_map/ppermute | solution.py:769
  12.6 0.9 %copy-start.7 = (f32[16]{0:T(128)S(1)}, f32[16]{0:T(128)}, u32[]{:S(2)}) copy-start(f32[16]{0:T(128)} %param.14) | copy-start | bytes 196
  12.6 6.7 %collective-permute-start.6 = (f32[72,128]{1,0:T(8,128)S(1)}, f32[72,128]{1,0:T(8,128)S(1)}, u32[]{:S(2)}, u32[]{:S(2)}) collective-permute-start(f32[72,128]{1,0:T(8,128)S(1)} %get-tuple-element.42), channel_id=1, source_target_pairs={{28,0},{24,4},{20,8},{16,12},{12,16},{8,20},{4,24},{0,28},{29,1},{... | collective-permute-start | bytes 110600 | tf_op jit(solution)/shard_map/ppermute | solution.py:769
  20.6 17.0 %all-to-all-start = ((f32[4,104,128]{2,1,0:T(8,128)}), f32[4,104,128]{2,1,0:T(8,128)S(1)}, u32[]{:S(2)}, u32[]{:S(2)}) async-start(f32[4,104,128]{2,1,0:T(8,128)} %get-tuple-element.58), calls=%async_computation | async-start | bytes 425984 | tf_op jit(solution)/shard_map/all_to_all | solution.py:818
  24.0 9.0 %collective-permute-start.8 = (f32[96,128]{1,0:T(8,128)S(1)}, f32[96,128]{1,0:T(8,128)S(1)}, u32[]{:S(2)}, u32[]{:S(2)}) collective-permute-start(f32[96,128]{1,0:T(8,128)S(1)} %get-tuple-element.50), channel_id=1, source_target_pairs={{1,2},{2,1},{3,4},{4,3},{5,6},{6,5},{7,8},{8,7},{9,10},{10,9},{11,... | collective-permute-start | bytes 147464 | tf_op jit(solution)/shard_map/ppermute | solution.py:808
  37.6 12.8 %all-to-all-start.1 = ((f32[4,200,128]{2,1,0:T(8,128)}), f32[4,200,128]{2,1,0:T(8,128)S(1)}, u32[]{:S(2)}, u32[]{:S(2)}) async-start(f32[4,200,128]{2,1,0:T(8,128)} %get-tuple-element.59.refs_0_), calls=%async_computation.1 | async-start | bytes 819200 | tf_op jit(solution)/shard_map/all_to_all | solution.py:818
  41.9 9.9 %collective-permute-start.10 = (f32[96,128]{1,0:T(8,128)S(1)}, f32[96,128]{1,0:T(8,128)S(1)}, u32[]{:S(2)}, u32[]{:S(2)}) collective-permute-start(f32[96,128]{1,0:T(8,128)S(1)} %get-tuple-element.62), channel_id=1, source_target_pairs={{1,2},{2,1},{3,4},{4,3},{5,6},{6,5},{7,8},{8,7},{9,10},{10,9},{11,... | collective-permute-start | bytes 147464 | tf_op jit(solution)/shard_map/ppermute | solution.py:732
  46.4 5.4 %collective-permute-start.9 = (f32[96,128]{1,0:T(8,128)S(1)}, f32[96,128]{1,0:T(8,128)S(1)}, u32[]{:S(2)}, u32[]{:S(2)}) collective-permute-start(f32[96,128]{1,0:T(8,128)S(1)} %get-tuple-element.61), channel_id=1, source_target_pairs={{1,0},{0,1},{3,2},{2,3},{5,4},{4,5},{7,6},{6,7},{9,8},{8,9},{11,10... | collective-permute-start | bytes 147464 | tf_op jit(solution)/shard_map/ppermute | solution.py:733
  52.1 4.5 %collective-permute-start.11 = (f32[96,128]{1,0:T(8,128)S(1)}, f32[96,128]{1,0:T(8,128)S(1)}, u32[]{:S(2)}, u32[]{:S(2)}) collective-permute-start(f32[96,128]{1,0:T(8,128)S(1)} %get-tuple-element.65), channel_id=1, source_target_pairs={{1,0},{0,1},{3,2},{2,3},{5,4},{4,5},{7,6},{6,7},{9,8},{8,9},{11,10... | collective-permute-start | bytes 147464 | tf_op jit(solution)/shard_map/ppermute | solution.py:733
  52.2 9.0 %collective-permute-start.12 = (f32[96,128]{1,0:T(8,128)S(1)}, f32[96,128]{1,0:T(8,128)S(1)}, u32[]{:S(2)}, u32[]{:S(2)}) collective-permute-start(f32[96,128]{1,0:T(8,128)S(1)} %get-tuple-element.66), channel_id=1, source_target_pairs={{1,2},{2,1},{3,4},{4,3},{5,6},{6,5},{7,8},{8,7},{9,10},{10,9},{11,... | collective-permute-start | bytes 147464 | tf_op jit(solution)/shard_map/ppermute | solution.py:732

commit v8 on v7

--- a/solution.py
+++ b/solution.py
@@ -361,9 +361,9 @@
 def flow_sources_body(places, *refs):
     state, edge = refs[0:2]
     messages = refs[2 : 2 + len(places)]
-    pair, spread, labels = refs[2 + len(places) : 5 + len(places)]
-    wide, rim, send, derived, lamb_rows, ends = refs[5 + len(places) : 11 + len(places)]
-    spare = refs[11 + len(places) :]
+    pair, spread, labels, _ = refs[2 + len(places) : 6 + len(places)]
+    wide, rim, send, derived, lamb_rows, ends = refs[6 + len(places) : 12 + len(places)]
+    spare = refs[12 + len(places) :]
     cells_x = state.shape[1]
     odd = is_odd("fy")
     beside, k = [], 0
@@ -387,15 +387,16 @@
     send[:, send.shape[1] - 8 :] = labels[...]
 
 
-def flow_stages_body(wide, rim, pair, spread, labels, _, out, send, derived, lamb_rows, ends, first, second):
-    def writer(target):
-        def write(i, f, value):
-            target[f, i] = value
-
-        return write
-
+def writer(target):
+    def write(i, f, value):
+        target[f, i] = value
+
+    return write
+
+
+def flow_stages_body(wide, rim, pair, spread, labels, second, derived, ends_out, send, lamb_rows, ends, first):
     planes = wide.shape[1]
-    cells_x = out.shape[1]
+    cells_x = planes - 2 * HALO
     size = (send.shape[1] - 8) // 2
     rim_start = [rim[f] for f in range(5)]
     derive_planes(wide, derived, 0, planes)
@@ -415,7 +416,10 @@
     lamb(derived, ends, 1, cells_x, lamb_rows)
     project(lamb_rows, pair, spread, send, size)
     send[:, 2 * size :] = labels[...]
-    to_ends(along_z, 2, 8, 0, cells_x, ends)
+    to_ends(along_z, 2, 8, 0, cells_x, ends_out)
+
+
+def flow_last_body(second, derived, ends, wide, out):
     flow_rate_section(second, derived, ends, wide, 2, MIXES[2], writer(out), inner=True)
 
 
@@ -596,8 +600,6 @@
 
 def tables_body(
     packed,
-    faces,
-    faces_out,
     near,
     far,
     deriv_rows,
@@ -607,7 +609,6 @@
     labels,
     speed,
 ):
-    faces_out[...] = faces[...]
     size = near.shape[1]
     count = size // 8
     blocks = spread.shape[0] // 8
@@ -745,7 +746,7 @@
         scratch=turning,
         last=1,
     )
-    got_a = lax.ppermute(to_a, names, near_pairs)
+    got_a, got_b = traces(to_a, to_b)
 
     six = 2 * HALO
     edge_rows = 5 * 8
@@ -762,11 +763,16 @@
     )
     flat = (size_x, size_y)
     steps = [[(1, 0), (-1, 0)]] if size_x == 2 else [[(1, 0)], [(-1, 0)]]
+    pairs = [(y_a, y_b, [(0, 0)])] + [(xy_a, xy_b, spots) for spots in steps]
+    moved = {}
+    for second in (True, False):
+        for k in reversed(range(len(pairs))):
+            kept, shift = pairs[k][1 if second else 0], pairs[k][2][0][0]
+            moved[k, second] = lax.ppermute(kept, ("fx", "fy"), partners(flat, 1, second, shift))
     places, messages = [], []
-    for first, second, spots in [(y_a, y_b, [(0, 0)])] + [(xy_a, xy_b, spots) for spots in steps]:
-        shift = spots[0][0]
-        for kept, side in ((first, False), (second, True)):
-            messages.append(lax.ppermute(kept, ("fx", "fy"), partners(flat, 1, side, shift)))
+    for k, (_, _, spots) in enumerate(pairs):
+        for second in (False, True):
+            messages.append(moved[k, second])
             places.append(tuple((dx, 1) for dx, _ in spots))
     for spots in steps:
         messages.append(lax.ppermute(along_x, ("fx", "fy"), shifted(flat, spots[0])))
@@ -789,10 +795,9 @@
         + piece(block_element.reshape(1, blocks), 26)
     )
     table = jax.ShapeDtypeStruct((5, size, size), BF16)
-    to_b, near, far, deriv_rows, deriv_lanes, pair, spread, labels, speed = call(
+    near, far, deriv_rows, deriv_lanes, pair, spread, labels, speed = call(
         tables_body,
         [
-            faces,
             table,
             table,
             (128, 64),
@@ -803,9 +808,7 @@
             (1, size),
         ],
         packed,
-        to_b,
-    )
-    got_b = lax.ppermute(to_b, names, far_pairs)
+    )
 
     fold = fold_of(size_y, blocks)
     wide = cells_x + 2 * HALO
@@ -827,6 +830,8 @@
         pair,
         spread,
         labels,
+        got_b,
+        last=1,
         scratch=[
             pltpu.VMEM((3, wide, 16, 128), F32),
             rows_scratch,
@@ -835,23 +840,20 @@
         + spare,
     )
     received = route(send)
-    flow_state, send = call(
+    second, derived, ends, send = call(
         flow_stages_body,
-        [(5, cells_x, 8, 128), (size_y, 2 * 192 // fold + 8, 128)],
+        [
+            planes(wide - 4),
+            planes(wide),
+            (5, cells_x, 8, 128),
+            (size_y, 2 * 192 // fold + 8, 128),
+        ],
         start,
         rim,
         pair,
         spread,
         labels,
-        got_b,
-        last=1,
-        scratch=[
-            pltpu.VMEM(planes(wide), F32),
-            rows_scratch,
-            pltpu.VMEM(planes(wide - 2), F32),
-            pltpu.VMEM(planes(wide - 2), F32),
-            pltpu.VMEM(planes(wide - 4), F32),
-        ],
+        scratch=[rows_scratch, pltpu.VMEM(planes(wide - 2), F32), pltpu.VMEM(planes(wide - 2), F32)],
     )
 
     def local_part(mix, now):
@@ -882,6 +884,7 @@
     )
     source_two, source_three = call(place_body, [(3, 64, 128)] * 2, route(send))
     got_a, got_b = traces(to_a, to_b)
+    flow_state = call(flow_last_body, [(5, cells_x, 8, 128)], second, derived, ends, start)[0]
     partial = local_part(MIXES[1], sound_one)
     sound_two, to_a, to_b = call(
         functools.partial(acoustic_far_body, MIXES[1], "second"),

time: 62.9 us -> 58.1 us (0.924)
  waiting for transfers between devices: 20.2 us -> 11.8 us
  starting transfers between devices: 27.9 us -> 30.6 us
    ppermute x6 -> x4, waiting for transfers between devices: 11 us -> 3.03 us  [per_device(): lax.ppermute(kept, ('fx', 'fy'), partners(flat, 1, second, shift))]
    ppermute x2 -> x3, starting transfers between devices: 8.5 us -> 15.6 us  [traces(): far_got = lax.ppermute(to_b, names, far_pairs)]
    ppermute x6 -> x4, starting transfers between devices: 10.1 us -> 5.59 us  [per_device(): lax.ppermute(kept, ('fx', 'fy'), partners(flat, 1, second, shift))]
    ppermute x2 -> x3, waiting for transfers between devices: 5.56 us -> 3.16 us  [traces(): far_got = lax.ppermute(to_b, names, far_pairs)]
    all_to_all x2, waiting for transfers between devices: 3.61 us -> 5.62 us  [route(): return lax.all_to_all(send, 'fy', split_axis=0, concat_axis=0, tiled=True)]
    pallas_call x13 -> x14, Pallas kernels: 11.3 us -> 11.6 us  [call(): pl.pallas_call(kernel, out_shape=outs, in_specs=specs, out_specs=[whole]...]
  transfers between devices with their start and end apart: 15 -> 15, of which waited for: 7 -> 7; matrix products, arithmetic and copies ran while one was open for 0% -> 0% of each run, Pallas kernels for 13% -> 15%
where the time goes in v8:
time: 58.1 us; the launch traced here: 57.7 us
  starting transfers between devices  30.6 us (53%)
  waiting for transfers between devices  11.8 us (20%)
  Pallas kernels  11.6 us (20%)
  local copies, waits for them, and re-layouts  1.81 us (3%)
  other arithmetic  1.01 us (2%)
  between operations  0.88 us (2%)
    ppermute x3, starting transfers between devices, traces(): far_got = lax.ppermute(to_b, names, far_pairs)  15.6 us
    pallas_call x14, Pallas kernels, call(): pl.pallas_call(kernel, out_shape=outs, in_specs=specs, out_specs=[whole]...  11.6 us
    all_to_all x2, starting transfers between devices, route(): return lax.all_to_all(send, 'fy', split_axis=0, concat_axis=0, tiled=True)  7.4 us
    all_to_all x2, waiting for transfers between devices, route(): return lax.all_to_all(send, 'fy', split_axis=0, concat_axis=0, tiled=True)  5.62 us
    ppermute x4, starting transfers between devices, per_device(): lax.ppermute(kept, ('fx', 'fy'), partners(flat, 1, second, shift))  5.59 us
    ppermute x3, waiting for transfers between devices, traces(): far_got = lax.ppermute(to_b, names, far_pairs)  3.16 us
    ppermute x4, waiting for transfers between devices, per_device(): lax.ppermute(kept, ('fx', 'fy'), partners(flat, 1, second, shift))  3.03 us
    unnamed x20, local copies, waits for them, and re-layouts  1.81 us
  transfers between devices with their start and end apart: 15, of which 7 were waited for; matrix products, arithmetic and copies ran while one was open for 0% of the time, Pallas kernels for 15%

profile of v8, /device:TPU:2, one launch (start us, length us, event | category | flops | bytes accessed | tf_op | source)
XLA Modules:
  0.0 57.7 jit_solution(17067989978221276467)
XLA Ops:
  0.7 1.0 %broadcast_multiply_fusion = f32[3,8,8,128]{3,2,1,0:T(8,128)S(1)} fusion(f32[3,8,8,128]{3,2,1,0:T(8,128)} %param.11, f32[8,8,128]{2,1,0:T(8,128)} %param.10), kind=kLoop, calls=%fused_computation.1 | loop fusion | flops 24576 | bytes 229376 | tf_op jit(solution)/shard_map/mul | solution.py:723
  1.9 1.6 %collective-permute-start.1 = (f32[24,128]{1,0:T(8,128)S(1)}, f32[24,128]{1,0:T(8,128)S(1)}, u32[]{:S(2)}, u32[]{:S(2)}) collective-permute-start(f32[24,128]{1,0:T(8,128)S(1)} %get-tuple-element.37.sent_b), channel_id=1, source_target_pairs={{3,0},{2,1},{1,2},{0,3},{7,4},{6,5},{5,6},{4,7},{11,8},{10,9},{9,1... | collective-permute-start | bytes 36872 | tf_op jit(solution)/shard_map/ppermute | solution.py:727
  3.5 0.7 %copy-done.4 = s32[16,6]{0,1:T(8,128)S(1)} copy-done((s32[16,6]{0,1:T(8,128)S(1)}, s32[16,6]{0,1:T(8,128)}, u32[]{:S(2)}) %copy-start.4) | copy-done | bytes 408
  4.2 0.6 shard_map.114
  5.0 0.5 copy-done.8
  5.5 5.1 %collective-permute-start.8 = (f32[96,128]{1,0:T(8,128)S(1)}, f32[96,128]{1,0:T(8,128)S(1)}, u32[]{:S(2)}, u32[]{:S(2)}) collective-permute-start(f32[96,128]{1,0:T(8,128)S(1)} %get-tuple-element.48), channel_id=1, source_target_pairs={{1,2},{2,1},{3,4},{4,3},{5,6},{6,5},{7,8},{8,7},{9,10},{10,9},{11,... | collective-permute-start | bytes 147464 | tf_op jit(solution)/shard_map/ppermute | solution.py:733
  10.8 0.6 copy-done.9
  11.4 1.0 %collective-permute-start.4 = (f32[160,128]{1,0:T(8,128)S(1)}, f32[160,128]{1,0:T(8,128)S(1)}, u32[]{:S(2)}, u32[]{:S(2)}) collective-permute-start(f32[160,128]{1,0:T(8,128)S(1)} %get-tuple-element.41), channel_id=1, source_target_pairs={{12,0},{8,4},{4,8},{0,12},{28,16},{24,20},{20,24},{16,28},{13,1},{... | collective-permute-start | bytes 245768 | tf_op jit(solution)/shard_map/ppermute | solution.py:771
  12.4 2.0 %collective-permute-start.5 = (f32[72,128]{1,0:T(8,128)S(1)}, f32[72,128]{1,0:T(8,128)S(1)}, u32[]{:S(2)}, u32[]{:S(2)}) collective-permute-start(f32[72,128]{1,0:T(8,128)S(1)} %get-tuple-element.42), channel_id=1, source_target_pairs={{20,0},{16,4},{28,8},{24,12},{4,16},{0,20},{12,24},{8,28},{21,1},{... | collective-permute-start | bytes 110600 | tf_op jit(solution)/shard_map/ppermute | solution.py:771
  14.4 0.3 collective-permute-done.8.refs_10_.got_b
  14.6 2.6 %collective-permute-start.6 = (f32[72,128]{1,0:T(8,128)S(1)}, f32[72,128]{1,0:T(8,128)S(1)}, u32[]{:S(2)}, u32[]{:S(2)}) collective-permute-start(f32[72,128]{1,0:T(8,128)S(1)} %get-tuple-element.43), channel_id=1, source_target_pairs={{28,0},{24,4},{20,8},{16,12},{12,16},{8,20},{4,24},{0,28},{29,1},{... | collective-permute-start | bytes 110600 | tf_op jit(solution)/shard_map/ppermute | solution.py:771
  17.3 1.0 %shard_map.116 = (bf16[5,128,128]{2,1,0:T(8,128)(2,1)S(1)}, bf16[5,128,128]{2,1,0:T(8,128)(2,1)S(1)}, f32[128,64]{1,0:T(8,128)S(1)}, f32[128,128]{1,0:T(8,128)S(...) custom-call(f32[32,16]{1,0:T(8,128)S(1)} %pad_add_fusion.1.packed), custom_call_target="tpu_custom_call" | custom-call | tf_op jit(solution)/shard_map/pallas_call | solution.py:71
  18.3 1.0 %collective-permute-done.5.refs_4_ = f32[72,128]{1,0:T(8,128)S(1)} collective-permute-done((f32[72,128]{1,0:T(8,128)S(1)}, f32[72,128]{1,0:T(8,128)S(1)}, u32[]{:S(2)}, u32[]{:S(2)}) %collective-permute-start.5) | collective-permute-done | bytes 36896 | tf_op jit(solution)/shard_map/ppermute | solution.py:771
  19.3 2.0 %collective-permute-done.6.refs_5_ = f32[72,128]{1,0:T(8,128)S(1)} collective-permute-done((f32[72,128]{1,0:T(8,128)S(1)}, f32[72,128]{1,0:T(8,128)S(1)}, u32[]{:S(2)}, u32[]{:S(2)}) %collective-permute-start.6) | collective-permute-done | bytes 36896 | tf_op jit(solution)/shard_map/ppermute | solution.py:771
  21.3 1.3 %shard_map.117 = (f32[5,14,16,128]{3,2,1,0:T(8,128)S(1)}, f32[5,16,256]{2,1,0:T(8,128)S(1)}, f32[4,104,128]{2,1,0:T(8,128)}) custom-call(f32[5,8,8,128]{3,2,1,0:T(8,128)S(1)} %pad_add_fusion.state.refs_0_, f32[40,128]{1,0:T(8,128)S(1)} %get-tuple-element.39.refs_1_, f32[160,128]{1,0:T(8,128)S(1)} %collective-permute-done.3.refs_2_, ...), custom_call_target="tpu_custom_call" | custom-call | tf_op jit(solution)/shard_map/pallas_call | solution.py:71
  22.6 3.9 %all-to-all-start = ((f32[4,104,128]{2,1,0:T(8,128)}), f32[4,104,128]{2,1,0:T(8,128)S(1)}, u32[]{:S(2)}, u32[]{:S(2)}) async-start(f32[4,104,128]{2,1,0:T(8,128)} %get-tuple-element.60), calls=%async_computation | async-start | bytes 425984 | tf_op jit(solution)/shard_map/all_to_all | solution.py:821
  26.5 3.9 %shard_map.118 = (f32[5,10,16,128]{3,2,1,0:T(8,128)S(1)}, f32[5,14,16,128]{3,2,1,0:T(8,128)S(1)}, f32[5,8,8,128]{3,2,1,0:T(8,128)S(1)}, f32[4,200,128]{2,1,0:T(8,128)}) custom-call(f32[5,14,16,128]{3,2,1,0:T(8,128)S(1)} %get-tuple-element.49.wide, f32[5,16,256]{2,1,0:T(8,128)S(1)} %get-tuple-element.50.rim, f32[64,64]{1,0:T(8,128)S(1)} %get-tuple-element.45.refs_7_.pair, ...), custom_call_target="tpu_custom_call" | custom-call | tf_op jit(solution)/shard_map/pallas_call | solution.py:71
  30.4 2.5 %all-to-all-done.received = f32[4,104,128]{2,1,0:T(8,128)S(1)} async-done(((f32[4,104,128]{2,1,0:T(8,128)}), f32[4,104,128]{2,1,0:T(8,128)S(1)}, u32[]{:S(2)}, u32[]{:S(2)}) %all-to-all-start) | async-done | bytes 213024 | tf_op jit(solution)/shard_map/all_to_all | solution.py:821
  32.9 3.5 %all-to-all-start.1 = ((f32[4,200,128]{2,1,0:T(8,128)}), f32[4,200,128]{2,1,0:T(8,128)S(1)}, u32[]{:S(2)}, u32[]{:S(2)}) async-start(f32[4,200,128]{2,1,0:T(8,128)} %get-tuple-element.61.refs_0_), calls=%async_computation.1 | async-start | bytes 819200 | tf_op jit(solution)/shard_map/all_to_all | solution.py:821
  36.4 0.3 shard_map.120.partial
  36.7 0.5 shard_map.121
  37.3 4.6 %collective-permute-start.10 = (f32[96,128]{1,0:T(8,128)S(1)}, f32[96,128]{1,0:T(8,128)S(1)}, u32[]{:S(2)}, u32[]{:S(2)}) collective-permute-start(f32[96,128]{1,0:T(8,128)S(1)} %get-tuple-element.64), channel_id=1, source_target_pairs={{1,2},{2,1},{3,4},{4,3},{5,6},{6,5},{7,8},{8,7},{9,10},{10,9},{11,... | collective-permute-start | bytes 147464 | tf_op jit(solution)/shard_map/ppermute | solution.py:733
  42.0 0.3 shard_map.122.partial
  42.3 3.1 %all-to-all-done.1.received = f32[4,200,128]{2,1,0:T(8,128)S(1)} async-done(((f32[4,200,128]{2,1,0:T(8,128)}), f32[4,200,128]{2,1,0:T(8,128)S(1)}, u32[]{:S(2)}, u32[]{:S(2)}) %all-to-all-start.1) | async-done | bytes 409632 | tf_op jit(solution)/shard_map/all_to_all | solution.py:821
  45.4 0.4 shard_map.123
  45.8 1.2 %collective-permute-done.10.got_b = f32[96,128]{1,0:T(8,128)S(1)} collective-permute-done((f32[96,128]{1,0:T(8,128)S(1)}, f32[96,128]{1,0:T(8,128)S(1)}, u32[]{:S(2)}, u32[]{:S(2)}) %collective-permute-start.10) | collective-permute-done | bytes 49184 | tf_op jit(solution)/shard_map/ppermute | solution.py:733
  47.0 0.3 shard_map.124
  47.4 5.9 %collective-permute-start.12 = (f32[96,128]{1,0:T(8,128)S(1)}, f32[96,128]{1,0:T(8,128)S(1)}, u32[]{:S(2)}, u32[]{:S(2)}) collective-permute-start(f32[96,128]{1,0:T(8,128)S(1)} %get-tuple-element.68), channel_id=1, source_target_pairs={{1,2},{2,1},{3,4},{4,3},{5,6},{6,5},{7,8},{8,7},{9,10},{10,9},{11,... | collective-permute-start | bytes 147464 | tf_op jit(solution)/shard_map/ppermute | solution.py:733
  53.3 1.0 %shard_map.119 = f32[5,8,8,128]{3,2,1,0:T(8,128)} custom-call(f32[5,10,16,128]{3,2,1,0:T(8,128)S(1)} %get-tuple-element.51.second, f32[5,14,16,128]{3,2,1,0:T(8,128)S(1)} %get-tuple-element.52.derived, f32[5,8,8,128]{3,2,1,0:T(8,128)S(1)} %get-tuple-element.53.ends, f32[5,14,16,128]{3,2,1,0:T(8,128)S(1)} %get-tuple-element.49.wide), custom_call_target="tpu_custom_call" | custom-call | tf_op jit(solution)/shard_map/pallas_call | solution.py:71
  54.3 0.3 shard_map.125.partial
  54.7 1.8 %collective-permute-done.12.got_b = f32[96,128]{1,0:T(8,128)S(1)} collective-permute-done((f32[96,128]{1,0:T(8,128)S(1)}, f32[96,128]{1,0:T(8,128)S(1)}, u32[]{:S(2)}, u32[]{:S(2)}) %collective-permute-start.12) | collective-permute-done | bytes 49184 | tf_op jit(solution)/shard_map/ppermute | solution.py:733
  56.4 1.3 %shard_map.126 = f32[16,4,512]{2,1,0:T(4,128)} custom-call(f32[4,64,128]{2,1,0:T(8,128)S(1)} %shard_map.125.partial, f32[96,128]{1,0:T(8,128)S(1)} %collective-permute-done.11.got_a, f32[96,128]{1,0:T(8,128)S(1)} %collective-permute-done.12.got_b, bf16[5,128,128]{2,1,0:T(8,128)(2,1)S(1)} %get-tuple-element.59.sides_far, ...), custom_call_target="tpu_custom_call" | custom-call | tf_op jit(solution)/shard_map/pallas_call | solution.py:71
  (39 shorter events, 0.8 us)
Async XLA Ops:
  0.6 1.0 %copy-start.2 = (f32[8,8,128]{2,1,0:T(8,128)S(1)}, f32[8,8,128]{2,1,0:T(8,128)}, u32[]{:S(2)}) copy-start(f32[8,8,128]{2,1,0:T(8,128)} %param.10) | copy-start | bytes 98308
  0.6 1.0 %copy-start.1 = (f32[3,8,8,128]{3,2,1,0:T(8,128)S(1)}, f32[3,8,8,128]{3,2,1,0:T(8,128)}, u32[]{:S(2)}) copy-start(f32[3,8,8,128]{3,2,1,0:T(8,128)} %param.11) | copy-start | bytes 294916
  0.6 1.0 %copy-start.3 = (f32[8,8,128]{2,1,0:T(8,128)S(1)}, f32[8,8,128]{2,1,0:T(8,128)}, u32[]{:S(2)}) copy-start(f32[8,8,128]{2,1,0:T(8,128)} %param.12) | copy-start | bytes 98308
  1.7 2.5 %copy-start = (f32[16,4,512]{2,1,0:T(4,128)S(1)}, f32[16,4,512]{2,1,0:T(4,128)}, u32[]{:S(2)}) copy-start(f32[16,4,512]{2,1,0:T(4,128)} %given.1) | copy-start | bytes 393220
  1.8 2.4 %collective-permute-start = (f32[24,128]{1,0:T(8,128)S(1)}, f32[24,128]{1,0:T(8,128)S(1)}, u32[]{:S(2)}, u32[]{:S(2)}) collective-permute-start(f32[24,128]{1,0:T(8,128)S(1)} %get-tuple-element.36.sent_a), channel_id=1, source_target_pairs={{1,0},{0,1},{3,2},{2,3},{5,4},{4,5},{7,6},{6,7},{9,8},{8,9},{11,10... | collective-permute-start | bytes 36872 | tf_op jit(solution)/shard_map/ppermute | solution.py:726
  1.9 8.7 %collective-permute-start.1 = (f32[24,128]{1,0:T(8,128)S(1)}, f32[24,128]{1,0:T(8,128)S(1)}, u32[]{:S(2)}, u32[]{:S(2)}) collective-permute-start(f32[24,128]{1,0:T(8,128)S(1)} %get-tuple-element.37.sent_b), channel_id=1, source_target_pairs={{3,0},{2,1},{1,2},{0,3},{7,4},{6,5},{5,6},{4,7},{11,8},{10,9},{9,1... | collective-permute-start | bytes 36872 | tf_op jit(solution)/shard_map/ppermute | solution.py:727
  3.5 0.7 %copy-start.4 = (s32[16,6]{0,1:T(8,128)S(1)}, s32[16,6]{0,1:T(8,128)}, u32[]{:S(2)}) copy-start(s32[16,6]{0,1:T(8,128)} %param.17) | copy-start | bytes 1156
  4.8 0.7 %copy-start.8 = (s32[1,1,1,16]{3,2,1,0:T(1,128)S(1)}, s32[1,1,1,16]{3,2,1,0:T(1,128)}, u32[]{:S(2)}) copy-start(s32[1,1,1,16]{3,2,1,0:T(1,128)} %param.19) | copy-start | bytes 196
  4.8 5.8 %collective-permute-start.2 = (f32[96,128]{1,0:T(8,128)S(1)}, f32[96,128]{1,0:T(8,128)S(1)}, u32[]{:S(2)}, u32[]{:S(2)}) collective-permute-start(f32[96,128]{1,0:T(8,128)S(1)} %get-tuple-element.38), channel_id=1, source_target_pairs={{1,0},{0,1},{3,2},{2,3},{5,4},{4,5},{7,6},{6,7},{9,8},{8,9},{11,10... | collective-permute-start | bytes 147464 | tf_op jit(solution)/shard_map/ppermute | solution.py:734
  5.5 9.2 %collective-permute-start.8 = (f32[96,128]{1,0:T(8,128)S(1)}, f32[96,128]{1,0:T(8,128)S(1)}, u32[]{:S(2)}, u32[]{:S(2)}) collective-permute-start(f32[96,128]{1,0:T(8,128)S(1)} %get-tuple-element.48), channel_id=1, source_target_pairs={{1,2},{2,1},{3,4},{4,3},{5,6},{6,5},{7,8},{8,7},{9,10},{10,9},{11,... | collective-permute-start | bytes 147464 | tf_op jit(solution)/shard_map/ppermute | solution.py:733
  10.7 0.7 %copy-start.9 = (s32[1,1,1,16,1]{3,4,2,1,0:T(1,128)S(1)}, s32[1,1,1,16,1]{3,4,2,1,0:T(1,128)}, u32[]{:S(2)}) copy-start(s32[1,1,1,16,1]{3,4,2,1,0:T(1,128)} %param.18) | copy-start | bytes 196
  10.7 10.6 %collective-permute-start.7 = (f32[280,128]{1,0:T(8,128)S(1)}, f32[280,128]{1,0:T(8,128)S(1)}, u32[]{:S(2)}, u32[]{:S(2)}) collective-permute-start(f32[280,128]{1,0:T(8,128)S(1)} %get-tuple-element.44), channel_id=1, source_target_pairs={{16,0},{20,4},{24,8},{28,12},{0,16},{4,20},{8,24},{12,28},{17,1},{... | collective-permute-start | bytes 430088 | tf_op jit(solution)/shard_map/ppermute | solution.py:778
  11.4 5.9 %copy-start.6 = (f32[8,8]{1,0:T(8,128)S(1)}, f32[8,8]{1,0:T(8,128)}, u32[]{:S(2)}) copy-start(f32[8,8]{1,0:T(8,128)} %param.15) | copy-start | bytes 772
  11.4 5.9 %copy-start.5 = (f32[8,8]{1,0:T(8,128)S(1)}, f32[8,8]{1,0:T(8,128)}, u32[]{:S(2)}) copy-start(f32[8,8]{1,0:T(8,128)} %param.16) | copy-start | bytes 772
  11.4 9.9 %collective-permute-start.3 = (f32[160,128]{1,0:T(8,128)S(1)}, f32[160,128]{1,0:T(8,128)S(1)}, u32[]{:S(2)}, u32[]{:S(2)}) collective-permute-start(f32[160,128]{1,0:T(8,128)S(1)} %get-tuple-element.40), channel_id=1, source_target_pairs={{4,0},{0,4},{12,8},{8,12},{20,16},{16,20},{28,24},{24,28},{5,1},{1... | collective-permute-start | bytes 245768 | tf_op jit(solution)/shard_map/ppermute | solution.py:771
  11.4 9.9 %collective-permute-start.4 = (f32[160,128]{1,0:T(8,128)S(1)}, f32[160,128]{1,0:T(8,128)S(1)}, u32[]{:S(2)}, u32[]{:S(2)}) collective-permute-start(f32[160,128]{1,0:T(8,128)S(1)} %get-tuple-element.41), channel_id=1, source_target_pairs={{12,0},{8,4},{4,8},{0,12},{28,16},{24,20},{20,24},{16,28},{13,1},{... | collective-permute-start | bytes 245768 | tf_op jit(solution)/shard_map/ppermute | solution.py:771
  12.4 6.9 %collective-permute-start.5 = (f32[72,128]{1,0:T(8,128)S(1)}, f32[72,128]{1,0:T(8,128)S(1)}, u32[]{:S(2)}, u32[]{:S(2)}) collective-permute-start(f32[72,128]{1,0:T(8,128)S(1)} %get-tuple-element.42), channel_id=1, source_target_pairs={{20,0},{16,4},{28,8},{24,12},{4,16},{0,20},{12,24},{8,28},{21,1},{... | collective-permute-start | bytes 110600 | tf_op jit(solution)/shard_map/ppermute | solution.py:771
  14.6 2.6 %copy-start.7 = (f32[16]{0:T(128)S(1)}, f32[16]{0:T(128)}, u32[]{:S(2)}) copy-start(f32[16]{0:T(128)} %param.14) | copy-start | bytes 196
  14.6 6.7 %collective-permute-start.6 = (f32[72,128]{1,0:T(8,128)S(1)}, f32[72,128]{1,0:T(8,128)S(1)}, u32[]{:S(2)}, u32[]{:S(2)}) collective-permute-start(f32[72,128]{1,0:T(8,128)S(1)} %get-tuple-element.43), channel_id=1, source_target_pairs={{28,0},{24,4},{20,8},{16,12},{12,16},{8,20},{4,24},{0,28},{29,1},{... | collective-permute-start | bytes 110600 | tf_op jit(solution)/shard_map/ppermute | solution.py:771
  22.6 10.3 %all-to-all-start = ((f32[4,104,128]{2,1,0:T(8,128)}), f32[4,104,128]{2,1,0:T(8,128)S(1)}, u32[]{:S(2)}, u32[]{:S(2)}) async-start(f32[4,104,128]{2,1,0:T(8,128)} %get-tuple-element.60), calls=%async_computation | async-start | bytes 425984 | tf_op jit(solution)/shard_map/all_to_all | solution.py:821
  32.9 12.5 %all-to-all-start.1 = ((f32[4,200,128]{2,1,0:T(8,128)}), f32[4,200,128]{2,1,0:T(8,128)S(1)}, u32[]{:S(2)}, u32[]{:S(2)}) async-start(f32[4,200,128]{2,1,0:T(8,128)} %get-tuple-element.61.refs_0_), calls=%async_computation.1 | async-start | bytes 819200 | tf_op jit(solution)/shard_map/all_to_all | solution.py:821
  37.3 9.7 %collective-permute-start.10 = (f32[96,128]{1,0:T(8,128)S(1)}, f32[96,128]{1,0:T(8,128)S(1)}, u32[]{:S(2)}, u32[]{:S(2)}) collective-permute-start(f32[96,128]{1,0:T(8,128)S(1)} %get-tuple-element.64), channel_id=1, source_target_pairs={{1,2},{2,1},{3,4},{4,3},{5,6},{6,5},{7,8},{8,7},{9,10},{10,9},{11,... | collective-permute-start | bytes 147464 | tf_op jit(solution)/shard_map/ppermute | solution.py:733
  41.9 5.1 %collective-permute-start.9 = (f32[96,128]{1,0:T(8,128)S(1)}, f32[96,128]{1,0:T(8,128)S(1)}, u32[]{:S(2)}, u32[]{:S(2)}) collective-permute-start(f32[96,128]{1,0:T(8,128)S(1)} %get-tuple-element.63), channel_id=1, source_target_pairs={{1,0},{0,1},{3,2},{2,3},{5,4},{4,5},{7,6},{6,7},{9,8},{8,9},{11,10... | collective-permute-start | bytes 147464 | tf_op jit(solution)/shard_map/ppermute | solution.py:734
  47.3 7.3 %collective-permute-start.11 = (f32[96,128]{1,0:T(8,128)S(1)}, f32[96,128]{1,0:T(8,128)S(1)}, u32[]{:S(2)}, u32[]{:S(2)}) collective-permute-start(f32[96,128]{1,0:T(8,128)S(1)} %get-tuple-element.67), channel_id=1, source_target_pairs={{1,0},{0,1},{3,2},{2,3},{5,4},{4,5},{7,6},{6,7},{9,8},{8,9},{11,10... | collective-permute-start | bytes 147464 | tf_op jit(solution)/shard_map/ppermute | solution.py:734
  47.4 9.0 %collective-permute-start.12 = (f32[96,128]{1,0:T(8,128)S(1)}, f32[96,128]{1,0:T(8,128)S(1)}, u32[]{:S(2)}, u32[]{:S(2)}) collective-permute-start(f32[96,128]{1,0:T(8,128)S(1)} %get-tuple-element.68), channel_id=1, source_target_pairs={{1,2},{2,1},{3,4},{4,3},{5,6},{6,5},{7,8},{8,7},{9,10},{10,9},{11,... | collective-permute-start | bytes 147464 | tf_op jit(solution)/shard_map/ppermute | solution.py:733

commit v9 on v8

--- a/solution.py
+++ b/solution.py
@@ -45,36 +45,18 @@
     return dot(left_high, right) + dot(left_low, right)
 
 
-def call(body, outs, *operands, scratch=(), fetch=False, last=0):
+def call(body, outs, *operands, scratch=(), last=0, cost=None):
     whole = pl.BlockSpec(memory_space=pltpu.VMEM)
     outs = [out if isinstance(out, jax.ShapeDtypeStruct) else jax.ShapeDtypeStruct(out, F32) for out in outs]
-    scratch = list(scratch)
-    anywhere = pl.BlockSpec(memory_space=pltpu.HBM)
-    specs = [anywhere if fetch else whole] * (len(operands) - last) + [anywhere] * last
-    kernel = body
-    if fetch:
-        count = len(operands)
-        total = count + len(outs)
-
-        def kernel(*refs):
-            held, sems = refs[total : total + count], refs[total + count]
-            copies = [
-                pltpu.make_async_copy(refs[i], held[i], sems.at[i]) for i in range(count)
-            ]
-            for copy in copies:
-                copy.start()
-            for copy in copies:
-                copy.wait()
-            body(*held, *refs[count:total], *refs[total + count + 1 :])
-
-        scratch = [pltpu.VMEM(o.shape, o.dtype) for o in operands] + [pltpu.SemaphoreType.DMA((count,))] + scratch
+    anywhere = pl.BlockSpec(memory_space=pl.ANY)
     return pl.pallas_call(
-        kernel,
+        body,
         out_shape=outs,
-        in_specs=specs,
+        in_specs=[whole] * (len(operands) - last) + [anywhere] * last,
         out_specs=[whole] * len(outs),
-        scratch_shapes=scratch,
+        scratch_shapes=list(scratch),
         compiler_params=PARAMS,
+        cost_estimate=None if cost is None else pl.CostEstimate(flops=cost, bytes_accessed=cost, transcendentals=0),
     )(*operands)
 
 
@@ -108,11 +90,9 @@
         message_b[tile * 8 : tile * 8 + 8] = second
 
 
-def pack_next_body(
-    state, sent_a, sent_b, got_a, got_b, _, edge, along_x, y_a, y_b, xy_a, xy_b
-):
+def pack_next_body(state, sent_a, sent_b, got_a, got_b, _, edge, along_x):
     cells_x = state.shape[1]
-    odd_z, odd = is_odd("fz"), is_odd("fy")
+    odd_z = is_odd("fz")
     high, low = paired(odd_z, sent_a[...], sent_b[...])
     above, below = paired(odd_z, got_a[...], got_b[...])
     row = lax.broadcasted_iota(jnp.int32, (8, 128), 0)
@@ -131,69 +111,84 @@
                 for x in range(1, cells_x):
                     total = total + spread[at + x * 8 : at + x * 8 + 8]
                 edge[f * 8 : f * 8 + 8] = total
-    planes = [cells_x - HALO + i for i in range(HALO)] + list(range(HALO))
     for f in range(5):
-        for s, x in enumerate(planes):
-            at = (f * len(planes) + s) * 8
+        for s, x in enumerate(x_planes(cells_x)):
+            at = (f * 2 * HALO + s) * 8
             along_x[at : at + 8] = state[f, x]
+    size = along_x.shape[0]
+    along_x[size - 40 : size] = edge[...]
+
+
+def x_planes(cells_x):
+    return [cells_x - HALO + i for i in range(HALO)] + list(range(HALO))
+
+
+def sides_of(beside_x):
+    return beside_x[0], beside_x[-1]
+
+
+def beyond(beside_x, f):
+    after, before = sides_of(beside_x)
+    at = after.shape[0] - 40 + f * 8
+    if after is before:
+        return after[at : at + 8]
+    lane = lax.broadcasted_iota(jnp.int32, (8, 128), 1)
+    return jnp.where(lane < 64, after[at : at + 8], before[at : at + 8])
+
+
+def pack_last_body(state, edge, *refs):
+    beside_x, (y_a, y_b) = refs[:-2], refs[-2:]
+    cells_x = state.shape[1]
+    odd = is_odd("fy")
+    after, before = sides_of(beside_x)
+
+    def put(at, values, height):
+        first, second = paired(odd, values[8 - height : 8], values[0:height])
+        y_a[at : at + height] = first
+        y_b[at : at + height] = second
+
+    lines = 5 * cells_x * HALO
+    for f in range(5):
         for x in range(cells_x):
-            at = (f * cells_x + x) * HALO
-            first, second = paired(odd, state[f, x, 8 - HALO : 8], state[f, x, 0:HALO])
-            y_a[at : at + HALO] = first
-            y_b[at : at + HALO] = second
-        at = f * 6
+            put((f * cells_x + x) * HALO, state[f, x], HALO)
+        at = lines + f * 6
         for slot, height in ((1, 1), (2, 2), (3, 2), (4, 1)):
-            x = planes[slot]
-            first, second = paired(odd, state[f, x, 8 - height : 8], state[f, x, 0:height])
-            xy_a[at : at + height] = first
-            xy_b[at : at + height] = second
+            source = (f * 2 * HALO + slot) * 8
+            put(at, (before if slot < HALO else after)[source : source + 8], height)
             at += height
-    for message in (along_x, y_a, y_b, xy_a, xy_b):
-        size = message.shape[0]
-        message[size - 40 : size] = edge[...]
-
-
-def assemble(wide, rim, state, edge, beside, cells_x):
-    for dx, dy, message in beside:
-        if dx == 0:
-            columns = [(HALO + x, x) for x in range(cells_x)]
-        elif dx < 0:
-            columns = [(i, i) for i in range(HALO)]
-        else:
-            columns = [(HALO + cells_x + i, HALO + i) for i in range(HALO)]
-        for f in range(5):
-            for plane, slot in columns:
-                height = 8 if dy == 0 else HALO
-                at = (f * (cells_x if dx == 0 else 2 * HALO) + slot) * height
-                if dx != 0 and dy != 0:
-                    if slot in (0, 5):
-                        continue
-                    height = (0, 1, 2, 2, 1)[slot]
-                    at = f * 6 + (0, 0, 1, 3, 5)[slot]
-                low, high = {0: (0, 8), 1: (8, 8 + height), -1: (16 - height, 16)}[dy]
-                wide[f, plane, low:high] = message[at : at + height]
-    edges = {(dx, dy): message for dx, dy, message in beside}
-    edges[0, 0] = edge
+        for message in (y_a, y_b):
+            at = message.shape[0] - 80 + f * 8
+            message[at : at + 8] = edge[f * 8 : f * 8 + 8]
+            message[at + 40 : at + 48] = beyond(beside_x, f)
+
+
+def assemble(wide, rim, state, edge, beside_x, above, below):
+    cells_x = state.shape[1]
+    after, before = sides_of(beside_x)
+    lines = 5 * cells_x * HALO
     row = lax.broadcasted_iota(jnp.int32, (8, 128), 0)
-    lane = lax.broadcasted_iota(jnp.int32, (8, 128), 1)
-
-    def part(f, dx, dy):
-        message = edges[dx, dy]
-        at = message.shape[0] - 40 + f * 8
-        return message[at : at + 8]
-
-    def beyond(f, dy):
-        if edges[1, dy] is edges[-1, dy]:
-            return part(f, 1, dy)
-        return jnp.where(lane < 64, part(f, 1, dy), part(f, -1, dy))
-
     for f in range(5):
         for x in range(cells_x):
             wide[f, HALO + x, 0:8] = state[f, x]
-        rim[f, 0:8, 0:128] = part(f, 0, 0)
-        rim[f, 0:8, 128:256] = beyond(f, 0)
-        rim[f, 8:16, 0:128] = jnp.where(row < 4, part(f, 0, 1), part(f, 0, -1))
-        rim[f, 8:16, 128:256] = jnp.where(row < 4, beyond(f, 1), beyond(f, -1))
+            at = (f * cells_x + x) * HALO
+            wide[f, HALO + x, 8 : 8 + HALO] = above[at : at + HALO]
+            wide[f, HALO + x, 16 - HALO : 16] = below[at : at + HALO]
+        for slot in range(2 * HALO):
+            plane = slot if slot < HALO else cells_x + slot
+            at = (f * 2 * HALO + slot) * 8
+            wide[f, plane, 0:8] = (before if slot < HALO else after)[at : at + 8]
+        at = lines + f * 6
+        for slot, height in ((1, 1), (2, 2), (3, 2), (4, 1)):
+            plane = slot if slot < HALO else cells_x + slot
+            wide[f, plane, 8 : 8 + height] = above[at : at + height]
+            wide[f, plane, 16 - height : 16] = below[at : at + height]
+            at += height
+        rim[f, 0:8, 0:128] = edge[f * 8 : f * 8 + 8]
+        rim[f, 0:8, 128:256] = beyond(beside_x, f)
+        at = above.shape[0] - 80 + f * 8
+        rim[f, 8:16, 0:128] = jnp.where(row < 4, above[at : at + 8], below[at : at + 8])
+        at += 40
+        rim[f, 8:16, 128:256] = jnp.where(row < 4, above[at : at + 8], below[at : at + 8])
 
 
 def primitive(rho, mx, my, mz, energy):
@@ -358,27 +353,13 @@
             send[peer, base + c * height : base + c * height + height] = folded
 
 
-def flow_sources_body(places, *refs):
-    state, edge = refs[0:2]
-    messages = refs[2 : 2 + len(places)]
-    pair, spread, labels, _ = refs[2 + len(places) : 6 + len(places)]
-    wide, rim, send, derived, lamb_rows, ends = refs[6 + len(places) : 12 + len(places)]
-    spare = refs[12 + len(places) :]
+def flow_sources_body(count, state, edge, *refs):
+    beside_x = refs[:count]
+    got_a, got_b, pair, spread, labels, _ = refs[count : count + 6]
+    wide, rim, send, derived, lamb_rows, ends, above, below = refs[count + 6 :]
     cells_x = state.shape[1]
-    odd = is_odd("fy")
-    beside, k = [], 0
-    while k < len(places):
-        if places[k][0][1] == 0:
-            beside.extend((dx, 0, messages[k]) for dx, _ in places[k])
-            k += 1
-            continue
-        above, below = spare[:2]
-        spare = spare[2:]
-        above[...], below[...] = paired(odd, messages[k][...], messages[k + 1][...])
-        beside.extend((dx, 1, above) for dx, _ in places[k])
-        beside.extend((dx, -1, below) for dx, _ in places[k])
-        k += 2
-    assemble(wide, rim, state, edge, beside, cells_x)
+    above[...], below[...] = paired(is_odd("fy"), got_a[...], got_b[...])
+    assemble(wide, rim, state, edge, beside_x, above, below)
     derive_speeds(wide, derived, HALO - 1, HALO + cells_x + 1)
     inverse = 1.0 / rim[0, 0:8]
     to_ends([rim[1, 0:8] * inverse, rim[2, 0:8] * inverse], 3, 8, 0, cells_x, ends)
@@ -507,7 +488,9 @@
             fields[c] = jnp.where(lane == z, pltpu.roll(piece, move, 1) if move else piece, fields[c])
     for c in range(4):
         state[c] = fields[c]
-    faces_sent(is_odd("fz"), state, message_a, message_b)
+    size = message_a.shape[0]
+    faces_sent(is_odd("fz"), state, message_a, message_b.at[0:size])
+    message_b[size:] = jnp.zeros((message_b.shape[0] - size, 128), F32)
 
 
 def natural_order(state, out, turned, stored):
@@ -552,7 +535,7 @@
     else:
         out, message_a, message_b, before, after = refs
     odd = is_odd("fz")
-    after[...], before[...] = paired(odd, got_a[...], got_b[...])
+    after[...], before[...] = paired(odd, got_a[0:96], got_b[0:96])
     out[0] = partial[0]
     for c in range(3):
         out[1 + c] = partial[1 + c] + (TIME_STEP * mix[1]) * received[c]
@@ -683,14 +666,12 @@
     return pairs
 
 
-def partners(sizes, axis, second, shift_x=0):
+def partners(sizes, axis, second):
     pairs = []
     for index in np.ndindex(*sizes):
         source = list(index)
         step = 1 if (index[axis] % 2 == 0) != second else -1
         source[axis] = (index[axis] + step) % sizes[axis]
-        if shift_x:
-            source[0] = (index[0] + shift_x) % sizes[0]
         pairs.append((int(np.ravel_multi_index(source, sizes)), int(np.ravel_multi_index(index, sizes))))
     return pairs
 
@@ -740,7 +721,7 @@
     turning = [pltpu.VMEM((512, 128), F32), pltpu.VMEM((4, 4 * elements, 128), F32)]
     sound, to_a, to_b = call(
         acoustic_start_body,
-        [held, faces, faces],
+        [held, faces, (3 * faces[0], size)],
         acoustic,
         edge_a,
         scratch=turning,
@@ -748,35 +729,24 @@
     )
     got_a, got_b = traces(to_a, to_b)
 
-    six = 2 * HALO
-    edge_rows = 5 * 8
-    shapes = [
-        (edge_rows, 128),
-        (5 * six * 8 + edge_rows, 128),
-        (5 * cells_x * HALO + edge_rows, 128),
-        (5 * cells_x * HALO + edge_rows, 128),
-        (32 + edge_rows, 128),
-        (32 + edge_rows, 128),
+    edge, along_x = call(
+        pack_next_body,
+        [(40, 128), (5 * 2 * HALO * 8 + 40, 128)],
+        state,
+        flow_a,
+        flow_b,
+        edge_a,
+        edge_b,
+        got_a,
+        last=1,
+    )
+    beside_x = [
+        lax.ppermute(along_x, "fx", shifted((size_x,), (step,))) for step in ((1,) if size_x == 2 else (1, -1))
     ]
-    edge, along_x, y_a, y_b, xy_a, xy_b = call(
-        pack_next_body, shapes, state, flow_a, flow_b, edge_a, edge_b, got_a, last=1
-    )
-    flat = (size_x, size_y)
-    steps = [[(1, 0), (-1, 0)]] if size_x == 2 else [[(1, 0)], [(-1, 0)]]
-    pairs = [(y_a, y_b, [(0, 0)])] + [(xy_a, xy_b, spots) for spots in steps]
-    moved = {}
-    for second in (True, False):
-        for k in reversed(range(len(pairs))):
-            kept, shift = pairs[k][1 if second else 0], pairs[k][2][0][0]
-            moved[k, second] = lax.ppermute(kept, ("fx", "fy"), partners(flat, 1, second, shift))
-    places, messages = [], []
-    for k, (_, _, spots) in enumerate(pairs):
-        for second in (False, True):
-            messages.append(moved[k, second])
-            places.append(tuple((dx, 1) for dx, _ in spots))
-    for spots in steps:
-        messages.append(lax.ppermute(along_x, ("fx", "fy"), shifted(flat, spots[0])))
-        places.append(tuple(spots))
+    y_shape = (5 * cells_x * HALO + 32 + 80, 128)
+    y_a, y_b = call(pack_last_body, [y_shape, y_shape], state, edge, *beside_x, cost=1)
+    y_second = lax.ppermute(y_b, "fy", partners((size_y,), 0, True))
+    y_first = lax.ppermute(y_a, "fy", partners((size_y,), 0, False))
 
     local = (neighbours - device * elements).T
     blocks = block_owner.size
@@ -808,6 +778,7 @@
             (1, size),
         ],
         packed,
+        cost=1,
     )
 
     fold = fold_of(size_y, blocks)
@@ -820,13 +791,14 @@
     def route(send):
         return lax.all_to_all(send, "fy", split_axis=0, concat_axis=0, tiled=True)
 
-    spare = [pltpu.VMEM(shapes[2], F32)] * 2 + [pltpu.VMEM(shapes[4], F32)] * (2 * len(steps))
     start, rim, send = call(
-        functools.partial(flow_sources_body, tuple(places)),
+        functools.partial(flow_sources_body, len(beside_x)),
         [planes(wide), (5, 16, 256), (size_y, 192 // fold + 8, 128)],
         state,
         edge,
-        *messages,
+        *beside_x,
+        y_first,
+        y_second,
         pair,
         spread,
         labels,
@@ -836,8 +808,9 @@
             pltpu.VMEM((3, wide, 16, 128), F32),
             rows_scratch,
             pltpu.VMEM((2, cells_x, 8, 128), F32),
-        ]
-        + spare,
+            pltpu.VMEM(y_shape, F32),
+            pltpu.VMEM(y_shape, F32),
+        ],
     )
     received = route(send)
     second, derived, ends, send = call(
@@ -867,6 +840,7 @@
             speed,
             near,
             scratch=sides,
+            cost=1,
         )[0]
 
     partial = local_part(MIXES[0], sound)

time: 58.1 us -> 60.2 us (1.036)
  waiting for transfers between devices: 11.8 us -> 18.7 us
  starting transfers between devices: 30.6 us -> 26.8 us
  local copies, waits for them, and re-layouts: 1.81 us -> 0.73 us
    all_to_all x2, waiting for transfers between devices: 5.62 us -> 9.3 us  [route(): return lax.all_to_all(send, 'fy', split_axis=0, concat_axis=0, tiled=True)]
    ppermute x5 -> x3, starting transfers between devices: 5.67 us -> 3.12 us  [the longest x1 2.45 us: per_device(): y_second = lax.ppermute(y_b, 'fy', partners((size_y,), 0, True))]
    ppermute x3, starting transfers between devices: 15.6 us -> 14.1 us  [traces(): far_got = lax.ppermute(to_b, names, far_pairs)]
    ppermute x3, waiting for transfers between devices: 3.16 us -> 4.41 us  [traces(): far_got = lax.ppermute(to_b, names, far_pairs)]
    unnamed x20, local copies, waits for them, and re-layouts: 1.81 us -> 0.73 us
    ppermute x1, waiting for transfers between devices: 0.01 us -> 0.83 us  [per_device(): edge_b = lax.ppermute(flow_b, 'fz', partners((size_z,), 0, True))]
    ppermute x5 -> x3, waiting for transfers between devices: 3.03 us -> 3.83 us  [the longest x1 2.32 us: per_device(): y_second = lax.ppermute(y_b, 'fy', partners((size_y,), 0, True))]
    pallas_call x14 -> x15, Pallas kernels: 11.6 us -> 11.6 us  [call(): pl.pallas_call(body, out_shape=outs, in_specs=[whole] * (len(operands) -...]
  transfers between devices with their start and end apart: 15 -> 13, of which waited for: 7 -> 7; matrix products, arithmetic and copies ran while one was open for 0% -> 0% of each run, Pallas kernels for 15% -> 14%
where the time goes in v9:
time: 60.2 us; the launch traced here: 59.8 us
  starting transfers between devices  26.8 us (45%)
  waiting for transfers between devices  18.7 us (31%)
  Pallas kernels  11.6 us (19%)
  other arithmetic  1.01 us (2%)
  between operations  0.91 us (2%)
  local copies, waits for them, and re-layouts  0.73 us (1%)
    ppermute x3, starting transfers between devices, traces(): far_got = lax.ppermute(to_b, names, far_pairs)  14.1 us
    pallas_call x15, Pallas kernels, call(): pl.pallas_call(body, out_shape=outs, in_specs=[whole] * (len(operands) -...  11.6 us
    all_to_all x2, waiting for transfers between devices, route(): return lax.all_to_all(send, 'fy', split_axis=0, concat_axis=0, tiled=True)  9.3 us
    all_to_all x2, starting transfers between devices, route(): return lax.all_to_all(send, 'fy', split_axis=0, concat_axis=0, tiled=True)  7.65 us
    ppermute x3, waiting for transfers between devices, traces(): far_got = lax.ppermute(to_b, names, far_pairs)  4.41 us
    ppermute x1, starting transfers between devices, per_device(): y_second = lax.ppermute(y_b, 'fy', partners((size_y,), 0, True))  2.45 us
    ppermute x1, waiting for transfers between devices, per_device(): y_second = lax.ppermute(y_b, 'fy', partners((size_y,), 0, True))  2.32 us
    ppermute x1, starting transfers between devices, per_device(): edge_b = lax.ppermute(flow_b, 'fz', partners((size_z,), 0, True))  1.64 us
  transfers between devices with their start and end apart: 13, of which 7 were waited for; matrix products, arithmetic and copies ran while one was open for 0% of the time, Pallas kernels for 14%

profile of v9, /device:TPU:2, one launch (start us, length us, event | category | flops | bytes accessed | tf_op | source)
XLA Modules:
  0.0 59.8 jit_solution(6731725594239501703)
XLA Ops:
  0.7 1.0 %broadcast_multiply_fusion = f32[3,8,8,128]{3,2,1,0:T(8,128)S(1)} fusion(f32[3,8,8,128]{3,2,1,0:T(8,128)} %param.11, f32[8,8,128]{2,1,0:T(8,128)} %param.10), kind=kLoop, calls=%fused_computation.1 | loop fusion | flops 24576 | bytes 229376 | tf_op jit(solution)/shard_map/mul | solution.py:704
  1.7 0.1 shard_map.113
  1.9 1.6 %collective-permute-start.1 = (f32[24,128]{1,0:T(8,128)S(1)}, f32[24,128]{1,0:T(8,128)S(1)}, u32[]{:S(2)}, u32[]{:S(2)}) collective-permute-start(f32[24,128]{1,0:T(8,128)S(1)} %get-tuple-element.35.sent_b), channel_id=1, source_target_pairs={{3,0},{2,1},{1,2},{0,3},{7,4},{6,5},{5,6},{4,7},{11,8},{10,9},{9,1... | collective-permute-start | bytes 36872 | tf_op jit(solution)/shard_map/ppermute | solution.py:708
  3.5 0.6 shard_map.114
  4.1 0.1 collective-permute-start.2
  4.3 0.8 %collective-permute-done.1.got_b = f32[24,128]{1,0:T(8,128)S(1)} collective-permute-done((f32[24,128]{1,0:T(8,128)S(1)}, f32[24,128]{1,0:T(8,128)S(1)}, u32[]{:S(2)}, u32[]{:S(2)}) %collective-permute-start.1) | collective-permute-done | bytes 12320 | tf_op jit(solution)/shard_map/ppermute | solution.py:708
  5.1 0.3 collective-permute-done.2._.got_a
  5.4 0.1 shard_map.115
  5.6 0.6 %collective-permute-start.3 = (f32[280,128]{1,0:T(8,128)S(1)}, f32[280,128]{1,0:T(8,128)S(1)}, u32[]{:S(2)}, u32[]{:S(2)}) collective-permute-start(f32[280,128]{1,0:T(8,128)S(1)} %get-tuple-element.38), channel_id=1, source_target_pairs={{16,0},{0,16},{17,1},{1,17},{18,2},{2,18},{19,3},{3,19},{20,4},{4,... | collective-permute-start | bytes 430088 | tf_op jit(solution)/shard_map/ppermute | solution.py:744
  6.2 6.8 %collective-permute-start.6 = (f32[288,128]{1,0:T(8,128)S(1)}, f32[288,128]{1,0:T(8,128)S(1)}, u32[]{:S(2)}, u32[]{:S(2)}) collective-permute-start(f32[288,128]{1,0:T(8,128)S(1)} %get-tuple-element.44), channel_id=1, source_target_pairs={{1,2},{2,1},{3,4},{4,3},{5,6},{6,5},{7,8},{8,7},{9,10},{10,9},{11,... | collective-permute-start | bytes 442376 | tf_op jit(solution)/shard_map/ppermute | solution.py:714
  13.2 2.4 %collective-permute-start.5 = (f32[232,128]{1,0:T(8,128)S(1)}, f32[232,128]{1,0:T(8,128)S(1)}, u32[]{:S(2)}, u32[]{:S(2)}) collective-permute-start(f32[232,128]{1,0:T(8,128)S(1)} %get-tuple-element.40), channel_id=1, source_target_pairs={{12,0},{8,4},{4,8},{0,12},{13,1},{9,5},{5,9},{1,13},{14,2},{10,6},... | collective-permute-start | bytes 356360 | tf_op jit(solution)/shard_map/ppermute | solution.py:748
  15.7 0.6 %copy-done.7 = f32[16]{0:T(128)S(1)} copy-done((f32[16]{0:T(128)S(1)}, f32[16]{0:T(128)}, u32[]{:S(2)}) %copy-start.7) | copy-done | bytes 88
  16.3 1.0 %shard_map.117 = (bf16[5,128,128]{2,1,0:T(8,128)(2,1)S(1)}, bf16[5,128,128]{2,1,0:T(8,128)(2,1)S(1)}, f32[128,64]{1,0:T(8,128)S(1)}, f32[128,128]{1,0:T(8,128)S(...) custom-call(f32[32,16]{1,0:T(8,128)S(1)} %pad_add_fusion.1.packed), custom_call_target="tpu_custom_call" | custom-call | flops 1 | bytes 1 | tf_op jit(solution)/shard_map/pallas_call | solution.py:52
  17.3 1.5 %collective-permute-done.4.refs_1_ = f32[232,128]{1,0:T(8,128)S(1)} collective-permute-done((f32[232,128]{1,0:T(8,128)S(1)}, f32[232,128]{1,0:T(8,128)S(1)}, u32[]{:S(2)}, u32[]{:S(2)}) %collective-permute-start.4) | collective-permute-done | bytes 118816 | tf_op jit(solution)/shard_map/ppermute | solution.py:749
  18.8 2.3 %collective-permute-done.5.refs_2_ = f32[232,128]{1,0:T(8,128)S(1)} collective-permute-done((f32[232,128]{1,0:T(8,128)S(1)}, f32[232,128]{1,0:T(8,128)S(1)}, u32[]{:S(2)}, u32[]{:S(2)}) %collective-permute-start.5) | collective-permute-done | bytes 118816 | tf_op jit(solution)/shard_map/ppermute | solution.py:748
  21.1 1.3 %shard_map.118 = (f32[5,14,16,128]{3,2,1,0:T(8,128)S(1)}, f32[5,16,256]{2,1,0:T(8,128)S(1)}, f32[4,104,128]{2,1,0:T(8,128)}) custom-call(f32[5,8,8,128]{3,2,1,0:T(8,128)S(1)} %pad_add_fusion.state, f32[40,128]{1,0:T(8,128)S(1)} %get-tuple-element.37.edge, f32[280,128]{1,0:T(8,128)S(1)} %collective-permute-done.3.refs_0_, ...), custom_call_target="tpu_custom_call" | custom-call | tf_op jit(solution)/shard_map/pallas_call | solution.py:52
  22.5 4.2 %all-to-all-start = ((f32[4,104,128]{2,1,0:T(8,128)}), f32[4,104,128]{2,1,0:T(8,128)S(1)}, u32[]{:S(2)}, u32[]{:S(2)}) async-start(f32[4,104,128]{2,1,0:T(8,128)} %get-tuple-element.56), calls=%async_computation | async-start | bytes 425984 | tf_op jit(solution)/shard_map/all_to_all | solution.py:792
  26.6 3.9 %shard_map.119 = (f32[5,10,16,128]{3,2,1,0:T(8,128)S(1)}, f32[5,14,16,128]{3,2,1,0:T(8,128)S(1)}, f32[5,8,8,128]{3,2,1,0:T(8,128)S(1)}, f32[4,200,128]{2,1,0:T(8,128)}) custom-call(f32[5,14,16,128]{3,2,1,0:T(8,128)S(1)} %get-tuple-element.45.wide, f32[5,16,256]{2,1,0:T(8,128)S(1)} %get-tuple-element.46.rim, f32[64,64]{1,0:T(8,128)S(1)} %get-tuple-element.41.refs_3_.pair, ...), custom_call_target="tpu_custom_call" | custom-call | tf_op jit(solution)/shard_map/pallas_call | solution.py:52
  30.5 4.1 %all-to-all-done.received = f32[4,104,128]{2,1,0:T(8,128)S(1)} async-done(((f32[4,104,128]{2,1,0:T(8,128)}), f32[4,104,128]{2,1,0:T(8,128)S(1)}, u32[]{:S(2)}, u32[]{:S(2)}) %all-to-all-start) | async-done | bytes 213024 | tf_op jit(solution)/shard_map/all_to_all | solution.py:792
  34.6 3.5 %all-to-all-start.1 = ((f32[4,200,128]{2,1,0:T(8,128)}), f32[4,200,128]{2,1,0:T(8,128)S(1)}, u32[]{:S(2)}, u32[]{:S(2)}) async-start(f32[4,200,128]{2,1,0:T(8,128)} %get-tuple-element.57.refs_0_), calls=%async_computation.1 | async-start | bytes 819200 | tf_op jit(solution)/shard_map/all_to_all | solution.py:792
  38.1 0.3 shard_map.121.partial
  38.5 0.5 shard_map.122
  39.1 4.1 %collective-permute-start.8 = (f32[96,128]{1,0:T(8,128)S(1)}, f32[96,128]{1,0:T(8,128)S(1)}, u32[]{:S(2)}, u32[]{:S(2)}) collective-permute-start(f32[96,128]{1,0:T(8,128)S(1)} %get-tuple-element.60), channel_id=1, source_target_pairs={{1,2},{2,1},{3,4},{4,3},{5,6},{6,5},{7,8},{8,7},{9,10},{10,9},{11,... | collective-permute-start | bytes 147464 | tf_op jit(solution)/shard_map/ppermute | solution.py:714
  43.2 0.3 shard_map.123.partial
  43.6 5.2 %all-to-all-done.1.received = f32[4,200,128]{2,1,0:T(8,128)S(1)} async-done(((f32[4,200,128]{2,1,0:T(8,128)}), f32[4,200,128]{2,1,0:T(8,128)S(1)}, u32[]{:S(2)}, u32[]{:S(2)}) %all-to-all-start.1) | async-done | bytes 409632 | tf_op jit(solution)/shard_map/all_to_all | solution.py:792
  48.7 0.4 shard_map.124
  49.1 0.3 shard_map.125
  49.5 3.2 %collective-permute-start.10 = (f32[96,128]{1,0:T(8,128)S(1)}, f32[96,128]{1,0:T(8,128)S(1)}, u32[]{:S(2)}, u32[]{:S(2)}) collective-permute-start(f32[96,128]{1,0:T(8,128)S(1)} %get-tuple-element.64), channel_id=1, source_target_pairs={{1,2},{2,1},{3,4},{4,3},{5,6},{6,5},{7,8},{8,7},{9,10},{10,9},{11,... | collective-permute-start | bytes 147464 | tf_op jit(solution)/shard_map/ppermute | solution.py:714
  52.7 1.0 %shard_map.120 = f32[5,8,8,128]{3,2,1,0:T(8,128)} custom-call(f32[5,10,16,128]{3,2,1,0:T(8,128)S(1)} %get-tuple-element.47.second, f32[5,14,16,128]{3,2,1,0:T(8,128)S(1)} %get-tuple-element.48.derived, f32[5,8,8,128]{3,2,1,0:T(8,128)S(1)} %get-tuple-element.49.ends, f32[5,14,16,128]{3,2,1,0:T(8,128)S(1)} %get-tuple-element.45.wide), custom_call_target="tpu_custom_call" | custom-call | tf_op jit(solution)/shard_map/pallas_call | solution.py:52
  53.8 0.3 shard_map.126.partial
  54.1 4.4 %collective-permute-done.10.got_b = f32[96,128]{1,0:T(8,128)S(1)} collective-permute-done((f32[96,128]{1,0:T(8,128)S(1)}, f32[96,128]{1,0:T(8,128)S(1)}, u32[]{:S(2)}, u32[]{:S(2)}) %collective-permute-start.10) | collective-permute-done | bytes 49184 | tf_op jit(solution)/shard_map/ppermute | solution.py:714
  58.5 1.3 %shard_map.127 = f32[16,4,512]{2,1,0:T(4,128)} custom-call(f32[4,64,128]{2,1,0:T(8,128)S(1)} %shard_map.126.partial, f32[96,128]{1,0:T(8,128)S(1)} %collective-permute-done.9.got_a, f32[96,128]{1,0:T(8,128)S(1)} %collective-permute-done.10.got_b, bf16[5,128,128]{2,1,0:T(8,128)(2,1)S(1)} %get-tuple-element.55.sides_far, ...), custom_call_target="tpu_custom_call" | custom-call | tf_op jit(solution)/shard_map/pallas_call | solution.py:52
  (36 shorter events, 0.5 us)
Async XLA Ops:
  0.6 1.0 %copy-start.2 = (f32[8,8,128]{2,1,0:T(8,128)S(1)}, f32[8,8,128]{2,1,0:T(8,128)}, u32[]{:S(2)}) copy-start(f32[8,8,128]{2,1,0:T(8,128)} %param.10) | copy-start | bytes 98308
  0.6 1.0 %copy-start.1 = (f32[3,8,8,128]{3,2,1,0:T(8,128)S(1)}, f32[3,8,8,128]{3,2,1,0:T(8,128)}, u32[]{:S(2)}) copy-start(f32[3,8,8,128]{3,2,1,0:T(8,128)} %param.11) | copy-start | bytes 294916
  0.6 1.0 %copy-start.3 = (f32[8,8,128]{2,1,0:T(8,128)S(1)}, f32[8,8,128]{2,1,0:T(8,128)}, u32[]{:S(2)}) copy-start(f32[8,8,128]{2,1,0:T(8,128)} %param.12) | copy-start | bytes 98308
  1.7 1.8 %copy-start = (f32[16,4,512]{2,1,0:T(4,128)S(1)}, f32[16,4,512]{2,1,0:T(4,128)}, u32[]{:S(2)}) copy-start(f32[16,4,512]{2,1,0:T(4,128)} %given.1) | copy-start | bytes 393220
  1.8 1.7 %collective-permute-start = (f32[24,128]{1,0:T(8,128)S(1)}, f32[24,128]{1,0:T(8,128)S(1)}, u32[]{:S(2)}, u32[]{:S(2)}) collective-permute-start(f32[24,128]{1,0:T(8,128)S(1)} %get-tuple-element.34.sent_a), channel_id=1, source_target_pairs={{1,0},{0,1},{3,2},{2,3},{5,4},{4,5},{7,6},{6,7},{9,8},{8,9},{11,10... | collective-permute-start | bytes 36872 | tf_op jit(solution)/shard_map/ppermute | solution.py:707
  1.9 3.2 %collective-permute-start.1 = (f32[24,128]{1,0:T(8,128)S(1)}, f32[24,128]{1,0:T(8,128)S(1)}, u32[]{:S(2)}, u32[]{:S(2)}) collective-permute-start(f32[24,128]{1,0:T(8,128)S(1)} %get-tuple-element.35.sent_b), channel_id=1, source_target_pairs={{3,0},{2,1},{1,2},{0,3},{7,4},{6,5},{5,6},{4,7},{11,8},{10,9},{9,1... | collective-permute-start | bytes 36872 | tf_op jit(solution)/shard_map/ppermute | solution.py:708
  3.5 0.7 %copy-start.4 = (s32[16,6]{0,1:T(8,128)S(1)}, s32[16,6]{0,1:T(8,128)}, u32[]{:S(2)}) copy-start(s32[16,6]{0,1:T(8,128)} %param.17) | copy-start | bytes 1156
  4.1 1.3 %collective-permute-start.2 = (f32[96,128]{1,0:T(8,128)S(1)}, f32[96,128]{1,0:T(8,128)S(1)}, u32[]{:S(2)}, u32[]{:S(2)}) collective-permute-start(f32[96,128]{1,0:T(8,128)S(1)} %get-tuple-element.36), channel_id=1, source_target_pairs={{1,0},{0,1},{3,2},{2,3},{5,4},{4,5},{7,6},{6,7},{9,8},{8,9},{11,10... | collective-permute-start | bytes 147464 | tf_op jit(solution)/shard_map/ppermute | solution.py:715
  5.5 0.7 %copy-start.8 = (s32[1,1,1,16]{3,2,1,0:T(1,128)S(1)}, s32[1,1,1,16]{3,2,1,0:T(1,128)}, u32[]{:S(2)}) copy-start(s32[1,1,1,16]{3,2,1,0:T(1,128)} %param.19) | copy-start | bytes 196
  5.6 7.4 %collective-permute-start.3 = (f32[280,128]{1,0:T(8,128)S(1)}, f32[280,128]{1,0:T(8,128)S(1)}, u32[]{:S(2)}, u32[]{:S(2)}) collective-permute-start(f32[280,128]{1,0:T(8,128)S(1)} %get-tuple-element.38), channel_id=1, source_target_pairs={{16,0},{0,16},{17,1},{1,17},{18,2},{2,18},{19,3},{3,19},{20,4},{4,... | collective-permute-start | bytes 430088 | tf_op jit(solution)/shard_map/ppermute | solution.py:744
  6.2 11.1 %collective-permute-start.6 = (f32[288,128]{1,0:T(8,128)S(1)}, f32[288,128]{1,0:T(8,128)S(1)}, u32[]{:S(2)}, u32[]{:S(2)}) collective-permute-start(f32[288,128]{1,0:T(8,128)S(1)} %get-tuple-element.44), channel_id=1, source_target_pairs={{1,2},{2,1},{3,4},{4,3},{5,6},{6,5},{7,8},{8,7},{9,10},{10,9},{11,... | collective-permute-start | bytes 442376 | tf_op jit(solution)/shard_map/ppermute | solution.py:714
  13.0 2.6 %copy-start.9 = (s32[1,1,1,16,1]{3,4,2,1,0:T(1,128)S(1)}, s32[1,1,1,16,1]{3,4,2,1,0:T(1,128)}, u32[]{:S(2)}) copy-start(s32[1,1,1,16,1]{3,4,2,1,0:T(1,128)} %param.18) | copy-start | bytes 196
  13.0 2.6 %copy-start.6 = (f32[8,8]{1,0:T(8,128)S(1)}, f32[8,8]{1,0:T(8,128)}, u32[]{:S(2)}) copy-start(f32[8,8]{1,0:T(8,128)} %param.15) | copy-start | bytes 772
  13.1 2.6 %copy-start.5 = (f32[8,8]{1,0:T(8,128)S(1)}, f32[8,8]{1,0:T(8,128)}, u32[]{:S(2)}) copy-start(f32[8,8]{1,0:T(8,128)} %param.16) | copy-start | bytes 772
  13.1 5.7 %collective-permute-start.4 = (f32[232,128]{1,0:T(8,128)S(1)}, f32[232,128]{1,0:T(8,128)S(1)}, u32[]{:S(2)}, u32[]{:S(2)}) collective-permute-start(f32[232,128]{1,0:T(8,128)S(1)} %get-tuple-element.39), channel_id=1, source_target_pairs={{4,0},{0,4},{12,8},{8,12},{5,1},{1,5},{13,9},{9,13},{6,2},{2,6},{1... | collective-permute-start | bytes 356360 | tf_op jit(solution)/shard_map/ppermute | solution.py:749
  13.2 8.0 %collective-permute-start.5 = (f32[232,128]{1,0:T(8,128)S(1)}, f32[232,128]{1,0:T(8,128)S(1)}, u32[]{:S(2)}, u32[]{:S(2)}) collective-permute-start(f32[232,128]{1,0:T(8,128)S(1)} %get-tuple-element.40), channel_id=1, source_target_pairs={{12,0},{8,4},{4,8},{0,12},{13,1},{9,5},{5,9},{1,13},{14,2},{10,6},... | collective-permute-start | bytes 356360 | tf_op jit(solution)/shard_map/ppermute | solution.py:748
  15.6 0.7 %copy-start.7 = (f32[16]{0:T(128)S(1)}, f32[16]{0:T(128)}, u32[]{:S(2)}) copy-start(f32[16]{0:T(128)} %param.14) | copy-start | bytes 196
  22.5 12.2 %all-to-all-start = ((f32[4,104,128]{2,1,0:T(8,128)}), f32[4,104,128]{2,1,0:T(8,128)S(1)}, u32[]{:S(2)}, u32[]{:S(2)}) async-start(f32[4,104,128]{2,1,0:T(8,128)} %get-tuple-element.56), calls=%async_computation | async-start | bytes 425984 | tf_op jit(solution)/shard_map/all_to_all | solution.py:792
  34.6 14.1 %all-to-all-start.1 = ((f32[4,200,128]{2,1,0:T(8,128)}), f32[4,200,128]{2,1,0:T(8,128)S(1)}, u32[]{:S(2)}, u32[]{:S(2)}) async-start(f32[4,200,128]{2,1,0:T(8,128)} %get-tuple-element.57.refs_0_), calls=%async_computation.1 | async-start | bytes 819200 | tf_op jit(solution)/shard_map/all_to_all | solution.py:792
  39.0 10.1 %collective-permute-start.7 = (f32[96,128]{1,0:T(8,128)S(1)}, f32[96,128]{1,0:T(8,128)S(1)}, u32[]{:S(2)}, u32[]{:S(2)}) collective-permute-start(f32[96,128]{1,0:T(8,128)S(1)} %get-tuple-element.59), channel_id=1, source_target_pairs={{1,0},{0,1},{3,2},{2,3},{5,4},{4,5},{7,6},{6,7},{9,8},{8,9},{11,10... | collective-permute-start | bytes 147464 | tf_op jit(solution)/shard_map/ppermute | solution.py:715
  39.1 10.1 %collective-permute-start.8 = (f32[96,128]{1,0:T(8,128)S(1)}, f32[96,128]{1,0:T(8,128)S(1)}, u32[]{:S(2)}, u32[]{:S(2)}) collective-permute-start(f32[96,128]{1,0:T(8,128)S(1)} %get-tuple-element.60), channel_id=1, source_target_pairs={{1,2},{2,1},{3,4},{4,3},{5,6},{6,5},{7,8},{8,7},{9,10},{10,9},{11,... | collective-permute-start | bytes 147464 | tf_op jit(solution)/shard_map/ppermute | solution.py:714
  49.5 9.0 %collective-permute-start.10 = (f32[96,128]{1,0:T(8,128)S(1)}, f32[96,128]{1,0:T(8,128)S(1)}, u32[]{:S(2)}, u32[]{:S(2)}) collective-permute-start(f32[96,128]{1,0:T(8,128)S(1)} %get-tuple-element.64), channel_id=1, source_target_pairs={{1,2},{2,1},{3,4},{4,3},{5,6},{6,5},{7,8},{8,7},{9,10},{10,9},{11,... | collective-permute-start | bytes 147464 | tf_op jit(solution)/shard_map/ppermute | solution.py:714
  52.7 5.8 %collective-permute-start.9 = (f32[96,128]{1,0:T(8,128)S(1)}, f32[96,128]{1,0:T(8,128)S(1)}, u32[]{:S(2)}, u32[]{:S(2)}) collective-permute-start(f32[96,128]{1,0:T(8,128)S(1)} %get-tuple-element.63), channel_id=1, source_target_pairs={{1,0},{0,1},{3,2},{2,3},{5,4},{4,5},{7,6},{6,7},{9,8},{8,9},{11,10... | collective-permute-start | bytes 147464 | tf_op jit(solution)/shard_map/ppermute | solution.py:715

commit v10 on v9

--- a/solution.py
+++ b/solution.py
@@ -156,17 +156,14 @@
             source = (f * 2 * HALO + slot) * 8
             put(at, (before if slot < HALO else after)[source : source + 8], height)
             at += height
-        for message in (y_a, y_b):
-            at = message.shape[0] - 80 + f * 8
-            message[at : at + 8] = edge[f * 8 : f * 8 + 8]
-            message[at + 40 : at + 48] = beyond(beside_x, f)
+        put(lines + 30 + f * 2, edge[f * 8 : f * 8 + 8], 2)
+        put(lines + 40 + f, beyond(beside_x, f), 1)
 
 
 def assemble(wide, rim, state, edge, beside_x, above, below):
     cells_x = state.shape[1]
     after, before = sides_of(beside_x)
     lines = 5 * cells_x * HALO
-    row = lax.broadcasted_iota(jnp.int32, (8, 128), 0)
     for f in range(5):
         for x in range(cells_x):
             wide[f, HALO + x, 0:8] = state[f, x]
@@ -185,10 +182,12 @@
             at += height
         rim[f, 0:8, 0:128] = edge[f * 8 : f * 8 + 8]
         rim[f, 0:8, 128:256] = beyond(beside_x, f)
-        at = above.shape[0] - 80 + f * 8
-        rim[f, 8:16, 0:128] = jnp.where(row < 4, above[at : at + 8], below[at : at + 8])
-        at += 40
-        rim[f, 8:16, 128:256] = jnp.where(row < 4, above[at : at + 8], below[at : at + 8])
+        at = lines + 30 + f * 2
+        rim[f, 8:10, 0:128] = above[at : at + 2]
+        rim[f, 14:16, 0:128] = below[at : at + 2]
+        at = lines + 40 + f
+        rim[f, 8:9, 128:256] = above[at : at + 1]
+        rim[f, 15:16, 128:256] = below[at : at + 1]
 
 
 def primitive(rho, mx, my, mz, energy):
@@ -423,8 +422,10 @@
 
 
 def faces_sent(odd, state, message_a, message_b):
+    size = message_a.shape[0]
     faces_out(state, message_b, message_a)
-    message_a[...], message_b[...] = paired(odd, message_a[...], message_b[...])
+    message_a[...], message_b[0:size] = paired(odd, message_a[...], message_b[0:size])
+    message_b[size:] = jnp.zeros((message_b.shape[0] - size, 128), F32)
 
 
 def lift(total, before, after, sides, factor):
@@ -488,9 +489,7 @@
             fields[c] = jnp.where(lane == z, pltpu.roll(piece, move, 1) if move else piece, fields[c])
     for c in range(4):
         state[c] = fields[c]
-    size = message_a.shape[0]
-    faces_sent(is_odd("fz"), state, message_a, message_b.at[0:size])
-    message_b[size:] = jnp.zeros((message_b.shape[0] - size, 128), F32)
+    faces_sent(is_odd("fz"), state, message_a, message_b)
 
 
 def natural_order(state, out, turned, stored):
@@ -743,7 +742,7 @@
     beside_x = [
         lax.ppermute(along_x, "fx", shifted((size_x,), (step,))) for step in ((1,) if size_x == 2 else (1, -1))
     ]
-    y_shape = (5 * cells_x * HALO + 32 + 80, 128)
+    y_shape = (5 * cells_x * HALO + 48, 128)
     y_a, y_b = call(pack_last_body, [y_shape, y_shape], state, edge, *beside_x, cost=1)
     y_second = lax.ppermute(y_b, "fy", partners((size_y,), 0, True))
     y_first = lax.ppermute(y_a, "fy", partners((size_y,), 0, False))
@@ -846,7 +845,7 @@
     partial = local_part(MIXES[0], sound)
     sound_one, to_a, to_b = call(
         functools.partial(acoustic_far_body, MIXES[0], "first"),
-        [held, faces, faces],
+        [held, faces, (faces[0] + 32, size)],
         partial,
         got_a,
         got_b,
@@ -862,7 +861,7 @@
     partial = local_part(MIXES[1], sound_one)
     sound_two, to_a, to_b = call(
         functools.partial(acoustic_far_body, MIXES[1], "second"),
-        [held, faces, faces],
+        [held, faces, (faces[0] + 32, size)],
         partial,
         got_a,
         got_b,

time: 60.2 us -> 59.3 us (0.985)
  waiting for transfers between devices: 18.7 us -> 16.6 us
  local copies, waits for them, and re-layouts: 0.73 us -> 1.81 us
    ppermute x1, waiting for transfers between devices: 0.01 us -> 4.51 us  [per_device(): lax.ppermute(along_x, 'fx', shifted((size_x,), (step,)))]
    all_to_all x2, waiting for transfers between devices: 9.3 us -> 5.43 us  [route(): return lax.all_to_all(send, 'fy', split_axis=0, concat_axis=0, tiled=True)]
    ppermute x3, starting transfers between devices: 14.1 us -> 15.5 us  [traces(): far_got = lax.ppermute(to_b, names, far_pairs)]
    ppermute x3, waiting for transfers between devices: 4.41 us -> 3.2 us  [traces(): far_got = lax.ppermute(to_b, names, far_pairs)]
    ppermute x1, waiting for transfers between devices: 2.32 us -> 1.16 us  [per_device(): y_second = lax.ppermute(y_b, 'fy', partners((size_y,), 0, True))]
    unnamed x20, local copies, waits for them, and re-layouts: 0.73 us -> 1.81 us
    ppermute x1, waiting for transfers between devices: 0.83 us -> 0.01 us  [per_device(): edge_b = lax.ppermute(flow_b, 'fz', partners((size_z,), 0, True))]
    all_to_all x2, starting transfers between devices: 7.65 us -> 6.84 us  [route(): return lax.all_to_all(send, 'fy', split_axis=0, concat_axis=0, tiled=True)]
where the time goes in v10:
time: 59.3 us; the launch traced here: 58.9 us
  starting transfers between devices  27 us (46%)
  waiting for transfers between devices  16.6 us (28%)
  Pallas kernels  11.6 us (20%)
  local copies, waits for them, and re-layouts  1.81 us (3%)
  other arithmetic  1.01 us (2%)
  between operations  0.92 us (2%)
    ppermute x3, starting transfers between devices, traces(): far_got = lax.ppermute(to_b, names, far_pairs)  15.5 us
    pallas_call x15, Pallas kernels, call(): pl.pallas_call(body, out_shape=outs, in_specs=[whole] * (len(operands) -...  11.6 us
    all_to_all x2, starting transfers between devices, route(): return lax.all_to_all(send, 'fy', split_axis=0, concat_axis=0, tiled=True)  6.84 us
    all_to_all x2, waiting for transfers between devices, route(): return lax.all_to_all(send, 'fy', split_axis=0, concat_axis=0, tiled=True)  5.43 us
    ppermute x1, waiting for transfers between devices, per_device(): lax.ppermute(along_x, 'fx', shifted((size_x,), (step,)))  4.51 us
    ppermute x3, waiting for transfers between devices, traces(): far_got = lax.ppermute(to_b, names, far_pairs)  3.2 us
    ppermute x1, waiting for transfers between devices, per_device(): y_first = lax.ppermute(y_a, 'fy', partners((size_y,), 0, False))  2.24 us
    ppermute x1, starting transfers between devices, per_device(): y_second = lax.ppermute(y_b, 'fy', partners((size_y,), 0, True))  2.03 us
  transfers between devices with their start and end apart: 13, of which 7 were waited for; matrix products, arithmetic and copies ran while one was open for 0% of the time, Pallas kernels for 14%

profile of v10, /device:TPU:2, one launch (start us, length us, event | category | flops | bytes accessed | tf_op | source)
XLA Modules:
  0.0 58.9 jit_solution(1825215328215613092)
XLA Ops:
  0.7 1.0 %broadcast_multiply_fusion = f32[3,8,8,128]{3,2,1,0:T(8,128)S(1)} fusion(f32[3,8,8,128]{3,2,1,0:T(8,128)} %param.11, f32[8,8,128]{2,1,0:T(8,128)} %param.10), kind=kLoop, calls=%fused_computation.1 | loop fusion | flops 24576 | bytes 229376 | tf_op jit(solution)/shard_map/mul | solution.py:703
  1.9 1.6 %collective-permute-start.1 = (f32[24,128]{1,0:T(8,128)S(1)}, f32[24,128]{1,0:T(8,128)S(1)}, u32[]{:S(2)}, u32[]{:S(2)}) collective-permute-start(f32[24,128]{1,0:T(8,128)S(1)} %get-tuple-element.35.sent_b), channel_id=1, source_target_pairs={{3,0},{2,1},{1,2},{0,3},{7,4},{6,5},{5,6},{4,7},{11,8},{10,9},{9,1... | collective-permute-start | bytes 36872 | tf_op jit(solution)/shard_map/ppermute | solution.py:707
  3.5 0.7 %copy-done.4 = s32[16,6]{0,1:T(8,128)S(1)} copy-done((s32[16,6]{0,1:T(8,128)S(1)}, s32[16,6]{0,1:T(8,128)}, u32[]{:S(2)}) %copy-start.4) | copy-done | bytes 408
  4.2 0.6 shard_map.114
  5.0 0.5 copy-done.8
  5.5 5.1 %collective-permute-start.6 = (f32[288,128]{1,0:T(8,128)S(1)}, f32[288,128]{1,0:T(8,128)S(1)}, u32[]{:S(2)}, u32[]{:S(2)}) collective-permute-start(f32[288,128]{1,0:T(8,128)S(1)} %get-tuple-element.44), channel_id=1, source_target_pairs={{1,2},{2,1},{3,4},{4,3},{5,6},{6,5},{7,8},{8,7},{9,10},{10,9},{11,... | collective-permute-start | bytes 442376 | tf_op jit(solution)/shard_map/ppermute | solution.py:713
  10.6 0.1 shard_map.115
  10.8 0.6 copy-done.9
  11.4 4.5 %collective-permute-done.3.refs_0_ = f32[280,128]{1,0:T(8,128)S(1)} collective-permute-done((f32[280,128]{1,0:T(8,128)S(1)}, f32[280,128]{1,0:T(8,128)S(1)}, u32[]{:S(2)}, u32[]{:S(2)}) %collective-permute-start.3) | collective-permute-done | bytes 143392 | tf_op jit(solution)/shard_map/ppermute | solution.py:743
  16.1 2.0 %collective-permute-start.5 = (f32[168,128]{1,0:T(8,128)S(1)}, f32[168,128]{1,0:T(8,128)S(1)}, u32[]{:S(2)}, u32[]{:S(2)}) collective-permute-start(f32[168,128]{1,0:T(8,128)S(1)} %get-tuple-element.40), channel_id=1, source_target_pairs={{12,0},{8,4},{4,8},{0,12},{13,1},{9,5},{5,9},{1,13},{14,2},{10,6},... | collective-permute-start | bytes 258056 | tf_op jit(solution)/shard_map/ppermute | solution.py:747
  18.1 1.0 %shard_map.117 = (bf16[5,128,128]{2,1,0:T(8,128)(2,1)S(1)}, bf16[5,128,128]{2,1,0:T(8,128)(2,1)S(1)}, f32[128,64]{1,0:T(8,128)S(1)}, f32[128,128]{1,0:T(8,128)S(...) custom-call(f32[32,16]{1,0:T(8,128)S(1)} %pad_add_fusion.1.packed), custom_call_target="tpu_custom_call" | custom-call | flops 1 | bytes 1 | tf_op jit(solution)/shard_map/pallas_call | solution.py:52
  19.1 2.2 %collective-permute-done.4.refs_1_ = f32[168,128]{1,0:T(8,128)S(1)} collective-permute-done((f32[168,128]{1,0:T(8,128)S(1)}, f32[168,128]{1,0:T(8,128)S(1)}, u32[]{:S(2)}, u32[]{:S(2)}) %collective-permute-start.4) | collective-permute-done | bytes 86048 | tf_op jit(solution)/shard_map/ppermute | solution.py:748
  21.4 1.2 %collective-permute-done.5.refs_2_ = f32[168,128]{1,0:T(8,128)S(1)} collective-permute-done((f32[168,128]{1,0:T(8,128)S(1)}, f32[168,128]{1,0:T(8,128)S(1)}, u32[]{:S(2)}, u32[]{:S(2)}) %collective-permute-start.5) | collective-permute-done | bytes 86048 | tf_op jit(solution)/shard_map/ppermute | solution.py:747
  22.5 1.3 %shard_map.118 = (f32[5,14,16,128]{3,2,1,0:T(8,128)S(1)}, f32[5,16,256]{2,1,0:T(8,128)S(1)}, f32[4,104,128]{2,1,0:T(8,128)}) custom-call(f32[5,8,8,128]{3,2,1,0:T(8,128)S(1)} %pad_add_fusion.state, f32[40,128]{1,0:T(8,128)S(1)} %get-tuple-element.37.edge, f32[280,128]{1,0:T(8,128)S(1)} %collective-permute-done.3.refs_0_, ...), custom_call_target="tpu_custom_call" | custom-call | tf_op jit(solution)/shard_map/pallas_call | solution.py:52
  23.8 3.4 %all-to-all-start = ((f32[4,104,128]{2,1,0:T(8,128)}), f32[4,104,128]{2,1,0:T(8,128)S(1)}, u32[]{:S(2)}, u32[]{:S(2)}) async-start(f32[4,104,128]{2,1,0:T(8,128)} %get-tuple-element.56), calls=%async_computation | async-start | bytes 425984 | tf_op jit(solution)/shard_map/all_to_all | solution.py:791
  27.2 3.9 %shard_map.119 = (f32[5,10,16,128]{3,2,1,0:T(8,128)S(1)}, f32[5,14,16,128]{3,2,1,0:T(8,128)S(1)}, f32[5,8,8,128]{3,2,1,0:T(8,128)S(1)}, f32[4,200,128]{2,1,0:T(8,128)}) custom-call(f32[5,14,16,128]{3,2,1,0:T(8,128)S(1)} %get-tuple-element.45.wide, f32[5,16,256]{2,1,0:T(8,128)S(1)} %get-tuple-element.46.rim, f32[64,64]{1,0:T(8,128)S(1)} %get-tuple-element.41.refs_3_.pair, ...), custom_call_target="tpu_custom_call" | custom-call | tf_op jit(solution)/shard_map/pallas_call | solution.py:52
  31.1 2.7 %all-to-all-done.received = f32[4,104,128]{2,1,0:T(8,128)S(1)} async-done(((f32[4,104,128]{2,1,0:T(8,128)}), f32[4,104,128]{2,1,0:T(8,128)S(1)}, u32[]{:S(2)}, u32[]{:S(2)}) %all-to-all-start) | async-done | bytes 213024 | tf_op jit(solution)/shard_map/all_to_all | solution.py:791
  33.8 3.5 %all-to-all-start.1 = ((f32[4,200,128]{2,1,0:T(8,128)}), f32[4,200,128]{2,1,0:T(8,128)S(1)}, u32[]{:S(2)}, u32[]{:S(2)}) async-start(f32[4,200,128]{2,1,0:T(8,128)} %get-tuple-element.57.refs_0_), calls=%async_computation.1 | async-start | bytes 819200 | tf_op jit(solution)/shard_map/all_to_all | solution.py:791
  37.2 0.3 shard_map.121.partial
  37.6 0.5 shard_map.122
  38.1 5.6 %collective-permute-start.8 = (f32[128,128]{1,0:T(8,128)S(1)}, f32[128,128]{1,0:T(8,128)S(1)}, u32[]{:S(2)}, u32[]{:S(2)}) collective-permute-start(f32[128,128]{1,0:T(8,128)S(1)} %get-tuple-element.60), channel_id=1, source_target_pairs={{1,2},{2,1},{3,4},{4,3},{5,6},{6,5},{7,8},{8,7},{9,10},{10,9},{11,... | collective-permute-start | bytes 196616 | tf_op jit(solution)/shard_map/ppermute | solution.py:713
  43.8 0.3 shard_map.123.partial
  44.1 2.8 %all-to-all-done.1.received = f32[4,200,128]{2,1,0:T(8,128)S(1)} async-done(((f32[4,200,128]{2,1,0:T(8,128)}), f32[4,200,128]{2,1,0:T(8,128)S(1)}, u32[]{:S(2)}, u32[]{:S(2)}) %all-to-all-start.1) | async-done | bytes 409632 | tf_op jit(solution)/shard_map/all_to_all | solution.py:791
  46.9 0.4 shard_map.124
  47.3 0.8 %collective-permute-done.8.got_b = f32[128,128]{1,0:T(8,128)S(1)} collective-permute-done((f32[128,128]{1,0:T(8,128)S(1)}, f32[128,128]{1,0:T(8,128)S(1)}, u32[]{:S(2)}, u32[]{:S(2)}) %collective-permute-start.8) | collective-permute-done | bytes 65568 | tf_op jit(solution)/shard_map/ppermute | solution.py:713
  48.0 0.3 shard_map.125
  48.4 4.8 %collective-permute-start.10 = (f32[128,128]{1,0:T(8,128)S(1)}, f32[128,128]{1,0:T(8,128)S(1)}, u32[]{:S(2)}, u32[]{:S(2)}) collective-permute-start(f32[128,128]{1,0:T(8,128)S(1)} %get-tuple-element.64), channel_id=1, source_target_pairs={{1,2},{2,1},{3,4},{4,3},{5,6},{6,5},{7,8},{8,7},{9,10},{10,9},{11,... | collective-permute-start | bytes 196616 | tf_op jit(solution)/shard_map/ppermute | solution.py:713
  53.2 0.6 collective-permute-start.9
  53.8 1.0 %shard_map.120 = f32[5,8,8,128]{3,2,1,0:T(8,128)} custom-call(f32[5,10,16,128]{3,2,1,0:T(8,128)S(1)} %get-tuple-element.47.second, f32[5,14,16,128]{3,2,1,0:T(8,128)S(1)} %get-tuple-element.48.derived, f32[5,8,8,128]{3,2,1,0:T(8,128)S(1)} %get-tuple-element.49.ends, f32[5,14,16,128]{3,2,1,0:T(8,128)S(1)} %get-tuple-element.45.wide), custom_call_target="tpu_custom_call" | custom-call | tf_op jit(solution)/shard_map/pallas_call | solution.py:52
  54.8 0.3 shard_map.126.partial
  55.1 2.4 %collective-permute-done.10.got_b = f32[128,128]{1,0:T(8,128)S(1)} collective-permute-done((f32[128,128]{1,0:T(8,128)S(1)}, f32[128,128]{1,0:T(8,128)S(1)}, u32[]{:S(2)}, u32[]{:S(2)}) %collective-permute-start.10) | collective-permute-done | bytes 65568 | tf_op jit(solution)/shard_map/ppermute | solution.py:713
  57.6 1.3 %shard_map.127 = f32[16,4,512]{2,1,0:T(4,128)} custom-call(f32[4,64,128]{2,1,0:T(8,128)S(1)} %shard_map.126.partial, f32[96,128]{1,0:T(8,128)S(1)} %collective-permute-done.9.got_a, f32[128,128]{1,0:T(8,128)S(1)} %collective-permute-done.10.got_b, bf16[5,128,128]{2,1,0:T(8,128)(2,1)S(1)} %get-tuple-element.55.sides_far, ...), custom_call_target="tpu_custom_call" | custom-call | tf_op jit(solution)/shard_map/pallas_call | solution.py:52
  (36 shorter events, 0.7 us)
Async XLA Ops:
  0.6 1.0 %copy-start.2 = (f32[8,8,128]{2,1,0:T(8,128)S(1)}, f32[8,8,128]{2,1,0:T(8,128)}, u32[]{:S(2)}) copy-start(f32[8,8,128]{2,1,0:T(8,128)} %param.10) | copy-start | bytes 98308
  0.6 1.0 %copy-start.1 = (f32[3,8,8,128]{3,2,1,0:T(8,128)S(1)}, f32[3,8,8,128]{3,2,1,0:T(8,128)}, u32[]{:S(2)}) copy-start(f32[3,8,8,128]{3,2,1,0:T(8,128)} %param.11) | copy-start | bytes 294916
  0.6 1.0 %copy-start.3 = (f32[8,8,128]{2,1,0:T(8,128)S(1)}, f32[8,8,128]{2,1,0:T(8,128)}, u32[]{:S(2)}) copy-start(f32[8,8,128]{2,1,0:T(8,128)} %param.12) | copy-start | bytes 98308
  1.7 2.5 %copy-start = (f32[16,4,512]{2,1,0:T(4,128)S(1)}, f32[16,4,512]{2,1,0:T(4,128)}, u32[]{:S(2)}) copy-start(f32[16,4,512]{2,1,0:T(4,128)} %given.1) | copy-start | bytes 393220
  1.8 2.4 %collective-permute-start = (f32[24,128]{1,0:T(8,128)S(1)}, f32[24,128]{1,0:T(8,128)S(1)}, u32[]{:S(2)}, u32[]{:S(2)}) collective-permute-start(f32[24,128]{1,0:T(8,128)S(1)} %get-tuple-element.34.sent_a), channel_id=1, source_target_pairs={{1,0},{0,1},{3,2},{2,3},{5,4},{4,5},{7,6},{6,7},{9,8},{8,9},{11,10... | collective-permute-start | bytes 36872 | tf_op jit(solution)/shard_map/ppermute | solution.py:706
  1.9 8.7 %collective-permute-start.1 = (f32[24,128]{1,0:T(8,128)S(1)}, f32[24,128]{1,0:T(8,128)S(1)}, u32[]{:S(2)}, u32[]{:S(2)}) collective-permute-start(f32[24,128]{1,0:T(8,128)S(1)} %get-tuple-element.35.sent_b), channel_id=1, source_target_pairs={{3,0},{2,1},{1,2},{0,3},{7,4},{6,5},{5,6},{4,7},{11,8},{10,9},{9,1... | collective-permute-start | bytes 36872 | tf_op jit(solution)/shard_map/ppermute | solution.py:707
  3.5 0.7 %copy-start.4 = (s32[16,6]{0,1:T(8,128)S(1)}, s32[16,6]{0,1:T(8,128)}, u32[]{:S(2)}) copy-start(s32[16,6]{0,1:T(8,128)} %param.17) | copy-start | bytes 1156
  4.8 0.7 %copy-start.8 = (s32[1,1,1,16]{3,2,1,0:T(1,128)S(1)}, s32[1,1,1,16]{3,2,1,0:T(1,128)}, u32[]{:S(2)}) copy-start(s32[1,1,1,16]{3,2,1,0:T(1,128)} %param.19) | copy-start | bytes 196
  4.8 5.8 %collective-permute-start.2 = (f32[96,128]{1,0:T(8,128)S(1)}, f32[96,128]{1,0:T(8,128)S(1)}, u32[]{:S(2)}, u32[]{:S(2)}) collective-permute-start(f32[96,128]{1,0:T(8,128)S(1)} %get-tuple-element.36), channel_id=1, source_target_pairs={{1,0},{0,1},{3,2},{2,3},{5,4},{4,5},{7,6},{6,7},{9,8},{8,9},{11,10... | collective-permute-start | bytes 147464 | tf_op jit(solution)/shard_map/ppermute | solution.py:714
  5.5 13.6 %collective-permute-start.6 = (f32[288,128]{1,0:T(8,128)S(1)}, f32[288,128]{1,0:T(8,128)S(1)}, u32[]{:S(2)}, u32[]{:S(2)}) collective-permute-start(f32[288,128]{1,0:T(8,128)S(1)} %get-tuple-element.44), channel_id=1, source_target_pairs={{1,2},{2,1},{3,4},{4,3},{5,6},{6,5},{7,8},{8,7},{9,10},{10,9},{11,... | collective-permute-start | bytes 442376 | tf_op jit(solution)/shard_map/ppermute | solution.py:713
  10.7 0.7 %copy-start.9 = (s32[1,1,1,16,1]{3,4,2,1,0:T(1,128)S(1)}, s32[1,1,1,16,1]{3,4,2,1,0:T(1,128)}, u32[]{:S(2)}) copy-start(s32[1,1,1,16,1]{3,4,2,1,0:T(1,128)} %param.18) | copy-start | bytes 196
  10.7 5.2 %collective-permute-start.3 = (f32[280,128]{1,0:T(8,128)S(1)}, f32[280,128]{1,0:T(8,128)S(1)}, u32[]{:S(2)}, u32[]{:S(2)}) collective-permute-start(f32[280,128]{1,0:T(8,128)S(1)} %get-tuple-element.38), channel_id=1, source_target_pairs={{16,0},{0,16},{17,1},{1,17},{18,2},{2,18},{19,3},{3,19},{20,4},{4,... | collective-permute-start | bytes 430088 | tf_op jit(solution)/shard_map/ppermute | solution.py:743
  15.9 2.2 %copy-start.6 = (f32[8,8]{1,0:T(8,128)S(1)}, f32[8,8]{1,0:T(8,128)}, u32[]{:S(2)}) copy-start(f32[8,8]{1,0:T(8,128)} %param.15) | copy-start | bytes 772
  16.0 2.1 %copy-start.5 = (f32[8,8]{1,0:T(8,128)S(1)}, f32[8,8]{1,0:T(8,128)}, u32[]{:S(2)}) copy-start(f32[8,8]{1,0:T(8,128)} %param.16) | copy-start | bytes 772
  16.0 5.4 %collective-permute-start.4 = (f32[168,128]{1,0:T(8,128)S(1)}, f32[168,128]{1,0:T(8,128)S(1)}, u32[]{:S(2)}, u32[]{:S(2)}) collective-permute-start(f32[168,128]{1,0:T(8,128)S(1)} %get-tuple-element.39), channel_id=1, source_target_pairs={{4,0},{0,4},{12,8},{8,12},{5,1},{1,5},{13,9},{9,13},{6,2},{2,6},{1... | collective-permute-start | bytes 258056 | tf_op jit(solution)/shard_map/ppermute | solution.py:748
  16.0 2.1 %copy-start.7 = (f32[16]{0:T(128)S(1)}, f32[16]{0:T(128)}, u32[]{:S(2)}) copy-start(f32[16]{0:T(128)} %param.14) | copy-start | bytes 196
  16.1 6.5 %collective-permute-start.5 = (f32[168,128]{1,0:T(8,128)S(1)}, f32[168,128]{1,0:T(8,128)S(1)}, u32[]{:S(2)}, u32[]{:S(2)}) collective-permute-start(f32[168,128]{1,0:T(8,128)S(1)} %get-tuple-element.40), channel_id=1, source_target_pairs={{12,0},{8,4},{4,8},{0,12},{13,1},{9,5},{5,9},{1,13},{14,2},{10,6},... | collective-permute-start | bytes 258056 | tf_op jit(solution)/shard_map/ppermute | solution.py:747
  23.8 9.9 %all-to-all-start = ((f32[4,104,128]{2,1,0:T(8,128)}), f32[4,104,128]{2,1,0:T(8,128)S(1)}, u32[]{:S(2)}, u32[]{:S(2)}) async-start(f32[4,104,128]{2,1,0:T(8,128)} %get-tuple-element.56), calls=%async_computation | async-start | bytes 425984 | tf_op jit(solution)/shard_map/all_to_all | solution.py:791
  33.8 13.1 %all-to-all-start.1 = ((f32[4,200,128]{2,1,0:T(8,128)}), f32[4,200,128]{2,1,0:T(8,128)S(1)}, u32[]{:S(2)}, u32[]{:S(2)}) async-start(f32[4,200,128]{2,1,0:T(8,128)} %get-tuple-element.57.refs_0_), calls=%async_computation.1 | async-start | bytes 819200 | tf_op jit(solution)/shard_map/all_to_all | solution.py:791
  38.1 9.9 %collective-permute-start.8 = (f32[128,128]{1,0:T(8,128)S(1)}, f32[128,128]{1,0:T(8,128)S(1)}, u32[]{:S(2)}, u32[]{:S(2)}) collective-permute-start(f32[128,128]{1,0:T(8,128)S(1)} %get-tuple-element.60), channel_id=1, source_target_pairs={{1,2},{2,1},{3,4},{4,3},{5,6},{6,5},{7,8},{8,7},{9,10},{10,9},{11,... | collective-permute-start | bytes 196616 | tf_op jit(solution)/shard_map/ppermute | solution.py:713
  43.7 3.6 %collective-permute-start.7 = (f32[96,128]{1,0:T(8,128)S(1)}, f32[96,128]{1,0:T(8,128)S(1)}, u32[]{:S(2)}, u32[]{:S(2)}) collective-permute-start(f32[96,128]{1,0:T(8,128)S(1)} %get-tuple-element.59), channel_id=1, source_target_pairs={{1,0},{0,1},{3,2},{2,3},{5,4},{4,5},{7,6},{6,7},{9,8},{8,9},{11,10... | collective-permute-start | bytes 147464 | tf_op jit(solution)/shard_map/ppermute | solution.py:714
  48.4 9.2 %collective-permute-start.10 = (f32[128,128]{1,0:T(8,128)S(1)}, f32[128,128]{1,0:T(8,128)S(1)}, u32[]{:S(2)}, u32[]{:S(2)}) collective-permute-start(f32[128,128]{1,0:T(8,128)S(1)} %get-tuple-element.64), channel_id=1, source_target_pairs={{1,2},{2,1},{3,4},{4,3},{5,6},{6,5},{7,8},{8,7},{9,10},{10,9},{11,... | collective-permute-start | bytes 196616 | tf_op jit(solution)/shard_map/ppermute | solution.py:713
  53.2 1.9 %collective-permute-start.9 = (f32[96,128]{1,0:T(8,128)S(1)}, f32[96,128]{1,0:T(8,128)S(1)}, u32[]{:S(2)}, u32[]{:S(2)}) collective-permute-start(f32[96,128]{1,0:T(8,128)S(1)} %get-tuple-element.63), channel_id=1, source_target_pairs={{1,0},{0,1},{3,2},{2,3},{5,4},{4,5},{7,6},{6,7},{9,8},{8,9},{11,10... | collective-permute-start | bytes 147464 | tf_op jit(solution)/shard_map/ppermute | solution.py:714

commit v11 on v10

--- a/solution.py
+++ b/solution.py
@@ -76,7 +76,7 @@
     return jnp.where(odd, to_last, to_next), jnp.where(odd, to_next, to_last)
 
 
-def pack_start_body(state, message_a, message_b):
+def pack_start_body(state, message_a, message_b, along_x):
     odd = is_odd("fz")
     rows = state[...].reshape(-1, 128)
     count = rows.shape[0]
@@ -88,9 +88,14 @@
         first, second = paired(odd, turned[120:128], turned[0:8])
         message_a[tile * 8 : tile * 8 + 8] = first
         message_b[tile * 8 : tile * 8 + 8] = second
-
-
-def pack_next_body(state, sent_a, sent_b, got_a, got_b, _, edge, along_x):
+    cells_x = state.shape[1]
+    for f in range(5):
+        for s, x in enumerate(x_planes(cells_x)):
+            at = (f * 2 * HALO + s) * 8
+            along_x[at : at + 8] = state[f, x]
+
+
+def pack_next_body(state, sent_a, sent_b, got_a, got_b, _, edge):
     cells_x = state.shape[1]
     odd_z = is_odd("fz")
     high, low = paired(odd_z, sent_a[...], sent_b[...])
@@ -111,12 +116,6 @@
                 for x in range(1, cells_x):
                     total = total + spread[at + x * 8 : at + x * 8 + 8]
                 edge[f * 8 : f * 8 + 8] = total
-    for f in range(5):
-        for s, x in enumerate(x_planes(cells_x)):
-            at = (f * 2 * HALO + s) * 8
-            along_x[at : at + 8] = state[f, x]
-    size = along_x.shape[0]
-    along_x[size - 40 : size] = edge[...]
 
 
 def x_planes(cells_x):
@@ -127,9 +126,9 @@
     return beside_x[0], beside_x[-1]
 
 
-def beyond(beside_x, f):
-    after, before = sides_of(beside_x)
-    at = after.shape[0] - 40 + f * 8
+def beyond(edges_x, f):
+    after, before = sides_of(edges_x)
+    at = f * 8
     if after is before:
         return after[at : at + 8]
     lane = lax.broadcasted_iota(jnp.int32, (8, 128), 1)
@@ -137,7 +136,8 @@
 
 
 def pack_last_body(state, edge, *refs):
-    beside_x, (y_a, y_b) = refs[:-2], refs[-2:]
+    (y_a, y_b), refs = refs[-2:], refs[:-2]
+    beside_x, edges_x = refs[: len(refs) // 2], refs[len(refs) // 2 :]
     cells_x = state.shape[1]
     odd = is_odd("fy")
     after, before = sides_of(beside_x)
@@ -157,10 +157,10 @@
             put(at, (before if slot < HALO else after)[source : source + 8], height)
             at += height
         put(lines + 30 + f * 2, edge[f * 8 : f * 8 + 8], 2)
-        put(lines + 40 + f, beyond(beside_x, f), 1)
-
-
-def assemble(wide, rim, state, edge, beside_x, above, below):
+        put(lines + 40 + f, beyond(edges_x, f), 1)
+
+
+def assemble(wide, rim, state, edge, beside_x, edges_x, above, below):
     cells_x = state.shape[1]
     after, before = sides_of(beside_x)
     lines = 5 * cells_x * HALO
@@ -181,7 +181,7 @@
             wide[f, plane, 16 - height : 16] = below[at : at + height]
             at += height
         rim[f, 0:8, 0:128] = edge[f * 8 : f * 8 + 8]
-        rim[f, 0:8, 128:256] = beyond(beside_x, f)
+        rim[f, 0:8, 128:256] = beyond(edges_x, f)
         at = lines + 30 + f * 2
         rim[f, 8:10, 0:128] = above[at : at + 2]
         rim[f, 14:16, 0:128] = below[at : at + 2]
@@ -353,12 +353,12 @@
 
 
 def flow_sources_body(count, state, edge, *refs):
-    beside_x = refs[:count]
-    got_a, got_b, pair, spread, labels, _ = refs[count : count + 6]
-    wide, rim, send, derived, lamb_rows, ends, above, below = refs[count + 6 :]
+    beside_x, edges_x, refs = refs[:count], refs[count : 2 * count], refs[2 * count :]
+    got_a, got_b, pair, spread, labels, _ = refs[:6]
+    wide, rim, send, derived, lamb_rows, ends, above, below = refs[6:]
     cells_x = state.shape[1]
     above[...], below[...] = paired(is_odd("fy"), got_a[...], got_b[...])
-    assemble(wide, rim, state, edge, beside_x, above, below)
+    assemble(wide, rim, state, edge, beside_x, edges_x, above, below)
     derive_speeds(wide, derived, HALO - 1, HALO + cells_x + 1)
     inverse = 1.0 / rim[0, 0:8]
     to_ends([rim[1, 0:8] * inverse, rim[2, 0:8] * inverse], 3, 8, 0, cells_x, ends)
@@ -702,9 +702,14 @@
     rest = ((0, 0), (0, 0), (0, 0))
     state = jnp.pad(density[None], ((0, 4),) + rest) + jnp.pad(density * velocity, ((1, 1),) + rest)
     state = state + jnp.pad(energy[None], ((4, 0),) + rest)
-    flow_a, flow_b = call(pack_start_body, [(tiles * 8, 128), (tiles * 8, 128)], state)
+    x_rows = 5 * 2 * HALO * 8
+    flow_a, flow_b, along_x = call(
+        pack_start_body, [(tiles * 8, 128), (tiles * 8, 128), (x_rows, 128)], state
+    )
     edge_a = lax.ppermute(flow_a, "fz", partners((size_z,), 0, False))
     edge_b = lax.ppermute(flow_b, "fz", partners((size_z,), 0, True))
+    x_steps = (1,) if size_x == 2 else (1, -1)
+    beside_x = [lax.ppermute(along_x, "fx", shifted((size_x,), (step,))) for step in x_steps]
 
     near_pairs = [(i ^ 1, i) for i in range(devices)]
     far_pairs = [pair for i in range(1, devices - 1, 2) for pair in ((i, i + 1), (i + 1, i))]
@@ -720,7 +725,7 @@
     turning = [pltpu.VMEM((512, 128), F32), pltpu.VMEM((4, 4 * elements, 128), F32)]
     sound, to_a, to_b = call(
         acoustic_start_body,
-        [held, faces, (3 * faces[0], size)],
+        [held, faces, (2 * faces[0], size)],
         acoustic,
         edge_a,
         scratch=turning,
@@ -728,9 +733,9 @@
     )
     got_a, got_b = traces(to_a, to_b)
 
-    edge, along_x = call(
+    edge = call(
         pack_next_body,
-        [(40, 128), (5 * 2 * HALO * 8 + 40, 128)],
+        [(40, 128)],
         state,
         flow_a,
         flow_b,
@@ -738,12 +743,10 @@
         edge_b,
         got_a,
         last=1,
-    )
-    beside_x = [
-        lax.ppermute(along_x, "fx", shifted((size_x,), (step,))) for step in ((1,) if size_x == 2 else (1, -1))
-    ]
+    )[0]
+    edges_x = [lax.ppermute(edge, "fx", shifted((size_x,), (step,))) for step in x_steps]
     y_shape = (5 * cells_x * HALO + 48, 128)
-    y_a, y_b = call(pack_last_body, [y_shape, y_shape], state, edge, *beside_x, cost=1)
+    y_a, y_b = call(pack_last_body, [y_shape, y_shape], state, edge, *beside_x, *edges_x, cost=1)
     y_second = lax.ppermute(y_b, "fy", partners((size_y,), 0, True))
     y_first = lax.ppermute(y_a, "fy", partners((size_y,), 0, False))
 
@@ -796,6 +799,7 @@
         state,
         edge,
         *beside_x,
+        *edges_x,
         y_first,
         y_second,
         pair,

time: 59.3 us -> 58.5 us (0.987)
  waiting for transfers between devices: 16.6 us -> 15.6 us
  starting transfers between devices: 27 us -> 27.6 us
    ppermute x1, waiting for transfers between devices: 4.51 us -> 0.01 us  [per_device(): lax.ppermute(along_x, 'fx', shifted((size_x,), (step,)))]
    ppermute x3, waiting for transfers between devices: 3.2 us -> 5.85 us  [traces(): far_got = lax.ppermute(to_b, names, far_pairs)]
    ppermute x1, waiting for transfers between devices: 2.24 us -> 0.01 us  [per_device(): y_first = lax.ppermute(y_a, 'fy', partners((size_y,), 0, False))]
    all_to_all x2, waiting for transfers between devices: 5.43 us -> 7.48 us  [route(): return lax.all_to_all(send, 'fy', split_axis=0, concat_axis=0, tiled=True)]
    ppermute x0 -> x1, starting transfers between devices: none -> 1.56 us  [per_device(): lax.ppermute(edge, 'fx', shifted((size_x,), (step,)))]
    ppermute x1, starting transfers between devices: 2.03 us -> 1.38 us  [per_device(): y_second = lax.ppermute(y_b, 'fy', partners((size_y,), 0, True))]
    ppermute x3, waiting for transfers between devices: 0.01 us -> 0.65 us  [traces(): return (lax.ppermute(to_a, names, near_pairs), far_got)]
  transfers between devices with their start and end apart: 13 -> 14, of which waited for: 7 -> 6; matrix products, arithmetic and copies ran while one was open for 0% -> 0% of each run, Pallas kernels for 14% -> 15%
where the time goes in v11:
time: 58.5 us; the launch traced here: 58.1 us
  starting transfers between devices  27.6 us (47%)
  waiting for transfers between devices  15.6 us (27%)
  Pallas kernels  11.6 us (20%)
  local copies, waits for them, and re-layouts  1.3 us (2%)
  other arithmetic  1.01 us (2%)
  between operations  0.92 us (2%)
    ppermute x3, starting transfers between devices, traces(): far_got = lax.ppermute(to_b, names, far_pairs)  15.1 us
    pallas_call x15, Pallas kernels, call(): pl.pallas_call(body, out_shape=outs, in_specs=[whole] * (len(operands) -...  11.6 us
    all_to_all x2, waiting for transfers between devices, route(): return lax.all_to_all(send, 'fy', split_axis=0, concat_axis=0, tiled=True)  7.48 us
    all_to_all x2, starting transfers between devices, route(): return lax.all_to_all(send, 'fy', split_axis=0, concat_axis=0, tiled=True)  7.06 us
    ppermute x3, waiting for transfers between devices, traces(): far_got = lax.ppermute(to_b, names, far_pairs)  5.85 us
    ppermute x1, waiting for transfers between devices, per_device(): y_second = lax.ppermute(y_b, 'fy', partners((size_y,), 0, True))  1.64 us
    ppermute x1, starting transfers between devices, per_device(): edge_b = lax.ppermute(flow_b, 'fz', partners((size_z,), 0, True))  1.64 us
    ppermute x1, starting transfers between devices, per_device(): lax.ppermute(edge, 'fx', shifted((size_x,), (step,)))  1.56 us
  transfers between devices with their start and end apart: 14, of which 6 were waited for; matrix products, arithmetic and copies ran while one was open for 0% of the time, Pallas kernels for 15%

profile of v11, /device:TPU:2, one launch (start us, length us, event | category | flops | bytes accessed | tf_op | source)
XLA Modules:
  0.0 58.1 jit_solution(2875232523305900465)
XLA Ops:
  0.7 1.0 %broadcast_multiply_fusion = f32[3,8,8,128]{3,2,1,0:T(8,128)S(1)} fusion(f32[3,8,8,128]{3,2,1,0:T(8,128)} %param.11, f32[8,8,128]{2,1,0:T(8,128)} %param.10), kind=kLoop, calls=%fused_computation.1 | loop fusion | flops 24576 | bytes 229376 | tf_op jit(solution)/shard_map/mul | solution.py:703
  1.7 0.1 shard_map.113
  1.9 1.6 %collective-permute-start.1 = (f32[24,128]{1,0:T(8,128)S(1)}, f32[24,128]{1,0:T(8,128)S(1)}, u32[]{:S(2)}, u32[]{:S(2)}) collective-permute-start(f32[24,128]{1,0:T(8,128)S(1)} %get-tuple-element.34.sent_b), channel_id=1, source_target_pairs={{3,0},{2,1},{1,2},{0,3},{7,4},{6,5},{5,6},{4,7},{11,8},{10,9},{9,1... | collective-permute-start | bytes 36872 | tf_op jit(solution)/shard_map/ppermute | solution.py:710
  3.5 0.5 collective-permute-start.3
  4.1 0.7 %copy-done.4 = s32[16,6]{0,1:T(8,128)S(1)} copy-done((s32[16,6]{0,1:T(8,128)S(1)}, s32[16,6]{0,1:T(8,128)}, u32[]{:S(2)}) %copy-start.4) | copy-done | bytes 408
  4.8 0.6 shard_map.114
  5.4 0.6 copy-done.8
  6.0 0.6 %collective-permute-done.2._.got_a = f32[96,128]{1,0:T(8,128)S(1)} collective-permute-done((f32[96,128]{1,0:T(8,128)S(1)}, f32[96,128]{1,0:T(8,128)S(1)}, u32[]{:S(2)}, u32[]{:S(2)}) %collective-permute-start.2) | collective-permute-done | bytes 49184 | tf_op jit(solution)/shard_map/ppermute | solution.py:719
  6.7 0.1 shard_map.115.edge
  6.8 1.6 %collective-permute-start.4 = (f32[40,128]{1,0:T(8,128)S(1)}, f32[40,128]{1,0:T(8,128)S(1)}, u32[]{:S(2)}, u32[]{:S(2)}) collective-permute-start(f32[40,128]{1,0:T(8,128)S(1)} %shard_map.115.edge), channel_id=1, source_target_pairs={{16,0},{0,16},{17,1},{1,17},{18,2},{2,18},{19,3},{3,19},{20,4},{4,... | collective-permute-start | bytes 61448 | tf_op jit(solution)/shard_map/ppermute | solution.py:747
  8.3 4.9 %collective-permute-start.7 = (f32[192,128]{1,0:T(8,128)S(1)}, f32[192,128]{1,0:T(8,128)S(1)}, u32[]{:S(2)}, u32[]{:S(2)}) collective-permute-start(f32[192,128]{1,0:T(8,128)S(1)} %get-tuple-element.42), channel_id=1, source_target_pairs={{1,2},{2,1},{3,4},{4,3},{5,6},{6,5},{7,8},{8,7},{9,10},{10,9},{11,... | collective-permute-start | bytes 294920 | tf_op jit(solution)/shard_map/ppermute | solution.py:718
  13.5 1.4 %collective-permute-start.6 = (f32[168,128]{1,0:T(8,128)S(1)}, f32[168,128]{1,0:T(8,128)S(1)}, u32[]{:S(2)}, u32[]{:S(2)}) collective-permute-start(f32[168,128]{1,0:T(8,128)S(1)} %get-tuple-element.38), channel_id=1, source_target_pairs={{12,0},{8,4},{4,8},{0,12},{13,1},{9,5},{5,9},{1,13},{14,2},{10,6},... | collective-permute-start | bytes 258056 | tf_op jit(solution)/shard_map/ppermute | solution.py:750
  14.9 1.0 %shard_map.117 = (bf16[5,128,128]{2,1,0:T(8,128)(2,1)S(1)}, bf16[5,128,128]{2,1,0:T(8,128)(2,1)S(1)}, f32[128,64]{1,0:T(8,128)S(1)}, f32[128,128]{1,0:T(8,128)S(...) custom-call(f32[32,16]{1,0:T(8,128)S(1)} %pad_add_fusion.1.packed), custom_call_target="tpu_custom_call" | custom-call | flops 1 | bytes 1 | tf_op jit(solution)/shard_map/pallas_call | solution.py:52
  15.8 2.7 %collective-permute-done.7.refs_7_.got_b = f32[192,128]{1,0:T(8,128)S(1)} collective-permute-done((f32[192,128]{1,0:T(8,128)S(1)}, f32[192,128]{1,0:T(8,128)S(1)}, u32[]{:S(2)}, u32[]{:S(2)}) %collective-permute-start.7) | collective-permute-done | bytes 98336 | tf_op jit(solution)/shard_map/ppermute | solution.py:718
  18.6 1.6 %collective-permute-done.6.refs_3_ = f32[168,128]{1,0:T(8,128)S(1)} collective-permute-done((f32[168,128]{1,0:T(8,128)S(1)}, f32[168,128]{1,0:T(8,128)S(1)}, u32[]{:S(2)}, u32[]{:S(2)}) %collective-permute-start.6) | collective-permute-done | bytes 86048 | tf_op jit(solution)/shard_map/ppermute | solution.py:750
  20.2 1.3 %shard_map.118 = (f32[5,14,16,128]{3,2,1,0:T(8,128)S(1)}, f32[5,16,256]{2,1,0:T(8,128)S(1)}, f32[4,104,128]{2,1,0:T(8,128)}) custom-call(f32[5,8,8,128]{3,2,1,0:T(8,128)S(1)} %pad_add_fusion.state, f32[40,128]{1,0:T(8,128)S(1)} %shard_map.115.edge, f32[240,128]{1,0:T(8,128)S(1)} %collective-permute-done.3.refs_0_, ...), custom_call_target="tpu_custom_call" | custom-call | tf_op jit(solution)/shard_map/pallas_call | solution.py:52
  21.6 3.6 %all-to-all-start = ((f32[4,104,128]{2,1,0:T(8,128)}), f32[4,104,128]{2,1,0:T(8,128)S(1)}, u32[]{:S(2)}, u32[]{:S(2)}) async-start(f32[4,104,128]{2,1,0:T(8,128)} %get-tuple-element.54), calls=%async_computation | async-start | bytes 425984 | tf_op jit(solution)/shard_map/all_to_all | solution.py:794
  25.2 3.9 %shard_map.119 = (f32[5,10,16,128]{3,2,1,0:T(8,128)S(1)}, f32[5,14,16,128]{3,2,1,0:T(8,128)S(1)}, f32[5,8,8,128]{3,2,1,0:T(8,128)S(1)}, f32[4,200,128]{2,1,0:T(8,128)}) custom-call(f32[5,14,16,128]{3,2,1,0:T(8,128)S(1)} %get-tuple-element.43.wide, f32[5,16,256]{2,1,0:T(8,128)S(1)} %get-tuple-element.44.rim, f32[64,64]{1,0:T(8,128)S(1)} %get-tuple-element.39.refs_4_.pair, ...), custom_call_target="tpu_custom_call" | custom-call | tf_op jit(solution)/shard_map/pallas_call | solution.py:52
  29.0 3.7 %all-to-all-done.received = f32[4,104,128]{2,1,0:T(8,128)S(1)} async-done(((f32[4,104,128]{2,1,0:T(8,128)}), f32[4,104,128]{2,1,0:T(8,128)S(1)}, u32[]{:S(2)}, u32[]{:S(2)}) %all-to-all-start) | async-done | bytes 213024 | tf_op jit(solution)/shard_map/all_to_all | solution.py:794
  32.7 3.5 %all-to-all-start.1 = ((f32[4,200,128]{2,1,0:T(8,128)}), f32[4,200,128]{2,1,0:T(8,128)S(1)}, u32[]{:S(2)}, u32[]{:S(2)}) async-start(f32[4,200,128]{2,1,0:T(8,128)} %get-tuple-element.55.refs_0_), calls=%async_computation.1 | async-start | bytes 819200 | tf_op jit(solution)/shard_map/all_to_all | solution.py:794
  36.2 0.3 shard_map.121.partial
  36.5 0.5 shard_map.122
  37.0 5.5 %collective-permute-start.9 = (f32[128,128]{1,0:T(8,128)S(1)}, f32[128,128]{1,0:T(8,128)S(1)}, u32[]{:S(2)}, u32[]{:S(2)}) collective-permute-start(f32[128,128]{1,0:T(8,128)S(1)} %get-tuple-element.58), channel_id=1, source_target_pairs={{1,2},{2,1},{3,4},{4,3},{5,6},{6,5},{7,8},{8,7},{9,10},{10,9},{11,... | collective-permute-start | bytes 196616 | tf_op jit(solution)/shard_map/ppermute | solution.py:718
  42.7 0.3 shard_map.123.partial
  43.0 3.8 %all-to-all-done.1.received = f32[4,200,128]{2,1,0:T(8,128)S(1)} async-done(((f32[4,200,128]{2,1,0:T(8,128)}), f32[4,200,128]{2,1,0:T(8,128)S(1)}, u32[]{:S(2)}, u32[]{:S(2)}) %all-to-all-start.1) | async-done | bytes 409632 | tf_op jit(solution)/shard_map/all_to_all | solution.py:794
  46.8 0.4 shard_map.124
  47.2 0.3 shard_map.125
  47.6 4.6 %collective-permute-start.11 = (f32[128,128]{1,0:T(8,128)S(1)}, f32[128,128]{1,0:T(8,128)S(1)}, u32[]{:S(2)}, u32[]{:S(2)}) collective-permute-start(f32[128,128]{1,0:T(8,128)S(1)} %get-tuple-element.62), channel_id=1, source_target_pairs={{1,2},{2,1},{3,4},{4,3},{5,6},{6,5},{7,8},{8,7},{9,10},{10,9},{11,... | collective-permute-start | bytes 196616 | tf_op jit(solution)/shard_map/ppermute | solution.py:718
  52.3 1.0 %shard_map.120 = f32[5,8,8,128]{3,2,1,0:T(8,128)} custom-call(f32[5,10,16,128]{3,2,1,0:T(8,128)S(1)} %get-tuple-element.45.second, f32[5,14,16,128]{3,2,1,0:T(8,128)S(1)} %get-tuple-element.46.derived, f32[5,8,8,128]{3,2,1,0:T(8,128)S(1)} %get-tuple-element.47.ends, f32[5,14,16,128]{3,2,1,0:T(8,128)S(1)} %get-tuple-element.43.wide), custom_call_target="tpu_custom_call" | custom-call | tf_op jit(solution)/shard_map/pallas_call | solution.py:52
  53.3 0.3 shard_map.126.partial
  53.7 3.1 %collective-permute-done.11.got_b = f32[128,128]{1,0:T(8,128)S(1)} collective-permute-done((f32[128,128]{1,0:T(8,128)S(1)}, f32[128,128]{1,0:T(8,128)S(1)}, u32[]{:S(2)}, u32[]{:S(2)}) %collective-permute-start.11) | collective-permute-done | bytes 65568 | tf_op jit(solution)/shard_map/ppermute | solution.py:718
  56.8 1.3 %shard_map.127 = f32[16,4,512]{2,1,0:T(4,128)} custom-call(f32[4,64,128]{2,1,0:T(8,128)S(1)} %shard_map.126.partial, f32[96,128]{1,0:T(8,128)S(1)} %collective-permute-done.10.got_a, f32[128,128]{1,0:T(8,128)S(1)} %collective-permute-done.11.got_b, bf16[5,128,128]{2,1,0:T(8,128)(2,1)S(1)} %get-tuple-element.53.sides_far, ...), custom_call_target="tpu_custom_call" | custom-call | tf_op jit(solution)/shard_map/pallas_call | solution.py:52
  (38 shorter events, 0.5 us)
Async XLA Ops:
  0.6 1.0 %copy-start.2 = (f32[8,8,128]{2,1,0:T(8,128)S(1)}, f32[8,8,128]{2,1,0:T(8,128)}, u32[]{:S(2)}) copy-start(f32[8,8,128]{2,1,0:T(8,128)} %param.10) | copy-start | bytes 98308
  0.6 1.0 %copy-start.1 = (f32[3,8,8,128]{3,2,1,0:T(8,128)S(1)}, f32[3,8,8,128]{3,2,1,0:T(8,128)}, u32[]{:S(2)}) copy-start(f32[3,8,8,128]{3,2,1,0:T(8,128)} %param.11) | copy-start | bytes 294916
  0.6 1.0 %copy-start.3 = (f32[8,8,128]{2,1,0:T(8,128)S(1)}, f32[8,8,128]{2,1,0:T(8,128)}, u32[]{:S(2)}) copy-start(f32[8,8,128]{2,1,0:T(8,128)} %param.12) | copy-start | bytes 98308
  1.7 3.1 %copy-start = (f32[16,4,512]{2,1,0:T(4,128)S(1)}, f32[16,4,512]{2,1,0:T(4,128)}, u32[]{:S(2)}) copy-start(f32[16,4,512]{2,1,0:T(4,128)} %given.1) | copy-start | bytes 393220
  1.8 2.9 %collective-permute-start = (f32[24,128]{1,0:T(8,128)S(1)}, f32[24,128]{1,0:T(8,128)S(1)}, u32[]{:S(2)}, u32[]{:S(2)}) collective-permute-start(f32[24,128]{1,0:T(8,128)S(1)} %get-tuple-element.33.sent_a), channel_id=1, source_target_pairs={{1,0},{0,1},{3,2},{2,3},{5,4},{4,5},{7,6},{6,7},{9,8},{8,9},{11,10... | collective-permute-start | bytes 36872 | tf_op jit(solution)/shard_map/ppermute | solution.py:709
  1.9 4.1 %collective-permute-start.1 = (f32[24,128]{1,0:T(8,128)S(1)}, f32[24,128]{1,0:T(8,128)S(1)}, u32[]{:S(2)}, u32[]{:S(2)}) collective-permute-start(f32[24,128]{1,0:T(8,128)S(1)} %get-tuple-element.34.sent_b), channel_id=1, source_target_pairs={{3,0},{2,1},{1,2},{0,3},{7,4},{6,5},{5,6},{4,7},{11,8},{10,9},{9,1... | collective-permute-start | bytes 36872 | tf_op jit(solution)/shard_map/ppermute | solution.py:710
  3.5 9.7 %collective-permute-start.3 = (f32[240,128]{1,0:T(8,128)S(1)}, f32[240,128]{1,0:T(8,128)S(1)}, u32[]{:S(2)}, u32[]{:S(2)}) collective-permute-start(f32[240,128]{1,0:T(8,128)S(1)} %get-tuple-element.36), channel_id=1, source_target_pairs={{16,0},{0,16},{17,1},{1,17},{18,2},{2,18},{19,3},{3,19},{20,4},{4,... | collective-permute-start | bytes 368648 | tf_op jit(solution)/shard_map/ppermute | solution.py:712
  4.1 0.7 %copy-start.4 = (s32[16,6]{0,1:T(8,128)S(1)}, s32[16,6]{0,1:T(8,128)}, u32[]{:S(2)}) copy-start(s32[16,6]{0,1:T(8,128)} %param.17) | copy-start | bytes 1156
  5.3 0.7 %copy-start.8 = (s32[1,1,1,16]{3,2,1,0:T(1,128)S(1)}, s32[1,1,1,16]{3,2,1,0:T(1,128)}, u32[]{:S(2)}) copy-start(s32[1,1,1,16]{3,2,1,0:T(1,128)} %param.19) | copy-start | bytes 196
  5.4 1.3 %collective-permute-start.2 = (f32[96,128]{1,0:T(8,128)S(1)}, f32[96,128]{1,0:T(8,128)S(1)}, u32[]{:S(2)}, u32[]{:S(2)}) collective-permute-start(f32[96,128]{1,0:T(8,128)S(1)} %get-tuple-element.35), channel_id=1, source_target_pairs={{1,0},{0,1},{3,2},{2,3},{5,4},{4,5},{7,6},{6,7},{9,8},{8,9},{11,10... | collective-permute-start | bytes 147464 | tf_op jit(solution)/shard_map/ppermute | solution.py:719
  6.0 2.3 %copy-start.9 = (s32[1,1,1,16,1]{3,4,2,1,0:T(1,128)S(1)}, s32[1,1,1,16,1]{3,4,2,1,0:T(1,128)}, u32[]{:S(2)}) copy-start(s32[1,1,1,16,1]{3,4,2,1,0:T(1,128)} %param.18) | copy-start | bytes 196
  6.8 6.5 %collective-permute-start.4 = (f32[40,128]{1,0:T(8,128)S(1)}, f32[40,128]{1,0:T(8,128)S(1)}, u32[]{:S(2)}, u32[]{:S(2)}) collective-permute-start(f32[40,128]{1,0:T(8,128)S(1)} %shard_map.115.edge), channel_id=1, source_target_pairs={{16,0},{0,16},{17,1},{1,17},{18,2},{2,18},{19,3},{3,19},{20,4},{4,... | collective-permute-start | bytes 61448 | tf_op jit(solution)/shard_map/ppermute | solution.py:747
  8.3 10.2 %collective-permute-start.7 = (f32[192,128]{1,0:T(8,128)S(1)}, f32[192,128]{1,0:T(8,128)S(1)}, u32[]{:S(2)}, u32[]{:S(2)}) collective-permute-start(f32[192,128]{1,0:T(8,128)S(1)} %get-tuple-element.42), channel_id=1, source_target_pairs={{1,2},{2,1},{3,4},{4,3},{5,6},{6,5},{7,8},{8,7},{9,10},{10,9},{11,... | collective-permute-start | bytes 294920 | tf_op jit(solution)/shard_map/ppermute | solution.py:718
  13.3 1.6 %copy-start.6 = (f32[8,8]{1,0:T(8,128)S(1)}, f32[8,8]{1,0:T(8,128)}, u32[]{:S(2)}) copy-start(f32[8,8]{1,0:T(8,128)} %param.15) | copy-start | bytes 772
  13.4 1.5 %copy-start.5 = (f32[8,8]{1,0:T(8,128)S(1)}, f32[8,8]{1,0:T(8,128)}, u32[]{:S(2)}) copy-start(f32[8,8]{1,0:T(8,128)} %param.16) | copy-start | bytes 772
  13.4 5.2 %collective-permute-start.5 = (f32[168,128]{1,0:T(8,128)S(1)}, f32[168,128]{1,0:T(8,128)S(1)}, u32[]{:S(2)}, u32[]{:S(2)}) collective-permute-start(f32[168,128]{1,0:T(8,128)S(1)} %get-tuple-element.37), channel_id=1, source_target_pairs={{4,0},{0,4},{12,8},{8,12},{5,1},{1,5},{13,9},{9,13},{6,2},{2,6},{1... | collective-permute-start | bytes 258056 | tf_op jit(solution)/shard_map/ppermute | solution.py:751
  13.4 1.4 %copy-start.7 = (f32[16]{0:T(128)S(1)}, f32[16]{0:T(128)}, u32[]{:S(2)}) copy-start(f32[16]{0:T(128)} %param.14) | copy-start | bytes 196
  13.5 6.8 %collective-permute-start.6 = (f32[168,128]{1,0:T(8,128)S(1)}, f32[168,128]{1,0:T(8,128)S(1)}, u32[]{:S(2)}, u32[]{:S(2)}) collective-permute-start(f32[168,128]{1,0:T(8,128)S(1)} %get-tuple-element.38), channel_id=1, source_target_pairs={{12,0},{8,4},{4,8},{0,12},{13,1},{9,5},{5,9},{1,13},{14,2},{10,6},... | collective-permute-start | bytes 258056 | tf_op jit(solution)/shard_map/ppermute | solution.py:750
  21.6 11.1 %all-to-all-start = ((f32[4,104,128]{2,1,0:T(8,128)}), f32[4,104,128]{2,1,0:T(8,128)S(1)}, u32[]{:S(2)}, u32[]{:S(2)}) async-start(f32[4,104,128]{2,1,0:T(8,128)} %get-tuple-element.54), calls=%async_computation | async-start | bytes 425984 | tf_op jit(solution)/shard_map/all_to_all | solution.py:794
  32.7 14.1 %all-to-all-start.1 = ((f32[4,200,128]{2,1,0:T(8,128)}), f32[4,200,128]{2,1,0:T(8,128)S(1)}, u32[]{:S(2)}, u32[]{:S(2)}) async-start(f32[4,200,128]{2,1,0:T(8,128)} %get-tuple-element.55.refs_0_), calls=%async_computation.1 | async-start | bytes 819200 | tf_op jit(solution)/shard_map/all_to_all | solution.py:794
  37.0 10.2 %collective-permute-start.9 = (f32[128,128]{1,0:T(8,128)S(1)}, f32[128,128]{1,0:T(8,128)S(1)}, u32[]{:S(2)}, u32[]{:S(2)}) collective-permute-start(f32[128,128]{1,0:T(8,128)S(1)} %get-tuple-element.58), channel_id=1, source_target_pairs={{1,2},{2,1},{3,4},{4,3},{5,6},{6,5},{7,8},{8,7},{9,10},{10,9},{11,... | collective-permute-start | bytes 196616 | tf_op jit(solution)/shard_map/ppermute | solution.py:718
  42.6 4.6 %collective-permute-start.8 = (f32[96,128]{1,0:T(8,128)S(1)}, f32[96,128]{1,0:T(8,128)S(1)}, u32[]{:S(2)}, u32[]{:S(2)}) collective-permute-start(f32[96,128]{1,0:T(8,128)S(1)} %get-tuple-element.57), channel_id=1, source_target_pairs={{1,0},{0,1},{3,2},{2,3},{5,4},{4,5},{7,6},{6,7},{9,8},{8,9},{11,10... | collective-permute-start | bytes 147464 | tf_op jit(solution)/shard_map/ppermute | solution.py:719
  47.6 9.2 %collective-permute-start.11 = (f32[128,128]{1,0:T(8,128)S(1)}, f32[128,128]{1,0:T(8,128)S(1)}, u32[]{:S(2)}, u32[]{:S(2)}) collective-permute-start(f32[128,128]{1,0:T(8,128)S(1)} %get-tuple-element.62), channel_id=1, source_target_pairs={{1,2},{2,1},{3,4},{4,3},{5,6},{6,5},{7,8},{8,7},{9,10},{10,9},{11,... | collective-permute-start | bytes 196616 | tf_op jit(solution)/shard_map/ppermute | solution.py:718
  52.2 1.4 %collective-permute-start.10 = (f32[96,128]{1,0:T(8,128)S(1)}, f32[96,128]{1,0:T(8,128)S(1)}, u32[]{:S(2)}, u32[]{:S(2)}) collective-permute-start(f32[96,128]{1,0:T(8,128)S(1)} %get-tuple-element.61), channel_id=1, source_target_pairs={{1,0},{0,1},{3,2},{2,3},{5,4},{4,5},{7,6},{6,7},{9,8},{8,9},{11,10... | collective-permute-start | bytes 147464 | tf_op jit(solution)/shard_map/ppermute | solution.py:719

commit v12 on v11

--- a/solution.py
+++ b/solution.py
@@ -76,7 +76,7 @@
     return jnp.where(odd, to_last, to_next), jnp.where(odd, to_next, to_last)
 
 
-def pack_start_body(state, message_a, message_b, along_x):
+def pack_start_body(state, message_a, message_b, along_x, y_a, y_b):
     odd = is_odd("fz")
     rows = state[...].reshape(-1, 128)
     count = rows.shape[0]
@@ -93,9 +93,18 @@
         for s, x in enumerate(x_planes(cells_x)):
             at = (f * 2 * HALO + s) * 8
             along_x[at : at + 8] = state[f, x]
-
-
-def pack_next_body(state, sent_a, sent_b, got_a, got_b, _, edge):
+        for x in range(cells_x):
+            put_rows(y_a, y_b, (f * cells_x + x) * HALO, state[f, x], HALO)
+
+
+def put_rows(message_a, message_b, at, values, height):
+    first, second = paired(is_odd("fy"), values[8 - height : 8], values[0:height])
+    message_a[at : at + height] = first
+    message_b[at : at + height] = second
+
+
+def pack_next_body(state, sent_a, sent_b, got_a, got_b, faces, _, edge, far_faces):
+    far_faces[...] = faces[...]
     cells_x = state.shape[1]
     odd_z = is_odd("fz")
     high, low = paired(odd_z, sent_a[...], sent_b[...])
@@ -135,35 +144,24 @@
     return jnp.where(lane < 64, after[at : at + 8], before[at : at + 8])
 
 
-def pack_last_body(state, edge, *refs):
+def pack_last_body(edge, *refs):
     (y_a, y_b), refs = refs[-2:], refs[:-2]
     beside_x, edges_x = refs[: len(refs) // 2], refs[len(refs) // 2 :]
-    cells_x = state.shape[1]
-    odd = is_odd("fy")
     after, before = sides_of(beside_x)
-
-    def put(at, values, height):
-        first, second = paired(odd, values[8 - height : 8], values[0:height])
-        y_a[at : at + height] = first
-        y_b[at : at + height] = second
-
-    lines = 5 * cells_x * HALO
     for f in range(5):
-        for x in range(cells_x):
-            put((f * cells_x + x) * HALO, state[f, x], HALO)
-        at = lines + f * 6
+        at = f * 6
         for slot, height in ((1, 1), (2, 2), (3, 2), (4, 1)):
             source = (f * 2 * HALO + slot) * 8
-            put(at, (before if slot < HALO else after)[source : source + 8], height)
+            values = (before if slot < HALO else after)[source : source + 8]
+            put_rows(y_a, y_b, at, values, height)
             at += height
-        put(lines + 30 + f * 2, edge[f * 8 : f * 8 + 8], 2)
-        put(lines + 40 + f, beyond(edges_x, f), 1)
-
-
-def assemble(wide, rim, state, edge, beside_x, edges_x, above, below):
+        put_rows(y_a, y_b, 30 + f * 2, edge[f * 8 : f * 8 + 8], 2)
+        put_rows(y_a, y_b, 40 + f, beyond(edges_x, f), 1)
+
+
+def assemble(wide, state, beside_x, above, below):
     cells_x = state.shape[1]
     after, before = sides_of(beside_x)
-    lines = 5 * cells_x * HALO
     for f in range(5):
         for x in range(cells_x):
             wide[f, HALO + x, 0:8] = state[f, x]
@@ -174,7 +172,12 @@
             plane = slot if slot < HALO else cells_x + slot
             at = (f * 2 * HALO + slot) * 8
             wide[f, plane, 0:8] = (before if slot < HALO else after)[at : at + 8]
-        at = lines + f * 6
+
+
+def assemble_rest(wide, rim, edge, edges_x, above, below):
+    cells_x = wide.shape[1] - 2 * HALO
+    for f in range(5):
+        at = f * 6
         for slot, height in ((1, 1), (2, 2), (3, 2), (4, 1)):
             plane = slot if slot < HALO else cells_x + slot
             wide[f, plane, 8 : 8 + height] = above[at : at + height]
@@ -182,10 +185,10 @@
             at += height
         rim[f, 0:8, 0:128] = edge[f * 8 : f * 8 + 8]
         rim[f, 0:8, 128:256] = beyond(edges_x, f)
-        at = lines + 30 + f * 2
+        at = 30 + f * 2
         rim[f, 8:10, 0:128] = above[at : at + 2]
         rim[f, 14:16, 0:128] = below[at : at + 2]
-        at = lines + 40 + f
+        at = 40 + f
         rim[f, 8:9, 128:256] = above[at : at + 1]
         rim[f, 15:16, 128:256] = below[at : at + 1]
 
@@ -353,15 +356,16 @@
 
 
 def flow_sources_body(count, state, edge, *refs):
-    beside_x, edges_x, refs = refs[:count], refs[count : 2 * count], refs[2 * count :]
+    beside_x, refs = refs[:count], refs[count:]
     got_a, got_b, pair, spread, labels, _ = refs[:6]
-    wide, rim, send, derived, lamb_rows, ends, above, below = refs[6:]
+    wide, send, derived, lamb_rows, ends, above, below = refs[6:]
     cells_x = state.shape[1]
     above[...], below[...] = paired(is_odd("fy"), got_a[...], got_b[...])
-    assemble(wide, rim, state, edge, beside_x, edges_x, above, below)
+    assemble(wide, state, beside_x, above, below)
     derive_speeds(wide, derived, HALO - 1, HALO + cells_x + 1)
-    inverse = 1.0 / rim[0, 0:8]
-    to_ends([rim[1, 0:8] * inverse, rim[2, 0:8] * inverse], 3, 8, 0, cells_x, ends)
+    inverse = 1.0 / edge[0:8]
+    speeds = [jnp.concatenate([edge[k * 8 : k * 8 + 8] * inverse] * 2, 1) for k in (1, 2)]
+    to_ends(speeds, 3, 8, 0, cells_x, ends)
     lamb(derived, ends, HALO, cells_x, lamb_rows)
     project(lamb_rows, pair, spread, send, 0)
     send[:, send.shape[1] - 8 :] = labels[...]
@@ -374,7 +378,13 @@
     return write
 
 
-def flow_stages_body(wide, rim, pair, spread, labels, second, derived, ends_out, send, lamb_rows, ends, first):
+def flow_stages_body(count, start, edge, *refs):
+    edges_x, refs = refs[:count], refs[count:]
+    got_a, got_b, pair, spread, labels, second, derived, ends_out, send, *refs = refs
+    lamb_rows, ends, first, wide, rim, above, below = refs
+    above[...], below[...] = paired(is_odd("fy"), got_a[...], got_b[...])
+    wide[...] = start[...]
+    assemble_rest(wide, rim, edge, edges_x, above, below)
     planes = wide.shape[1]
     cells_x = planes - 2 * HALO
     size = (send.shape[1] - 8) // 2
@@ -425,7 +435,8 @@
     size = message_a.shape[0]
     faces_out(state, message_b, message_a)
     message_a[...], message_b[0:size] = paired(odd, message_a[...], message_b[0:size])
-    message_b[size:] = jnp.zeros((message_b.shape[0] - size, 128), F32)
+    if message_b.shape[0] > size:
+        message_b[size:] = jnp.zeros((message_b.shape[0] - size, 128), F32)
 
 
 def lift(total, before, after, sides, factor):
@@ -703,13 +714,20 @@
     state = jnp.pad(density[None], ((0, 4),) + rest) + jnp.pad(density * velocity, ((1, 1),) + rest)
     state = state + jnp.pad(energy[None], ((4, 0),) + rest)
     x_rows = 5 * 2 * HALO * 8
-    flow_a, flow_b, along_x = call(
-        pack_start_body, [(tiles * 8, 128), (tiles * 8, 128), (x_rows, 128)], state
+    y_shape, y_last_shape = (5 * cells_x * HALO, 128), (48, 128)
+    flow_a, flow_b, along_x, y_a, y_b = call(
+        pack_start_body, [(tiles * 8, 128), (tiles * 8, 128), (x_rows, 128), y_shape, y_shape], state
     )
     edge_a = lax.ppermute(flow_a, "fz", partners((size_z,), 0, False))
     edge_b = lax.ppermute(flow_b, "fz", partners((size_z,), 0, True))
     x_steps = (1,) if size_x == 2 else (1, -1)
     beside_x = [lax.ppermute(along_x, "fx", shifted((size_x,), (step,))) for step in x_steps]
+
+    def along_y(to_a, to_b):
+        second = lax.ppermute(to_b, "fy", partners((size_y,), 0, True))
+        return lax.ppermute(to_a, "fy", partners((size_y,), 0, False)), second
+
+    y_first, y_second = along_y(y_a, y_b)
 
     near_pairs = [(i ^ 1, i) for i in range(devices)]
     far_pairs = [pair for i in range(1, devices - 1, 2) for pair in ((i, i + 1), (i + 1, i))]
@@ -725,30 +743,30 @@
     turning = [pltpu.VMEM((512, 128), F32), pltpu.VMEM((4, 4 * elements, 128), F32)]
     sound, to_a, to_b = call(
         acoustic_start_body,
-        [held, faces, (2 * faces[0], size)],
+        [held, faces, faces],
         acoustic,
         edge_a,
         scratch=turning,
         last=1,
     )
-    got_a, got_b = traces(to_a, to_b)
-
-    edge = call(
+    got_a = lax.ppermute(to_a, names, near_pairs)
+
+    edge, to_b = call(
         pack_next_body,
-        [(40, 128)],
+        [(40, 128), to_b.shape],
         state,
         flow_a,
         flow_b,
         edge_a,
         edge_b,
+        to_b,
         got_a,
         last=1,
-    )[0]
+    )
+    got_b = lax.ppermute(to_b, names, far_pairs)
     edges_x = [lax.ppermute(edge, "fx", shifted((size_x,), (step,))) for step in x_steps]
-    y_shape = (5 * cells_x * HALO + 48, 128)
-    y_a, y_b = call(pack_last_body, [y_shape, y_shape], state, edge, *beside_x, *edges_x, cost=1)
-    y_second = lax.ppermute(y_b, "fy", partners((size_y,), 0, True))
-    y_first = lax.ppermute(y_a, "fy", partners((size_y,), 0, False))
+    y_a, y_b = call(pack_last_body, [y_last_shape] * 2, edge, *beside_x, *edges_x, cost=1)
+    y_first_last, y_second_last = along_y(y_a, y_b)
 
     local = (neighbours - device * elements).T
     blocks = block_owner.size
@@ -793,13 +811,12 @@
     def route(send):
         return lax.all_to_all(send, "fy", split_axis=0, concat_axis=0, tiled=True)
 
-    start, rim, send = call(
+    start, send = call(
         functools.partial(flow_sources_body, len(beside_x)),
-        [planes(wide), (5, 16, 256), (size_y, 192 // fold + 8, 128)],
+        [planes(wide), (size_y, 192 // fold + 8, 128)],
         state,
         edge,
         *beside_x,
-        *edges_x,
         y_first,
         y_second,
         pair,
@@ -817,7 +834,7 @@
     )
     received = route(send)
     second, derived, ends, send = call(
-        flow_stages_body,
+        functools.partial(flow_stages_body, len(edges_x)),
         [
             planes(wide - 4),
             planes(wide),
@@ -825,11 +842,22 @@
             (size_y, 2 * 192 // fold + 8, 128),
         ],
         start,
-        rim,
+        edge,
+        *edges_x,
+        y_first_last,
+        y_second_last,
         pair,
         spread,
         labels,
-        scratch=[rows_scratch, pltpu.VMEM(planes(wide - 2), F32), pltpu.VMEM(planes(wide - 2), F32)],
+        scratch=[
+            rows_scratch,
+            pltpu.VMEM(planes(wide - 2), F32),
+            pltpu.VMEM(planes(wide - 2), F32),
+            pltpu.VMEM(planes(wide), F32),
+            pltpu.VMEM((5, 16, 256), F32),
+            pltpu.VMEM(y_last_shape, F32),
+            pltpu.VMEM(y_last_shape, F32),
+        ],
     )
 
     def local_part(mix, now):

time: 58.5 us -> 65.6 us (1.12)
  waiting for transfers between devices: 15.6 us -> 23 us
  starting transfers between devices: 27.6 us -> 26.8 us
    ppermute x2 -> x6, starting transfers between devices: 1.45 us -> 12.4 us  [the longest x2 4.84 us: along_y(): second = lax.ppermute(to_b, 'fy', partners((size_y,), 0, True))]
    ppermute x3 -> x2, starting transfers between devices: 15.1 us -> 4.96 us  [traces(): far_got = lax.ppermute(to_b, names, far_pairs)]
    ppermute x2 -> x6, waiting for transfers between devices: 1.64 us -> 7.95 us  [the longest x1 4.05 us: per_device(): got_b = lax.ppermute(to_b, names, far_pairs)]
    ppermute x1, waiting for transfers between devices: 0.01 us -> 3.77 us  [per_device(): lax.ppermute(edge, 'fx', shifted((size_x,), (step,)))]
    all_to_all x2, waiting for transfers between devices: 7.48 us -> 5.44 us  [route(): return lax.all_to_all(send, 'fy', split_axis=0, concat_axis=0, tiled=True)]
    ppermute x1, starting transfers between devices: 1.56 us -> 0.07 us  [per_device(): lax.ppermute(edge, 'fx', shifted((size_x,), (step,)))]
    ppermute x3 -> x2, waiting for transfers between devices: 5.85 us -> 5.81 us  [traces(): far_got = lax.ppermute(to_b, names, far_pairs)]
  transfers between devices with their start and end apart: 14 -> 16, of which waited for: 6 -> 7; matrix products, arithmetic and copies ran while one was open for 0% -> 0% of each run, Pallas kernels for 15% -> 13%
where the time goes in v12:
time: 65.6 us; the launch traced here: 65.2 us
  starting transfers between devices  26.8 us (41%)
  waiting for transfers between devices  23 us (35%)
  Pallas kernels  11.5 us (18%)
  local copies, waits for them, and re-layouts  1.94 us (3%)
  other arithmetic  1.01 us (2%)
  between operations  0.92 us (1%)
    pallas_call x15, Pallas kernels, call(): pl.pallas_call(body, out_shape=outs, in_specs=[whole] * (len(operands) -...  11.5 us
    all_to_all x2, starting transfers between devices, route(): return lax.all_to_all(send, 'fy', split_axis=0, concat_axis=0, tiled=True)  7 us
    ppermute x2, waiting for transfers between devices, traces(): far_got = lax.ppermute(to_b, names, far_pairs)  5.81 us
    all_to_all x2, waiting for transfers between devices, route(): return lax.all_to_all(send, 'fy', split_axis=0, concat_axis=0, tiled=True)  5.44 us
    ppermute x2, starting transfers between devices, traces(): far_got = lax.ppermute(to_b, names, far_pairs)  4.96 us
    ppermute x2, starting transfers between devices, along_y(): second = lax.ppermute(to_b, 'fy', partners((size_y,), 0, True))  4.84 us
    ppermute x1, waiting for transfers between devices, per_device(): got_b = lax.ppermute(to_b, names, far_pairs)  4.05 us
    ppermute x1, starting transfers between devices, per_device(): got_b = lax.ppermute(to_b, names, far_pairs)  3.89 us
  transfers between devices with their start and end apart: 16, of which 7 were waited for; matrix products, arithmetic and copies ran while one was open for 0% of the time, Pallas kernels for 13%

profile of v12, /device:TPU:2, one launch (start us, length us, event | category | flops | bytes accessed | tf_op | source)
XLA Modules:
  0.0 65.2 jit_solution(5841991038999879283)
XLA Ops:
  0.7 1.0 %broadcast_multiply_fusion = f32[3,8,8,128]{3,2,1,0:T(8,128)S(1)} fusion(f32[3,8,8,128]{3,2,1,0:T(8,128)} %param.11, f32[8,8,128]{2,1,0:T(8,128)} %param.10), kind=kLoop, calls=%fused_computation.1 | loop fusion | flops 24576 | bytes 229376 | tf_op jit(solution)/shard_map/mul | solution.py:714
  1.9 1.6 %collective-permute-start.1 = (f32[24,128]{1,0:T(8,128)S(1)}, f32[24,128]{1,0:T(8,128)S(1)}, u32[]{:S(2)}, u32[]{:S(2)}) collective-permute-start(f32[24,128]{1,0:T(8,128)S(1)} %get-tuple-element.37.sent_b), channel_id=1, source_target_pairs={{3,0},{2,1},{1,2},{0,3},{7,4},{6,5},{5,6},{4,7},{11,8},{10,9},{9,1... | collective-permute-start | bytes 36872 | tf_op jit(solution)/shard_map/ppermute | solution.py:722
  3.5 0.5 collective-permute-start.3
  4.1 1.6 %collective-permute-start.4 = (f32[120,128]{1,0:T(8,128)S(1)}, f32[120,128]{1,0:T(8,128)S(1)}, u32[]{:S(2)}, u32[]{:S(2)}) collective-permute-start(f32[120,128]{1,0:T(8,128)S(1)} %get-tuple-element.42), channel_id=1, source_target_pairs={{4,0},{0,4},{12,8},{8,12},{5,1},{1,5},{13,9},{9,13},{6,2},{2,6},{1... | collective-permute-start | bytes 184328 | tf_op jit(solution)/shard_map/ppermute | solution.py:728
  5.7 2.5 %collective-permute-start.5 = (f32[120,128]{1,0:T(8,128)S(1)}, f32[120,128]{1,0:T(8,128)S(1)}, u32[]{:S(2)}, u32[]{:S(2)}) collective-permute-start(f32[120,128]{1,0:T(8,128)S(1)} %get-tuple-element.43), channel_id=1, source_target_pairs={{12,0},{8,4},{4,8},{0,12},{13,1},{9,5},{5,9},{1,13},{14,2},{10,6},... | collective-permute-start | bytes 184328 | tf_op jit(solution)/shard_map/ppermute | solution.py:727
  8.1 0.7 %copy-done.4 = s32[16,6]{0,1:T(8,128)S(1)} copy-done((s32[16,6]{0,1:T(8,128)S(1)}, s32[16,6]{0,1:T(8,128)}, u32[]{:S(2)}) %copy-start.4) | copy-done | bytes 408
  8.8 0.6 copy-done.8
  9.5 0.6 shard_map.114
  10.1 0.6 copy-done.9
  10.7 0.6 collective-permute-done.2._.got_a
  11.5 3.9 %collective-permute-start.6 = (f32[96,128]{1,0:T(8,128)S(1)}, f32[96,128]{1,0:T(8,128)S(1)}, u32[]{:S(2)}, u32[]{:S(2)}) collective-permute-start(f32[96,128]{1,0:T(8,128)S(1)} %get-tuple-element.47), channel_id=1, source_target_pairs={{1,2},{2,1},{3,4},{4,3},{5,6},{6,5},{7,8},{8,7},{9,10},{10,9},{11,... | collective-permute-start | bytes 147464 | tf_op jit(solution)/shard_map/ppermute | solution.py:766
  15.5 1.0 %shard_map.116 = (bf16[5,128,128]{2,1,0:T(8,128)(2,1)S(1)}, bf16[5,128,128]{2,1,0:T(8,128)(2,1)S(1)}, f32[128,64]{1,0:T(8,128)S(1)}, f32[128,128]{1,0:T(8,128)S(...) custom-call(f32[32,16]{1,0:T(8,128)S(1)} %pad_add_fusion.1.packed), custom_call_target="tpu_custom_call" | custom-call | flops 1 | bytes 1 | tf_op jit(solution)/shard_map/pallas_call | solution.py:52
  16.5 4.0 %collective-permute-done.6.refs_6_.got_b = f32[96,128]{1,0:T(8,128)S(1)} collective-permute-done((f32[96,128]{1,0:T(8,128)S(1)}, f32[96,128]{1,0:T(8,128)S(1)}, u32[]{:S(2)}, u32[]{:S(2)}) %collective-permute-start.6) | collective-permute-done | bytes 49184 | tf_op jit(solution)/shard_map/ppermute | solution.py:766
  20.5 1.3 %shard_map.117 = (f32[5,14,16,128]{3,2,1,0:T(8,128)S(1)}, f32[4,104,128]{2,1,0:T(8,128)}) custom-call(f32[5,8,8,128]{3,2,1,0:T(8,128)S(1)} %pad_add_fusion.state, f32[40,128]{1,0:T(8,128)S(1)} %get-tuple-element.40.edge, f32[240,128]{1,0:T(8,128)S(1)} %collective-permute-done.3.refs_0_, f32[120,128]{1,0:T(8,128)S(1)} %collective-permute-done.4.refs_1_, ...), custom_call_target="tpu_custom_call" | custom-call | tf_op jit(solution)/shard_map/pallas_call | solution.py:52
  21.8 3.4 %all-to-all-start = ((f32[4,104,128]{2,1,0:T(8,128)}), f32[4,104,128]{2,1,0:T(8,128)S(1)}, u32[]{:S(2)}, u32[]{:S(2)}) async-start(f32[4,104,128]{2,1,0:T(8,128)} %get-tuple-element.60), calls=%async_computation | async-start | bytes 425984 | tf_op jit(solution)/shard_map/all_to_all | solution.py:812
  25.3 3.8 %collective-permute-done.7.refs_1_.refs_0_ = f32[40,128]{1,0:T(8,128)S(1)} collective-permute-done((f32[40,128]{1,0:T(8,128)S(1)}, f32[40,128]{1,0:T(8,128)S(1)}, u32[]{:S(2)}, u32[]{:S(2)}) %collective-permute-start.7) | collective-permute-done | bytes 20512 | tf_op jit(solution)/shard_map/ppermute | solution.py:767
  29.1 2.0 %collective-permute-start.8 = (f32[48,128]{1,0:T(8,128)S(1)}, f32[48,128]{1,0:T(8,128)S(1)}, u32[]{:S(2)}, u32[]{:S(2)}) collective-permute-start(f32[48,128]{1,0:T(8,128)S(1)} %get-tuple-element.49), channel_id=1, source_target_pairs={{4,0},{0,4},{12,8},{8,12},{5,1},{1,5},{13,9},{9,13},{6,2},{2,6},{1... | collective-permute-start | bytes 73736 | tf_op jit(solution)/shard_map/ppermute | solution.py:728
  31.1 2.4 %collective-permute-start.9 = (f32[48,128]{1,0:T(8,128)S(1)}, f32[48,128]{1,0:T(8,128)S(1)}, u32[]{:S(2)}, u32[]{:S(2)}) collective-permute-start(f32[48,128]{1,0:T(8,128)S(1)} %get-tuple-element.50), channel_id=1, source_target_pairs={{12,0},{8,4},{4,8},{0,12},{13,1},{9,5},{5,9},{1,13},{14,2},{10,6},... | collective-permute-start | bytes 73736 | tf_op jit(solution)/shard_map/ppermute | solution.py:727
  33.4 3.3 %collective-permute-done.9.refs_2_ = f32[48,128]{1,0:T(8,128)S(1)} collective-permute-done((f32[48,128]{1,0:T(8,128)S(1)}, f32[48,128]{1,0:T(8,128)S(1)}, u32[]{:S(2)}, u32[]{:S(2)}) %collective-permute-start.9) | collective-permute-done | bytes 24608 | tf_op jit(solution)/shard_map/ppermute | solution.py:727
  36.7 3.9 %shard_map.119 = (f32[5,10,16,128]{3,2,1,0:T(8,128)S(1)}, f32[5,14,16,128]{3,2,1,0:T(8,128)S(1)}, f32[5,8,8,128]{3,2,1,0:T(8,128)S(1)}, f32[4,200,128]{2,1,0:T(8,128)}) custom-call(f32[5,14,16,128]{3,2,1,0:T(8,128)S(1)} %get-tuple-element.48.start.wide, f32[40,128]{1,0:T(8,128)S(1)} %get-tuple-element.40.edge, ...), custom_call_target="tpu_custom_call" | custom-call | tf_op jit(solution)/shard_map/pallas_call | solution.py:52
  40.6 3.6 %all-to-all-start.1 = ((f32[4,200,128]{2,1,0:T(8,128)}), f32[4,200,128]{2,1,0:T(8,128)S(1)}, u32[]{:S(2)}, u32[]{:S(2)}) async-start(f32[4,200,128]{2,1,0:T(8,128)} %get-tuple-element.61.refs_0_), calls=%async_computation.1 | async-start | bytes 819200 | tf_op jit(solution)/shard_map/all_to_all | solution.py:812
  44.5 0.5 shard_map.122
  45.1 2.3 %collective-permute-start.11 = (f32[128,128]{1,0:T(8,128)S(1)}, f32[128,128]{1,0:T(8,128)S(1)}, u32[]{:S(2)}, u32[]{:S(2)}) collective-permute-start(f32[128,128]{1,0:T(8,128)S(1)} %get-tuple-element.64), channel_id=1, source_target_pairs={{1,2},{2,1},{3,4},{4,3},{5,6},{6,5},{7,8},{8,7},{9,10},{10,9},{11,... | collective-permute-start | bytes 196616 | tf_op jit(solution)/shard_map/ppermute | solution.py:736
  47.5 0.3 shard_map.123.partial
  47.8 5.4 %all-to-all-done.1.received = f32[4,200,128]{2,1,0:T(8,128)S(1)} async-done(((f32[4,200,128]{2,1,0:T(8,128)}), f32[4,200,128]{2,1,0:T(8,128)S(1)}, u32[]{:S(2)}, u32[]{:S(2)}) %all-to-all-start.1) | async-done | bytes 409632 | tf_op jit(solution)/shard_map/all_to_all | solution.py:812
  53.3 0.4 shard_map.124
  53.6 0.7 %collective-permute-done.11.got_b = f32[128,128]{1,0:T(8,128)S(1)} collective-permute-done((f32[128,128]{1,0:T(8,128)S(1)}, f32[128,128]{1,0:T(8,128)S(1)}, u32[]{:S(2)}, u32[]{:S(2)}) %collective-permute-start.11) | collective-permute-done | bytes 65568 | tf_op jit(solution)/shard_map/ppermute | solution.py:736
  54.4 0.3 shard_map.125
  54.7 2.6 %collective-permute-start.13 = (f32[128,128]{1,0:T(8,128)S(1)}, f32[128,128]{1,0:T(8,128)S(1)}, u32[]{:S(2)}, u32[]{:S(2)}) collective-permute-start(f32[128,128]{1,0:T(8,128)S(1)} %get-tuple-element.68), channel_id=1, source_target_pairs={{1,2},{2,1},{3,4},{4,3},{5,6},{6,5},{7,8},{8,7},{9,10},{10,9},{11,... | collective-permute-start | bytes 196616 | tf_op jit(solution)/shard_map/ppermute | solution.py:736
  57.4 1.0 %shard_map.120 = f32[5,8,8,128]{3,2,1,0:T(8,128)} custom-call(f32[5,10,16,128]{3,2,1,0:T(8,128)S(1)} %get-tuple-element.51.second, f32[5,14,16,128]{3,2,1,0:T(8,128)S(1)} %get-tuple-element.52.derived, f32[5,8,8,128]{3,2,1,0:T(8,128)S(1)} %get-tuple-element.53.ends, f32[5,14,16,128]{3,2,1,0:T(8,128)S(1)} %get-tuple-element.48.start.wide), custom_call_target="tpu_custom_call" | custom-call | tf_op jit(solution)/shard_map/pallas_call | solution.py:52
  58.8 5.1 %collective-permute-done.13.got_b = f32[128,128]{1,0:T(8,128)S(1)} collective-permute-done((f32[128,128]{1,0:T(8,128)S(1)}, f32[128,128]{1,0:T(8,128)S(1)}, u32[]{:S(2)}, u32[]{:S(2)}) %collective-permute-start.13) | collective-permute-done | bytes 65568 | tf_op jit(solution)/shard_map/ppermute | solution.py:736
  63.9 1.3 %shard_map.127 = f32[16,4,512]{2,1,0:T(4,128)} custom-call(f32[4,64,128]{2,1,0:T(8,128)S(1)} %shard_map.126.partial, f32[96,128]{1,0:T(8,128)S(1)} %collective-permute-done.12.got_a, f32[128,128]{1,0:T(8,128)S(1)} %collective-permute-done.13.got_b, bf16[5,128,128]{2,1,0:T(8,128)(2,1)S(1)} %get-tuple-element.59.sides_far, ...), custom_call_target="tpu_custom_call" | custom-call | tf_op jit(solution)/shard_map/pallas_call | solution.py:52
  (42 shorter events, 1.4 us)
Async XLA Ops:
  0.6 1.0 %copy-start.2 = (f32[8,8,128]{2,1,0:T(8,128)S(1)}, f32[8,8,128]{2,1,0:T(8,128)}, u32[]{:S(2)}) copy-start(f32[8,8,128]{2,1,0:T(8,128)} %param.10) | copy-start | bytes 98308
  0.6 1.0 %copy-start.1 = (f32[3,8,8,128]{3,2,1,0:T(8,128)S(1)}, f32[3,8,8,128]{3,2,1,0:T(8,128)}, u32[]{:S(2)}) copy-start(f32[3,8,8,128]{3,2,1,0:T(8,128)} %param.11) | copy-start | bytes 294916
  0.6 1.0 %copy-start.3 = (f32[8,8,128]{2,1,0:T(8,128)S(1)}, f32[8,8,128]{2,1,0:T(8,128)}, u32[]{:S(2)}) copy-start(f32[8,8,128]{2,1,0:T(8,128)} %param.12) | copy-start | bytes 98308
  1.7 7.8 %copy-start = (f32[16,4,512]{2,1,0:T(4,128)S(1)}, f32[16,4,512]{2,1,0:T(4,128)}, u32[]{:S(2)}) copy-start(f32[16,4,512]{2,1,0:T(4,128)} %given.1) | copy-start | bytes 393220
  1.8 7.7 %collective-permute-start = (f32[24,128]{1,0:T(8,128)S(1)}, f32[24,128]{1,0:T(8,128)S(1)}, u32[]{:S(2)}, u32[]{:S(2)}) collective-permute-start(f32[24,128]{1,0:T(8,128)S(1)} %get-tuple-element.36.sent_a), channel_id=1, source_target_pairs={{1,0},{0,1},{3,2},{2,3},{5,4},{4,5},{7,6},{6,7},{9,8},{8,9},{11,10... | collective-permute-start | bytes 36872 | tf_op jit(solution)/shard_map/ppermute | solution.py:721
  1.9 8.8 %collective-permute-start.1 = (f32[24,128]{1,0:T(8,128)S(1)}, f32[24,128]{1,0:T(8,128)S(1)}, u32[]{:S(2)}, u32[]{:S(2)}) collective-permute-start(f32[24,128]{1,0:T(8,128)S(1)} %get-tuple-element.37.sent_b), channel_id=1, source_target_pairs={{3,0},{2,1},{1,2},{0,3},{7,4},{6,5},{5,6},{4,7},{11,8},{10,9},{9,1... | collective-permute-start | bytes 36872 | tf_op jit(solution)/shard_map/ppermute | solution.py:722
  3.5 17.0 %collective-permute-start.3 = (f32[240,128]{1,0:T(8,128)S(1)}, f32[240,128]{1,0:T(8,128)S(1)}, u32[]{:S(2)}, u32[]{:S(2)}) collective-permute-start(f32[240,128]{1,0:T(8,128)S(1)} %get-tuple-element.41), channel_id=1, source_target_pairs={{16,0},{0,16},{17,1},{1,17},{18,2},{2,18},{19,3},{3,19},{20,4},{4,... | collective-permute-start | bytes 368648 | tf_op jit(solution)/shard_map/ppermute | solution.py:724
  4.1 12.4 %collective-permute-start.4 = (f32[120,128]{1,0:T(8,128)S(1)}, f32[120,128]{1,0:T(8,128)S(1)}, u32[]{:S(2)}, u32[]{:S(2)}) collective-permute-start(f32[120,128]{1,0:T(8,128)S(1)} %get-tuple-element.42), channel_id=1, source_target_pairs={{4,0},{0,4},{12,8},{8,12},{5,1},{1,5},{13,9},{9,13},{6,2},{2,6},{1... | collective-permute-start | bytes 184328 | tf_op jit(solution)/shard_map/ppermute | solution.py:728
  5.7 10.8 %collective-permute-start.5 = (f32[120,128]{1,0:T(8,128)S(1)}, f32[120,128]{1,0:T(8,128)S(1)}, u32[]{:S(2)}, u32[]{:S(2)}) collective-permute-start(f32[120,128]{1,0:T(8,128)S(1)} %get-tuple-element.43), channel_id=1, source_target_pairs={{12,0},{8,4},{4,8},{0,12},{13,1},{9,5},{5,9},{1,13},{14,2},{10,6},... | collective-permute-start | bytes 184328 | tf_op jit(solution)/shard_map/ppermute | solution.py:727
  8.1 0.7 %copy-start.4 = (s32[16,6]{0,1:T(8,128)S(1)}, s32[16,6]{0,1:T(8,128)}, u32[]{:S(2)}) copy-start(s32[16,6]{0,1:T(8,128)} %param.17) | copy-start | bytes 1156
  8.8 0.7 %copy-start.8 = (s32[1,1,1,16]{3,2,1,0:T(1,128)S(1)}, s32[1,1,1,16]{3,2,1,0:T(1,128)}, u32[]{:S(2)}) copy-start(s32[1,1,1,16]{3,2,1,0:T(1,128)} %param.19) | copy-start | bytes 196
  10.1 0.7 %copy-start.9 = (s32[1,1,1,16,1]{3,4,2,1,0:T(1,128)S(1)}, s32[1,1,1,16,1]{3,4,2,1,0:T(1,128)}, u32[]{:S(2)}) copy-start(s32[1,1,1,16,1]{3,4,2,1,0:T(1,128)} %param.18) | copy-start | bytes 196
  10.1 1.3 %collective-permute-start.2 = (f32[96,128]{1,0:T(8,128)S(1)}, f32[96,128]{1,0:T(8,128)S(1)}, u32[]{:S(2)}, u32[]{:S(2)}) collective-permute-start(f32[96,128]{1,0:T(8,128)S(1)} %get-tuple-element.39), channel_id=1, source_target_pairs={{1,0},{0,1},{3,2},{2,3},{5,4},{4,5},{7,6},{6,7},{9,8},{8,9},{11,10... | collective-permute-start | bytes 147464 | tf_op jit(solution)/shard_map/ppermute | solution.py:752
  11.4 4.0 %copy-start.5 = (f32[8,8]{1,0:T(8,128)S(1)}, f32[8,8]{1,0:T(8,128)}, u32[]{:S(2)}) copy-start(f32[8,8]{1,0:T(8,128)} %param.16) | copy-start | bytes 772
  11.4 4.1 %copy-start.6 = (f32[8,8]{1,0:T(8,128)S(1)}, f32[8,8]{1,0:T(8,128)}, u32[]{:S(2)}) copy-start(f32[8,8]{1,0:T(8,128)} %param.15) | copy-start | bytes 772
  11.5 3.9 %copy-start.7 = (f32[16]{0:T(128)S(1)}, f32[16]{0:T(128)}, u32[]{:S(2)}) copy-start(f32[16]{0:T(128)} %param.14) | copy-start | bytes 196
  11.5 9.0 %collective-permute-start.6 = (f32[96,128]{1,0:T(8,128)S(1)}, f32[96,128]{1,0:T(8,128)S(1)}, u32[]{:S(2)}, u32[]{:S(2)}) collective-permute-start(f32[96,128]{1,0:T(8,128)S(1)} %get-tuple-element.47), channel_id=1, source_target_pairs={{1,2},{2,1},{3,4},{4,3},{5,6},{6,5},{7,8},{8,7},{9,10},{10,9},{11,... | collective-permute-start | bytes 147464 | tf_op jit(solution)/shard_map/ppermute | solution.py:766
  21.8 18.7 %all-to-all-start = ((f32[4,104,128]{2,1,0:T(8,128)}), f32[4,104,128]{2,1,0:T(8,128)S(1)}, u32[]{:S(2)}, u32[]{:S(2)}) async-start(f32[4,104,128]{2,1,0:T(8,128)} %get-tuple-element.60), calls=%async_computation | async-start | bytes 425984 | tf_op jit(solution)/shard_map/all_to_all | solution.py:812
  25.2 3.8 %collective-permute-start.7 = (f32[40,128]{1,0:T(8,128)S(1)}, f32[40,128]{1,0:T(8,128)S(1)}, u32[]{:S(2)}, u32[]{:S(2)}) collective-permute-start(f32[40,128]{1,0:T(8,128)S(1)} %get-tuple-element.40.edge), channel_id=1, source_target_pairs={{16,0},{0,16},{17,1},{1,17},{18,2},{2,18},{19,3},{3,19},{20,4},{4,... | collective-permute-start | bytes 61448 | tf_op jit(solution)/shard_map/ppermute | solution.py:767
  29.1 4.4 %collective-permute-start.8 = (f32[48,128]{1,0:T(8,128)S(1)}, f32[48,128]{1,0:T(8,128)S(1)}, u32[]{:S(2)}, u32[]{:S(2)}) collective-permute-start(f32[48,128]{1,0:T(8,128)S(1)} %get-tuple-element.49), channel_id=1, source_target_pairs={{4,0},{0,4},{12,8},{8,12},{5,1},{1,5},{13,9},{9,13},{6,2},{2,6},{1... | collective-permute-start | bytes 73736 | tf_op jit(solution)/shard_map/ppermute | solution.py:728
  31.1 5.6 %collective-permute-start.9 = (f32[48,128]{1,0:T(8,128)S(1)}, f32[48,128]{1,0:T(8,128)S(1)}, u32[]{:S(2)}, u32[]{:S(2)}) collective-permute-start(f32[48,128]{1,0:T(8,128)S(1)} %get-tuple-element.50), channel_id=1, source_target_pairs={{12,0},{8,4},{4,8},{0,12},{13,1},{9,5},{5,9},{1,13},{14,2},{10,6},... | collective-permute-start | bytes 73736 | tf_op jit(solution)/shard_map/ppermute | solution.py:727
  40.6 12.7 %all-to-all-start.1 = ((f32[4,200,128]{2,1,0:T(8,128)}), f32[4,200,128]{2,1,0:T(8,128)S(1)}, u32[]{:S(2)}, u32[]{:S(2)}) async-start(f32[4,200,128]{2,1,0:T(8,128)} %get-tuple-element.61.refs_0_), calls=%async_computation.1 | async-start | bytes 819200 | tf_op jit(solution)/shard_map/all_to_all | solution.py:812
  45.1 9.3 %collective-permute-start.11 = (f32[128,128]{1,0:T(8,128)S(1)}, f32[128,128]{1,0:T(8,128)S(1)}, u32[]{:S(2)}, u32[]{:S(2)}) collective-permute-start(f32[128,128]{1,0:T(8,128)S(1)} %get-tuple-element.64), channel_id=1, source_target_pairs={{1,2},{2,1},{3,4},{4,3},{5,6},{6,5},{7,8},{8,7},{9,10},{10,9},{11,... | collective-permute-start | bytes 196616 | tf_op jit(solution)/shard_map/ppermute | solution.py:736
  47.4 6.2 %collective-permute-start.10 = (f32[96,128]{1,0:T(8,128)S(1)}, f32[96,128]{1,0:T(8,128)S(1)}, u32[]{:S(2)}, u32[]{:S(2)}) collective-permute-start(f32[96,128]{1,0:T(8,128)S(1)} %get-tuple-element.63), channel_id=1, source_target_pairs={{1,0},{0,1},{3,2},{2,3},{5,4},{4,5},{7,6},{6,7},{9,8},{8,9},{11,10... | collective-permute-start | bytes 147464 | tf_op jit(solution)/shard_map/ppermute | solution.py:737
  54.7 9.2 %collective-permute-start.13 = (f32[128,128]{1,0:T(8,128)S(1)}, f32[128,128]{1,0:T(8,128)S(1)}, u32[]{:S(2)}, u32[]{:S(2)}) collective-permute-start(f32[128,128]{1,0:T(8,128)S(1)} %get-tuple-element.68), channel_id=1, source_target_pairs={{1,2},{2,1},{3,4},{4,3},{5,6},{6,5},{7,8},{8,7},{9,10},{10,9},{11,... | collective-permute-start | bytes 196616 | tf_op jit(solution)/shard_map/ppermute | solution.py:736
  57.4 1.4 %collective-permute-start.12 = (f32[96,128]{1,0:T(8,128)S(1)}, f32[96,128]{1,0:T(8,128)S(1)}, u32[]{:S(2)}, u32[]{:S(2)}) collective-permute-start(f32[96,128]{1,0:T(8,128)S(1)} %get-tuple-element.67), channel_id=1, source_target_pairs={{1,0},{0,1},{3,2},{2,3},{5,4},{4,5},{7,6},{6,7},{9,8},{8,9},{11,10... | collective-permute-start | bytes 147464 | tf_op jit(solution)/shard_map/ppermute | solution.py:737

commit v13 on v11

--- a/solution.py
+++ b/solution.py
@@ -158,6 +158,20 @@
             at += height
         put(lines + 30 + f * 2, edge[f * 8 : f * 8 + 8], 2)
         put(lines + 40 + f, beyond(edges_x, f), 1)
+
+
+def assemble_speeds(wide, state, beside_x, above, below):
+    cells_x = state.shape[1]
+    after, before = sides_of(beside_x)
+    for f in range(4):
+        for x in range(cells_x):
+            wide[f, 1 + x, 0:8] = state[f, x]
+            at = (f * cells_x + x) * HALO
+            wide[f, 1 + x, 8:9] = above[at : at + 1]
+            wide[f, 1 + x, 15:16] = below[at + HALO - 1 : at + HALO]
+        for slot, plane, source in ((HALO - 1, 0, before), (HALO, cells_x + 1, after)):
+            at = (f * 2 * HALO + slot) * 8
+            wide[f, plane, 0:8] = source[at : at + 8]
 
 
 def assemble(wide, rim, state, edge, beside_x, edges_x, above, below):
@@ -353,16 +367,16 @@
 
 
 def flow_sources_body(count, state, edge, *refs):
-    beside_x, edges_x, refs = refs[:count], refs[count : 2 * count], refs[2 * count :]
-    got_a, got_b, pair, spread, labels, _ = refs[:6]
-    wide, rim, send, derived, lamb_rows, ends, above, below = refs[6:]
+    beside_x, refs = refs[:count], refs[count:]
+    got_a, got_b, pair, spread, labels, _, send, wide, derived, lamb_rows, ends, above, below = refs
     cells_x = state.shape[1]
     above[...], below[...] = paired(is_odd("fy"), got_a[...], got_b[...])
-    assemble(wide, rim, state, edge, beside_x, edges_x, above, below)
-    derive_speeds(wide, derived, HALO - 1, HALO + cells_x + 1)
-    inverse = 1.0 / rim[0, 0:8]
-    to_ends([rim[1, 0:8] * inverse, rim[2, 0:8] * inverse], 3, 8, 0, cells_x, ends)
-    lamb(derived, ends, HALO, cells_x, lamb_rows)
+    assemble_speeds(wide, state, beside_x, above, below)
+    derive_speeds(wide, derived, 0, cells_x + 2)
+    inverse = 1.0 / edge[0:8]
+    speeds = [jnp.concatenate([edge[k * 8 : k * 8 + 8] * inverse] * 2, 1) for k in (1, 2)]
+    to_ends(speeds, 3, 8, 0, cells_x, ends)
+    lamb(derived, ends, 1, cells_x, lamb_rows)
     project(lamb_rows, pair, spread, send, 0)
     send[:, send.shape[1] - 8 :] = labels[...]
 
@@ -374,10 +388,15 @@
     return write
 
 
-def flow_stages_body(wide, rim, pair, spread, labels, second, derived, ends_out, send, lamb_rows, ends, first):
+def flow_stages_body(count, state, edge, *refs):
+    beside_x, edges_x, refs = refs[:count], refs[count : 2 * count], refs[2 * count :]
+    got_a, got_b, pair, spread, _, second, derived, ends_out, send, *refs = refs
+    lamb_rows, ends, first, wide, rim, above, below = refs
+    above[...], below[...] = paired(is_odd("fy"), got_a[...], got_b[...])
+    assemble(wide, rim, state, edge, beside_x, edges_x, above, below)
     planes = wide.shape[1]
     cells_x = planes - 2 * HALO
-    size = (send.shape[1] - 8) // 2
+    size = send.shape[1] // 2
     rim_start = [rim[f] for f in range(5)]
     derive_planes(wide, derived, 0, planes)
     _, along_z, rim_first = rim_section(rim_start, None, MIXES[0])
@@ -395,12 +414,11 @@
     to_ends(other[0:2], 3, 8, 0, cells_x, ends)
     lamb(derived, ends, 1, cells_x, lamb_rows)
     project(lamb_rows, pair, spread, send, size)
-    send[:, 2 * size :] = labels[...]
     to_ends(along_z, 2, 8, 0, cells_x, ends_out)
 
 
-def flow_last_body(second, derived, ends, wide, out):
-    flow_rate_section(second, derived, ends, wide, 2, MIXES[2], writer(out), inner=True)
+def flow_last_body(second, derived, ends, state, out):
+    flow_rate_section(second, derived, ends, state, -1, MIXES[2], writer(out), inner=True)
 
 
 def faces_out(state, rear, front):
@@ -529,10 +547,12 @@
         given_out, before, after, out, turned, stored = refs
     elif kind == "first":
         _, out, message_a, message_b, before, after, source = refs
-        place_body(received, source)
+        place(received, received, source, 0)
         received = source
     else:
-        out, message_a, message_b, before, after = refs
+        labelled, out, message_a, message_b, before, after, source = refs
+        place(received, labelled, source, 0)
+        received = source
     odd = is_odd("fz")
     after[...], before[...] = paired(odd, got_a[0:96], got_b[0:96])
     out[0] = partial[0]
@@ -545,29 +565,32 @@
         faces_sent(odd, out, message_a, message_b)
 
 
-def place_body(received, *outs):
-    peers, size = received.shape[0], received.shape[1]
-    fold = 192 * len(outs) // (size - 8)
+def place(received, labelled, out, base):
+    peers, size = labelled.shape[0], labelled.shape[1]
+    fold = 192 // (size - 8)
     height = 64 // fold
     target = lax.broadcasted_iota(jnp.int32, (128, 128), 0)
     lane = lax.broadcasted_iota(jnp.int32, (128, 128), 1)
     total = None
     for peer in range(peers):
-        label = received[peer, size - 8 : size - 7, :]
+        label = labelled[peer, size - 8 : size - 7, :]
         label = jnp.broadcast_to(label, (128, 128)).astype(jnp.int32)
         hit = (label == target % 16) & (lane % 8 == target // 16)
         chosen = [jnp.where(hit & (lane // (128 // fold) == g), 1.0, 0.0) for g in range(fold)]
         chosen = jnp.concatenate(chosen, 0).astype(BF16)
-        high, low = parts(received[peer, 0 : size - 8])
+        high, low = parts(received[peer, base : base + 3 * height])
         dims = (((1,), (1,)), ((), ()))
         value = lax.dot_general(high, chosen, dims, preferred_element_type=F32)
         value = value + lax.dot_general(low, chosen, dims, preferred_element_type=F32)
         total = value if total is None else total + value
-    for k, out in enumerate(outs):
-        for c in range(3):
-            for g in range(fold):
-                at = (k * 3 + c) * height
-                out[c, g * height : g * height + height] = total[at : at + height, g * 128 : g * 128 + 128]
+    for c in range(3):
+        for g in range(fold):
+            at = c * height
+            out[c, g * height : g * height + height] = total[at : at + height, g * 128 : g * 128 + 128]
+
+
+def place_last_body(received, labelled, out):
+    place(received, labelled, out, received.shape[1] // 2)
 
 
 def kron_part(matrix, shape, rows_by, columns_by):
@@ -793,45 +816,6 @@
     def route(send):
         return lax.all_to_all(send, "fy", split_axis=0, concat_axis=0, tiled=True)
 
-    start, rim, send = call(
-        functools.partial(flow_sources_body, len(beside_x)),
-        [planes(wide), (5, 16, 256), (size_y, 192 // fold + 8, 128)],
-        state,
-        edge,
-        *beside_x,
-        *edges_x,
-        y_first,
-        y_second,
-        pair,
-        spread,
-        labels,
-        got_b,
-        last=1,
-        scratch=[
-            pltpu.VMEM((3, wide, 16, 128), F32),
-            rows_scratch,
-            pltpu.VMEM((2, cells_x, 8, 128), F32),
-            pltpu.VMEM(y_shape, F32),
-            pltpu.VMEM(y_shape, F32),
-        ],
-    )
-    received = route(send)
-    second, derived, ends, send = call(
-        flow_stages_body,
-        [
-            planes(wide - 4),
-            planes(wide),
-            (5, cells_x, 8, 128),
-            (size_y, 2 * 192 // fold + 8, 128),
-        ],
-        start,
-        rim,
-        pair,
-        spread,
-        labels,
-        scratch=[rows_scratch, pltpu.VMEM(planes(wide - 2), F32), pltpu.VMEM(planes(wide - 2), F32)],
-    )
-
     def local_part(mix, now):
         return call(
             functools.partial(acoustic_local_body, mix),
@@ -847,6 +831,57 @@
         )[0]
 
     partial = local_part(MIXES[0], sound)
+    y_scratch = [pltpu.VMEM(y_shape, F32), pltpu.VMEM(y_shape, F32)]
+    send = call(
+        functools.partial(flow_sources_body, len(beside_x)),
+        [(size_y, 192 // fold + 8, 128)],
+        state,
+        edge,
+        *beside_x,
+        y_first,
+        y_second,
+        pair,
+        spread,
+        labels,
+        got_b,
+        last=1,
+        scratch=[
+            pltpu.VMEM((4, cells_x + 2, 16, 128), F32),
+            pltpu.VMEM((3, cells_x + 2, 16, 128), F32),
+            rows_scratch,
+            pltpu.VMEM((2, cells_x, 8, 128), F32),
+        ]
+        + y_scratch,
+    )[0]
+    received = route(send)
+    second, derived, ends, send = call(
+        functools.partial(flow_stages_body, len(edges_x)),
+        [
+            planes(wide - 4),
+            planes(wide),
+            (5, cells_x, 8, 128),
+            (size_y, 2 * 192 // fold, 128),
+        ],
+        state,
+        edge,
+        *beside_x,
+        *edges_x,
+        y_first,
+        y_second,
+        pair,
+        spread,
+        partial,
+        last=1,
+        scratch=[
+            rows_scratch,
+            pltpu.VMEM(planes(wide - 2), F32),
+            pltpu.VMEM(planes(wide - 2), F32),
+            pltpu.VMEM(planes(wide), F32),
+            pltpu.VMEM((5, 16, 256), F32),
+        ]
+        + y_scratch,
+    )
+
     sound_one, to_a, to_b = call(
         functools.partial(acoustic_far_body, MIXES[0], "first"),
         [held, faces, (faces[0] + 32, size)],
@@ -859,9 +894,9 @@
         scratch=sides + [rows_scratch],
         last=1,
     )
-    source_two, source_three = call(place_body, [(3, 64, 128)] * 2, route(send))
+    labelled, received = received, route(send)
     got_a, got_b = traces(to_a, to_b)
-    flow_state = call(flow_last_body, [(5, cells_x, 8, 128)], second, derived, ends, start)[0]
+    flow_state = call(flow_last_body, [(5, cells_x, 8, 128)], second, derived, ends, state)[0]
     partial = local_part(MIXES[1], sound_one)
     sound_two, to_a, to_b = call(
         functools.partial(acoustic_far_body, MIXES[1], "second"),
@@ -870,9 +905,11 @@
         got_a,
         got_b,
         far,
-        source_two,
-        scratch=sides,
-    )
+        received,
+        labelled,
+        scratch=sides + [rows_scratch],
+    )
+    source_three = call(place_last_body, [(3, 64, 128)], received, labelled)[0]
     got_a, got_b = traces(to_a, to_b)
     partial = local_part(MIXES[2], sound_two)
     sound_state = call(

time: 58.5 us -> 58.3 us (level)
    all_to_all x2, waiting for transfers between devices: 7.48 us -> 3.32 us  [route(): return lax.all_to_all(send, 'fy', split_axis=0, concat_axis=0, tiled=True)]
    ppermute x3, waiting for transfers between devices: 5.85 us -> 8.94 us  [traces(): far_got = lax.ppermute(to_b, names, far_pairs)]
    ppermute x3, waiting for transfers between devices: 0.65 us -> 1.51 us  [traces(): return (lax.ppermute(to_a, names, near_pairs), far_got)]
  transfers between devices with their start and end apart: 14 -> 14, of which waited for: 6 -> 7; matrix products, arithmetic and copies ran while one was open for 0% -> 0% of each run, Pallas kernels for 15% -> 15%
where the time goes in v13:
time: 58.3 us; the launch traced here: 57.9 us
  starting transfers between devices  27.6 us (47%)
  waiting for transfers between devices  15.4 us (26%)
  Pallas kernels  11.8 us (20%)
  local copies, waits for them, and re-layouts  1.3 us (2%)
  other arithmetic  1 us (2%)
  between operations  0.9 us (2%)
    ppermute x3, starting transfers between devices, traces(): far_got = lax.ppermute(to_b, names, far_pairs)  15 us
    pallas_call x15, Pallas kernels, call(): pl.pallas_call(body, out_shape=outs, in_specs=[whole] * (len(operands) -...  11.8 us
    ppermute x3, waiting for transfers between devices, traces(): far_got = lax.ppermute(to_b, names, far_pairs)  8.94 us
    all_to_all x2, starting transfers between devices, route(): return lax.all_to_all(send, 'fy', split_axis=0, concat_axis=0, tiled=True)  7.06 us
    all_to_all x2, waiting for transfers between devices, route(): return lax.all_to_all(send, 'fy', split_axis=0, concat_axis=0, tiled=True)  3.32 us
    ppermute x1, waiting for transfers between devices, per_device(): y_second = lax.ppermute(y_b, 'fy', partners((size_y,), 0, True))  1.64 us
    ppermute x1, starting transfers between devices, per_device(): edge_b = lax.ppermute(flow_b, 'fz', partners((size_z,), 0, True))  1.64 us
    ppermute x1, starting transfers between devices, per_device(): lax.ppermute(edge, 'fx', shifted((size_x,), (step,)))  1.56 us
  transfers between devices with their start and end apart: 14, of which 7 were waited for; matrix products, arithmetic and copies ran while one was open for 0% of the time, Pallas kernels for 15%

profile of v13, /device:TPU:2, one launch (start us, length us, event | category | flops | bytes accessed | tf_op | source)
XLA Modules:
  0.0 57.9 jit_solution(9348405657422520382)
XLA Ops:
  0.7 0.9 %broadcast_multiply_fusion = f32[3,8,8,128]{3,2,1,0:T(8,128)S(1)} fusion(f32[3,8,8,128]{3,2,1,0:T(8,128)} %param.11, f32[8,8,128]{2,1,0:T(8,128)} %param.10), kind=kLoop, calls=%fused_computation.1 | loop fusion | flops 24576 | bytes 229376 | tf_op jit(solution)/shard_map/mul | solution.py:726
  1.9 1.6 %collective-permute-start.1 = (f32[24,128]{1,0:T(8,128)S(1)}, f32[24,128]{1,0:T(8,128)S(1)}, u32[]{:S(2)}, u32[]{:S(2)}) collective-permute-start(f32[24,128]{1,0:T(8,128)S(1)} %get-tuple-element.29.sent_b), channel_id=1, source_target_pairs={{3,0},{2,1},{1,2},{0,3},{7,4},{6,5},{5,6},{4,7},{11,8},{10,9},{9,1... | collective-permute-start | bytes 36872 | tf_op jit(solution)/shard_map/ppermute | solution.py:733
  3.5 0.5 collective-permute-start.3
  4.1 0.7 %copy-done.4 = s32[16,6]{0,1:T(8,128)S(1)} copy-done((s32[16,6]{0,1:T(8,128)S(1)}, s32[16,6]{0,1:T(8,128)}, u32[]{:S(2)}) %copy-start.4) | copy-done | bytes 408
  4.8 0.6 shard_map.114
  5.4 0.6 copy-done.8
  6.0 0.6 %collective-permute-done.2._.got_a = f32[96,128]{1,0:T(8,128)S(1)} collective-permute-done((f32[96,128]{1,0:T(8,128)S(1)}, f32[96,128]{1,0:T(8,128)S(1)}, u32[]{:S(2)}, u32[]{:S(2)}) %collective-permute-start.2) | collective-permute-done | bytes 49184 | tf_op jit(solution)/shard_map/ppermute | solution.py:742
  6.6 0.1 shard_map.115.edge
  6.8 1.6 %collective-permute-start.4 = (f32[40,128]{1,0:T(8,128)S(1)}, f32[40,128]{1,0:T(8,128)S(1)}, u32[]{:S(2)}, u32[]{:S(2)}) collective-permute-start(f32[40,128]{1,0:T(8,128)S(1)} %shard_map.115.edge), channel_id=1, source_target_pairs={{16,0},{0,16},{17,1},{1,17},{18,2},{2,18},{19,3},{3,19},{20,4},{4,... | collective-permute-start | bytes 61448 | tf_op jit(solution)/shard_map/ppermute | solution.py:770
  8.3 4.9 %collective-permute-start.7 = (f32[192,128]{1,0:T(8,128)S(1)}, f32[192,128]{1,0:T(8,128)S(1)}, u32[]{:S(2)}, u32[]{:S(2)}) collective-permute-start(f32[192,128]{1,0:T(8,128)S(1)} %get-tuple-element.44), channel_id=1, source_target_pairs={{1,2},{2,1},{3,4},{4,3},{5,6},{6,5},{7,8},{8,7},{9,10},{10,9},{11,... | collective-permute-start | bytes 294920 | tf_op jit(solution)/shard_map/ppermute | solution.py:741
  13.4 1.4 %collective-permute-start.6 = (f32[168,128]{1,0:T(8,128)S(1)}, f32[168,128]{1,0:T(8,128)S(1)}, u32[]{:S(2)}, u32[]{:S(2)}) collective-permute-start(f32[168,128]{1,0:T(8,128)S(1)} %get-tuple-element.33), channel_id=1, source_target_pairs={{12,0},{8,4},{4,8},{0,12},{13,1},{9,5},{5,9},{1,13},{14,2},{10,6},... | collective-permute-start | bytes 258056 | tf_op jit(solution)/shard_map/ppermute | solution.py:773
  14.8 1.0 %shard_map.117 = (bf16[5,128,128]{2,1,0:T(8,128)(2,1)S(1)}, bf16[5,128,128]{2,1,0:T(8,128)(2,1)S(1)}, f32[128,64]{1,0:T(8,128)S(1)}, f32[128,128]{1,0:T(8,128)S(...) custom-call(f32[32,16]{1,0:T(8,128)S(1)} %pad_add_fusion.1.packed), custom_call_target="tpu_custom_call" | custom-call | flops 1 | bytes 1 | tf_op jit(solution)/shard_map/pallas_call | solution.py:52
  15.8 2.7 %collective-permute-done.7.refs_6_.got_b = f32[192,128]{1,0:T(8,128)S(1)} collective-permute-done((f32[192,128]{1,0:T(8,128)S(1)}, f32[192,128]{1,0:T(8,128)S(1)}, u32[]{:S(2)}, u32[]{:S(2)}) %collective-permute-start.7) | collective-permute-done | bytes 98336 | tf_op jit(solution)/shard_map/ppermute | solution.py:741
  18.6 1.6 %collective-permute-done.6.refs_3_.refs_2_ = f32[168,128]{1,0:T(8,128)S(1)} collective-permute-done((f32[168,128]{1,0:T(8,128)S(1)}, f32[168,128]{1,0:T(8,128)S(1)}, u32[]{:S(2)}, u32[]{:S(2)}) %collective-permute-start.6) | collective-permute-done | bytes 86048 | tf_op jit(solution)/shard_map/ppermute | solution.py:773
  20.2 1.3 %shard_map.121 = f32[4,104,128]{2,1,0:T(8,128)} custom-call(f32[5,8,8,128]{3,2,1,0:T(8,128)S(1)} %pad_add_fusion.state, f32[40,128]{1,0:T(8,128)S(1)} %shard_map.115.edge, f32[240,128]{1,0:T(8,128)S(1)} %collective-permute-done.3.refs_0_, f32[168,128]{1,0:T(8,128)S(1)} %collective-permute-done.5.refs_2_.refs_1_, ...), custom_call_target="tpu_custom_call" | custom-call | tf_op jit(solution)/shard_map/pallas_call | solution.py:52
  21.5 3.6 %all-to-all-start = ((f32[4,104,128]{2,1,0:T(8,128)}), f32[4,104,128]{2,1,0:T(8,128)S(1)}, u32[]{:S(2)}, u32[]{:S(2)}) async-start(f32[4,104,128]{2,1,0:T(8,128)} %shard_map.121), calls=%async_computation | async-start | bytes 425984 | tf_op jit(solution)/shard_map/all_to_all | solution.py:817
  25.1 0.3 shard_map.118.refs_6_.partial
  25.5 3.9 %shard_map.119 = (f32[5,10,16,128]{3,2,1,0:T(8,128)S(1)}, f32[5,14,16,128]{3,2,1,0:T(8,128)S(1)}, f32[5,8,8,128]{3,2,1,0:T(8,128)S(1)}, f32[4,192,128]{2,1,0:T(8,128)}) custom-call(f32[5,8,8,128]{3,2,1,0:T(8,128)S(1)} %pad_add_fusion.state, f32[40,128]{1,0:T(8,128)S(1)} %shard_map.115.edge, f32[240,128]{1,0:T(8,128)S(1)} %collective-permute-done.3.refs_0_, ...), custom_call_target="tpu_custom_call" | custom-call | tf_op jit(solution)/shard_map/pallas_call | solution.py:52
  29.4 3.3 %all-to-all-done.received.refs_0_.labelled = f32[4,104,128]{2,1,0:T(8,128)S(1)} async-done(((f32[4,104,128]{2,1,0:T(8,128)}), f32[4,104,128]{2,1,0:T(8,128)S(1)}, u32[]{:S(2)}, u32[]{:S(2)}) %all-to-all-start) | async-done | bytes 213024 | tf_op jit(solution)/shard_map/all_to_all | solution.py:817
  32.7 3.5 %all-to-all-start.1 = ((f32[4,192,128]{2,1,0:T(8,128)}), f32[4,192,128]{2,1,0:T(8,128)S(1)}, u32[]{:S(2)}, u32[]{:S(2)}) async-start(f32[4,192,128]{2,1,0:T(8,128)} %get-tuple-element.47.refs_0_), calls=%async_computation.1 | async-start | bytes 786432 | tf_op jit(solution)/shard_map/all_to_all | solution.py:817
  36.2 0.5 shard_map.122
  36.7 5.5 %collective-permute-start.9 = (f32[128,128]{1,0:T(8,128)S(1)}, f32[128,128]{1,0:T(8,128)S(1)}, u32[]{:S(2)}, u32[]{:S(2)}) collective-permute-start(f32[128,128]{1,0:T(8,128)S(1)} %get-tuple-element.50), channel_id=1, source_target_pairs={{1,2},{2,1},{3,4},{4,3},{5,6},{6,5},{7,8},{8,7},{9,10},{10,9},{11,... | collective-permute-start | bytes 196616 | tf_op jit(solution)/shard_map/ppermute | solution.py:741
  42.3 0.3 shard_map.123.partial
  42.7 0.9 %collective-permute-done.8.got_a = f32[96,128]{1,0:T(8,128)S(1)} collective-permute-done((f32[96,128]{1,0:T(8,128)S(1)}, f32[96,128]{1,0:T(8,128)S(1)}, u32[]{:S(2)}, u32[]{:S(2)}) %collective-permute-start.8) | collective-permute-done | bytes 49184 | tf_op jit(solution)/shard_map/ppermute | solution.py:742
  43.5 3.4 %collective-permute-done.9.got_b = f32[128,128]{1,0:T(8,128)S(1)} collective-permute-done((f32[128,128]{1,0:T(8,128)S(1)}, f32[128,128]{1,0:T(8,128)S(1)}, u32[]{:S(2)}, u32[]{:S(2)}) %collective-permute-start.9) | collective-permute-done | bytes 65568 | tf_op jit(solution)/shard_map/ppermute | solution.py:741
  46.9 0.5 shard_map.124
  47.5 4.6 %collective-permute-start.11 = (f32[128,128]{1,0:T(8,128)S(1)}, f32[128,128]{1,0:T(8,128)S(1)}, u32[]{:S(2)}, u32[]{:S(2)}) collective-permute-start(f32[128,128]{1,0:T(8,128)S(1)} %get-tuple-element.53), channel_id=1, source_target_pairs={{1,2},{2,1},{3,4},{4,3},{5,6},{6,5},{7,8},{8,7},{9,10},{10,9},{11,... | collective-permute-start | bytes 196616 | tf_op jit(solution)/shard_map/ppermute | solution.py:741
  52.1 1.0 %shard_map.120 = f32[5,8,8,128]{3,2,1,0:T(8,128)} custom-call(f32[5,10,16,128]{3,2,1,0:T(8,128)S(1)} %get-tuple-element.41.second, f32[5,14,16,128]{3,2,1,0:T(8,128)S(1)} %get-tuple-element.42.derived, f32[5,8,8,128]{3,2,1,0:T(8,128)S(1)} %get-tuple-element.43.ends, f32[5,8,8,128]{3,2,1,0:T(8,128)S(1)} %pad_add_fusion.state), custom_call_target="tpu_custom_call" | custom-call | tf_op jit(solution)/shard_map/pallas_call | solution.py:52
  53.2 0.3 shard_map.125.partial
  53.5 0.3 shard_map.126.received
  53.8 2.8 %collective-permute-done.11.got_b = f32[128,128]{1,0:T(8,128)S(1)} collective-permute-done((f32[128,128]{1,0:T(8,128)S(1)}, f32[128,128]{1,0:T(8,128)S(1)}, u32[]{:S(2)}, u32[]{:S(2)}) %collective-permute-start.11) | collective-permute-done | bytes 65568 | tf_op jit(solution)/shard_map/ppermute | solution.py:741
  56.6 1.3 %shard_map.127 = f32[16,4,512]{2,1,0:T(4,128)} custom-call(f32[4,64,128]{2,1,0:T(8,128)S(1)} %shard_map.125.partial, f32[96,128]{1,0:T(8,128)S(1)} %collective-permute-done.10.got_a, f32[128,128]{1,0:T(8,128)S(1)} %collective-permute-done.11.got_b, bf16[5,128,128]{2,1,0:T(8,128)(2,1)S(1)} %get-tuple-element.45.sides_far, f32[3,64,128]{2,1,0:T(8,128)S(1)} %shard_map.126.received), custom_call_target="tpu_custom_call" | custom-call | tf_op jit(solution)/shard_map/pallas_call | solution.py:52
  (38 shorter events, 0.6 us)
Async XLA Ops:
  0.6 1.0 %copy-start.1 = (f32[3,8,8,128]{3,2,1,0:T(8,128)S(1)}, f32[3,8,8,128]{3,2,1,0:T(8,128)}, u32[]{:S(2)}) copy-start(f32[3,8,8,128]{3,2,1,0:T(8,128)} %param.11) | copy-start | bytes 294916
  0.6 1.0 %copy-start.2 = (f32[8,8,128]{2,1,0:T(8,128)S(1)}, f32[8,8,128]{2,1,0:T(8,128)}, u32[]{:S(2)}) copy-start(f32[8,8,128]{2,1,0:T(8,128)} %param.10) | copy-start | bytes 98308
  0.6 1.0 %copy-start.3 = (f32[8,8,128]{2,1,0:T(8,128)S(1)}, f32[8,8,128]{2,1,0:T(8,128)}, u32[]{:S(2)}) copy-start(f32[8,8,128]{2,1,0:T(8,128)} %param.12) | copy-start | bytes 98308
  1.7 3.1 %copy-start = (f32[16,4,512]{2,1,0:T(4,128)S(1)}, f32[16,4,512]{2,1,0:T(4,128)}, u32[]{:S(2)}) copy-start(f32[16,4,512]{2,1,0:T(4,128)} %given.1) | copy-start | bytes 393220
  1.8 2.9 %collective-permute-start = (f32[24,128]{1,0:T(8,128)S(1)}, f32[24,128]{1,0:T(8,128)S(1)}, u32[]{:S(2)}, u32[]{:S(2)}) collective-permute-start(f32[24,128]{1,0:T(8,128)S(1)} %get-tuple-element.28.sent_a), channel_id=1, source_target_pairs={{1,0},{0,1},{3,2},{2,3},{5,4},{4,5},{7,6},{6,7},{9,8},{8,9},{11,10... | collective-permute-start | bytes 36872 | tf_op jit(solution)/shard_map/ppermute | solution.py:732
  1.9 4.1 %collective-permute-start.1 = (f32[24,128]{1,0:T(8,128)S(1)}, f32[24,128]{1,0:T(8,128)S(1)}, u32[]{:S(2)}, u32[]{:S(2)}) collective-permute-start(f32[24,128]{1,0:T(8,128)S(1)} %get-tuple-element.29.sent_b), channel_id=1, source_target_pairs={{3,0},{2,1},{1,2},{0,3},{7,4},{6,5},{5,6},{4,7},{11,8},{10,9},{9,1... | collective-permute-start | bytes 36872 | tf_op jit(solution)/shard_map/ppermute | solution.py:733
  3.5 9.7 %collective-permute-start.3 = (f32[240,128]{1,0:T(8,128)S(1)}, f32[240,128]{1,0:T(8,128)S(1)}, u32[]{:S(2)}, u32[]{:S(2)}) collective-permute-start(f32[240,128]{1,0:T(8,128)S(1)} %get-tuple-element.31), channel_id=1, source_target_pairs={{16,0},{0,16},{17,1},{1,17},{18,2},{2,18},{19,3},{3,19},{20,4},{4,... | collective-permute-start | bytes 368648 | tf_op jit(solution)/shard_map/ppermute | solution.py:735
  4.1 0.7 %copy-start.4 = (s32[16,6]{0,1:T(8,128)S(1)}, s32[16,6]{0,1:T(8,128)}, u32[]{:S(2)}) copy-start(s32[16,6]{0,1:T(8,128)} %param.17) | copy-start | bytes 1156
  5.3 0.7 %copy-start.8 = (s32[1,1,1,16]{3,2,1,0:T(1,128)S(1)}, s32[1,1,1,16]{3,2,1,0:T(1,128)}, u32[]{:S(2)}) copy-start(s32[1,1,1,16]{3,2,1,0:T(1,128)} %param.19) | copy-start | bytes 196
  5.3 1.3 %collective-permute-start.2 = (f32[96,128]{1,0:T(8,128)S(1)}, f32[96,128]{1,0:T(8,128)S(1)}, u32[]{:S(2)}, u32[]{:S(2)}) collective-permute-start(f32[96,128]{1,0:T(8,128)S(1)} %get-tuple-element.30), channel_id=1, source_target_pairs={{1,0},{0,1},{3,2},{2,3},{5,4},{4,5},{7,6},{6,7},{9,8},{8,9},{11,10... | collective-permute-start | bytes 147464 | tf_op jit(solution)/shard_map/ppermute | solution.py:742
  6.0 2.3 %copy-start.9 = (s32[1,1,1,16,1]{3,4,2,1,0:T(1,128)S(1)}, s32[1,1,1,16,1]{3,4,2,1,0:T(1,128)}, u32[]{:S(2)}) copy-start(s32[1,1,1,16,1]{3,4,2,1,0:T(1,128)} %param.18) | copy-start | bytes 196
  6.8 6.5 %collective-permute-start.4 = (f32[40,128]{1,0:T(8,128)S(1)}, f32[40,128]{1,0:T(8,128)S(1)}, u32[]{:S(2)}, u32[]{:S(2)}) collective-permute-start(f32[40,128]{1,0:T(8,128)S(1)} %shard_map.115.edge), channel_id=1, source_target_pairs={{16,0},{0,16},{17,1},{1,17},{18,2},{2,18},{19,3},{3,19},{20,4},{4,... | collective-permute-start | bytes 61448 | tf_op jit(solution)/shard_map/ppermute | solution.py:770
  8.3 10.2 %collective-permute-start.7 = (f32[192,128]{1,0:T(8,128)S(1)}, f32[192,128]{1,0:T(8,128)S(1)}, u32[]{:S(2)}, u32[]{:S(2)}) collective-permute-start(f32[192,128]{1,0:T(8,128)S(1)} %get-tuple-element.44), channel_id=1, source_target_pairs={{1,2},{2,1},{3,4},{4,3},{5,6},{6,5},{7,8},{8,7},{9,10},{10,9},{11,... | collective-permute-start | bytes 294920 | tf_op jit(solution)/shard_map/ppermute | solution.py:741
  13.3 1.6 %copy-start.6 = (f32[8,8]{1,0:T(8,128)S(1)}, f32[8,8]{1,0:T(8,128)}, u32[]{:S(2)}) copy-start(f32[8,8]{1,0:T(8,128)} %param.15) | copy-start | bytes 772
  13.3 1.5 %copy-start.5 = (f32[8,8]{1,0:T(8,128)S(1)}, f32[8,8]{1,0:T(8,128)}, u32[]{:S(2)}) copy-start(f32[8,8]{1,0:T(8,128)} %param.16) | copy-start | bytes 772
  13.4 5.2 %collective-permute-start.5 = (f32[168,128]{1,0:T(8,128)S(1)}, f32[168,128]{1,0:T(8,128)S(1)}, u32[]{:S(2)}, u32[]{:S(2)}) collective-permute-start(f32[168,128]{1,0:T(8,128)S(1)} %get-tuple-element.32), channel_id=1, source_target_pairs={{4,0},{0,4},{12,8},{8,12},{5,1},{1,5},{13,9},{9,13},{6,2},{2,6},{1... | collective-permute-start | bytes 258056 | tf_op jit(solution)/shard_map/ppermute | solution.py:774
  13.4 1.4 %copy-start.7 = (f32[16]{0:T(128)S(1)}, f32[16]{0:T(128)}, u32[]{:S(2)}) copy-start(f32[16]{0:T(128)} %param.14) | copy-start | bytes 196
  13.4 6.8 %collective-permute-start.6 = (f32[168,128]{1,0:T(8,128)S(1)}, f32[168,128]{1,0:T(8,128)S(1)}, u32[]{:S(2)}, u32[]{:S(2)}) collective-permute-start(f32[168,128]{1,0:T(8,128)S(1)} %get-tuple-element.33), channel_id=1, source_target_pairs={{12,0},{8,4},{4,8},{0,12},{13,1},{9,5},{5,9},{1,13},{14,2},{10,6},... | collective-permute-start | bytes 258056 | tf_op jit(solution)/shard_map/ppermute | solution.py:773
  21.5 11.1 %all-to-all-start = ((f32[4,104,128]{2,1,0:T(8,128)}), f32[4,104,128]{2,1,0:T(8,128)S(1)}, u32[]{:S(2)}, u32[]{:S(2)}) async-start(f32[4,104,128]{2,1,0:T(8,128)} %shard_map.121), calls=%async_computation | async-start | bytes 425984 | tf_op jit(solution)/shard_map/all_to_all | solution.py:817
  32.7 14.2 %all-to-all-start.1 = ((f32[4,192,128]{2,1,0:T(8,128)}), f32[4,192,128]{2,1,0:T(8,128)S(1)}, u32[]{:S(2)}, u32[]{:S(2)}) async-start(f32[4,192,128]{2,1,0:T(8,128)} %get-tuple-element.47.refs_0_), calls=%async_computation.1 | async-start | bytes 786432 | tf_op jit(solution)/shard_map/all_to_all | solution.py:817
  36.7 10.2 %collective-permute-start.9 = (f32[128,128]{1,0:T(8,128)S(1)}, f32[128,128]{1,0:T(8,128)S(1)}, u32[]{:S(2)}, u32[]{:S(2)}) collective-permute-start(f32[128,128]{1,0:T(8,128)S(1)} %get-tuple-element.50), channel_id=1, source_target_pairs={{1,2},{2,1},{3,4},{4,3},{5,6},{6,5},{7,8},{8,7},{9,10},{10,9},{11,... | collective-permute-start | bytes 196616 | tf_op jit(solution)/shard_map/ppermute | solution.py:741
  42.2 1.3 %collective-permute-start.8 = (f32[96,128]{1,0:T(8,128)S(1)}, f32[96,128]{1,0:T(8,128)S(1)}, u32[]{:S(2)}, u32[]{:S(2)}) collective-permute-start(f32[96,128]{1,0:T(8,128)S(1)} %get-tuple-element.49), channel_id=1, source_target_pairs={{1,0},{0,1},{3,2},{2,3},{5,4},{4,5},{7,6},{6,7},{9,8},{8,9},{11,10... | collective-permute-start | bytes 147464 | tf_op jit(solution)/shard_map/ppermute | solution.py:742
  47.5 9.2 %collective-permute-start.11 = (f32[128,128]{1,0:T(8,128)S(1)}, f32[128,128]{1,0:T(8,128)S(1)}, u32[]{:S(2)}, u32[]{:S(2)}) collective-permute-start(f32[128,128]{1,0:T(8,128)S(1)} %get-tuple-element.53), channel_id=1, source_target_pairs={{1,2},{2,1},{3,4},{4,3},{5,6},{6,5},{7,8},{8,7},{9,10},{10,9},{11,... | collective-permute-start | bytes 196616 | tf_op jit(solution)/shard_map/ppermute | solution.py:741
  52.1 1.8 %collective-permute-start.10 = (f32[96,128]{1,0:T(8,128)S(1)}, f32[96,128]{1,0:T(8,128)S(1)}, u32[]{:S(2)}, u32[]{:S(2)}) collective-permute-start(f32[96,128]{1,0:T(8,128)S(1)} %get-tuple-element.52), channel_id=1, source_target_pairs={{1,0},{0,1},{3,2},{2,3},{5,4},{4,5},{7,6},{6,7},{9,8},{8,9},{11,10... | collective-permute-start | bytes 147464 | tf_op jit(solution)/shard_map/ppermute | solution.py:742

commit v14 on v13

--- a/solution.py
+++ b/solution.py
@@ -368,7 +368,7 @@
 
 def flow_sources_body(count, state, edge, *refs):
     beside_x, refs = refs[:count], refs[count:]
-    got_a, got_b, pair, spread, labels, _, send, wide, derived, lamb_rows, ends, above, below = refs
+    got_a, got_b, pair, spread, labels, send, wide, derived, lamb_rows, ends, above, below = refs
     cells_x = state.shape[1]
     above[...], below[...] = paired(is_odd("fy"), got_a[...], got_b[...])
     assemble_speeds(wide, state, beside_x, above, below)
@@ -390,7 +390,7 @@
 
 def flow_stages_body(count, state, edge, *refs):
     beside_x, edges_x, refs = refs[:count], refs[count : 2 * count], refs[2 * count :]
-    got_a, got_b, pair, spread, _, second, derived, ends_out, send, *refs = refs
+    got_a, got_b, pair, spread, _, _, second, derived, ends_out, send, *refs = refs
     lamb_rows, ends, first, wide, rim, above, below = refs
     above[...], below[...] = paired(is_odd("fy"), got_a[...], got_b[...])
     assemble(wide, rim, state, edge, beside_x, edges_x, above, below)
@@ -443,7 +443,8 @@
     size = message_a.shape[0]
     faces_out(state, message_b, message_a)
     message_a[...], message_b[0:size] = paired(odd, message_a[...], message_b[0:size])
-    message_b[size:] = jnp.zeros((message_b.shape[0] - size, 128), F32)
+    if message_b.shape[0] > size:
+        message_b[size:] = jnp.zeros((message_b.shape[0] - size, 128), F32)
 
 
 def lift(total, before, after, sides, factor):
@@ -605,6 +606,8 @@
 
 def tables_body(
     packed,
+    faces,
+    far_faces,
     near,
     far,
     deriv_rows,
@@ -614,6 +617,8 @@
     labels,
     speed,
 ):
+    far_faces[0 : faces.shape[0]] = faces[...]
+    far_faces[faces.shape[0] :] = jnp.zeros((far_faces.shape[0] - faces.shape[0], 128), F32)
     size = near.shape[1]
     count = size // 8
     blocks = spread.shape[0] // 8
@@ -748,13 +753,13 @@
     turning = [pltpu.VMEM((512, 128), F32), pltpu.VMEM((4, 4 * elements, 128), F32)]
     sound, to_a, to_b = call(
         acoustic_start_body,
-        [held, faces, (2 * faces[0], size)],
+        [held, faces, faces],
         acoustic,
         edge_a,
         scratch=turning,
         last=1,
     )
-    got_a, got_b = traces(to_a, to_b)
+    got_a = lax.ppermute(to_a, names, near_pairs)
 
     edge = call(
         pack_next_body,
@@ -790,9 +795,10 @@
         + piece(block_element.reshape(1, blocks), 26)
     )
     table = jax.ShapeDtypeStruct((5, size, size), BF16)
-    near, far, deriv_rows, deriv_lanes, pair, spread, labels, speed = call(
+    to_b, near, far, deriv_rows, deriv_lanes, pair, spread, labels, speed = call(
         tables_body,
         [
+            (256, size),
             table,
             table,
             (128, 64),
@@ -803,8 +809,10 @@
             (1, size),
         ],
         packed,
+        to_b,
         cost=1,
     )
+    got_b = lax.ppermute(to_b, names, far_pairs)
 
     fold = fold_of(size_y, blocks)
     wide = cells_x + 2 * HALO
@@ -843,8 +851,6 @@
         pair,
         spread,
         labels,
-        got_b,
-        last=1,
         scratch=[
             pltpu.VMEM((4, cells_x + 2, 16, 128), F32),
             pltpu.VMEM((3, cells_x + 2, 16, 128), F32),
@@ -871,7 +877,8 @@
         pair,
         spread,
         partial,
-        last=1,
+        got_b,
+        last=2,
         scratch=[
             rows_scratch,
             pltpu.VMEM(planes(wide - 2), F32),

time: 58.3 us -> 64.1 us (1.099)
  waiting for transfers between devices: 15.4 us -> 21.4 us
    ppermute x3 -> x2, starting transfers between devices: 15 us -> 8.03 us  [traces(): far_got = lax.ppermute(to_b, names, far_pairs)]
    ppermute x0 -> x2, waiting for transfers between devices: none -> 6.26 us  [the longest x1 5.62 us: per_device(): got_b = lax.ppermute(to_b, names, far_pairs)]
    ppermute x0 -> x2, starting transfers between devices: none -> 3.97 us  [the longest x1 3.9 us: per_device(): got_b = lax.ppermute(to_b, names, far_pairs)]
    all_to_all x2, waiting for transfers between devices: 3.32 us -> 0.01 us  [route(): return lax.all_to_all(send, 'fy', split_axis=0, concat_axis=0, tiled=True)]
    ppermute x1, waiting for transfers between devices: 0.01 us -> 2.29 us  [per_device(): lax.ppermute(edge, 'fx', shifted((size_x,), (step,)))]
    ppermute x1, starting transfers between devices: 0.07 us -> 1.64 us  [per_device(): y_first = lax.ppermute(y_a, 'fy', partners((size_y,), 0, False))]
    ppermute x1, waiting for transfers between devices: 1.64 us -> 2.78 us  [per_device(): y_second = lax.ppermute(y_b, 'fy', partners((size_y,), 0, True))]
    ppermute x1, starting transfers between devices: 1.38 us -> 2.47 us  [per_device(): y_second = lax.ppermute(y_b, 'fy', partners((size_y,), 0, True))]
  transfers between devices with their start and end apart: 14 -> 14, of which waited for: 7 -> 7; matrix products, arithmetic and copies ran while one was open for 0% -> 0% of each run, Pallas kernels for 15% -> 13%
where the time goes in v14:
time: 64.1 us; the launch traced here: 63.7 us
  starting transfers between devices  27.4 us (43%)
  waiting for transfers between devices  21.4 us (33%)
  Pallas kernels  11.8 us (18%)
  local copies, waits for them, and re-layouts  1.29 us (2%)
  other arithmetic  1 us (2%)
  between operations  0.87 us (1%)
    pallas_call x15, Pallas kernels, call(): pl.pallas_call(body, out_shape=outs, in_specs=[whole] * (len(operands) -...  11.8 us
    ppermute x2, waiting for transfers between devices, traces(): far_got = lax.ppermute(to_b, names, far_pairs)  9.21 us
    ppermute x2, starting transfers between devices, traces(): far_got = lax.ppermute(to_b, names, far_pairs)  8.03 us
    all_to_all x2, starting transfers between devices, route(): return lax.all_to_all(send, 'fy', split_axis=0, concat_axis=0, tiled=True)  7.31 us
    ppermute x1, waiting for transfers between devices, per_device(): got_b = lax.ppermute(to_b, names, far_pairs)  5.62 us
    ppermute x1, starting transfers between devices, per_device(): got_b = lax.ppermute(to_b, names, far_pairs)  3.9 us
    ppermute x1, waiting for transfers between devices, per_device(): y_second = lax.ppermute(y_b, 'fy', partners((size_y,), 0, True))  2.78 us
    ppermute x1, starting transfers between devices, per_device(): y_second = lax.ppermute(y_b, 'fy', partners((size_y,), 0, True))  2.47 us
  transfers between devices with their start and end apart: 14, of which 7 were waited for; matrix products, arithmetic and copies ran while one was open for 0% of the time, Pallas kernels for 13%

profile of v14, /device:TPU:2, one launch (start us, length us, event | category | flops | bytes accessed | tf_op | source)
XLA Modules:
  0.0 63.7 jit_solution(2090558307762452787)
XLA Ops:
  0.7 0.9 %broadcast_multiply_fusion = f32[3,8,8,128]{3,2,1,0:T(8,128)S(1)} fusion(f32[3,8,8,128]{3,2,1,0:T(8,128)} %param.11, f32[8,8,128]{2,1,0:T(8,128)} %param.10), kind=kLoop, calls=%fused_computation.1 | loop fusion | flops 24576 | bytes 229376 | tf_op jit(solution)/shard_map/mul | solution.py:731
  1.9 1.6 %collective-permute-start.1 = (f32[24,128]{1,0:T(8,128)S(1)}, f32[24,128]{1,0:T(8,128)S(1)}, u32[]{:S(2)}, u32[]{:S(2)}) collective-permute-start(f32[24,128]{1,0:T(8,128)S(1)} %get-tuple-element.30.sent_b), channel_id=1, source_target_pairs={{3,0},{2,1},{1,2},{0,3},{7,4},{6,5},{5,6},{4,7},{11,8},{10,9},{9,1... | collective-permute-start | bytes 36872 | tf_op jit(solution)/shard_map/ppermute | solution.py:738
  3.5 0.5 collective-permute-start.3
  4.1 0.7 %copy-done.4 = s32[16,6]{0,1:T(8,128)S(1)} copy-done((s32[16,6]{0,1:T(8,128)S(1)}, s32[16,6]{0,1:T(8,128)}, u32[]{:S(2)}) %copy-start.4) | copy-done | bytes 408
  4.8 0.6 shard_map.114
  5.4 0.6 copy-done.8
  6.0 0.6 %collective-permute-done.2._.got_a = f32[96,128]{1,0:T(8,128)S(1)} collective-permute-done((f32[96,128]{1,0:T(8,128)S(1)}, f32[96,128]{1,0:T(8,128)S(1)}, u32[]{:S(2)}, u32[]{:S(2)}) %collective-permute-start.2) | collective-permute-done | bytes 49184 | tf_op jit(solution)/shard_map/ppermute | solution.py:762
  6.8 1.6 %collective-permute-start.4 = (f32[40,128]{1,0:T(8,128)S(1)}, f32[40,128]{1,0:T(8,128)S(1)}, u32[]{:S(2)}, u32[]{:S(2)}) collective-permute-start(f32[40,128]{1,0:T(8,128)S(1)} %shard_map.115.edge), channel_id=1, source_target_pairs={{16,0},{0,16},{17,1},{1,17},{18,2},{2,18},{19,3},{3,19},{20,4},{4,... | collective-permute-start | bytes 61448 | tf_op jit(solution)/shard_map/ppermute | solution.py:775
  8.3 2.3 %collective-permute-done.4.refs_1_ = f32[40,128]{1,0:T(8,128)S(1)} collective-permute-done((f32[40,128]{1,0:T(8,128)S(1)}, f32[40,128]{1,0:T(8,128)S(1)}, u32[]{:S(2)}, u32[]{:S(2)}) %collective-permute-start.4) | collective-permute-done | bytes 20512 | tf_op jit(solution)/shard_map/ppermute | solution.py:775
  10.7 1.6 %collective-permute-start.5 = (f32[168,128]{1,0:T(8,128)S(1)}, f32[168,128]{1,0:T(8,128)S(1)}, u32[]{:S(2)}, u32[]{:S(2)}) collective-permute-start(f32[168,128]{1,0:T(8,128)S(1)} %get-tuple-element.33), channel_id=1, source_target_pairs={{4,0},{0,4},{12,8},{8,12},{5,1},{1,5},{13,9},{9,13},{6,2},{2,6},{1... | collective-permute-start | bytes 258056 | tf_op jit(solution)/shard_map/ppermute | solution.py:779
  12.3 2.5 %collective-permute-start.6 = (f32[168,128]{1,0:T(8,128)S(1)}, f32[168,128]{1,0:T(8,128)S(1)}, u32[]{:S(2)}, u32[]{:S(2)}) collective-permute-start(f32[168,128]{1,0:T(8,128)S(1)} %get-tuple-element.34), channel_id=1, source_target_pairs={{12,0},{8,4},{4,8},{0,12},{13,1},{9,5},{5,9},{1,13},{14,2},{10,6},... | collective-permute-start | bytes 258056 | tf_op jit(solution)/shard_map/ppermute | solution.py:778
  14.8 1.0 %shard_map.117 = (f32[256,128]{1,0:T(8,128)S(1)}, bf16[5,128,128]{2,1,0:T(8,128)(2,1)S(1)}, bf16[5,128,128]{2,1,0:T(8,128)(2,1)S(1)}, f32[128,64]{1,0:T(8,128)S(...) custom-call(f32[32,16]{1,0:T(8,128)S(1)} %pad_add_fusion.1.packed, ...), custom_call_target="tpu_custom_call" | custom-call | flops 1 | bytes 1 | tf_op jit(solution)/shard_map/pallas_call | solution.py:52
  15.8 2.8 %collective-permute-done.6.refs_3_.refs_2_ = f32[168,128]{1,0:T(8,128)S(1)} collective-permute-done((f32[168,128]{1,0:T(8,128)S(1)}, f32[168,128]{1,0:T(8,128)S(1)}, u32[]{:S(2)}, u32[]{:S(2)}) %collective-permute-start.6) | collective-permute-done | bytes 86048 | tf_op jit(solution)/shard_map/ppermute | solution.py:778
  18.6 1.3 %shard_map.121 = f32[4,104,128]{2,1,0:T(8,128)} custom-call(f32[5,8,8,128]{3,2,1,0:T(8,128)S(1)} %pad_add_fusion.state, f32[40,128]{1,0:T(8,128)S(1)} %shard_map.115.edge, f32[240,128]{1,0:T(8,128)S(1)} %collective-permute-done.3.refs_0_, f32[168,128]{1,0:T(8,128)S(1)} %collective-permute-done.5.refs_2_.refs_1_, ...), custom_call_target="tpu_custom_call" | custom-call | tf_op jit(solution)/shard_map/pallas_call | solution.py:52
  19.9 3.9 %all-to-all-start = ((f32[4,104,128]{2,1,0:T(8,128)}), f32[4,104,128]{2,1,0:T(8,128)S(1)}, u32[]{:S(2)}, u32[]{:S(2)}) async-start(f32[4,104,128]{2,1,0:T(8,128)} %shard_map.121), calls=%async_computation | async-start | bytes 425984 | tf_op jit(solution)/shard_map/all_to_all | solution.py:825
  23.8 3.9 %collective-permute-start.7 = (f32[256,128]{1,0:T(8,128)S(1)}, f32[256,128]{1,0:T(8,128)S(1)}, u32[]{:S(2)}, u32[]{:S(2)}) collective-permute-start(f32[256,128]{1,0:T(8,128)S(1)} %get-tuple-element.43), channel_id=1, source_target_pairs={{1,2},{2,1},{3,4},{4,3},{5,6},{6,5},{7,8},{8,7},{9,10},{10,9},{11,... | collective-permute-start | bytes 393224 | tf_op jit(solution)/shard_map/ppermute | solution.py:815
  27.7 0.3 shard_map.118.refs_6_.partial
  28.0 5.6 %collective-permute-done.7.refs_7_.got_b = f32[256,128]{1,0:T(8,128)S(1)} collective-permute-done((f32[256,128]{1,0:T(8,128)S(1)}, f32[256,128]{1,0:T(8,128)S(1)}, u32[]{:S(2)}, u32[]{:S(2)}) %collective-permute-start.7) | collective-permute-done | bytes 131104 | tf_op jit(solution)/shard_map/ppermute | solution.py:815
  33.7 3.9 %shard_map.119 = (f32[5,10,16,128]{3,2,1,0:T(8,128)S(1)}, f32[5,14,16,128]{3,2,1,0:T(8,128)S(1)}, f32[5,8,8,128]{3,2,1,0:T(8,128)S(1)}, f32[4,192,128]{2,1,0:T(8,128)}) custom-call(f32[5,8,8,128]{3,2,1,0:T(8,128)S(1)} %pad_add_fusion.state, f32[40,128]{1,0:T(8,128)S(1)} %shard_map.115.edge, f32[240,128]{1,0:T(8,128)S(1)} %collective-permute-done.3.refs_0_, ...), custom_call_target="tpu_custom_call" | custom-call | tf_op jit(solution)/shard_map/pallas_call | solution.py:52
  37.6 3.5 %all-to-all-start.1 = ((f32[4,192,128]{2,1,0:T(8,128)}), f32[4,192,128]{2,1,0:T(8,128)S(1)}, u32[]{:S(2)}, u32[]{:S(2)}) async-start(f32[4,192,128]{2,1,0:T(8,128)} %get-tuple-element.49.refs_0_), calls=%async_computation.1 | async-start | bytes 786432 | tf_op jit(solution)/shard_map/all_to_all | solution.py:825
  41.0 0.5 shard_map.122
  41.6 5.0 %collective-permute-start.9 = (f32[128,128]{1,0:T(8,128)S(1)}, f32[128,128]{1,0:T(8,128)S(1)}, u32[]{:S(2)}, u32[]{:S(2)}) collective-permute-start(f32[128,128]{1,0:T(8,128)S(1)} %get-tuple-element.52), channel_id=1, source_target_pairs={{1,2},{2,1},{3,4},{4,3},{5,6},{6,5},{7,8},{8,7},{9,10},{10,9},{11,... | collective-permute-start | bytes 196616 | tf_op jit(solution)/shard_map/ppermute | solution.py:746
  46.6 0.3 shard_map.123.partial
  47.0 0.9 %collective-permute-done.8.got_a = f32[96,128]{1,0:T(8,128)S(1)} collective-permute-done((f32[96,128]{1,0:T(8,128)S(1)}, f32[96,128]{1,0:T(8,128)S(1)}, u32[]{:S(2)}, u32[]{:S(2)}) %collective-permute-start.8) | collective-permute-done | bytes 49184 | tf_op jit(solution)/shard_map/ppermute | solution.py:747
  47.8 4.9 %collective-permute-done.9.got_b = f32[128,128]{1,0:T(8,128)S(1)} collective-permute-done((f32[128,128]{1,0:T(8,128)S(1)}, f32[128,128]{1,0:T(8,128)S(1)}, u32[]{:S(2)}, u32[]{:S(2)}) %collective-permute-start.9) | collective-permute-done | bytes 65568 | tf_op jit(solution)/shard_map/ppermute | solution.py:746
  52.7 0.5 shard_map.124
  53.2 3.1 %collective-permute-start.11 = (f32[128,128]{1,0:T(8,128)S(1)}, f32[128,128]{1,0:T(8,128)S(1)}, u32[]{:S(2)}, u32[]{:S(2)}) collective-permute-start(f32[128,128]{1,0:T(8,128)S(1)} %get-tuple-element.55), channel_id=1, source_target_pairs={{1,2},{2,1},{3,4},{4,3},{5,6},{6,5},{7,8},{8,7},{9,10},{10,9},{11,... | collective-permute-start | bytes 196616 | tf_op jit(solution)/shard_map/ppermute | solution.py:746
  56.4 1.0 %shard_map.120 = f32[5,8,8,128]{3,2,1,0:T(8,128)} custom-call(f32[5,10,16,128]{3,2,1,0:T(8,128)S(1)} %get-tuple-element.44.second, f32[5,14,16,128]{3,2,1,0:T(8,128)S(1)} %get-tuple-element.45.derived, f32[5,8,8,128]{3,2,1,0:T(8,128)S(1)} %get-tuple-element.46.ends, f32[5,8,8,128]{3,2,1,0:T(8,128)S(1)} %pad_add_fusion.state), custom_call_target="tpu_custom_call" | custom-call | tf_op jit(solution)/shard_map/pallas_call | solution.py:52
  57.4 0.3 shard_map.125.partial
  57.8 0.3 shard_map.126.received
  58.1 4.3 %collective-permute-done.11.got_b = f32[128,128]{1,0:T(8,128)S(1)} collective-permute-done((f32[128,128]{1,0:T(8,128)S(1)}, f32[128,128]{1,0:T(8,128)S(1)}, u32[]{:S(2)}, u32[]{:S(2)}) %collective-permute-start.11) | collective-permute-done | bytes 65568 | tf_op jit(solution)/shard_map/ppermute | solution.py:746
  62.4 1.3 %shard_map.127 = f32[16,4,512]{2,1,0:T(4,128)} custom-call(f32[4,64,128]{2,1,0:T(8,128)S(1)} %shard_map.125.partial, f32[96,128]{1,0:T(8,128)S(1)} %collective-permute-done.10.got_a, f32[128,128]{1,0:T(8,128)S(1)} %collective-permute-done.11.got_b, bf16[5,128,128]{2,1,0:T(8,128)(2,1)S(1)} %get-tuple-element.47.sides_far, f32[3,64,128]{2,1,0:T(8,128)S(1)} %shard_map.126.received), custom_call_target="tpu_custom_call" | custom-call | tf_op jit(solution)/shard_map/pallas_call | solution.py:52
  (38 shorter events, 0.7 us)
Async XLA Ops:
  0.6 1.0 %copy-start.1 = (f32[3,8,8,128]{3,2,1,0:T(8,128)S(1)}, f32[3,8,8,128]{3,2,1,0:T(8,128)}, u32[]{:S(2)}) copy-start(f32[3,8,8,128]{3,2,1,0:T(8,128)} %param.11) | copy-start | bytes 294916
  0.6 1.0 %copy-start.2 = (f32[8,8,128]{2,1,0:T(8,128)S(1)}, f32[8,8,128]{2,1,0:T(8,128)}, u32[]{:S(2)}) copy-start(f32[8,8,128]{2,1,0:T(8,128)} %param.10) | copy-start | bytes 98308
  0.6 1.0 %copy-start.3 = (f32[8,8,128]{2,1,0:T(8,128)S(1)}, f32[8,8,128]{2,1,0:T(8,128)}, u32[]{:S(2)}) copy-start(f32[8,8,128]{2,1,0:T(8,128)} %param.12) | copy-start | bytes 98308
  1.7 3.1 %copy-start = (f32[16,4,512]{2,1,0:T(4,128)S(1)}, f32[16,4,512]{2,1,0:T(4,128)}, u32[]{:S(2)}) copy-start(f32[16,4,512]{2,1,0:T(4,128)} %given.1) | copy-start | bytes 393220
  1.8 2.9 %collective-permute-start = (f32[24,128]{1,0:T(8,128)S(1)}, f32[24,128]{1,0:T(8,128)S(1)}, u32[]{:S(2)}, u32[]{:S(2)}) collective-permute-start(f32[24,128]{1,0:T(8,128)S(1)} %get-tuple-element.29.sent_a), channel_id=1, source_target_pairs={{1,0},{0,1},{3,2},{2,3},{5,4},{4,5},{7,6},{6,7},{9,8},{8,9},{11,10... | collective-permute-start | bytes 36872 | tf_op jit(solution)/shard_map/ppermute | solution.py:737
  1.9 4.1 %collective-permute-start.1 = (f32[24,128]{1,0:T(8,128)S(1)}, f32[24,128]{1,0:T(8,128)S(1)}, u32[]{:S(2)}, u32[]{:S(2)}) collective-permute-start(f32[24,128]{1,0:T(8,128)S(1)} %get-tuple-element.30.sent_b), channel_id=1, source_target_pairs={{3,0},{2,1},{1,2},{0,3},{7,4},{6,5},{5,6},{4,7},{11,8},{10,9},{9,1... | collective-permute-start | bytes 36872 | tf_op jit(solution)/shard_map/ppermute | solution.py:738
  3.5 7.1 %collective-permute-start.3 = (f32[240,128]{1,0:T(8,128)S(1)}, f32[240,128]{1,0:T(8,128)S(1)}, u32[]{:S(2)}, u32[]{:S(2)}) collective-permute-start(f32[240,128]{1,0:T(8,128)S(1)} %get-tuple-element.32), channel_id=1, source_target_pairs={{16,0},{0,16},{17,1},{1,17},{18,2},{2,18},{19,3},{3,19},{20,4},{4,... | collective-permute-start | bytes 368648 | tf_op jit(solution)/shard_map/ppermute | solution.py:740
  4.1 0.7 %copy-start.4 = (s32[16,6]{0,1:T(8,128)S(1)}, s32[16,6]{0,1:T(8,128)}, u32[]{:S(2)}) copy-start(s32[16,6]{0,1:T(8,128)} %param.17) | copy-start | bytes 1156
  5.3 0.7 %copy-start.8 = (s32[1,1,1,16]{3,2,1,0:T(1,128)S(1)}, s32[1,1,1,16]{3,2,1,0:T(1,128)}, u32[]{:S(2)}) copy-start(s32[1,1,1,16]{3,2,1,0:T(1,128)} %param.19) | copy-start | bytes 196
  5.3 1.3 %collective-permute-start.2 = (f32[96,128]{1,0:T(8,128)S(1)}, f32[96,128]{1,0:T(8,128)S(1)}, u32[]{:S(2)}, u32[]{:S(2)}) collective-permute-start(f32[96,128]{1,0:T(8,128)S(1)} %get-tuple-element.31), channel_id=1, source_target_pairs={{1,0},{0,1},{3,2},{2,3},{5,4},{4,5},{7,6},{6,7},{9,8},{8,9},{11,10... | collective-permute-start | bytes 147464 | tf_op jit(solution)/shard_map/ppermute | solution.py:762
  6.0 2.3 %copy-start.9 = (s32[1,1,1,16,1]{3,4,2,1,0:T(1,128)S(1)}, s32[1,1,1,16,1]{3,4,2,1,0:T(1,128)}, u32[]{:S(2)}) copy-start(s32[1,1,1,16,1]{3,4,2,1,0:T(1,128)} %param.18) | copy-start | bytes 196
  6.8 3.8 %collective-permute-start.4 = (f32[40,128]{1,0:T(8,128)S(1)}, f32[40,128]{1,0:T(8,128)S(1)}, u32[]{:S(2)}, u32[]{:S(2)}) collective-permute-start(f32[40,128]{1,0:T(8,128)S(1)} %shard_map.115.edge), channel_id=1, source_target_pairs={{16,0},{0,16},{17,1},{1,17},{18,2},{2,18},{19,3},{3,19},{20,4},{4,... | collective-permute-start | bytes 61448 | tf_op jit(solution)/shard_map/ppermute | solution.py:775
  10.6 4.2 %copy-start.6 = (f32[8,8]{1,0:T(8,128)S(1)}, f32[8,8]{1,0:T(8,128)}, u32[]{:S(2)}) copy-start(f32[8,8]{1,0:T(8,128)} %param.15) | copy-start | bytes 772
  10.7 4.1 %copy-start.5 = (f32[8,8]{1,0:T(8,128)S(1)}, f32[8,8]{1,0:T(8,128)}, u32[]{:S(2)}) copy-start(f32[8,8]{1,0:T(8,128)} %param.16) | copy-start | bytes 772
  10.7 5.1 %collective-permute-start.5 = (f32[168,128]{1,0:T(8,128)S(1)}, f32[168,128]{1,0:T(8,128)S(1)}, u32[]{:S(2)}, u32[]{:S(2)}) collective-permute-start(f32[168,128]{1,0:T(8,128)S(1)} %get-tuple-element.33), channel_id=1, source_target_pairs={{4,0},{0,4},{12,8},{8,12},{5,1},{1,5},{13,9},{9,13},{6,2},{2,6},{1... | collective-permute-start | bytes 258056 | tf_op jit(solution)/shard_map/ppermute | solution.py:779
  12.3 2.5 %copy-start.7 = (f32[16]{0:T(128)S(1)}, f32[16]{0:T(128)}, u32[]{:S(2)}) copy-start(f32[16]{0:T(128)} %param.14) | copy-start | bytes 196
  12.3 6.3 %collective-permute-start.6 = (f32[168,128]{1,0:T(8,128)S(1)}, f32[168,128]{1,0:T(8,128)S(1)}, u32[]{:S(2)}, u32[]{:S(2)}) collective-permute-start(f32[168,128]{1,0:T(8,128)S(1)} %get-tuple-element.34), channel_id=1, source_target_pairs={{12,0},{8,4},{4,8},{0,12},{13,1},{9,5},{5,9},{1,13},{14,2},{10,6},... | collective-permute-start | bytes 258056 | tf_op jit(solution)/shard_map/ppermute | solution.py:778
  19.9 17.6 %all-to-all-start = ((f32[4,104,128]{2,1,0:T(8,128)}), f32[4,104,128]{2,1,0:T(8,128)S(1)}, u32[]{:S(2)}, u32[]{:S(2)}) async-start(f32[4,104,128]{2,1,0:T(8,128)} %shard_map.121), calls=%async_computation | async-start | bytes 425984 | tf_op jit(solution)/shard_map/all_to_all | solution.py:825
  23.8 9.9 %collective-permute-start.7 = (f32[256,128]{1,0:T(8,128)S(1)}, f32[256,128]{1,0:T(8,128)S(1)}, u32[]{:S(2)}, u32[]{:S(2)}) collective-permute-start(f32[256,128]{1,0:T(8,128)S(1)} %get-tuple-element.43), channel_id=1, source_target_pairs={{1,2},{2,1},{3,4},{4,3},{5,6},{6,5},{7,8},{8,7},{9,10},{10,9},{11,... | collective-permute-start | bytes 393224 | tf_op jit(solution)/shard_map/ppermute | solution.py:815
  37.6 15.1 %all-to-all-start.1 = ((f32[4,192,128]{2,1,0:T(8,128)}), f32[4,192,128]{2,1,0:T(8,128)S(1)}, u32[]{:S(2)}, u32[]{:S(2)}) async-start(f32[4,192,128]{2,1,0:T(8,128)} %get-tuple-element.49.refs_0_), calls=%async_computation.1 | async-start | bytes 786432 | tf_op jit(solution)/shard_map/all_to_all | solution.py:825
  41.6 11.1 %collective-permute-start.9 = (f32[128,128]{1,0:T(8,128)S(1)}, f32[128,128]{1,0:T(8,128)S(1)}, u32[]{:S(2)}, u32[]{:S(2)}) collective-permute-start(f32[128,128]{1,0:T(8,128)S(1)} %get-tuple-element.52), channel_id=1, source_target_pairs={{1,2},{2,1},{3,4},{4,3},{5,6},{6,5},{7,8},{8,7},{9,10},{10,9},{11,... | collective-permute-start | bytes 196616 | tf_op jit(solution)/shard_map/ppermute | solution.py:746
  46.5 1.3 %collective-permute-start.8 = (f32[96,128]{1,0:T(8,128)S(1)}, f32[96,128]{1,0:T(8,128)S(1)}, u32[]{:S(2)}, u32[]{:S(2)}) collective-permute-start(f32[96,128]{1,0:T(8,128)S(1)} %get-tuple-element.51), channel_id=1, source_target_pairs={{1,0},{0,1},{3,2},{2,3},{5,4},{4,5},{7,6},{6,7},{9,8},{8,9},{11,10... | collective-permute-start | bytes 147464 | tf_op jit(solution)/shard_map/ppermute | solution.py:747
  53.2 9.2 %collective-permute-start.11 = (f32[128,128]{1,0:T(8,128)S(1)}, f32[128,128]{1,0:T(8,128)S(1)}, u32[]{:S(2)}, u32[]{:S(2)}) collective-permute-start(f32[128,128]{1,0:T(8,128)S(1)} %get-tuple-element.55), channel_id=1, source_target_pairs={{1,2},{2,1},{3,4},{4,3},{5,6},{6,5},{7,8},{8,7},{9,10},{10,9},{11,... | collective-permute-start | bytes 196616 | tf_op jit(solution)/shard_map/ppermute | solution.py:746
  56.3 1.8 %collective-permute-start.10 = (f32[96,128]{1,0:T(8,128)S(1)}, f32[96,128]{1,0:T(8,128)S(1)}, u32[]{:S(2)}, u32[]{:S(2)}) collective-permute-start(f32[96,128]{1,0:T(8,128)S(1)} %get-tuple-element.54), channel_id=1, source_target_pairs={{1,0},{0,1},{3,2},{2,3},{5,4},{4,5},{7,6},{6,7},{9,8},{8,9},{11,10... | collective-permute-start | bytes 147464 | tf_op jit(solution)/shard_map/ppermute | solution.py:747

commit v15 on v13

--- a/solution.py
+++ b/solution.py
@@ -136,7 +136,7 @@
 
 
 def pack_last_body(state, edge, *refs):
-    (y_a, y_b), refs = refs[-2:], refs[:-2]
+    (y_a, y_b), refs = refs[-2:], refs[:-3]
     beside_x, edges_x = refs[: len(refs) // 2], refs[len(refs) // 2 :]
     cells_x = state.shape[1]
     odd = is_odd("fy")
@@ -368,9 +368,9 @@
 
 def flow_sources_body(count, state, edge, *refs):
     beside_x, refs = refs[:count], refs[count:]
-    got_a, got_b, pair, spread, labels, _, send, wide, derived, lamb_rows, ends, above, below = refs
+    got_b, got_a, pair, spread, labels, _, send, wide, derived, lamb_rows, ends, above, below = refs
     cells_x = state.shape[1]
-    above[...], below[...] = paired(is_odd("fy"), got_a[...], got_b[...])
+    above[...], below[...] = paired(is_odd("fy"), got_a[...], got_b[0 : got_a.shape[0]])
     assemble_speeds(wide, state, beside_x, above, below)
     derive_speeds(wide, derived, 0, cells_x + 2)
     inverse = 1.0 / edge[0:8]
@@ -390,9 +390,9 @@
 
 def flow_stages_body(count, state, edge, *refs):
     beside_x, edges_x, refs = refs[:count], refs[count : 2 * count], refs[2 * count :]
-    got_a, got_b, pair, spread, _, second, derived, ends_out, send, *refs = refs
+    got_b, got_a, pair, spread, _, second, derived, ends_out, send, *refs = refs
     lamb_rows, ends, first, wide, rim, above, below = refs
-    above[...], below[...] = paired(is_odd("fy"), got_a[...], got_b[...])
+    above[...], below[...] = paired(is_odd("fy"), got_a[...], got_b[0 : got_a.shape[0]])
     assemble(wide, rim, state, edge, beside_x, edges_x, above, below)
     planes = wide.shape[1]
     cells_x = planes - 2 * HALO
@@ -443,7 +443,8 @@
     size = message_a.shape[0]
     faces_out(state, message_b, message_a)
     message_a[...], message_b[0:size] = paired(odd, message_a[...], message_b[0:size])
-    message_b[size:] = jnp.zeros((message_b.shape[0] - size, 128), F32)
+    if message_b.shape[0] > size:
+        message_b[size:] = jnp.zeros((message_b.shape[0] - size, 128), F32)
 
 
 def lift(total, before, after, sides, factor):
@@ -748,7 +749,7 @@
     turning = [pltpu.VMEM((512, 128), F32), pltpu.VMEM((4, 4 * elements, 128), F32)]
     sound, to_a, to_b = call(
         acoustic_start_body,
-        [held, faces, (2 * faces[0], size)],
+        [held, faces, faces],
         acoustic,
         edge_a,
         scratch=turning,
@@ -764,12 +765,12 @@
         flow_b,
         edge_a,
         edge_b,
-        got_a,
+        to_a,
         last=1,
     )[0]
     edges_x = [lax.ppermute(edge, "fx", shifted((size_x,), (step,))) for step in x_steps]
     y_shape = (5 * cells_x * HALO + 48, 128)
-    y_a, y_b = call(pack_last_body, [y_shape, y_shape], state, edge, *beside_x, *edges_x, cost=1)
+    y_a, y_b = call(pack_last_body, [y_shape, (y_shape[0] + 8, 128)], state, edge, *beside_x, *edges_x, got_a, last=1, cost=1)
     y_second = lax.ppermute(y_b, "fy", partners((size_y,), 0, True))
     y_first = lax.ppermute(y_a, "fy", partners((size_y,), 0, False))
 
@@ -838,8 +839,8 @@
         state,
         edge,
         *beside_x,
+        y_second,
         y_first,
-        y_second,
         pair,
         spread,
         labels,
@@ -866,8 +867,8 @@
         edge,
         *beside_x,
         *edges_x,
+        y_second,
         y_first,
-        y_second,
         pair,
         spread,
         partial,

time: 58.3 us -> 56.4 us (0.967)
  waiting for transfers between devices: 15.4 us -> 12.3 us
  local copies, waits for them, and re-layouts: 1.3 us -> 2.02 us
    ppermute x3, waiting for transfers between devices: 8.94 us -> 6.77 us  [traces(): far_got = lax.ppermute(to_b, names, far_pairs)]
    ppermute x3, starting transfers between devices: 15 us -> 16.3 us  [traces(): far_got = lax.ppermute(to_b, names, far_pairs)]
    ppermute x1, waiting for transfers between devices: 0.01 us -> 1.25 us  [per_device(): y_first = lax.ppermute(y_a, 'fy', partners((size_y,), 0, False))]
    all_to_all x2, waiting for transfers between devices: 3.32 us -> 2.31 us  [route(): return lax.all_to_all(send, 'fy', split_axis=0, concat_axis=0, tiled=True)]
    unnamed x20, local copies, waits for them, and re-layouts: 1.3 us -> 2.02 us
    ppermute x1, starting transfers between devices: 1.38 us -> 0.69 us  [per_device(): y_second = lax.ppermute(y_b, 'fy', partners((size_y,), 0, True))]
    ppermute x3, waiting for transfers between devices: 1.51 us -> 0.88 us  [traces(): return (lax.ppermute(to_a, names, near_pairs), far_got)]
where the time goes in v15:
time: 56.4 us; the launch traced here: 56 us
  starting transfers between devices  28 us (50%)
  waiting for transfers between devices  12.3 us (22%)
  Pallas kernels  11.7 us (21%)
  local copies, waits for them, and re-layouts  2.02 us (4%)
  other arithmetic  1 us (2%)
  between operations  0.9 us (2%)
    ppermute x3, starting transfers between devices, traces(): far_got = lax.ppermute(to_b, names, far_pairs)  16.3 us
    pallas_call x15, Pallas kernels, call(): pl.pallas_call(body, out_shape=outs, in_specs=[whole] * (len(operands) -...  11.7 us
    all_to_all x2, starting transfers between devices, route(): return lax.all_to_all(send, 'fy', split_axis=0, concat_axis=0, tiled=True)  7.05 us
    ppermute x3, waiting for transfers between devices, traces(): far_got = lax.ppermute(to_b, names, far_pairs)  6.77 us
    all_to_all x2, waiting for transfers between devices, route(): return lax.all_to_all(send, 'fy', split_axis=0, concat_axis=0, tiled=True)  2.31 us
    unnamed x20, local copies, waits for them, and re-layouts  2.02 us
    ppermute x1, starting transfers between devices, per_device(): edge_b = lax.ppermute(flow_b, 'fz', partners((size_z,), 0, True))  1.64 us
    ppermute x1, starting transfers between devices, per_device(): lax.ppermute(edge, 'fx', shifted((size_x,), (step,)))  1.56 us
  transfers between devices with their start and end apart: 14, of which 7 were waited for; matrix products, arithmetic and copies ran while one was open for 0% of the time, Pallas kernels for 15%

profile of v15, /device:TPU:2, one launch (start us, length us, event | category | flops | bytes accessed | tf_op | source)
XLA Modules:
  0.0 56.0 jit_solution(5951763865919469702)
XLA Ops:
  0.7 0.9 %broadcast_multiply_fusion = f32[3,8,8,128]{3,2,1,0:T(8,128)S(1)} fusion(f32[3,8,8,128]{3,2,1,0:T(8,128)} %param.11, f32[8,8,128]{2,1,0:T(8,128)} %param.10), kind=kLoop, calls=%fused_computation.1 | loop fusion | flops 24576 | bytes 229376 | tf_op jit(solution)/shard_map/mul | solution.py:727
  1.9 1.6 %collective-permute-start.1 = (f32[24,128]{1,0:T(8,128)S(1)}, f32[24,128]{1,0:T(8,128)S(1)}, u32[]{:S(2)}, u32[]{:S(2)}) collective-permute-start(f32[24,128]{1,0:T(8,128)S(1)} %get-tuple-element.29.sent_b), channel_id=1, source_target_pairs={{3,0},{2,1},{1,2},{0,3},{7,4},{6,5},{5,6},{4,7},{11,8},{10,9},{9,1... | collective-permute-start | bytes 36872 | tf_op jit(solution)/shard_map/ppermute | solution.py:734
  3.5 0.5 collective-permute-start.2
  4.1 0.7 %copy-done.4 = s32[16,6]{0,1:T(8,128)S(1)} copy-done((s32[16,6]{0,1:T(8,128)S(1)}, s32[16,6]{0,1:T(8,128)}, u32[]{:S(2)}) %copy-start.4) | copy-done | bytes 408
  4.8 0.6 %copy-done.8 = s32[1,1,1,16]{3,2,1,0:T(1,128)S(1)} copy-done((s32[1,1,1,16]{3,2,1,0:T(1,128)S(1)}, s32[1,1,1,16]{3,2,1,0:T(1,128)}, u32[]{:S(2)}) %copy-start.8) | copy-done | bytes 88
  5.4 0.6 %shard_map.114 = (f32[4,64,128]{2,1,0:T(8,128)S(1)}, f32[96,128]{1,0:T(8,128)S(1)}, f32[96,128]{1,0:T(8,128)S(1)}) custom-call(f32[16,4,512]{2,1,0:T(4,128)S(1)} %copy-done, f32[24,128]{1,0:T(8,128)S(1)} %collective-permute-done._.got_a), custom_call_target="tpu_custom_call" | custom-call | tf_op jit(solution)/shard_map/pallas_call | solution.py:52
  6.2 1.6 %collective-permute-start.3 = (f32[40,128]{1,0:T(8,128)S(1)}, f32[40,128]{1,0:T(8,128)S(1)}, u32[]{:S(2)}, u32[]{:S(2)}) collective-permute-start(f32[40,128]{1,0:T(8,128)S(1)} %shard_map.115.edge), channel_id=1, source_target_pairs={{16,0},{0,16},{17,1},{1,17},{18,2},{2,18},{19,3},{3,19},{20,4},{4,... | collective-permute-start | bytes 61448 | tf_op jit(solution)/shard_map/ppermute | solution.py:771
  7.8 5.2 %collective-permute-start.7 = (f32[96,128]{1,0:T(8,128)S(1)}, f32[96,128]{1,0:T(8,128)S(1)}, u32[]{:S(2)}, u32[]{:S(2)}) collective-permute-start(f32[96,128]{1,0:T(8,128)S(1)} %get-tuple-element.44), channel_id=1, source_target_pairs={{1,2},{2,1},{3,4},{4,3},{5,6},{6,5},{7,8},{8,7},{9,10},{10,9},{11,... | collective-permute-start | bytes 147464 | tf_op jit(solution)/shard_map/ppermute | solution.py:742
  13.1 0.7 %collective-permute-start.5 = (f32[176,128]{1,0:T(8,128)S(1)}, f32[176,128]{1,0:T(8,128)S(1)}, u32[]{:S(2)}, u32[]{:S(2)}) collective-permute-start(f32[176,128]{1,0:T(8,128)S(1)} %get-tuple-element.32), channel_id=1, source_target_pairs={{12,0},{8,4},{4,8},{0,12},{13,1},{9,5},{5,9},{1,13},{14,2},{10,6},... | collective-permute-start | bytes 270344 | tf_op jit(solution)/shard_map/ppermute | solution.py:774
  13.8 0.6 %copy-done.7 = f32[16]{0:T(128)S(1)} copy-done((f32[16]{0:T(128)S(1)}, f32[16]{0:T(128)}, u32[]{:S(2)}) %copy-start.7) | copy-done | bytes 88
  14.5 1.0 %shard_map.117 = (bf16[5,128,128]{2,1,0:T(8,128)(2,1)S(1)}, bf16[5,128,128]{2,1,0:T(8,128)(2,1)S(1)}, f32[128,64]{1,0:T(8,128)S(1)}, f32[128,128]{1,0:T(8,128)S(...) custom-call(f32[32,16]{1,0:T(8,128)S(1)} %pad_add_fusion.1.packed), custom_call_target="tpu_custom_call" | custom-call | flops 1 | bytes 1 | tf_op jit(solution)/shard_map/pallas_call | solution.py:52
  15.5 1.7 %collective-permute-done.7.refs_6_.got_b = f32[96,128]{1,0:T(8,128)S(1)} collective-permute-done((f32[96,128]{1,0:T(8,128)S(1)}, f32[96,128]{1,0:T(8,128)S(1)}, u32[]{:S(2)}, u32[]{:S(2)}) %collective-permute-start.7) | collective-permute-done | bytes 49184 | tf_op jit(solution)/shard_map/ppermute | solution.py:742
  17.2 1.3 %collective-permute-done.6.refs_3_.refs_2_ = f32[168,128]{1,0:T(8,128)S(1)} collective-permute-done((f32[168,128]{1,0:T(8,128)S(1)}, f32[168,128]{1,0:T(8,128)S(1)}, u32[]{:S(2)}, u32[]{:S(2)}) %collective-permute-start.6) | collective-permute-done | bytes 86048 | tf_op jit(solution)/shard_map/ppermute | solution.py:775
  18.4 1.1 %collective-permute-done.5.refs_2_.refs_1_ = f32[176,128]{1,0:T(8,128)S(1)} collective-permute-done((f32[176,128]{1,0:T(8,128)S(1)}, f32[176,128]{1,0:T(8,128)S(1)}, u32[]{:S(2)}, u32[]{:S(2)}) %collective-permute-start.5) | collective-permute-done | bytes 90144 | tf_op jit(solution)/shard_map/ppermute | solution.py:774
  19.5 1.3 %shard_map.121 = f32[4,104,128]{2,1,0:T(8,128)} custom-call(f32[5,8,8,128]{3,2,1,0:T(8,128)S(1)} %pad_add_fusion.state, f32[40,128]{1,0:T(8,128)S(1)} %shard_map.115.edge, f32[240,128]{1,0:T(8,128)S(1)} %collective-permute-done.2.refs_0_, f32[176,128]{1,0:T(8,128)S(1)} %collective-permute-done.5.refs_2_.refs_1_, ...), custom_call_target="tpu_custom_call" | custom-call | tf_op jit(solution)/shard_map/pallas_call | solution.py:52
  20.9 3.6 %all-to-all-start = ((f32[4,104,128]{2,1,0:T(8,128)}), f32[4,104,128]{2,1,0:T(8,128)S(1)}, u32[]{:S(2)}, u32[]{:S(2)}) async-start(f32[4,104,128]{2,1,0:T(8,128)} %shard_map.121), calls=%async_computation | async-start | bytes 425984 | tf_op jit(solution)/shard_map/all_to_all | solution.py:818
  24.4 0.3 shard_map.118.refs_6_.partial
  24.8 3.9 %shard_map.119 = (f32[5,10,16,128]{3,2,1,0:T(8,128)S(1)}, f32[5,14,16,128]{3,2,1,0:T(8,128)S(1)}, f32[5,8,8,128]{3,2,1,0:T(8,128)S(1)}, f32[4,192,128]{2,1,0:T(8,128)}) custom-call(f32[5,8,8,128]{3,2,1,0:T(8,128)S(1)} %pad_add_fusion.state, f32[40,128]{1,0:T(8,128)S(1)} %shard_map.115.edge, f32[240,128]{1,0:T(8,128)S(1)} %collective-permute-done.2.refs_0_, ...), custom_call_target="tpu_custom_call" | custom-call | tf_op jit(solution)/shard_map/pallas_call | solution.py:52
  28.7 2.3 %all-to-all-done.received.refs_0_.labelled = f32[4,104,128]{2,1,0:T(8,128)S(1)} async-done(((f32[4,104,128]{2,1,0:T(8,128)}), f32[4,104,128]{2,1,0:T(8,128)S(1)}, u32[]{:S(2)}, u32[]{:S(2)}) %all-to-all-start) | async-done | bytes 213024 | tf_op jit(solution)/shard_map/all_to_all | solution.py:818
  31.0 3.5 %all-to-all-start.1 = ((f32[4,192,128]{2,1,0:T(8,128)}), f32[4,192,128]{2,1,0:T(8,128)S(1)}, u32[]{:S(2)}, u32[]{:S(2)}) async-start(f32[4,192,128]{2,1,0:T(8,128)} %get-tuple-element.47.refs_0_), calls=%async_computation.1 | async-start | bytes 786432 | tf_op jit(solution)/shard_map/all_to_all | solution.py:818
  34.4 0.5 shard_map.122
  35.0 6.0 %collective-permute-start.9 = (f32[128,128]{1,0:T(8,128)S(1)}, f32[128,128]{1,0:T(8,128)S(1)}, u32[]{:S(2)}, u32[]{:S(2)}) collective-permute-start(f32[128,128]{1,0:T(8,128)S(1)} %get-tuple-element.50), channel_id=1, source_target_pairs={{1,2},{2,1},{3,4},{4,3},{5,6},{6,5},{7,8},{8,7},{9,10},{10,9},{11,... | collective-permute-start | bytes 196616 | tf_op jit(solution)/shard_map/ppermute | solution.py:742
  41.0 0.3 shard_map.123.partial
  41.4 0.9 %collective-permute-done.8.got_a = f32[96,128]{1,0:T(8,128)S(1)} collective-permute-done((f32[96,128]{1,0:T(8,128)S(1)}, f32[96,128]{1,0:T(8,128)S(1)}, u32[]{:S(2)}, u32[]{:S(2)}) %collective-permute-start.8) | collective-permute-done | bytes 49184 | tf_op jit(solution)/shard_map/ppermute | solution.py:743
  42.2 2.8 %collective-permute-done.9.got_b = f32[128,128]{1,0:T(8,128)S(1)} collective-permute-done((f32[128,128]{1,0:T(8,128)S(1)}, f32[128,128]{1,0:T(8,128)S(1)}, u32[]{:S(2)}, u32[]{:S(2)}) %collective-permute-start.9) | collective-permute-done | bytes 65568 | tf_op jit(solution)/shard_map/ppermute | solution.py:742
  45.0 0.5 shard_map.124
  45.6 5.1 %collective-permute-start.11 = (f32[128,128]{1,0:T(8,128)S(1)}, f32[128,128]{1,0:T(8,128)S(1)}, u32[]{:S(2)}, u32[]{:S(2)}) collective-permute-start(f32[128,128]{1,0:T(8,128)S(1)} %get-tuple-element.53), channel_id=1, source_target_pairs={{1,2},{2,1},{3,4},{4,3},{5,6},{6,5},{7,8},{8,7},{9,10},{10,9},{11,... | collective-permute-start | bytes 196616 | tf_op jit(solution)/shard_map/ppermute | solution.py:742
  50.7 1.0 %shard_map.120 = f32[5,8,8,128]{3,2,1,0:T(8,128)} custom-call(f32[5,10,16,128]{3,2,1,0:T(8,128)S(1)} %get-tuple-element.41.second, f32[5,14,16,128]{3,2,1,0:T(8,128)S(1)} %get-tuple-element.42.derived, f32[5,8,8,128]{3,2,1,0:T(8,128)S(1)} %get-tuple-element.43.ends, f32[5,8,8,128]{3,2,1,0:T(8,128)S(1)} %pad_add_fusion.state), custom_call_target="tpu_custom_call" | custom-call | tf_op jit(solution)/shard_map/pallas_call | solution.py:52
  51.7 0.3 shard_map.125.partial
  52.1 0.3 shard_map.126.received
  52.4 2.3 %collective-permute-done.11.got_b = f32[128,128]{1,0:T(8,128)S(1)} collective-permute-done((f32[128,128]{1,0:T(8,128)S(1)}, f32[128,128]{1,0:T(8,128)S(1)}, u32[]{:S(2)}, u32[]{:S(2)}) %collective-permute-start.11) | collective-permute-done | bytes 65568 | tf_op jit(solution)/shard_map/ppermute | solution.py:742
  54.7 1.3 %shard_map.127 = f32[16,4,512]{2,1,0:T(4,128)} custom-call(f32[4,64,128]{2,1,0:T(8,128)S(1)} %shard_map.125.partial, f32[96,128]{1,0:T(8,128)S(1)} %collective-permute-done.10.got_a, f32[128,128]{1,0:T(8,128)S(1)} %collective-permute-done.11.got_b, bf16[5,128,128]{2,1,0:T(8,128)(2,1)S(1)} %get-tuple-element.45.sides_far, f32[3,64,128]{2,1,0:T(8,128)S(1)} %shard_map.126.received), custom_call_target="tpu_custom_call" | custom-call | tf_op jit(solution)/shard_map/pallas_call | solution.py:52
  (38 shorter events, 0.7 us)
Async XLA Ops:
  0.6 1.0 %copy-start.1 = (f32[3,8,8,128]{3,2,1,0:T(8,128)S(1)}, f32[3,8,8,128]{3,2,1,0:T(8,128)}, u32[]{:S(2)}) copy-start(f32[3,8,8,128]{3,2,1,0:T(8,128)} %param.11) | copy-start | bytes 294916
  0.6 1.0 %copy-start.2 = (f32[8,8,128]{2,1,0:T(8,128)S(1)}, f32[8,8,128]{2,1,0:T(8,128)}, u32[]{:S(2)}) copy-start(f32[8,8,128]{2,1,0:T(8,128)} %param.10) | copy-start | bytes 98308
  0.6 1.0 %copy-start.3 = (f32[8,8,128]{2,1,0:T(8,128)S(1)}, f32[8,8,128]{2,1,0:T(8,128)}, u32[]{:S(2)}) copy-start(f32[8,8,128]{2,1,0:T(8,128)} %param.12) | copy-start | bytes 98308
  1.7 3.7 %copy-start = (f32[16,4,512]{2,1,0:T(4,128)S(1)}, f32[16,4,512]{2,1,0:T(4,128)}, u32[]{:S(2)}) copy-start(f32[16,4,512]{2,1,0:T(4,128)} %given.1) | copy-start | bytes 393220
  1.8 3.6 %collective-permute-start = (f32[24,128]{1,0:T(8,128)S(1)}, f32[24,128]{1,0:T(8,128)S(1)}, u32[]{:S(2)}, u32[]{:S(2)}) collective-permute-start(f32[24,128]{1,0:T(8,128)S(1)} %get-tuple-element.28.sent_a), channel_id=1, source_target_pairs={{1,0},{0,1},{3,2},{2,3},{5,4},{4,5},{7,6},{6,7},{9,8},{8,9},{11,10... | collective-permute-start | bytes 36872 | tf_op jit(solution)/shard_map/ppermute | solution.py:733
  1.9 4.2 %collective-permute-start.1 = (f32[24,128]{1,0:T(8,128)S(1)}, f32[24,128]{1,0:T(8,128)S(1)}, u32[]{:S(2)}, u32[]{:S(2)}) collective-permute-start(f32[24,128]{1,0:T(8,128)S(1)} %get-tuple-element.29.sent_b), channel_id=1, source_target_pairs={{3,0},{2,1},{1,2},{0,3},{7,4},{6,5},{5,6},{4,7},{11,8},{10,9},{9,1... | collective-permute-start | bytes 36872 | tf_op jit(solution)/shard_map/ppermute | solution.py:734
  3.5 9.5 %collective-permute-start.2 = (f32[240,128]{1,0:T(8,128)S(1)}, f32[240,128]{1,0:T(8,128)S(1)}, u32[]{:S(2)}, u32[]{:S(2)}) collective-permute-start(f32[240,128]{1,0:T(8,128)S(1)} %get-tuple-element.31), channel_id=1, source_target_pairs={{16,0},{0,16},{17,1},{1,17},{18,2},{2,18},{19,3},{3,19},{20,4},{4,... | collective-permute-start | bytes 368648 | tf_op jit(solution)/shard_map/ppermute | solution.py:736
  4.1 0.7 %copy-start.4 = (s32[16,6]{0,1:T(8,128)S(1)}, s32[16,6]{0,1:T(8,128)}, u32[]{:S(2)}) copy-start(s32[16,6]{0,1:T(8,128)} %param.17) | copy-start | bytes 1156
  4.8 0.7 %copy-start.8 = (s32[1,1,1,16]{3,2,1,0:T(1,128)S(1)}, s32[1,1,1,16]{3,2,1,0:T(1,128)}, u32[]{:S(2)}) copy-start(s32[1,1,1,16]{3,2,1,0:T(1,128)} %param.19) | copy-start | bytes 196
  6.0 1.8 %copy-start.9 = (s32[1,1,1,16,1]{3,4,2,1,0:T(1,128)S(1)}, s32[1,1,1,16,1]{3,4,2,1,0:T(1,128)}, u32[]{:S(2)}) copy-start(s32[1,1,1,16,1]{3,4,2,1,0:T(1,128)} %param.18) | copy-start | bytes 196
  6.0 7.0 %collective-permute-start.4 = (f32[96,128]{1,0:T(8,128)S(1)}, f32[96,128]{1,0:T(8,128)S(1)}, u32[]{:S(2)}, u32[]{:S(2)}) collective-permute-start(f32[96,128]{1,0:T(8,128)S(1)} %get-tuple-element.30._), channel_id=1, source_target_pairs={{1,0},{0,1},{3,2},{2,3},{5,4},{4,5},{7,6},{6,7},{9,8},{8,9},{11,10... | collective-permute-start | bytes 147464 | tf_op jit(solution)/shard_map/ppermute | solution.py:743
  6.2 6.8 %collective-permute-start.3 = (f32[40,128]{1,0:T(8,128)S(1)}, f32[40,128]{1,0:T(8,128)S(1)}, u32[]{:S(2)}, u32[]{:S(2)}) collective-permute-start(f32[40,128]{1,0:T(8,128)S(1)} %shard_map.115.edge), channel_id=1, source_target_pairs={{16,0},{0,16},{17,1},{1,17},{18,2},{2,18},{19,3},{3,19},{20,4},{4,... | collective-permute-start | bytes 61448 | tf_op jit(solution)/shard_map/ppermute | solution.py:771
  7.8 9.4 %collective-permute-start.7 = (f32[96,128]{1,0:T(8,128)S(1)}, f32[96,128]{1,0:T(8,128)S(1)}, u32[]{:S(2)}, u32[]{:S(2)}) collective-permute-start(f32[96,128]{1,0:T(8,128)S(1)} %get-tuple-element.44), channel_id=1, source_target_pairs={{1,2},{2,1},{3,4},{4,3},{5,6},{6,5},{7,8},{8,7},{9,10},{10,9},{11,... | collective-permute-start | bytes 147464 | tf_op jit(solution)/shard_map/ppermute | solution.py:742
  13.1 0.8 %copy-start.6 = (f32[8,8]{1,0:T(8,128)S(1)}, f32[8,8]{1,0:T(8,128)}, u32[]{:S(2)}) copy-start(f32[8,8]{1,0:T(8,128)} %param.15) | copy-start | bytes 772
  13.1 0.7 %copy-start.5 = (f32[8,8]{1,0:T(8,128)S(1)}, f32[8,8]{1,0:T(8,128)}, u32[]{:S(2)}) copy-start(f32[8,8]{1,0:T(8,128)} %param.16) | copy-start | bytes 772
  13.1 6.4 %collective-permute-start.5 = (f32[176,128]{1,0:T(8,128)S(1)}, f32[176,128]{1,0:T(8,128)S(1)}, u32[]{:S(2)}, u32[]{:S(2)}) collective-permute-start(f32[176,128]{1,0:T(8,128)S(1)} %get-tuple-element.32), channel_id=1, source_target_pairs={{12,0},{8,4},{4,8},{0,12},{13,1},{9,5},{5,9},{1,13},{14,2},{10,6},... | collective-permute-start | bytes 270344 | tf_op jit(solution)/shard_map/ppermute | solution.py:774
  13.8 0.7 %copy-start.7 = (f32[16]{0:T(128)S(1)}, f32[16]{0:T(128)}, u32[]{:S(2)}) copy-start(f32[16]{0:T(128)} %param.14) | copy-start | bytes 196
  13.8 4.6 %collective-permute-start.6 = (f32[168,128]{1,0:T(8,128)S(1)}, f32[168,128]{1,0:T(8,128)S(1)}, u32[]{:S(2)}, u32[]{:S(2)}) collective-permute-start(f32[168,128]{1,0:T(8,128)S(1)} %get-tuple-element.33), channel_id=1, source_target_pairs={{4,0},{0,4},{12,8},{8,12},{5,1},{1,5},{13,9},{9,13},{6,2},{2,6},{1... | collective-permute-start | bytes 258056 | tf_op jit(solution)/shard_map/ppermute | solution.py:775
  20.9 10.1 %all-to-all-start = ((f32[4,104,128]{2,1,0:T(8,128)}), f32[4,104,128]{2,1,0:T(8,128)S(1)}, u32[]{:S(2)}, u32[]{:S(2)}) async-start(f32[4,104,128]{2,1,0:T(8,128)} %shard_map.121), calls=%async_computation | async-start | bytes 425984 | tf_op jit(solution)/shard_map/all_to_all | solution.py:818
  31.0 14.1 %all-to-all-start.1 = ((f32[4,192,128]{2,1,0:T(8,128)}), f32[4,192,128]{2,1,0:T(8,128)S(1)}, u32[]{:S(2)}, u32[]{:S(2)}) async-start(f32[4,192,128]{2,1,0:T(8,128)} %get-tuple-element.47.refs_0_), calls=%async_computation.1 | async-start | bytes 786432 | tf_op jit(solution)/shard_map/all_to_all | solution.py:818
  35.0 10.1 %collective-permute-start.9 = (f32[128,128]{1,0:T(8,128)S(1)}, f32[128,128]{1,0:T(8,128)S(1)}, u32[]{:S(2)}, u32[]{:S(2)}) collective-permute-start(f32[128,128]{1,0:T(8,128)S(1)} %get-tuple-element.50), channel_id=1, source_target_pairs={{1,2},{2,1},{3,4},{4,3},{5,6},{6,5},{7,8},{8,7},{9,10},{10,9},{11,... | collective-permute-start | bytes 196616 | tf_op jit(solution)/shard_map/ppermute | solution.py:742
  40.9 1.3 %collective-permute-start.8 = (f32[96,128]{1,0:T(8,128)S(1)}, f32[96,128]{1,0:T(8,128)S(1)}, u32[]{:S(2)}, u32[]{:S(2)}) collective-permute-start(f32[96,128]{1,0:T(8,128)S(1)} %get-tuple-element.49), channel_id=1, source_target_pairs={{1,0},{0,1},{3,2},{2,3},{5,4},{4,5},{7,6},{6,7},{9,8},{8,9},{11,10... | collective-permute-start | bytes 147464 | tf_op jit(solution)/shard_map/ppermute | solution.py:743
  45.6 9.2 %collective-permute-start.11 = (f32[128,128]{1,0:T(8,128)S(1)}, f32[128,128]{1,0:T(8,128)S(1)}, u32[]{:S(2)}, u32[]{:S(2)}) collective-permute-start(f32[128,128]{1,0:T(8,128)S(1)} %get-tuple-element.53), channel_id=1, source_target_pairs={{1,2},{2,1},{3,4},{4,3},{5,6},{6,5},{7,8},{8,7},{9,10},{10,9},{11,... | collective-permute-start | bytes 196616 | tf_op jit(solution)/shard_map/ppermute | solution.py:742
  50.7 1.7 %collective-permute-start.10 = (f32[96,128]{1,0:T(8,128)S(1)}, f32[96,128]{1,0:T(8,128)S(1)}, u32[]{:S(2)}, u32[]{:S(2)}) collective-permute-start(f32[96,128]{1,0:T(8,128)S(1)} %get-tuple-element.52), channel_id=1, source_target_pairs={{1,0},{0,1},{3,2},{2,3},{5,4},{4,5},{7,6},{6,7},{9,8},{8,9},{11,10... | collective-permute-start | bytes 147464 | tf_op jit(solution)/shard_map/ppermute | solution.py:743

commit v16 on v15

--- a/solution.py
+++ b/solution.py
@@ -490,7 +490,7 @@
     lift(out, front, rear, sides, TIME_STEP * mix[1] * PENALTY)
 
 
-def acoustic_start_body(given, _, state, message_a, message_b, turned, stored):
+def acoustic_start_body(given, local, _, state, message_a, message_b, turned, stored):
     count = given.shape[0]
     for e in range(count):
         for t in range(4):
@@ -509,6 +509,7 @@
     for c in range(4):
         state[c] = fields[c]
     faces_sent(is_odd("fz"), state, message_a, message_b)
+    message_b[96:104] = local[...]
 
 
 def natural_order(state, out, turned, stored):
@@ -543,27 +544,62 @@
         out[c] += value[c * 64 : c * 64 + 64]
 
 
-def acoustic_far_body(mix, kind, partial, got_a, got_b, sides_far, received, *refs):
-    if kind == "last":
-        given_out, before, after, out, turned, stored = refs
-    elif kind == "first":
-        _, out, message_a, message_b, before, after, source = refs
-        place(received, received, source, 0)
-        received = source
-    else:
-        labelled, out, message_a, message_b, before, after, source = refs
-        place(received, labelled, source, 0)
-        received = source
+def arrived(odd, got_a, got_b, before, after):
+    none = jnp.zeros((96, 128), F32)
+    near = none if got_a is None else got_a[0:96]
+    after[...], before[...] = paired(odd, near, none if got_b is None else got_b[0:96])
+
+
+def acoustic_first_body(partial, got_a, got_b, sides_far, received, _, out, message_a, message_b, before, after, source):
     odd = is_odd("fz")
-    after[...], before[...] = paired(odd, got_a[0:96], got_b[0:96])
+    place(received, received, source, 0)
+    arrived(odd, got_a, got_b, before, after)
     out[0] = partial[0]
     for c in range(3):
-        out[1 + c] = partial[1 + c] + (TIME_STEP * mix[1]) * received[c]
-    remote_part(out, before, after, sides_far, TIME_STEP * mix[1] * PENALTY)
-    if kind == "last":
-        natural_order(out, given_out, turned, stored)
-    else:
-        faces_sent(odd, out, message_a, message_b)
+        out[1 + c] = partial[1 + c] + (TIME_STEP * MIXES[0][1]) * source[c]
+    remote_part(out, before, after, sides_far, TIME_STEP * MIXES[0][1] * PENALTY)
+    faces_sent(odd, out, message_a, message_b)
+
+
+def acoustic_near_body(
+    partial, got_a, sides_far, received, labelled, out, message_b, before, after, source, spare
+):
+    odd = is_odd("fz")
+    place(received, labelled, source, 0)
+    arrived(odd, got_a, None, before, after)
+    out[0] = partial[0]
+    for c in range(3):
+        out[1 + c] = partial[1 + c] + (TIME_STEP * MIXES[1][1]) * source[c]
+    remote_part(out, before, after, sides_far, TIME_STEP * MIXES[1][1] * PENALTY)
+    faces_sent(odd, out, spare, message_b)
+
+
+def acoustic_rest_body(partial, got_b, sides_far, out, message_a, before, after, spare):
+    odd = is_odd("fz")
+    arrived(odd, None, got_b, before, after)
+    out[...] = partial[...]
+    remote_part(out, before, after, sides_far, TIME_STEP * MIXES[1][1] * PENALTY)
+    faces_sent(odd, out, message_a, spare)
+
+
+def mirror_body(sent_b, sides_partner, change, before, after, spare, state):
+    odd = jnp.logical_not(is_odd("fz"))
+    arrived(odd, None, sent_b, before, after)
+    state[...] = jnp.zeros(state.shape, F32)
+    remote_part(state, before, after, sides_partner, TIME_STEP * MIXES[1][1] * PENALTY)
+    faces_sent(odd, state, spare, change)
+
+
+def acoustic_last_body(
+    partial, got_a, got_b, change, sides_far, source, given_out, before, after, out, turned, stored
+):
+    odd = is_odd("fz")
+    after[...], before[...] = paired(odd, got_a[0:96], got_b[0:96] + change[...])
+    out[0] = partial[0]
+    for c in range(3):
+        out[1 + c] = partial[1 + c] + (TIME_STEP * MIXES[2][1]) * source[c]
+    remote_part(out, before, after, sides_far, TIME_STEP * MIXES[2][1] * PENALTY)
+    natural_order(out, given_out, turned, stored)
 
 
 def place(received, labelled, out, base):
@@ -604,6 +640,30 @@
     return dot_full(dot_full(left, matrix), right)
 
 
+def far_tables(wanted, count, far):
+    size = 8 * count
+    row = lax.broadcasted_iota(jnp.int32, (size, size), 0)
+    level_out = lax.broadcasted_iota(jnp.int32, (size, size), 1) // count
+    level, element = row // count, row % count
+    for facet in range(4):
+        shift = -count if facet % 2 == 0 else count
+        choice = jnp.broadcast_to(wanted[facet : facet + 1], (size, size))
+        far[facet] = jnp.where((level == level_out) & (element + shift == choice), 1.0, 0.0).astype(BF16)
+    lower = jnp.broadcast_to(wanted[4:5], (size, size))
+    upper = jnp.broadcast_to(wanted[5:6], (size, size))
+    hit = (level == 0) & (level_out == 0) & (element - count == lower)
+    hit = hit | ((level == 1) & (level_out == 7) & (element + count == upper))
+    far[4] = jnp.where(hit, 1.0, 0.0).astype(BF16)
+
+
+def partner_tables_body(count, got_b, far):
+    row = lax.broadcasted_iota(jnp.int32, (count, 8 * count), 0)
+    column = lax.broadcasted_iota(jnp.int32, (count, 8 * count), 1)
+    repeat = (column % count == row).astype(F32)
+    wanted = dot_full(got_b[96:104, 0:count], repeat).astype(jnp.int32)
+    far_tables(wanted, count, far)
+
+
 def tables_body(
     packed,
     near,
@@ -630,18 +690,14 @@
     level, element = row // count, row % count
     level_out = column // count
     for facet in range(4):
-        shift = -count if facet % 2 == 0 else count
         choice = jnp.broadcast_to(wanted[facet : facet + 1], (size, size))
         near[facet] = jnp.where((level == level_out) & (element == choice), 1.0, 0.0).astype(BF16)
-        far[facet] = jnp.where((level == level_out) & (element + shift == choice), 1.0, 0.0).astype(BF16)
     lower = jnp.broadcast_to(wanted[4:5], (size, size))
     upper = jnp.broadcast_to(wanted[5:6], (size, size))
     hit = (level == 7) & (level_out == 0) & (element == lower)
     hit = hit | ((level == 0) & (level_out == 7) & (element == upper))
     near[4] = jnp.where(hit, 1.0, 0.0).astype(BF16)
-    hit = (level == 0) & (level_out == 0) & (element - count == lower)
-    hit = hit | ((level == 1) & (level_out == 7) & (element + count == upper))
-    far[4] = jnp.where(hit, 1.0, 0.0).astype(BF16)
+    far_tables(wanted, count, far)
 
     row, column = place_of((64, 64))
     slopes, modes = packed[0:8, 0:8], packed[8:16, 0:8]
@@ -735,6 +791,8 @@
     x_steps = (1,) if size_x == 2 else (1, -1)
     beside_x = [lax.ppermute(along_x, "fx", shifted((size_x,), (step,))) for step in x_steps]
 
+    local = (neighbours - device * elements).T
+
     near_pairs = [(i ^ 1, i) for i in range(devices)]
     far_pairs = [pair for i in range(1, devices - 1, 2) for pair in ((i, i + 1), (i + 1, i))]
 
@@ -749,8 +807,9 @@
     turning = [pltpu.VMEM((512, 128), F32), pltpu.VMEM((4, 4 * elements, 128), F32)]
     sound, to_a, to_b = call(
         acoustic_start_body,
-        [held, faces, faces],
+        [held, faces, (faces[0] + 8, size)],
         acoustic,
+        jnp.pad(local.astype(F32), ((0, 2), (0, size - elements))),
         edge_a,
         scratch=turning,
         last=1,
@@ -774,7 +833,6 @@
     y_second = lax.ppermute(y_b, "fy", partners((size_y,), 0, True))
     y_first = lax.ppermute(y_a, "fy", partners((size_y,), 0, False))
 
-    local = (neighbours - device * elements).T
     blocks = block_owner.size
     width = max(elements, blocks)
 
@@ -883,9 +941,12 @@
         + y_scratch,
     )
 
+    far_partner = call(functools.partial(partner_tables_body, elements), [table], got_b)[0]
+    longer = (faces[0] + 32, size)
+    near_face = pltpu.VMEM(faces, F32)
     sound_one, to_a, to_b = call(
-        functools.partial(acoustic_far_body, MIXES[0], "first"),
-        [held, faces, (faces[0] + 32, size)],
+        acoustic_first_body,
+        [held, faces, longer],
         partial,
         got_a,
         got_b,
@@ -899,26 +960,33 @@
     got_a, got_b = traces(to_a, to_b)
     flow_state = call(flow_last_body, [(5, cells_x, 8, 128)], second, derived, ends, state)[0]
     partial = local_part(MIXES[1], sound_one)
-    sound_two, to_a, to_b = call(
-        functools.partial(acoustic_far_body, MIXES[1], "second"),
-        [held, faces, (faces[0] + 32, size)],
+    change = call(
+        mirror_body, [faces], to_b, far_partner, scratch=sides + [near_face, pltpu.VMEM(held, F32)], cost=1
+    )[0]
+    partial, to_b = call(
+        acoustic_near_body,
+        [held, longer],
         partial,
         got_a,
-        got_b,
         far,
         received,
         labelled,
-        scratch=sides + [rows_scratch],
-    )
+        scratch=sides + [rows_scratch, near_face],
+    )
+    got_b_last = lax.ppermute(to_b, names, far_pairs)
+    sound_two, to_a = call(
+        acoustic_rest_body, [held, faces], partial, got_b, far, scratch=sides + [near_face]
+    )
+    got_a = lax.ppermute(to_a, names, near_pairs)
     source_three = call(place_last_body, [(3, 64, 128)], received, labelled)[0]
-    got_a, got_b = traces(to_a, to_b)
     partial = local_part(MIXES[2], sound_two)
     sound_state = call(
-        functools.partial(acoustic_far_body, MIXES[2], "last"),
+        acoustic_last_body,
         [(elements, 4, 512)],
         partial,
         got_a,
-        got_b,
+        got_b_last,
+        change,
         far,
         source_three,
         scratch=sides + [pltpu.VMEM(held, F32)] + turning,

time: 56.4 us -> 57.2 us (1.014)
  the two profiles are of different devices: /device:TPU:2 before, /device:TPU:0 now
where the time goes in v16:
time: 57.2 us; the launch traced here: 56.8 us
  starting transfers between devices  27.1 us (47%)
  waiting for transfers between devices  13.1 us (23%)
  Pallas kernels  12.6 us (22%)
  local copies, waits for them, and re-layouts  2.02 us (4%)
  other arithmetic  1 us (2%)
  between operations  0.91 us (2%)
    pallas_call x18, Pallas kernels, call(): pl.pallas_call(body, out_shape=outs, in_specs=[whole] * (len(operands) -...  12.6 us
    all_to_all x2, waiting for transfers between devices, route(): return lax.all_to_all(send, 'fy', split_axis=0, concat_axis=0, tiled=True)  7.1 us
    all_to_all x2, starting transfers between devices, route(): return lax.all_to_all(send, 'fy', split_axis=0, concat_axis=0, tiled=True)  6.83 us
    ppermute x1, starting transfers between devices, per_device(): got_a = lax.ppermute(to_a, names, near_pairs)  5.13 us
    ppermute x2, starting transfers between devices, traces(): return (lax.ppermute(to_a, names, near_pairs), far_got)  4.26 us
    ppermute x1, starting transfers between devices, per_device(): y_second = lax.ppermute(y_b, 'fy', partners((size_y,), 0, True))  3.67 us
    ppermute x1, waiting for transfers between devices, per_device(): y_first = lax.ppermute(y_a, 'fy', partners((size_y,), 0, False))  2.9 us
    ppermute x1, starting transfers between devices, per_device(): edge_b = lax.ppermute(flow_b, 'fz', partners((size_z,), 0, True))  2.64 us
  transfers between devices with their start and end apart: 14, of which 5 were waited for; matrix products, arithmetic and copies ran while one was open for 0% of the time, Pallas kernels for 17%

profile of v16, /device:TPU:0, one launch (start us, length us, event | category | flops | bytes accessed | tf_op | source)
XLA Modules:
  0.0 56.8 jit_solution(8023391961219730259)
XLA Ops:
  0.7 0.9 %broadcast_multiply_fusion = f32[3,8,8,128]{3,2,1,0:T(8,128)S(1)} fusion(f32[3,8,8,128]{3,2,1,0:T(8,128)} %param.11, f32[8,8,128]{2,1,0:T(8,128)} %param.10), kind=kLoop, calls=%fused_computation.1 | loop fusion | flops 24576 | bytes 229376 | tf_op jit(solution)/shard_map/mul | solution.py:783
  1.8 0.5 collective-permute-start
  2.3 2.6 %collective-permute-start.1 = (f32[24,128]{1,0:T(8,128)S(1)}, f32[24,128]{1,0:T(8,128)S(1)}, u32[]{:S(2)}, u32[]{:S(2)}) collective-permute-start(f32[24,128]{1,0:T(8,128)S(1)} %get-tuple-element.30.sent_b), channel_id=1, source_target_pairs={{3,0},{2,1},{1,2},{0,3},{7,4},{6,5},{5,6},{4,7},{11,8},{10,9},{9,1... | collective-permute-start | bytes 36872 | tf_op jit(solution)/shard_map/ppermute | solution.py:790
  5.0 1.5 %collective-permute-start.2 = (f32[240,128]{1,0:T(8,128)S(1)}, f32[240,128]{1,0:T(8,128)S(1)}, u32[]{:S(2)}, u32[]{:S(2)}) collective-permute-start(f32[240,128]{1,0:T(8,128)S(1)} %get-tuple-element.32), channel_id=1, source_target_pairs={{16,0},{0,16},{17,1},{1,17},{18,2},{2,18},{19,3},{3,19},{20,4},{4,... | collective-permute-start | bytes 368648 | tf_op jit(solution)/shard_map/ppermute | solution.py:792
  6.5 0.7 %copy-done.4 = s32[16,6]{0,1:T(8,128)S(1)} copy-done((s32[16,6]{0,1:T(8,128)S(1)}, s32[16,6]{0,1:T(8,128)}, u32[]{:S(2)}) %copy-start.4) | copy-done | bytes 408
  7.2 0.6 %copy-done.8 = s32[1,1,1,16]{3,2,1,0:T(1,128)S(1)} copy-done((s32[1,1,1,16]{3,2,1,0:T(1,128)S(1)}, s32[1,1,1,16]{3,2,1,0:T(1,128)}, u32[]{:S(2)}) %copy-start.8) | copy-done | bytes 88
  7.8 0.6 shard_map.114
  8.6 0.6 %collective-permute-start.3 = (f32[40,128]{1,0:T(8,128)S(1)}, f32[40,128]{1,0:T(8,128)S(1)}, u32[]{:S(2)}, u32[]{:S(2)}) collective-permute-start(f32[40,128]{1,0:T(8,128)S(1)} %shard_map.115.edge), channel_id=1, source_target_pairs={{16,0},{0,16},{17,1},{1,17},{18,2},{2,18},{19,3},{3,19},{20,4},{4,... | collective-permute-start | bytes 61448 | tf_op jit(solution)/shard_map/ppermute | solution.py:830
  9.2 0.7 %collective-permute-start.7 = (f32[104,128]{1,0:T(8,128)S(1)}, f32[104,128]{1,0:T(8,128)S(1)}, u32[]{:S(2)}, u32[]{:S(2)}) collective-permute-start(f32[104,128]{1,0:T(8,128)S(1)} %get-tuple-element.45), channel_id=1, source_target_pairs={{1,2},{2,1},{3,4},{4,3},{5,6},{6,5},{7,8},{8,7},{9,10},{10,9},{11,... | collective-permute-start | bytes 159752 | tf_op jit(solution)/shard_map/ppermute | solution.py:800
  9.9 2.6 %collective-permute-done.3.refs_1_ = f32[40,128]{1,0:T(8,128)S(1)} collective-permute-done((f32[40,128]{1,0:T(8,128)S(1)}, f32[40,128]{1,0:T(8,128)S(1)}, u32[]{:S(2)}, u32[]{:S(2)}) %collective-permute-start.3) | collective-permute-done | bytes 20512 | tf_op jit(solution)/shard_map/ppermute | solution.py:830
  12.6 3.7 %collective-permute-start.5 = (f32[176,128]{1,0:T(8,128)S(1)}, f32[176,128]{1,0:T(8,128)S(1)}, u32[]{:S(2)}, u32[]{:S(2)}) collective-permute-start(f32[176,128]{1,0:T(8,128)S(1)} %get-tuple-element.33), channel_id=1, source_target_pairs={{12,0},{8,4},{4,8},{0,12},{13,1},{9,5},{5,9},{1,13},{14,2},{10,6},... | collective-permute-start | bytes 270344 | tf_op jit(solution)/shard_map/ppermute | solution.py:833
  16.3 0.6 %copy-done.7 = f32[16]{0:T(128)S(1)} copy-done((f32[16]{0:T(128)S(1)}, f32[16]{0:T(128)}, u32[]{:S(2)}) %copy-start.7) | copy-done | bytes 88
  16.9 1.0 %shard_map.117 = (bf16[5,128,128]{2,1,0:T(8,128)(2,1)S(1)}, bf16[5,128,128]{2,1,0:T(8,128)(2,1)S(1)}, f32[128,64]{1,0:T(8,128)S(1)}, f32[128,128]{1,0:T(8,128)S(...) custom-call(f32[32,16]{1,0:T(8,128)S(1)} %pad_add_fusion.1.packed), custom_call_target="tpu_custom_call" | custom-call | flops 1 | bytes 1 | tf_op jit(solution)/shard_map/pallas_call | solution.py:52
  17.9 2.9 %collective-permute-done.6.refs_3_.refs_2_ = f32[168,128]{1,0:T(8,128)S(1)} collective-permute-done((f32[168,128]{1,0:T(8,128)S(1)}, f32[168,128]{1,0:T(8,128)S(1)}, u32[]{:S(2)}, u32[]{:S(2)}) %collective-permute-start.6) | collective-permute-done | bytes 86048 | tf_op jit(solution)/shard_map/ppermute | solution.py:834
  20.8 1.3 %shard_map.121 = f32[4,104,128]{2,1,0:T(8,128)} custom-call(f32[5,8,8,128]{3,2,1,0:T(8,128)S(1)} %pad_add_fusion.state, f32[40,128]{1,0:T(8,128)S(1)} %shard_map.115.edge, f32[240,128]{1,0:T(8,128)S(1)} %collective-permute-done.2.refs_0_, f32[176,128]{1,0:T(8,128)S(1)} %collective-permute-done.5.refs_2_.refs_1_, ...), custom_call_target="tpu_custom_call" | custom-call | tf_op jit(solution)/shard_map/pallas_call | solution.py:52
  22.1 3.4 %all-to-all-start = ((f32[4,104,128]{2,1,0:T(8,128)}), f32[4,104,128]{2,1,0:T(8,128)S(1)}, u32[]{:S(2)}, u32[]{:S(2)}) async-start(f32[4,104,128]{2,1,0:T(8,128)} %shard_map.121), calls=%async_computation | async-start | bytes 425984 | tf_op jit(solution)/shard_map/all_to_all | solution.py:876
  25.5 0.3 shard_map.118.refs_6_.partial
  25.9 3.9 %shard_map.119 = (f32[5,10,16,128]{3,2,1,0:T(8,128)S(1)}, f32[5,14,16,128]{3,2,1,0:T(8,128)S(1)}, f32[5,8,8,128]{3,2,1,0:T(8,128)S(1)}, f32[4,192,128]{2,1,0:T(8,128)}) custom-call(f32[5,8,8,128]{3,2,1,0:T(8,128)S(1)} %pad_add_fusion.state, f32[40,128]{1,0:T(8,128)S(1)} %shard_map.115.edge, f32[240,128]{1,0:T(8,128)S(1)} %collective-permute-done.2.refs_0_, ...), custom_call_target="tpu_custom_call" | custom-call | tf_op jit(solution)/shard_map/pallas_call | solution.py:52
  29.7 3.3 %all-to-all-done.received.labelled = f32[4,104,128]{2,1,0:T(8,128)S(1)} async-done(((f32[4,104,128]{2,1,0:T(8,128)}), f32[4,104,128]{2,1,0:T(8,128)S(1)}, u32[]{:S(2)}, u32[]{:S(2)}) %all-to-all-start) | async-done | bytes 213024 | tf_op jit(solution)/shard_map/all_to_all | solution.py:876
  33.0 3.5 %all-to-all-start.1 = ((f32[4,192,128]{2,1,0:T(8,128)}), f32[4,192,128]{2,1,0:T(8,128)S(1)}, u32[]{:S(2)}, u32[]{:S(2)}) async-start(f32[4,192,128]{2,1,0:T(8,128)} %get-tuple-element.48._), calls=%async_computation.1 | async-start | bytes 786432 | tf_op jit(solution)/shard_map/all_to_all | solution.py:876
  36.5 0.5 shard_map.122
  37.0 0.7 %collective-permute-start.9 = (f32[128,128]{1,0:T(8,128)S(1)}, f32[128,128]{1,0:T(8,128)S(1)}, u32[]{:S(2)}, u32[]{:S(2)}) collective-permute-start(f32[128,128]{1,0:T(8,128)S(1)} %get-tuple-element.52.sent_b), channel_id=1, source_target_pairs={{1,2},{2,1},{3,4},{4,3},{5,6},{6,5},{7,8},{8,7},{9,10},{10,9},{11,... | collective-permute-start | bytes 196616 | tf_op jit(solution)/shard_map/ppermute | solution.py:800
  37.7 4.2 %collective-permute-start.8 = (f32[96,128]{1,0:T(8,128)S(1)}, f32[96,128]{1,0:T(8,128)S(1)}, u32[]{:S(2)}, u32[]{:S(2)}) collective-permute-start(f32[96,128]{1,0:T(8,128)S(1)} %get-tuple-element.50), channel_id=1, source_target_pairs={{1,0},{0,1},{3,2},{2,3},{5,4},{4,5},{7,6},{6,7},{9,8},{8,9},{11,10... | collective-permute-start | bytes 147464 | tf_op jit(solution)/shard_map/ppermute | solution.py:801
  42.2 0.5 collective-permute-done.8.got_a
  42.7 3.8 %all-to-all-done.1.received = f32[4,192,128]{2,1,0:T(8,128)S(1)} async-done(((f32[4,192,128]{2,1,0:T(8,128)}), f32[4,192,128]{2,1,0:T(8,128)S(1)}, u32[]{:S(2)}, u32[]{:S(2)}) %all-to-all-start.1) | async-done | bytes 393248 | tf_op jit(solution)/shard_map/all_to_all | solution.py:876
  46.6 0.5 shard_map.124
  47.1 0.7 %collective-permute-start.11 = (f32[128,128]{1,0:T(8,128)S(1)}, f32[128,128]{1,0:T(8,128)S(1)}, u32[]{:S(2)}, u32[]{:S(2)}) collective-permute-start(f32[128,128]{1,0:T(8,128)S(1)} %get-tuple-element.55), channel_id=1, source_target_pairs={{1,2},{2,1},{3,4},{4,3},{5,6},{6,5},{7,8},{8,7},{9,10},{10,9},{11,... | collective-permute-start | bytes 196616 | tf_op jit(solution)/shard_map/ppermute | solution.py:976
  47.8 0.3 shard_map.125
  48.1 5.1 %collective-permute-start.10 = (f32[96,128]{1,0:T(8,128)S(1)}, f32[96,128]{1,0:T(8,128)S(1)}, u32[]{:S(2)}, u32[]{:S(2)}) collective-permute-start(f32[96,128]{1,0:T(8,128)S(1)} %get-tuple-element.54), channel_id=1, source_target_pairs={{1,0},{0,1},{3,2},{2,3},{5,4},{4,5},{7,6},{6,7},{9,8},{8,9},{11,10... | collective-permute-start | bytes 147464 | tf_op jit(solution)/shard_map/ppermute | solution.py:980
  53.4 1.0 %shard_map.120 = f32[5,8,8,128]{3,2,1,0:T(8,128)} custom-call(f32[5,10,16,128]{3,2,1,0:T(8,128)S(1)} %get-tuple-element.42.second, f32[5,14,16,128]{3,2,1,0:T(8,128)S(1)} %get-tuple-element.43.derived, f32[5,8,8,128]{3,2,1,0:T(8,128)S(1)} %get-tuple-element.44.ends, f32[5,8,8,128]{3,2,1,0:T(8,128)S(1)} %pad_add_fusion.state), custom_call_target="tpu_custom_call" | custom-call | tf_op jit(solution)/shard_map/pallas_call | solution.py:52
  54.5 0.3 shard_map.128.change
  55.5 1.3 %shard_map.130 = f32[16,4,512]{2,1,0:T(4,128)} custom-call(f32[4,64,128]{2,1,0:T(8,128)S(1)} %shard_map.126.partial, f32[96,128]{1,0:T(8,128)S(1)} %collective-permute-done.10.got_a, f32[128,128]{1,0:T(8,128)S(1)} %collective-permute-done.11.got_b, f32[96,128]{1,0:T(8,128)S(1)} %shard_map.128.change, bf16[5,128,128]{2,1,0:T(8,128)(2,1)S(1)} %get-tuple-element.46.sides_far, ...), custom_call_target="tpu_custom_call" | custom-call | tf_op jit(solution)/shard_map/pallas_call | solution.py:52
  (42 shorter events, 1.7 us)
Async XLA Ops:
  0.6 1.0 %copy-start.1 = (f32[3,8,8,128]{3,2,1,0:T(8,128)S(1)}, f32[3,8,8,128]{3,2,1,0:T(8,128)}, u32[]{:S(2)}) copy-start(f32[3,8,8,128]{3,2,1,0:T(8,128)} %param.11) | copy-start | bytes 294916
  0.6 1.0 %copy-start.2 = (f32[8,8,128]{2,1,0:T(8,128)S(1)}, f32[8,8,128]{2,1,0:T(8,128)}, u32[]{:S(2)}) copy-start(f32[8,8,128]{2,1,0:T(8,128)} %param.10) | copy-start | bytes 98308
  0.6 1.0 %copy-start.3 = (f32[8,8,128]{2,1,0:T(8,128)S(1)}, f32[8,8,128]{2,1,0:T(8,128)}, u32[]{:S(2)}) copy-start(f32[8,8,128]{2,1,0:T(8,128)} %param.12) | copy-start | bytes 98308
  1.7 6.1 %copy-start = (f32[16,4,512]{2,1,0:T(4,128)S(1)}, f32[16,4,512]{2,1,0:T(4,128)}, u32[]{:S(2)}) copy-start(f32[16,4,512]{2,1,0:T(4,128)} %given.1) | copy-start | bytes 393220
  1.8 6.0 %collective-permute-start = (f32[24,128]{1,0:T(8,128)S(1)}, f32[24,128]{1,0:T(8,128)S(1)}, u32[]{:S(2)}, u32[]{:S(2)}) collective-permute-start(f32[24,128]{1,0:T(8,128)S(1)} %get-tuple-element.29.sent_a), channel_id=1, source_target_pairs={{1,0},{0,1},{3,2},{2,3},{5,4},{4,5},{7,6},{6,7},{9,8},{8,9},{11,10... | collective-permute-start | bytes 36872 | tf_op jit(solution)/shard_map/ppermute | solution.py:789
  2.3 6.2 %collective-permute-start.1 = (f32[24,128]{1,0:T(8,128)S(1)}, f32[24,128]{1,0:T(8,128)S(1)}, u32[]{:S(2)}, u32[]{:S(2)}) collective-permute-start(f32[24,128]{1,0:T(8,128)S(1)} %get-tuple-element.30.sent_b), channel_id=1, source_target_pairs={{3,0},{2,1},{1,2},{0,3},{7,4},{6,5},{5,6},{4,7},{11,8},{10,9},{9,1... | collective-permute-start | bytes 36872 | tf_op jit(solution)/shard_map/ppermute | solution.py:790
  5.0 7.5 %collective-permute-start.2 = (f32[240,128]{1,0:T(8,128)S(1)}, f32[240,128]{1,0:T(8,128)S(1)}, u32[]{:S(2)}, u32[]{:S(2)}) collective-permute-start(f32[240,128]{1,0:T(8,128)S(1)} %get-tuple-element.32), channel_id=1, source_target_pairs={{16,0},{0,16},{17,1},{1,17},{18,2},{2,18},{19,3},{3,19},{20,4},{4,... | collective-permute-start | bytes 368648 | tf_op jit(solution)/shard_map/ppermute | solution.py:792
  6.5 0.7 %copy-start.4 = (s32[16,6]{0,1:T(8,128)S(1)}, s32[16,6]{0,1:T(8,128)}, u32[]{:S(2)}) copy-start(s32[16,6]{0,1:T(8,128)} %param.17) | copy-start | bytes 1156
  7.2 0.7 %copy-start.8 = (s32[1,1,1,16]{3,2,1,0:T(1,128)S(1)}, s32[1,1,1,16]{3,2,1,0:T(1,128)}, u32[]{:S(2)}) copy-start(s32[1,1,1,16]{3,2,1,0:T(1,128)} %param.19) | copy-start | bytes 196
  8.4 0.8 %copy-start.9 = (s32[1,1,1,16,1]{3,4,2,1,0:T(1,128)S(1)}, s32[1,1,1,16,1]{3,4,2,1,0:T(1,128)}, u32[]{:S(2)}) copy-start(s32[1,1,1,16,1]{3,4,2,1,0:T(1,128)} %param.18) | copy-start | bytes 196
  8.4 4.1 %collective-permute-start.4 = (f32[96,128]{1,0:T(8,128)S(1)}, f32[96,128]{1,0:T(8,128)S(1)}, u32[]{:S(2)}, u32[]{:S(2)}) collective-permute-start(f32[96,128]{1,0:T(8,128)S(1)} %get-tuple-element.31._), channel_id=1, source_target_pairs={{1,0},{0,1},{3,2},{2,3},{5,4},{4,5},{7,6},{6,7},{9,8},{8,9},{11,10... | collective-permute-start | bytes 147464 | tf_op jit(solution)/shard_map/ppermute | solution.py:801
  8.6 3.8 %collective-permute-start.3 = (f32[40,128]{1,0:T(8,128)S(1)}, f32[40,128]{1,0:T(8,128)S(1)}, u32[]{:S(2)}, u32[]{:S(2)}) collective-permute-start(f32[40,128]{1,0:T(8,128)S(1)} %shard_map.115.edge), channel_id=1, source_target_pairs={{16,0},{0,16},{17,1},{1,17},{18,2},{2,18},{19,3},{3,19},{20,4},{4,... | collective-permute-start | bytes 61448 | tf_op jit(solution)/shard_map/ppermute | solution.py:830
  9.2 8.7 %collective-permute-start.7 = (f32[104,128]{1,0:T(8,128)S(1)}, f32[104,128]{1,0:T(8,128)S(1)}, u32[]{:S(2)}, u32[]{:S(2)}) collective-permute-start(f32[104,128]{1,0:T(8,128)S(1)} %get-tuple-element.45), channel_id=1, source_target_pairs={{1,2},{2,1},{3,4},{4,3},{5,6},{6,5},{7,8},{8,7},{9,10},{10,9},{11,... | collective-permute-start | bytes 159752 | tf_op jit(solution)/shard_map/ppermute | solution.py:800
  12.5 3.8 %copy-start.6 = (f32[8,8]{1,0:T(8,128)S(1)}, f32[8,8]{1,0:T(8,128)}, u32[]{:S(2)}) copy-start(f32[8,8]{1,0:T(8,128)} %param.15) | copy-start | bytes 772
  12.6 3.7 %copy-start.5 = (f32[8,8]{1,0:T(8,128)S(1)}, f32[8,8]{1,0:T(8,128)}, u32[]{:S(2)}) copy-start(f32[8,8]{1,0:T(8,128)} %param.16) | copy-start | bytes 772
  12.6 8.2 %collective-permute-start.5 = (f32[176,128]{1,0:T(8,128)S(1)}, f32[176,128]{1,0:T(8,128)S(1)}, u32[]{:S(2)}, u32[]{:S(2)}) collective-permute-start(f32[176,128]{1,0:T(8,128)S(1)} %get-tuple-element.33), channel_id=1, source_target_pairs={{12,0},{8,4},{4,8},{0,12},{13,1},{9,5},{5,9},{1,13},{14,2},{10,6},... | collective-permute-start | bytes 270344 | tf_op jit(solution)/shard_map/ppermute | solution.py:833
  16.2 0.7 %copy-start.7 = (f32[16]{0:T(128)S(1)}, f32[16]{0:T(128)}, u32[]{:S(2)}) copy-start(f32[16]{0:T(128)} %param.14) | copy-start | bytes 196
  16.2 4.6 %collective-permute-start.6 = (f32[168,128]{1,0:T(8,128)S(1)}, f32[168,128]{1,0:T(8,128)S(1)}, u32[]{:S(2)}, u32[]{:S(2)}) collective-permute-start(f32[168,128]{1,0:T(8,128)S(1)} %get-tuple-element.34), channel_id=1, source_target_pairs={{4,0},{0,4},{12,8},{8,12},{5,1},{1,5},{13,9},{9,13},{6,2},{2,6},{1... | collective-permute-start | bytes 258056 | tf_op jit(solution)/shard_map/ppermute | solution.py:834
  22.1 10.9 %all-to-all-start = ((f32[4,104,128]{2,1,0:T(8,128)}), f32[4,104,128]{2,1,0:T(8,128)S(1)}, u32[]{:S(2)}, u32[]{:S(2)}) async-start(f32[4,104,128]{2,1,0:T(8,128)} %shard_map.121), calls=%async_computation | async-start | bytes 425984 | tf_op jit(solution)/shard_map/all_to_all | solution.py:876
  33.0 13.6 %all-to-all-start.1 = ((f32[4,192,128]{2,1,0:T(8,128)}), f32[4,192,128]{2,1,0:T(8,128)S(1)}, u32[]{:S(2)}, u32[]{:S(2)}) async-start(f32[4,192,128]{2,1,0:T(8,128)} %get-tuple-element.48._), calls=%async_computation.1 | async-start | bytes 786432 | tf_op jit(solution)/shard_map/all_to_all | solution.py:876
  37.0 10.8 %collective-permute-start.9 = (f32[128,128]{1,0:T(8,128)S(1)}, f32[128,128]{1,0:T(8,128)S(1)}, u32[]{:S(2)}, u32[]{:S(2)}) collective-permute-start(f32[128,128]{1,0:T(8,128)S(1)} %get-tuple-element.52.sent_b), channel_id=1, source_target_pairs={{1,2},{2,1},{3,4},{4,3},{5,6},{6,5},{7,8},{8,7},{9,10},{10,9},{11,... | collective-permute-start | bytes 196616 | tf_op jit(solution)/shard_map/ppermute | solution.py:800
  37.7 5.1 %collective-permute-start.8 = (f32[96,128]{1,0:T(8,128)S(1)}, f32[96,128]{1,0:T(8,128)S(1)}, u32[]{:S(2)}, u32[]{:S(2)}) collective-permute-start(f32[96,128]{1,0:T(8,128)S(1)} %get-tuple-element.50), channel_id=1, source_target_pairs={{1,0},{0,1},{3,2},{2,3},{5,4},{4,5},{7,6},{6,7},{9,8},{8,9},{11,10... | collective-permute-start | bytes 147464 | tf_op jit(solution)/shard_map/ppermute | solution.py:801
  47.1 8.4 %collective-permute-start.11 = (f32[128,128]{1,0:T(8,128)S(1)}, f32[128,128]{1,0:T(8,128)S(1)}, u32[]{:S(2)}, u32[]{:S(2)}) collective-permute-start(f32[128,128]{1,0:T(8,128)S(1)} %get-tuple-element.55), channel_id=1, source_target_pairs={{1,2},{2,1},{3,4},{4,3},{5,6},{6,5},{7,8},{8,7},{9,10},{10,9},{11,... | collective-permute-start | bytes 196616 | tf_op jit(solution)/shard_map/ppermute | solution.py:976
  48.1 7.4 %collective-permute-start.10 = (f32[96,128]{1,0:T(8,128)S(1)}, f32[96,128]{1,0:T(8,128)S(1)}, u32[]{:S(2)}, u32[]{:S(2)}) collective-permute-start(f32[96,128]{1,0:T(8,128)S(1)} %get-tuple-element.54), channel_id=1, source_target_pairs={{1,0},{0,1},{3,2},{2,3},{5,4},{4,5},{7,6},{6,7},{9,8},{8,9},{11,10... | collective-permute-start | bytes 147464 | tf_op jit(solution)/shard_map/ppermute | solution.py:980

commit v17 on v16

--- a/solution.py
+++ b/solution.py
@@ -562,7 +562,7 @@
 
 
 def acoustic_near_body(
-    partial, got_a, sides_far, received, labelled, out, message_b, before, after, source, spare
+    partial, got_a, sides_far, received, labelled, _, __, out, message_b, before, after, source, spare
 ):
     odd = is_odd("fz")
     place(received, labelled, source, 0)
@@ -971,6 +971,9 @@
         far,
         received,
         labelled,
+        change,
+        flow_state,
+        last=2,
         scratch=sides + [rows_scratch, near_face],
     )
     got_b_last = lax.ppermute(to_b, names, far_pairs)

time: 57.2 us -> 56 us (0.979)
  the two profiles are of different devices: /device:TPU:0 before, /device:TPU:2 now
where the time goes in v17:
time: 56 us; the launch traced here: 54.9 us
  starting transfers between devices  28.3 us (51%)
  Pallas kernels  12.6 us (22%)
  waiting for transfers between devices  10 us (18%)
  local copies, waits for them, and re-layouts  2.03 us (4%)
  other arithmetic  1 us (2%)
  between operations  0.94 us (2%)
    pallas_call x18, Pallas kernels, call(): pl.pallas_call(body, out_shape=outs, in_specs=[whole] * (len(operands) -...  12.6 us
    ppermute x2, starting transfers between devices, traces(): far_got = lax.ppermute(to_b, names, far_pairs)  11.2 us
    all_to_all x2, starting transfers between devices, route(): return lax.all_to_all(send, 'fy', split_axis=0, concat_axis=0, tiled=True)  7.09 us
    ppermute x1, starting transfers between devices, per_device(): got_b_last = lax.ppermute(to_b, names, far_pairs)  5.28 us
    all_to_all x2, waiting for transfers between devices, route(): return lax.all_to_all(send, 'fy', split_axis=0, concat_axis=0, tiled=True)  3.18 us
    ppermute x1, waiting for transfers between devices, per_device(): got_b_last = lax.ppermute(to_b, names, far_pairs)  2.24 us
    unnamed x22, local copies, waits for them, and re-layouts  2.03 us
    ppermute x2, waiting for transfers between devices, traces(): far_got = lax.ppermute(to_b, names, far_pairs)  1.78 us
  transfers between devices with their start and end apart: 14, of which 7 were waited for; matrix products, arithmetic and copies ran while one was open for 0% of the time, Pallas kernels for 18%

profile of v17, /device:TPU:2, one launch (start us, length us, event | category | flops | bytes accessed | tf_op | source)
XLA Modules:
  0.0 54.9 jit_solution(1048968776395201488)
XLA Ops:
  0.7 0.9 %broadcast_multiply_fusion = f32[3,8,8,128]{3,2,1,0:T(8,128)S(1)} fusion(f32[3,8,8,128]{3,2,1,0:T(8,128)} %param.11, f32[8,8,128]{2,1,0:T(8,128)} %param.10), kind=kLoop, calls=%fused_computation.1 | loop fusion | flops 24576 | bytes 229376 | tf_op jit(solution)/shard_map/mul | solution.py:783
  1.9 1.6 %collective-permute-start.1 = (f32[24,128]{1,0:T(8,128)S(1)}, f32[24,128]{1,0:T(8,128)S(1)}, u32[]{:S(2)}, u32[]{:S(2)}) collective-permute-start(f32[24,128]{1,0:T(8,128)S(1)} %get-tuple-element.30.sent_b), channel_id=1, source_target_pairs={{3,0},{2,1},{1,2},{0,3},{7,4},{6,5},{5,6},{4,7},{11,8},{10,9},{9,1... | collective-permute-start | bytes 36872 | tf_op jit(solution)/shard_map/ppermute | solution.py:790
  3.5 0.5 collective-permute-start.2
  4.1 0.7 %copy-done.5 = s32[16,6]{0,1:T(8,128)S(1)} copy-done((s32[16,6]{0,1:T(8,128)S(1)}, s32[16,6]{0,1:T(8,128)}, u32[]{:S(2)}) %copy-start.5) | copy-done | bytes 408
  4.8 0.6 %copy-done.9 = s32[1,1,1,16]{3,2,1,0:T(1,128)S(1)} copy-done((s32[1,1,1,16]{3,2,1,0:T(1,128)S(1)}, s32[1,1,1,16]{3,2,1,0:T(1,128)}, u32[]{:S(2)}) %copy-start.9) | copy-done | bytes 88
  5.4 0.6 %shard_map.114 = (f32[4,64,128]{2,1,0:T(8,128)S(1)}, f32[96,128]{1,0:T(8,128)S(1)}, f32[104,128]{1,0:T(8,128)S(1)}) custom-call(f32[16,4,512]{2,1,0:T(4,128)S(1)} %copy-done.1, f32[8,128]{1,0:T(8,128)S(1)} %pad.43.local, f32[24,128]{1,0:T(8,128)S(1)} %collective-permute-done._.got_a), custom_call_target="tpu_custom_call" | custom-call | tf_op jit(solution)/shard_map/pallas_call | solution.py:52
  6.2 1.6 %collective-permute-start.3 = (f32[40,128]{1,0:T(8,128)S(1)}, f32[40,128]{1,0:T(8,128)S(1)}, u32[]{:S(2)}, u32[]{:S(2)}) collective-permute-start(f32[40,128]{1,0:T(8,128)S(1)} %shard_map.115.edge), channel_id=1, source_target_pairs={{16,0},{0,16},{17,1},{1,17},{18,2},{2,18},{19,3},{3,19},{20,4},{4,... | collective-permute-start | bytes 61448 | tf_op jit(solution)/shard_map/ppermute | solution.py:830
  7.8 5.2 %collective-permute-start.7 = (f32[104,128]{1,0:T(8,128)S(1)}, f32[104,128]{1,0:T(8,128)S(1)}, u32[]{:S(2)}, u32[]{:S(2)}) collective-permute-start(f32[104,128]{1,0:T(8,128)S(1)} %get-tuple-element.45), channel_id=1, source_target_pairs={{1,2},{2,1},{3,4},{4,3},{5,6},{6,5},{7,8},{8,7},{9,10},{10,9},{11,... | collective-permute-start | bytes 159752 | tf_op jit(solution)/shard_map/ppermute | solution.py:800
  13.2 0.7 %collective-permute-start.5 = (f32[176,128]{1,0:T(8,128)S(1)}, f32[176,128]{1,0:T(8,128)S(1)}, u32[]{:S(2)}, u32[]{:S(2)}) collective-permute-start(f32[176,128]{1,0:T(8,128)S(1)} %get-tuple-element.33), channel_id=1, source_target_pairs={{12,0},{8,4},{4,8},{0,12},{13,1},{9,5},{5,9},{1,13},{14,2},{10,6},... | collective-permute-start | bytes 270344 | tf_op jit(solution)/shard_map/ppermute | solution.py:833
  13.9 0.6 %copy-done.8 = f32[16]{0:T(128)S(1)} copy-done((f32[16]{0:T(128)S(1)}, f32[16]{0:T(128)}, u32[]{:S(2)}) %copy-start.8) | copy-done | bytes 88
  14.5 1.0 %shard_map.117 = (bf16[5,128,128]{2,1,0:T(8,128)(2,1)S(1)}, bf16[5,128,128]{2,1,0:T(8,128)(2,1)S(1)}, f32[128,64]{1,0:T(8,128)S(1)}, f32[128,128]{1,0:T(8,128)S(...) custom-call(f32[32,16]{1,0:T(8,128)S(1)} %pad_add_fusion.1.packed), custom_call_target="tpu_custom_call" | custom-call | flops 1 | bytes 1 | tf_op jit(solution)/shard_map/pallas_call | solution.py:52
  15.5 1.8 %collective-permute-done.7.refs_6_.got_b = f32[104,128]{1,0:T(8,128)S(1)} collective-permute-done((f32[104,128]{1,0:T(8,128)S(1)}, f32[104,128]{1,0:T(8,128)S(1)}, u32[]{:S(2)}, u32[]{:S(2)}) %collective-permute-start.7) | collective-permute-done | bytes 53280 | tf_op jit(solution)/shard_map/ppermute | solution.py:800
  17.3 1.2 %collective-permute-done.6.refs_3_.refs_2_ = f32[168,128]{1,0:T(8,128)S(1)} collective-permute-done((f32[168,128]{1,0:T(8,128)S(1)}, f32[168,128]{1,0:T(8,128)S(1)}, u32[]{:S(2)}, u32[]{:S(2)}) %collective-permute-start.6) | collective-permute-done | bytes 86048 | tf_op jit(solution)/shard_map/ppermute | solution.py:834
  18.5 1.1 %collective-permute-done.5.refs_2_.refs_1_ = f32[176,128]{1,0:T(8,128)S(1)} collective-permute-done((f32[176,128]{1,0:T(8,128)S(1)}, f32[176,128]{1,0:T(8,128)S(1)}, u32[]{:S(2)}, u32[]{:S(2)}) %collective-permute-start.5) | collective-permute-done | bytes 90144 | tf_op jit(solution)/shard_map/ppermute | solution.py:833
  19.5 1.3 %shard_map.121 = f32[4,104,128]{2,1,0:T(8,128)} custom-call(f32[5,8,8,128]{3,2,1,0:T(8,128)S(1)} %pad_add_fusion.state, f32[40,128]{1,0:T(8,128)S(1)} %shard_map.115.edge, f32[240,128]{1,0:T(8,128)S(1)} %collective-permute-done.2.refs_0_, f32[176,128]{1,0:T(8,128)S(1)} %collective-permute-done.5.refs_2_.refs_1_, ...), custom_call_target="tpu_custom_call" | custom-call | tf_op jit(solution)/shard_map/pallas_call | solution.py:52
  20.9 3.6 %all-to-all-start = ((f32[4,104,128]{2,1,0:T(8,128)}), f32[4,104,128]{2,1,0:T(8,128)S(1)}, u32[]{:S(2)}, u32[]{:S(2)}) async-start(f32[4,104,128]{2,1,0:T(8,128)} %shard_map.121), calls=%async_computation | async-start | bytes 425984 | tf_op jit(solution)/shard_map/all_to_all | solution.py:876
  24.8 3.9 %shard_map.119 = (f32[5,10,16,128]{3,2,1,0:T(8,128)S(1)}, f32[5,14,16,128]{3,2,1,0:T(8,128)S(1)}, f32[5,8,8,128]{3,2,1,0:T(8,128)S(1)}, f32[4,192,128]{2,1,0:T(8,128)}) custom-call(f32[5,8,8,128]{3,2,1,0:T(8,128)S(1)} %pad_add_fusion.state, f32[40,128]{1,0:T(8,128)S(1)} %shard_map.115.edge, f32[240,128]{1,0:T(8,128)S(1)} %collective-permute-done.2.refs_0_, ...), custom_call_target="tpu_custom_call" | custom-call | tf_op jit(solution)/shard_map/pallas_call | solution.py:52
  28.7 2.3 %all-to-all-done.received.labelled = f32[4,104,128]{2,1,0:T(8,128)S(1)} async-done(((f32[4,104,128]{2,1,0:T(8,128)}), f32[4,104,128]{2,1,0:T(8,128)S(1)}, u32[]{:S(2)}, u32[]{:S(2)}) %all-to-all-start) | async-done | bytes 213024 | tf_op jit(solution)/shard_map/all_to_all | solution.py:876
  31.0 3.5 %all-to-all-start.1 = ((f32[4,192,128]{2,1,0:T(8,128)}), f32[4,192,128]{2,1,0:T(8,128)S(1)}, u32[]{:S(2)}, u32[]{:S(2)}) async-start(f32[4,192,128]{2,1,0:T(8,128)} %get-tuple-element.48._), calls=%async_computation.1 | async-start | bytes 786432 | tf_op jit(solution)/shard_map/all_to_all | solution.py:876
  34.4 0.5 shard_map.122
  35.0 6.0 %collective-permute-start.9 = (f32[128,128]{1,0:T(8,128)S(1)}, f32[128,128]{1,0:T(8,128)S(1)}, u32[]{:S(2)}, u32[]{:S(2)}) collective-permute-start(f32[128,128]{1,0:T(8,128)S(1)} %get-tuple-element.51.sent_b), channel_id=1, source_target_pairs={{1,2},{2,1},{3,4},{4,3},{5,6},{6,5},{7,8},{8,7},{9,10},{10,9},{11,... | collective-permute-start | bytes 196616 | tf_op jit(solution)/shard_map/ppermute | solution.py:800
  41.3 1.0 %shard_map.120.__ = f32[5,8,8,128]{3,2,1,0:T(8,128)} custom-call(f32[5,10,16,128]{3,2,1,0:T(8,128)S(1)} %get-tuple-element.42.second, f32[5,14,16,128]{3,2,1,0:T(8,128)S(1)} %get-tuple-element.43.derived, f32[5,8,8,128]{3,2,1,0:T(8,128)S(1)} %get-tuple-element.44.ends, f32[5,8,8,128]{3,2,1,0:T(8,128)S(1)} %pad_add_fusion.state), custom_call_target="tpu_custom_call" | custom-call | tf_op jit(solution)/shard_map/pallas_call | solution.py:52
  42.3 0.3 shard_map.123.partial
  42.7 0.4 shard_map.125._.change
  43.0 0.9 %all-to-all-done.1.received = f32[4,192,128]{2,1,0:T(8,128)S(1)} async-done(((f32[4,192,128]{2,1,0:T(8,128)}), f32[4,192,128]{2,1,0:T(8,128)S(1)}, u32[]{:S(2)}, u32[]{:S(2)}) %all-to-all-start.1) | async-done | bytes 393248 | tf_op jit(solution)/shard_map/all_to_all | solution.py:876
  43.9 0.5 shard_map.126
  44.5 5.3 %collective-permute-start.11 = (f32[128,128]{1,0:T(8,128)S(1)}, f32[128,128]{1,0:T(8,128)S(1)}, u32[]{:S(2)}, u32[]{:S(2)}) collective-permute-start(f32[128,128]{1,0:T(8,128)S(1)} %get-tuple-element.55), channel_id=1, source_target_pairs={{1,2},{2,1},{3,4},{4,3},{5,6},{6,5},{7,8},{8,7},{9,10},{10,9},{11,... | collective-permute-start | bytes 196616 | tf_op jit(solution)/shard_map/ppermute | solution.py:979
  49.7 0.3 shard_map.127
  50.2 0.3 shard_map.128.partial
  50.8 0.6 %collective-permute-done.10.got_a = f32[96,128]{1,0:T(8,128)S(1)} collective-permute-done((f32[96,128]{1,0:T(8,128)S(1)}, f32[96,128]{1,0:T(8,128)S(1)}, u32[]{:S(2)}, u32[]{:S(2)}) %collective-permute-start.10) | collective-permute-done | bytes 49184 | tf_op jit(solution)/shard_map/ppermute | solution.py:983
  51.4 2.2 %collective-permute-done.11.got_b = f32[128,128]{1,0:T(8,128)S(1)} collective-permute-done((f32[128,128]{1,0:T(8,128)S(1)}, f32[128,128]{1,0:T(8,128)S(1)}, u32[]{:S(2)}, u32[]{:S(2)}) %collective-permute-start.11) | collective-permute-done | bytes 65568 | tf_op jit(solution)/shard_map/ppermute | solution.py:979
  53.6 1.3 %shard_map.130 = f32[16,4,512]{2,1,0:T(4,128)} custom-call(f32[4,64,128]{2,1,0:T(8,128)S(1)} %shard_map.128.partial, f32[96,128]{1,0:T(8,128)S(1)} %collective-permute-done.10.got_a, f32[128,128]{1,0:T(8,128)S(1)} %collective-permute-done.11.got_b, f32[96,128]{1,0:T(8,128)S(1)} %shard_map.125._.change, bf16[5,128,128]{2,1,0:T(8,128)(2,1)S(1)} %get-tuple-element.46.sides_far, ...), custom_call_target="tpu_custom_call" | custom-call | tf_op jit(solution)/shard_map/pallas_call | solution.py:52
  (44 shorter events, 1.5 us)
Async XLA Ops:
  0.6 1.0 %copy-start.2 = (f32[3,8,8,128]{3,2,1,0:T(8,128)S(1)}, f32[3,8,8,128]{3,2,1,0:T(8,128)}, u32[]{:S(2)}) copy-start(f32[3,8,8,128]{3,2,1,0:T(8,128)} %param.11) | copy-start | bytes 294916
  0.6 1.0 %copy-start.3 = (f32[8,8,128]{2,1,0:T(8,128)S(1)}, f32[8,8,128]{2,1,0:T(8,128)}, u32[]{:S(2)}) copy-start(f32[8,8,128]{2,1,0:T(8,128)} %param.10) | copy-start | bytes 98308
  0.6 1.0 %copy-start.4 = (f32[8,8,128]{2,1,0:T(8,128)S(1)}, f32[8,8,128]{2,1,0:T(8,128)}, u32[]{:S(2)}) copy-start(f32[8,8,128]{2,1,0:T(8,128)} %param.12) | copy-start | bytes 98308
  1.7 3.7 %copy-start.1 = (f32[16,4,512]{2,1,0:T(4,128)S(1)}, f32[16,4,512]{2,1,0:T(4,128)}, u32[]{:S(2)}) copy-start(f32[16,4,512]{2,1,0:T(4,128)} %given.1) | copy-start | bytes 393220
  1.8 3.6 %collective-permute-start = (f32[24,128]{1,0:T(8,128)S(1)}, f32[24,128]{1,0:T(8,128)S(1)}, u32[]{:S(2)}, u32[]{:S(2)}) collective-permute-start(f32[24,128]{1,0:T(8,128)S(1)} %get-tuple-element.29.sent_a), channel_id=1, source_target_pairs={{1,0},{0,1},{3,2},{2,3},{5,4},{4,5},{7,6},{6,7},{9,8},{8,9},{11,10... | collective-permute-start | bytes 36872 | tf_op jit(solution)/shard_map/ppermute | solution.py:789
  1.9 4.2 %collective-permute-start.1 = (f32[24,128]{1,0:T(8,128)S(1)}, f32[24,128]{1,0:T(8,128)S(1)}, u32[]{:S(2)}, u32[]{:S(2)}) collective-permute-start(f32[24,128]{1,0:T(8,128)S(1)} %get-tuple-element.30.sent_b), channel_id=1, source_target_pairs={{3,0},{2,1},{1,2},{0,3},{7,4},{6,5},{5,6},{4,7},{11,8},{10,9},{9,1... | collective-permute-start | bytes 36872 | tf_op jit(solution)/shard_map/ppermute | solution.py:790
  3.5 9.5 %collective-permute-start.2 = (f32[240,128]{1,0:T(8,128)S(1)}, f32[240,128]{1,0:T(8,128)S(1)}, u32[]{:S(2)}, u32[]{:S(2)}) collective-permute-start(f32[240,128]{1,0:T(8,128)S(1)} %get-tuple-element.32), channel_id=1, source_target_pairs={{16,0},{0,16},{17,1},{1,17},{18,2},{2,18},{19,3},{3,19},{20,4},{4,... | collective-permute-start | bytes 368648 | tf_op jit(solution)/shard_map/ppermute | solution.py:792
  4.1 0.7 %copy-start.5 = (s32[16,6]{0,1:T(8,128)S(1)}, s32[16,6]{0,1:T(8,128)}, u32[]{:S(2)}) copy-start(s32[16,6]{0,1:T(8,128)} %param.17) | copy-start | bytes 1156
  4.8 0.7 %copy-start.9 = (s32[1,1,1,16]{3,2,1,0:T(1,128)S(1)}, s32[1,1,1,16]{3,2,1,0:T(1,128)}, u32[]{:S(2)}) copy-start(s32[1,1,1,16]{3,2,1,0:T(1,128)} %param.19) | copy-start | bytes 196
  6.0 1.8 %copy-start.10 = (s32[1,1,1,16,1]{3,4,2,1,0:T(1,128)S(1)}, s32[1,1,1,16,1]{3,4,2,1,0:T(1,128)}, u32[]{:S(2)}) copy-start(s32[1,1,1,16,1]{3,4,2,1,0:T(1,128)} %param.18) | copy-start | bytes 196
  6.0 7.0 %collective-permute-start.4 = (f32[96,128]{1,0:T(8,128)S(1)}, f32[96,128]{1,0:T(8,128)S(1)}, u32[]{:S(2)}, u32[]{:S(2)}) collective-permute-start(f32[96,128]{1,0:T(8,128)S(1)} %get-tuple-element.31._), channel_id=1, source_target_pairs={{1,0},{0,1},{3,2},{2,3},{5,4},{4,5},{7,6},{6,7},{9,8},{8,9},{11,10... | collective-permute-start | bytes 147464 | tf_op jit(solution)/shard_map/ppermute | solution.py:801
  6.2 6.8 %collective-permute-start.3 = (f32[40,128]{1,0:T(8,128)S(1)}, f32[40,128]{1,0:T(8,128)S(1)}, u32[]{:S(2)}, u32[]{:S(2)}) collective-permute-start(f32[40,128]{1,0:T(8,128)S(1)} %shard_map.115.edge), channel_id=1, source_target_pairs={{16,0},{0,16},{17,1},{1,17},{18,2},{2,18},{19,3},{3,19},{20,4},{4,... | collective-permute-start | bytes 61448 | tf_op jit(solution)/shard_map/ppermute | solution.py:830
  7.8 9.5 %collective-permute-start.7 = (f32[104,128]{1,0:T(8,128)S(1)}, f32[104,128]{1,0:T(8,128)S(1)}, u32[]{:S(2)}, u32[]{:S(2)}) collective-permute-start(f32[104,128]{1,0:T(8,128)S(1)} %get-tuple-element.45), channel_id=1, source_target_pairs={{1,2},{2,1},{3,4},{4,3},{5,6},{6,5},{7,8},{8,7},{9,10},{10,9},{11,... | collective-permute-start | bytes 159752 | tf_op jit(solution)/shard_map/ppermute | solution.py:800
  13.1 0.8 %copy-start.7 = (f32[8,8]{1,0:T(8,128)S(1)}, f32[8,8]{1,0:T(8,128)}, u32[]{:S(2)}) copy-start(f32[8,8]{1,0:T(8,128)} %param.15) | copy-start | bytes 772
  13.1 0.7 %copy-start.6 = (f32[8,8]{1,0:T(8,128)S(1)}, f32[8,8]{1,0:T(8,128)}, u32[]{:S(2)}) copy-start(f32[8,8]{1,0:T(8,128)} %param.16) | copy-start | bytes 772
  13.2 6.4 %collective-permute-start.5 = (f32[176,128]{1,0:T(8,128)S(1)}, f32[176,128]{1,0:T(8,128)S(1)}, u32[]{:S(2)}, u32[]{:S(2)}) collective-permute-start(f32[176,128]{1,0:T(8,128)S(1)} %get-tuple-element.33), channel_id=1, source_target_pairs={{12,0},{8,4},{4,8},{0,12},{13,1},{9,5},{5,9},{1,13},{14,2},{10,6},... | collective-permute-start | bytes 270344 | tf_op jit(solution)/shard_map/ppermute | solution.py:833
  13.8 0.7 %copy-start.8 = (f32[16]{0:T(128)S(1)}, f32[16]{0:T(128)}, u32[]{:S(2)}) copy-start(f32[16]{0:T(128)} %param.14) | copy-start | bytes 196
  13.8 4.6 %collective-permute-start.6 = (f32[168,128]{1,0:T(8,128)S(1)}, f32[168,128]{1,0:T(8,128)S(1)}, u32[]{:S(2)}, u32[]{:S(2)}) collective-permute-start(f32[168,128]{1,0:T(8,128)S(1)} %get-tuple-element.34), channel_id=1, source_target_pairs={{4,0},{0,4},{12,8},{8,12},{5,1},{1,5},{13,9},{9,13},{6,2},{2,6},{1... | collective-permute-start | bytes 258056 | tf_op jit(solution)/shard_map/ppermute | solution.py:834
  20.9 10.1 %all-to-all-start = ((f32[4,104,128]{2,1,0:T(8,128)}), f32[4,104,128]{2,1,0:T(8,128)S(1)}, u32[]{:S(2)}, u32[]{:S(2)}) async-start(f32[4,104,128]{2,1,0:T(8,128)} %shard_map.121), calls=%async_computation | async-start | bytes 425984 | tf_op jit(solution)/shard_map/all_to_all | solution.py:876
  31.0 13.0 %all-to-all-start.1 = ((f32[4,192,128]{2,1,0:T(8,128)}), f32[4,192,128]{2,1,0:T(8,128)S(1)}, u32[]{:S(2)}, u32[]{:S(2)}) async-start(f32[4,192,128]{2,1,0:T(8,128)} %get-tuple-element.48._), calls=%async_computation.1 | async-start | bytes 786432 | tf_op jit(solution)/shard_map/all_to_all | solution.py:876
  35.0 14.8 %collective-permute-start.9 = (f32[128,128]{1,0:T(8,128)S(1)}, f32[128,128]{1,0:T(8,128)S(1)}, u32[]{:S(2)}, u32[]{:S(2)}) collective-permute-start(f32[128,128]{1,0:T(8,128)S(1)} %get-tuple-element.51.sent_b), channel_id=1, source_target_pairs={{1,2},{2,1},{3,4},{4,3},{5,6},{6,5},{7,8},{8,7},{9,10},{10,9},{11,... | collective-permute-start | bytes 196616 | tf_op jit(solution)/shard_map/ppermute | solution.py:800
  41.0 2.0 %collective-permute-start.8 = (f32[96,128]{1,0:T(8,128)S(1)}, f32[96,128]{1,0:T(8,128)S(1)}, u32[]{:S(2)}, u32[]{:S(2)}) collective-permute-start(f32[96,128]{1,0:T(8,128)S(1)} %get-tuple-element.50), channel_id=1, source_target_pairs={{1,0},{0,1},{3,2},{2,3},{5,4},{4,5},{7,6},{6,7},{9,8},{8,9},{11,10... | collective-permute-start | bytes 147464 | tf_op jit(solution)/shard_map/ppermute | solution.py:801
  42.6 1.3 %copy-start = (f32[5,8,8,128]{3,2,1,0:T(8,128)S(1)}, f32[5,8,8,128]{3,2,1,0:T(8,128)}, u32[]{:S(2)}) copy-start(f32[5,8,8,128]{3,2,1,0:T(8,128)} %shard_map.120.__) | copy-start | bytes 491524
  44.5 9.2 %collective-permute-start.11 = (f32[128,128]{1,0:T(8,128)S(1)}, f32[128,128]{1,0:T(8,128)S(1)}, u32[]{:S(2)}, u32[]{:S(2)}) collective-permute-start(f32[128,128]{1,0:T(8,128)S(1)} %get-tuple-element.55), channel_id=1, source_target_pairs={{1,2},{2,1},{3,4},{4,3},{5,6},{6,5},{7,8},{8,7},{9,10},{10,9},{11,... | collective-permute-start | bytes 196616 | tf_op jit(solution)/shard_map/ppermute | solution.py:979
  50.1 1.3 %collective-permute-start.10 = (f32[96,128]{1,0:T(8,128)S(1)}, f32[96,128]{1,0:T(8,128)S(1)}, u32[]{:S(2)}, u32[]{:S(2)}) collective-permute-start(f32[96,128]{1,0:T(8,128)S(1)} %get-tuple-element.54), channel_id=1, source_target_pairs={{1,0},{0,1},{3,2},{2,3},{5,4},{4,5},{7,6},{6,7},{9,8},{8,9},{11,10... | collective-permute-start | bytes 147464 | tf_op jit(solution)/shard_map/ppermute | solution.py:983

commit v18 on v17

--- a/solution.py
+++ b/solution.py
@@ -417,7 +417,8 @@
     to_ends(along_z, 2, 8, 0, cells_x, ends_out)
 
 
-def flow_last_body(second, derived, ends, state, out):
+def flow_last_body(second, derived, ends, state, out, done):
+    done[...] = jnp.zeros(done.shape, F32)
     flow_rate_section(second, derived, ends, state, -1, MIXES[2], writer(out), inner=True)
 
 
@@ -958,7 +959,9 @@
     )
     labelled, received = received, route(send)
     got_a, got_b = traces(to_a, to_b)
-    flow_state = call(flow_last_body, [(5, cells_x, 8, 128)], second, derived, ends, state)[0]
+    flow_state, done = call(
+        flow_last_body, [(5, cells_x, 8, 128), (8, 128)], second, derived, ends, state
+    )
     partial = local_part(MIXES[1], sound_one)
     change = call(
         mirror_body, [faces], to_b, far_partner, scratch=sides + [near_face, pltpu.VMEM(held, F32)], cost=1
@@ -972,8 +975,7 @@
         received,
         labelled,
         change,
-        flow_state,
-        last=2,
+        done,
         scratch=sides + [rows_scratch, near_face],
     )
     got_b_last = lax.ppermute(to_b, names, far_pairs)

time: 56 us -> 57 us (1.018); the launches traced: 54.9 us -> 56.5 us
  starting transfers between devices: 28.3 us -> 29.2 us
  waiting for transfers between devices: 10 us -> 10.8 us
    ppermute x2, starting transfers between devices: 11.2 us -> 13.8 us  [traces(): far_got = lax.ppermute(to_b, names, far_pairs)]
    ppermute x1, starting transfers between devices: 5.28 us -> 3.66 us  [per_device(): got_b_last = lax.ppermute(to_b, names, far_pairs)]
    ppermute x1, waiting for transfers between devices: 2.24 us -> 3.86 us  [per_device(): got_b_last = lax.ppermute(to_b, names, far_pairs)]
    all_to_all x2, waiting for transfers between devices: 3.18 us -> 2.28 us  [route(): return lax.all_to_all(send, 'fy', split_axis=0, concat_axis=0, tiled=True)]
    unnamed x22 -> x20, local copies, waits for them, and re-layouts: 2.03 us -> 2.02 us
  transfers between devices with their start and end apart: 14 -> 14, of which waited for: 7 -> 6; matrix products, arithmetic and copies ran while one was open for 0% -> 0% of each run, Pallas kernels for 18% -> 18%
where the time goes in v18:
time: 57 us; the launch traced here: 56.5 us
  starting transfers between devices  29.2 us (51%)
  Pallas kernels  12.6 us (22%)
  waiting for transfers between devices  10.8 us (19%)
  local copies, waits for them, and re-layouts  2.02 us (4%)
  other arithmetic  1 us (2%)
  between operations  0.94 us (2%)
    ppermute x2, starting transfers between devices, traces(): far_got = lax.ppermute(to_b, names, far_pairs)  13.8 us
    pallas_call x18, Pallas kernels, call(): pl.pallas_call(body, out_shape=outs, in_specs=[whole] * (len(operands) -...  12.6 us
    all_to_all x2, starting transfers between devices, route(): return lax.all_to_all(send, 'fy', split_axis=0, concat_axis=0, tiled=True)  7.09 us
    ppermute x1, waiting for transfers between devices, per_device(): got_b_last = lax.ppermute(to_b, names, far_pairs)  3.86 us
    ppermute x1, starting transfers between devices, per_device(): got_b_last = lax.ppermute(to_b, names, far_pairs)  3.66 us
    all_to_all x2, waiting for transfers between devices, route(): return lax.all_to_all(send, 'fy', split_axis=0, concat_axis=0, tiled=True)  2.28 us
    unnamed x20, local copies, waits for them, and re-layouts  2.02 us
    ppermute x2, waiting for transfers between devices, traces(): far_got = lax.ppermute(to_b, names, far_pairs)  1.78 us
  transfers between devices with their start and end apart: 14, of which 6 were waited for; matrix products, arithmetic and copies ran while one was open for 0% of the time, Pallas kernels for 18%

profile of v18, /device:TPU:2, one launch (start us, length us, event | category | flops | bytes accessed | tf_op | source)
XLA Modules:
  0.0 56.5 jit_solution(12577151950723162864)
XLA Ops:
  0.7 0.9 %broadcast_multiply_fusion = f32[3,8,8,128]{3,2,1,0:T(8,128)S(1)} fusion(f32[3,8,8,128]{3,2,1,0:T(8,128)} %param.11, f32[8,8,128]{2,1,0:T(8,128)} %param.10), kind=kLoop, calls=%fused_computation.1 | loop fusion | flops 24576 | bytes 229376 | tf_op jit(solution)/shard_map/mul | solution.py:784
  1.9 1.6 %collective-permute-start.1 = (f32[24,128]{1,0:T(8,128)S(1)}, f32[24,128]{1,0:T(8,128)S(1)}, u32[]{:S(2)}, u32[]{:S(2)}) collective-permute-start(f32[24,128]{1,0:T(8,128)S(1)} %get-tuple-element.32.sent_b), channel_id=1, source_target_pairs={{3,0},{2,1},{1,2},{0,3},{7,4},{6,5},{5,6},{4,7},{11,8},{10,9},{9,1... | collective-permute-start | bytes 36872 | tf_op jit(solution)/shard_map/ppermute | solution.py:791
  3.5 0.5 collective-permute-start.2
  4.1 0.7 %copy-done.4 = s32[16,6]{0,1:T(8,128)S(1)} copy-done((s32[16,6]{0,1:T(8,128)S(1)}, s32[16,6]{0,1:T(8,128)}, u32[]{:S(2)}) %copy-start.4) | copy-done | bytes 408
  4.8 0.6 %copy-done.8 = s32[1,1,1,16]{3,2,1,0:T(1,128)S(1)} copy-done((s32[1,1,1,16]{3,2,1,0:T(1,128)S(1)}, s32[1,1,1,16]{3,2,1,0:T(1,128)}, u32[]{:S(2)}) %copy-start.8) | copy-done | bytes 88
  5.4 0.6 %shard_map.114 = (f32[4,64,128]{2,1,0:T(8,128)S(1)}, f32[96,128]{1,0:T(8,128)S(1)}, f32[104,128]{1,0:T(8,128)S(1)}) custom-call(f32[16,4,512]{2,1,0:T(4,128)S(1)} %copy-done, f32[8,128]{1,0:T(8,128)S(1)} %pad.43.local, f32[24,128]{1,0:T(8,128)S(1)} %collective-permute-done._.got_a), custom_call_target="tpu_custom_call" | custom-call | tf_op jit(solution)/shard_map/pallas_call | solution.py:52
  6.2 1.6 %collective-permute-start.3 = (f32[40,128]{1,0:T(8,128)S(1)}, f32[40,128]{1,0:T(8,128)S(1)}, u32[]{:S(2)}, u32[]{:S(2)}) collective-permute-start(f32[40,128]{1,0:T(8,128)S(1)} %shard_map.115.edge), channel_id=1, source_target_pairs={{16,0},{0,16},{17,1},{1,17},{18,2},{2,18},{19,3},{3,19},{20,4},{4,... | collective-permute-start | bytes 61448 | tf_op jit(solution)/shard_map/ppermute | solution.py:831
  7.8 5.2 %collective-permute-start.7 = (f32[104,128]{1,0:T(8,128)S(1)}, f32[104,128]{1,0:T(8,128)S(1)}, u32[]{:S(2)}, u32[]{:S(2)}) collective-permute-start(f32[104,128]{1,0:T(8,128)S(1)} %get-tuple-element.48), channel_id=1, source_target_pairs={{1,2},{2,1},{3,4},{4,3},{5,6},{6,5},{7,8},{8,7},{9,10},{10,9},{11,... | collective-permute-start | bytes 159752 | tf_op jit(solution)/shard_map/ppermute | solution.py:801
  13.2 0.7 %collective-permute-start.5 = (f32[176,128]{1,0:T(8,128)S(1)}, f32[176,128]{1,0:T(8,128)S(1)}, u32[]{:S(2)}, u32[]{:S(2)}) collective-permute-start(f32[176,128]{1,0:T(8,128)S(1)} %get-tuple-element.35), channel_id=1, source_target_pairs={{12,0},{8,4},{4,8},{0,12},{13,1},{9,5},{5,9},{1,13},{14,2},{10,6},... | collective-permute-start | bytes 270344 | tf_op jit(solution)/shard_map/ppermute | solution.py:834
  13.9 0.6 %copy-done.7 = f32[16]{0:T(128)S(1)} copy-done((f32[16]{0:T(128)S(1)}, f32[16]{0:T(128)}, u32[]{:S(2)}) %copy-start.7) | copy-done | bytes 88
  14.5 1.0 %shard_map.117 = (bf16[5,128,128]{2,1,0:T(8,128)(2,1)S(1)}, bf16[5,128,128]{2,1,0:T(8,128)(2,1)S(1)}, f32[128,64]{1,0:T(8,128)S(1)}, f32[128,128]{1,0:T(8,128)S(...) custom-call(f32[32,16]{1,0:T(8,128)S(1)} %pad_add_fusion.1.packed), custom_call_target="tpu_custom_call" | custom-call | flops 1 | bytes 1 | tf_op jit(solution)/shard_map/pallas_call | solution.py:52
  15.5 1.8 %collective-permute-done.7.refs_6_.got_b = f32[104,128]{1,0:T(8,128)S(1)} collective-permute-done((f32[104,128]{1,0:T(8,128)S(1)}, f32[104,128]{1,0:T(8,128)S(1)}, u32[]{:S(2)}, u32[]{:S(2)}) %collective-permute-start.7) | collective-permute-done | bytes 53280 | tf_op jit(solution)/shard_map/ppermute | solution.py:801
  17.3 1.2 %collective-permute-done.6.refs_3_.refs_2_ = f32[168,128]{1,0:T(8,128)S(1)} collective-permute-done((f32[168,128]{1,0:T(8,128)S(1)}, f32[168,128]{1,0:T(8,128)S(1)}, u32[]{:S(2)}, u32[]{:S(2)}) %collective-permute-start.6) | collective-permute-done | bytes 86048 | tf_op jit(solution)/shard_map/ppermute | solution.py:835
  18.5 1.1 %collective-permute-done.5.refs_2_.refs_1_ = f32[176,128]{1,0:T(8,128)S(1)} collective-permute-done((f32[176,128]{1,0:T(8,128)S(1)}, f32[176,128]{1,0:T(8,128)S(1)}, u32[]{:S(2)}, u32[]{:S(2)}) %collective-permute-start.5) | collective-permute-done | bytes 90144 | tf_op jit(solution)/shard_map/ppermute | solution.py:834
  19.5 1.3 %shard_map.121 = f32[4,104,128]{2,1,0:T(8,128)} custom-call(f32[5,8,8,128]{3,2,1,0:T(8,128)S(1)} %pad_add_fusion.state, f32[40,128]{1,0:T(8,128)S(1)} %shard_map.115.edge, f32[240,128]{1,0:T(8,128)S(1)} %collective-permute-done.2.refs_0_, f32[176,128]{1,0:T(8,128)S(1)} %collective-permute-done.5.refs_2_.refs_1_, ...), custom_call_target="tpu_custom_call" | custom-call | tf_op jit(solution)/shard_map/pallas_call | solution.py:52
  20.9 3.6 %all-to-all-start = ((f32[4,104,128]{2,1,0:T(8,128)}), f32[4,104,128]{2,1,0:T(8,128)S(1)}, u32[]{:S(2)}, u32[]{:S(2)}) async-start(f32[4,104,128]{2,1,0:T(8,128)} %shard_map.121), calls=%async_computation | async-start | bytes 425984 | tf_op jit(solution)/shard_map/all_to_all | solution.py:877
  24.5 0.3 shard_map.118.refs_6_.partial
  24.8 3.9 %shard_map.119 = (f32[5,10,16,128]{3,2,1,0:T(8,128)S(1)}, f32[5,14,16,128]{3,2,1,0:T(8,128)S(1)}, f32[5,8,8,128]{3,2,1,0:T(8,128)S(1)}, f32[4,192,128]{2,1,0:T(8,128)}) custom-call(f32[5,8,8,128]{3,2,1,0:T(8,128)S(1)} %pad_add_fusion.state, f32[40,128]{1,0:T(8,128)S(1)} %shard_map.115.edge, f32[240,128]{1,0:T(8,128)S(1)} %collective-permute-done.2.refs_0_, ...), custom_call_target="tpu_custom_call" | custom-call | tf_op jit(solution)/shard_map/pallas_call | solution.py:52
  28.7 2.3 %all-to-all-done.received.labelled = f32[4,104,128]{2,1,0:T(8,128)S(1)} async-done(((f32[4,104,128]{2,1,0:T(8,128)}), f32[4,104,128]{2,1,0:T(8,128)S(1)}, u32[]{:S(2)}, u32[]{:S(2)}) %all-to-all-start) | async-done | bytes 213024 | tf_op jit(solution)/shard_map/all_to_all | solution.py:877
  31.0 3.5 %all-to-all-start.1 = ((f32[4,192,128]{2,1,0:T(8,128)}), f32[4,192,128]{2,1,0:T(8,128)S(1)}, u32[]{:S(2)}, u32[]{:S(2)}) async-start(f32[4,192,128]{2,1,0:T(8,128)} %get-tuple-element.51._), calls=%async_computation.1 | async-start | bytes 786432 | tf_op jit(solution)/shard_map/all_to_all | solution.py:877
  34.4 0.5 shard_map.122
  35.0 8.5 %collective-permute-start.9 = (f32[128,128]{1,0:T(8,128)S(1)}, f32[128,128]{1,0:T(8,128)S(1)}, u32[]{:S(2)}, u32[]{:S(2)}) collective-permute-start(f32[128,128]{1,0:T(8,128)S(1)} %get-tuple-element.54.sent_b), channel_id=1, source_target_pairs={{1,2},{2,1},{3,4},{4,3},{5,6},{6,5},{7,8},{8,7},{9,10},{10,9},{11,... | collective-permute-start | bytes 196616 | tf_op jit(solution)/shard_map/ppermute | solution.py:801
  43.8 1.0 %shard_map.120 = (f32[5,8,8,128]{3,2,1,0:T(8,128)}, f32[8,128]{1,0:T(8,128)S(1)}) custom-call(f32[5,10,16,128]{3,2,1,0:T(8,128)S(1)} %get-tuple-element.44.second, f32[5,14,16,128]{3,2,1,0:T(8,128)S(1)} %get-tuple-element.45.derived, f32[5,8,8,128]{3,2,1,0:T(8,128)S(1)} %get-tuple-element.46.ends, f32[5,8,8,128]{3,2,1,0:T(8,128)S(1)} %pad_add_fusion.state), custom_call_target="tpu_custom_call" | custom-call | tf_op jit(solution)/shard_map/pallas_call | solution.py:52
  44.8 0.3 shard_map.123.partial
  45.2 0.3 shard_map.125._.change
  45.5 0.5 shard_map.126
  46.1 3.7 %collective-permute-start.11 = (f32[128,128]{1,0:T(8,128)S(1)}, f32[128,128]{1,0:T(8,128)S(1)}, u32[]{:S(2)}, u32[]{:S(2)}) collective-permute-start(f32[128,128]{1,0:T(8,128)S(1)} %get-tuple-element.59), channel_id=1, source_target_pairs={{1,2},{2,1},{3,4},{4,3},{5,6},{6,5},{7,8},{8,7},{9,10},{10,9},{11,... | collective-permute-start | bytes 196616 | tf_op jit(solution)/shard_map/ppermute | solution.py:981
  49.7 0.3 shard_map.127
  50.2 0.3 shard_map.128.partial
  50.8 0.6 collective-permute-done.10.got_a
  51.4 3.9 %collective-permute-done.11.got_b = f32[128,128]{1,0:T(8,128)S(1)} collective-permute-done((f32[128,128]{1,0:T(8,128)S(1)}, f32[128,128]{1,0:T(8,128)S(1)}, u32[]{:S(2)}, u32[]{:S(2)}) %collective-permute-start.11) | collective-permute-done | bytes 65568 | tf_op jit(solution)/shard_map/ppermute | solution.py:981
  55.2 1.3 %shard_map.130 = f32[16,4,512]{2,1,0:T(4,128)} custom-call(f32[4,64,128]{2,1,0:T(8,128)S(1)} %shard_map.128.partial, f32[96,128]{1,0:T(8,128)S(1)} %collective-permute-done.10.got_a, f32[128,128]{1,0:T(8,128)S(1)} %collective-permute-done.11.got_b, f32[96,128]{1,0:T(8,128)S(1)} %shard_map.125._.change, bf16[5,128,128]{2,1,0:T(8,128)(2,1)S(1)} %get-tuple-element.49.sides_far, ...), custom_call_target="tpu_custom_call" | custom-call | tf_op jit(solution)/shard_map/pallas_call | solution.py:52
  (42 shorter events, 1.2 us)
Async XLA Ops:
  0.6 1.0 %copy-start.1 = (f32[3,8,8,128]{3,2,1,0:T(8,128)S(1)}, f32[3,8,8,128]{3,2,1,0:T(8,128)}, u32[]{:S(2)}) copy-start(f32[3,8,8,128]{3,2,1,0:T(8,128)} %param.11) | copy-start | bytes 294916
  0.6 1.0 %copy-start.2 = (f32[8,8,128]{2,1,0:T(8,128)S(1)}, f32[8,8,128]{2,1,0:T(8,128)}, u32[]{:S(2)}) copy-start(f32[8,8,128]{2,1,0:T(8,128)} %param.10) | copy-start | bytes 98308
  0.6 1.0 %copy-start.3 = (f32[8,8,128]{2,1,0:T(8,128)S(1)}, f32[8,8,128]{2,1,0:T(8,128)}, u32[]{:S(2)}) copy-start(f32[8,8,128]{2,1,0:T(8,128)} %param.12) | copy-start | bytes 98308
  1.7 3.7 %copy-start = (f32[16,4,512]{2,1,0:T(4,128)S(1)}, f32[16,4,512]{2,1,0:T(4,128)}, u32[]{:S(2)}) copy-start(f32[16,4,512]{2,1,0:T(4,128)} %given.1) | copy-start | bytes 393220
  1.8 3.6 %collective-permute-start = (f32[24,128]{1,0:T(8,128)S(1)}, f32[24,128]{1,0:T(8,128)S(1)}, u32[]{:S(2)}, u32[]{:S(2)}) collective-permute-start(f32[24,128]{1,0:T(8,128)S(1)} %get-tuple-element.31.sent_a), channel_id=1, source_target_pairs={{1,0},{0,1},{3,2},{2,3},{5,4},{4,5},{7,6},{6,7},{9,8},{8,9},{11,10... | collective-permute-start | bytes 36872 | tf_op jit(solution)/shard_map/ppermute | solution.py:790
  1.9 4.2 %collective-permute-start.1 = (f32[24,128]{1,0:T(8,128)S(1)}, f32[24,128]{1,0:T(8,128)S(1)}, u32[]{:S(2)}, u32[]{:S(2)}) collective-permute-start(f32[24,128]{1,0:T(8,128)S(1)} %get-tuple-element.32.sent_b), channel_id=1, source_target_pairs={{3,0},{2,1},{1,2},{0,3},{7,4},{6,5},{5,6},{4,7},{11,8},{10,9},{9,1... | collective-permute-start | bytes 36872 | tf_op jit(solution)/shard_map/ppermute | solution.py:791
  3.5 9.5 %collective-permute-start.2 = (f32[240,128]{1,0:T(8,128)S(1)}, f32[240,128]{1,0:T(8,128)S(1)}, u32[]{:S(2)}, u32[]{:S(2)}) collective-permute-start(f32[240,128]{1,0:T(8,128)S(1)} %get-tuple-element.34), channel_id=1, source_target_pairs={{16,0},{0,16},{17,1},{1,17},{18,2},{2,18},{19,3},{3,19},{20,4},{4,... | collective-permute-start | bytes 368648 | tf_op jit(solution)/shard_map/ppermute | solution.py:793
  4.1 0.7 %copy-start.4 = (s32[16,6]{0,1:T(8,128)S(1)}, s32[16,6]{0,1:T(8,128)}, u32[]{:S(2)}) copy-start(s32[16,6]{0,1:T(8,128)} %param.17) | copy-start | bytes 1156
  4.8 0.7 %copy-start.8 = (s32[1,1,1,16]{3,2,1,0:T(1,128)S(1)}, s32[1,1,1,16]{3,2,1,0:T(1,128)}, u32[]{:S(2)}) copy-start(s32[1,1,1,16]{3,2,1,0:T(1,128)} %param.19) | copy-start | bytes 196
  6.0 1.8 %copy-start.9 = (s32[1,1,1,16,1]{3,4,2,1,0:T(1,128)S(1)}, s32[1,1,1,16,1]{3,4,2,1,0:T(1,128)}, u32[]{:S(2)}) copy-start(s32[1,1,1,16,1]{3,4,2,1,0:T(1,128)} %param.18) | copy-start | bytes 196
  6.0 7.0 %collective-permute-start.4 = (f32[96,128]{1,0:T(8,128)S(1)}, f32[96,128]{1,0:T(8,128)S(1)}, u32[]{:S(2)}, u32[]{:S(2)}) collective-permute-start(f32[96,128]{1,0:T(8,128)S(1)} %get-tuple-element.33._), channel_id=1, source_target_pairs={{1,0},{0,1},{3,2},{2,3},{5,4},{4,5},{7,6},{6,7},{9,8},{8,9},{11,10... | collective-permute-start | bytes 147464 | tf_op jit(solution)/shard_map/ppermute | solution.py:802
  6.2 6.8 %collective-permute-start.3 = (f32[40,128]{1,0:T(8,128)S(1)}, f32[40,128]{1,0:T(8,128)S(1)}, u32[]{:S(2)}, u32[]{:S(2)}) collective-permute-start(f32[40,128]{1,0:T(8,128)S(1)} %shard_map.115.edge), channel_id=1, source_target_pairs={{16,0},{0,16},{17,1},{1,17},{18,2},{2,18},{19,3},{3,19},{20,4},{4,... | collective-permute-start | bytes 61448 | tf_op jit(solution)/shard_map/ppermute | solution.py:831
  7.8 9.5 %collective-permute-start.7 = (f32[104,128]{1,0:T(8,128)S(1)}, f32[104,128]{1,0:T(8,128)S(1)}, u32[]{:S(2)}, u32[]{:S(2)}) collective-permute-start(f32[104,128]{1,0:T(8,128)S(1)} %get-tuple-element.48), channel_id=1, source_target_pairs={{1,2},{2,1},{3,4},{4,3},{5,6},{6,5},{7,8},{8,7},{9,10},{10,9},{11,... | collective-permute-start | bytes 159752 | tf_op jit(solution)/shard_map/ppermute | solution.py:801
  13.1 0.8 %copy-start.6 = (f32[8,8]{1,0:T(8,128)S(1)}, f32[8,8]{1,0:T(8,128)}, u32[]{:S(2)}) copy-start(f32[8,8]{1,0:T(8,128)} %param.15) | copy-start | bytes 772
  13.1 0.7 %copy-start.5 = (f32[8,8]{1,0:T(8,128)S(1)}, f32[8,8]{1,0:T(8,128)}, u32[]{:S(2)}) copy-start(f32[8,8]{1,0:T(8,128)} %param.16) | copy-start | bytes 772
  13.2 6.4 %collective-permute-start.5 = (f32[176,128]{1,0:T(8,128)S(1)}, f32[176,128]{1,0:T(8,128)S(1)}, u32[]{:S(2)}, u32[]{:S(2)}) collective-permute-start(f32[176,128]{1,0:T(8,128)S(1)} %get-tuple-element.35), channel_id=1, source_target_pairs={{12,0},{8,4},{4,8},{0,12},{13,1},{9,5},{5,9},{1,13},{14,2},{10,6},... | collective-permute-start | bytes 270344 | tf_op jit(solution)/shard_map/ppermute | solution.py:834
  13.8 0.7 %copy-start.7 = (f32[16]{0:T(128)S(1)}, f32[16]{0:T(128)}, u32[]{:S(2)}) copy-start(f32[16]{0:T(128)} %param.14) | copy-start | bytes 196
  13.8 4.6 %collective-permute-start.6 = (f32[168,128]{1,0:T(8,128)S(1)}, f32[168,128]{1,0:T(8,128)S(1)}, u32[]{:S(2)}, u32[]{:S(2)}) collective-permute-start(f32[168,128]{1,0:T(8,128)S(1)} %get-tuple-element.36), channel_id=1, source_target_pairs={{4,0},{0,4},{12,8},{8,12},{5,1},{1,5},{13,9},{9,13},{6,2},{2,6},{1... | collective-permute-start | bytes 258056 | tf_op jit(solution)/shard_map/ppermute | solution.py:835
  20.9 10.1 %all-to-all-start = ((f32[4,104,128]{2,1,0:T(8,128)}), f32[4,104,128]{2,1,0:T(8,128)S(1)}, u32[]{:S(2)}, u32[]{:S(2)}) async-start(f32[4,104,128]{2,1,0:T(8,128)} %shard_map.121), calls=%async_computation | async-start | bytes 425984 | tf_op jit(solution)/shard_map/all_to_all | solution.py:877
  31.0 14.6 %all-to-all-start.1 = ((f32[4,192,128]{2,1,0:T(8,128)}), f32[4,192,128]{2,1,0:T(8,128)S(1)}, u32[]{:S(2)}, u32[]{:S(2)}) async-start(f32[4,192,128]{2,1,0:T(8,128)} %get-tuple-element.51._), calls=%async_computation.1 | async-start | bytes 786432 | tf_op jit(solution)/shard_map/all_to_all | solution.py:877
  35.0 10.5 %collective-permute-start.8 = (f32[96,128]{1,0:T(8,128)S(1)}, f32[96,128]{1,0:T(8,128)S(1)}, u32[]{:S(2)}, u32[]{:S(2)}) collective-permute-start(f32[96,128]{1,0:T(8,128)S(1)} %get-tuple-element.53), channel_id=1, source_target_pairs={{1,0},{0,1},{3,2},{2,3},{5,4},{4,5},{7,6},{6,7},{9,8},{8,9},{11,10... | collective-permute-start | bytes 147464 | tf_op jit(solution)/shard_map/ppermute | solution.py:802
  35.0 14.7 %collective-permute-start.9 = (f32[128,128]{1,0:T(8,128)S(1)}, f32[128,128]{1,0:T(8,128)S(1)}, u32[]{:S(2)}, u32[]{:S(2)}) collective-permute-start(f32[128,128]{1,0:T(8,128)S(1)} %get-tuple-element.54.sent_b), channel_id=1, source_target_pairs={{1,2},{2,1},{3,4},{4,3},{5,6},{6,5},{7,8},{8,7},{9,10},{10,9},{11,... | collective-permute-start | bytes 196616 | tf_op jit(solution)/shard_map/ppermute | solution.py:801
  46.1 9.2 %collective-permute-start.11 = (f32[128,128]{1,0:T(8,128)S(1)}, f32[128,128]{1,0:T(8,128)S(1)}, u32[]{:S(2)}, u32[]{:S(2)}) collective-permute-start(f32[128,128]{1,0:T(8,128)S(1)} %get-tuple-element.59), channel_id=1, source_target_pairs={{1,2},{2,1},{3,4},{4,3},{5,6},{6,5},{7,8},{8,7},{9,10},{10,9},{11,... | collective-permute-start | bytes 196616 | tf_op jit(solution)/shard_map/ppermute | solution.py:981
  50.1 1.3 %collective-permute-start.10 = (f32[96,128]{1,0:T(8,128)S(1)}, f32[96,128]{1,0:T(8,128)S(1)}, u32[]{:S(2)}, u32[]{:S(2)}) collective-permute-start(f32[96,128]{1,0:T(8,128)S(1)} %get-tuple-element.58), channel_id=1, source_target_pairs={{1,0},{0,1},{3,2},{2,3},{5,4},{4,5},{7,6},{6,7},{9,8},{8,9},{11,10... | collective-permute-start | bytes 147464 | tf_op jit(solution)/shard_map/ppermute | solution.py:985

commit v19 on v18

--- a/solution.py
+++ b/solution.py
@@ -583,7 +583,8 @@
     faces_sent(odd, out, message_a, spare)
 
 
-def mirror_body(sent_b, sides_partner, change, before, after, spare, state):
+def mirror_body(sent_b, sides_partner, sent_a, change, later_a, before, after, spare, state):
+    later_a[...] = sent_a[...]
     odd = jnp.logical_not(is_odd("fz"))
     arrived(odd, None, sent_b, before, after)
     state[...] = jnp.zeros(state.shape, F32)
@@ -958,14 +959,21 @@
         last=1,
     )
     labelled, received = received, route(send)
-    got_a, got_b = traces(to_a, to_b)
+    got_b = lax.ppermute(to_b, names, far_pairs)
+    change, to_a = call(
+        mirror_body,
+        [faces, faces],
+        to_b,
+        far_partner,
+        to_a,
+        scratch=sides + [near_face, pltpu.VMEM(held, F32)],
+        cost=1,
+    )
+    got_a = lax.ppermute(to_a, names, near_pairs)
     flow_state, done = call(
         flow_last_body, [(5, cells_x, 8, 128), (8, 128)], second, derived, ends, state
     )
     partial = local_part(MIXES[1], sound_one)
-    change = call(
-        mirror_body, [faces], to_b, far_partner, scratch=sides + [near_face, pltpu.VMEM(held, F32)], cost=1
-    )[0]
     partial, to_b = call(
         acoustic_near_body,
         [held, longer],

time: 57 us -> 57 us (level)
    ppermute x2 -> x1, starting transfers between devices: 13.8 us -> 5.23 us  [traces(): far_got = lax.ppermute(to_b, names, far_pairs)]
    ppermute x0 -> x1, starting transfers between devices: none -> 8.54 us  [per_device(): got_b = lax.ppermute(to_b, names, far_pairs)]
    ppermute x2 -> x1, waiting for transfers between devices: 1.78 us -> 1.77 us  [traces(): far_got = lax.ppermute(to_b, names, far_pairs)]
where the time goes in v19:
time: 57 us; the launch traced here: 56.5 us
  starting transfers between devices  29.2 us (51%)
  Pallas kernels  12.6 us (22%)
  waiting for transfers between devices  10.7 us (19%)
  local copies, waits for them, and re-layouts  2.02 us (4%)
  other arithmetic  1 us (2%)
  between operations  0.94 us (2%)
    pallas_call x18, Pallas kernels, call(): pl.pallas_call(body, out_shape=outs, in_specs=[whole] * (len(operands) -...  12.6 us
    ppermute x1, starting transfers between devices, per_device(): got_b = lax.ppermute(to_b, names, far_pairs)  8.54 us
    all_to_all x2, starting transfers between devices, route(): return lax.all_to_all(send, 'fy', split_axis=0, concat_axis=0, tiled=True)  7.09 us
    ppermute x1, starting transfers between devices, traces(): far_got = lax.ppermute(to_b, names, far_pairs)  5.23 us
    ppermute x1, waiting for transfers between devices, per_device(): got_b_last = lax.ppermute(to_b, names, far_pairs)  3.82 us
    ppermute x1, starting transfers between devices, per_device(): got_b_last = lax.ppermute(to_b, names, far_pairs)  3.69 us
    all_to_all x2, waiting for transfers between devices, route(): return lax.all_to_all(send, 'fy', split_axis=0, concat_axis=0, tiled=True)  2.26 us
    unnamed x20, local copies, waits for them, and re-layouts  2.02 us
  transfers between devices with their start and end apart: 14, of which 6 were waited for; matrix products, arithmetic and copies ran while one was open for 0% of the time, Pallas kernels for 18%

profile of v19, /device:TPU:2, one launch (start us, length us, event | category | flops | bytes accessed | tf_op | source)
XLA Modules:
  0.0 56.5 jit_solution(15377029333371523403)
XLA Ops:
  0.7 0.9 %broadcast_multiply_fusion = f32[3,8,8,128]{3,2,1,0:T(8,128)S(1)} fusion(f32[3,8,8,128]{3,2,1,0:T(8,128)} %param.11, f32[8,8,128]{2,1,0:T(8,128)} %param.10), kind=kLoop, calls=%fused_computation.1 | loop fusion | flops 24576 | bytes 229376 | tf_op jit(solution)/shard_map/mul | solution.py:785
  1.9 1.6 %collective-permute-start.1 = (f32[24,128]{1,0:T(8,128)S(1)}, f32[24,128]{1,0:T(8,128)S(1)}, u32[]{:S(2)}, u32[]{:S(2)}) collective-permute-start(f32[24,128]{1,0:T(8,128)S(1)} %get-tuple-element.34.sent_b), channel_id=1, source_target_pairs={{3,0},{2,1},{1,2},{0,3},{7,4},{6,5},{5,6},{4,7},{11,8},{10,9},{9,1... | collective-permute-start | bytes 36872 | tf_op jit(solution)/shard_map/ppermute | solution.py:792
  3.5 0.5 collective-permute-start.2
  4.1 0.7 %copy-done.4 = s32[16,6]{0,1:T(8,128)S(1)} copy-done((s32[16,6]{0,1:T(8,128)S(1)}, s32[16,6]{0,1:T(8,128)}, u32[]{:S(2)}) %copy-start.4) | copy-done | bytes 408
  4.8 0.6 %copy-done.8 = s32[1,1,1,16]{3,2,1,0:T(1,128)S(1)} copy-done((s32[1,1,1,16]{3,2,1,0:T(1,128)S(1)}, s32[1,1,1,16]{3,2,1,0:T(1,128)}, u32[]{:S(2)}) %copy-start.8) | copy-done | bytes 88
  5.4 0.6 %shard_map.114 = (f32[4,64,128]{2,1,0:T(8,128)S(1)}, f32[96,128]{1,0:T(8,128)S(1)}, f32[104,128]{1,0:T(8,128)S(1)}) custom-call(f32[16,4,512]{2,1,0:T(4,128)S(1)} %copy-done, f32[8,128]{1,0:T(8,128)S(1)} %pad.43.local, f32[24,128]{1,0:T(8,128)S(1)} %collective-permute-done._.got_a), custom_call_target="tpu_custom_call" | custom-call | tf_op jit(solution)/shard_map/pallas_call | solution.py:52
  6.2 1.6 %collective-permute-start.3 = (f32[40,128]{1,0:T(8,128)S(1)}, f32[40,128]{1,0:T(8,128)S(1)}, u32[]{:S(2)}, u32[]{:S(2)}) collective-permute-start(f32[40,128]{1,0:T(8,128)S(1)} %shard_map.115.edge), channel_id=1, source_target_pairs={{16,0},{0,16},{17,1},{1,17},{18,2},{2,18},{19,3},{3,19},{20,4},{4,... | collective-permute-start | bytes 61448 | tf_op jit(solution)/shard_map/ppermute | solution.py:832
  7.8 5.2 %collective-permute-start.7 = (f32[104,128]{1,0:T(8,128)S(1)}, f32[104,128]{1,0:T(8,128)S(1)}, u32[]{:S(2)}, u32[]{:S(2)}) collective-permute-start(f32[104,128]{1,0:T(8,128)S(1)} %get-tuple-element.50), channel_id=1, source_target_pairs={{1,2},{2,1},{3,4},{4,3},{5,6},{6,5},{7,8},{8,7},{9,10},{10,9},{11,... | collective-permute-start | bytes 159752 | tf_op jit(solution)/shard_map/ppermute | solution.py:802
  13.2 0.7 %collective-permute-start.5 = (f32[176,128]{1,0:T(8,128)S(1)}, f32[176,128]{1,0:T(8,128)S(1)}, u32[]{:S(2)}, u32[]{:S(2)}) collective-permute-start(f32[176,128]{1,0:T(8,128)S(1)} %get-tuple-element.37), channel_id=1, source_target_pairs={{12,0},{8,4},{4,8},{0,12},{13,1},{9,5},{5,9},{1,13},{14,2},{10,6},... | collective-permute-start | bytes 270344 | tf_op jit(solution)/shard_map/ppermute | solution.py:835
  13.9 0.6 %copy-done.7 = f32[16]{0:T(128)S(1)} copy-done((f32[16]{0:T(128)S(1)}, f32[16]{0:T(128)}, u32[]{:S(2)}) %copy-start.7) | copy-done | bytes 88
  14.5 1.0 %shard_map.117 = (bf16[5,128,128]{2,1,0:T(8,128)(2,1)S(1)}, bf16[5,128,128]{2,1,0:T(8,128)(2,1)S(1)}, f32[128,64]{1,0:T(8,128)S(1)}, f32[128,128]{1,0:T(8,128)S(...) custom-call(f32[32,16]{1,0:T(8,128)S(1)} %pad_add_fusion.1.packed), custom_call_target="tpu_custom_call" | custom-call | flops 1 | bytes 1 | tf_op jit(solution)/shard_map/pallas_call | solution.py:52
  15.5 1.8 %collective-permute-done.7.refs_6_.got_b = f32[104,128]{1,0:T(8,128)S(1)} collective-permute-done((f32[104,128]{1,0:T(8,128)S(1)}, f32[104,128]{1,0:T(8,128)S(1)}, u32[]{:S(2)}, u32[]{:S(2)}) %collective-permute-start.7) | collective-permute-done | bytes 53280 | tf_op jit(solution)/shard_map/ppermute | solution.py:802
  17.3 1.2 %collective-permute-done.6.refs_3_.refs_2_ = f32[168,128]{1,0:T(8,128)S(1)} collective-permute-done((f32[168,128]{1,0:T(8,128)S(1)}, f32[168,128]{1,0:T(8,128)S(1)}, u32[]{:S(2)}, u32[]{:S(2)}) %collective-permute-start.6) | collective-permute-done | bytes 86048 | tf_op jit(solution)/shard_map/ppermute | solution.py:836
  18.5 1.1 %collective-permute-done.5.refs_2_.refs_1_ = f32[176,128]{1,0:T(8,128)S(1)} collective-permute-done((f32[176,128]{1,0:T(8,128)S(1)}, f32[176,128]{1,0:T(8,128)S(1)}, u32[]{:S(2)}, u32[]{:S(2)}) %collective-permute-start.5) | collective-permute-done | bytes 90144 | tf_op jit(solution)/shard_map/ppermute | solution.py:835
  19.5 1.3 %shard_map.121 = f32[4,104,128]{2,1,0:T(8,128)} custom-call(f32[5,8,8,128]{3,2,1,0:T(8,128)S(1)} %pad_add_fusion.state, f32[40,128]{1,0:T(8,128)S(1)} %shard_map.115.edge, f32[240,128]{1,0:T(8,128)S(1)} %collective-permute-done.2.refs_0_, f32[176,128]{1,0:T(8,128)S(1)} %collective-permute-done.5.refs_2_.refs_1_, ...), custom_call_target="tpu_custom_call" | custom-call | tf_op jit(solution)/shard_map/pallas_call | solution.py:52
  20.9 3.6 %all-to-all-start = ((f32[4,104,128]{2,1,0:T(8,128)}), f32[4,104,128]{2,1,0:T(8,128)S(1)}, u32[]{:S(2)}, u32[]{:S(2)}) async-start(f32[4,104,128]{2,1,0:T(8,128)} %shard_map.121), calls=%async_computation | async-start | bytes 425984 | tf_op jit(solution)/shard_map/all_to_all | solution.py:878
  24.5 0.3 shard_map.118.refs_6_.partial
  24.8 3.9 %shard_map.119 = (f32[5,10,16,128]{3,2,1,0:T(8,128)S(1)}, f32[5,14,16,128]{3,2,1,0:T(8,128)S(1)}, f32[5,8,8,128]{3,2,1,0:T(8,128)S(1)}, f32[4,192,128]{2,1,0:T(8,128)}) custom-call(f32[5,8,8,128]{3,2,1,0:T(8,128)S(1)} %pad_add_fusion.state, f32[40,128]{1,0:T(8,128)S(1)} %shard_map.115.edge, f32[240,128]{1,0:T(8,128)S(1)} %collective-permute-done.2.refs_0_, ...), custom_call_target="tpu_custom_call" | custom-call | tf_op jit(solution)/shard_map/pallas_call | solution.py:52
  28.7 2.3 %all-to-all-done.received.labelled = f32[4,104,128]{2,1,0:T(8,128)S(1)} async-done(((f32[4,104,128]{2,1,0:T(8,128)}), f32[4,104,128]{2,1,0:T(8,128)S(1)}, u32[]{:S(2)}, u32[]{:S(2)}) %all-to-all-start) | async-done | bytes 213024 | tf_op jit(solution)/shard_map/all_to_all | solution.py:878
  31.0 3.5 %all-to-all-start.1 = ((f32[4,192,128]{2,1,0:T(8,128)}), f32[4,192,128]{2,1,0:T(8,128)S(1)}, u32[]{:S(2)}, u32[]{:S(2)}) async-start(f32[4,192,128]{2,1,0:T(8,128)} %get-tuple-element.53._), calls=%async_computation.1 | async-start | bytes 786432 | tf_op jit(solution)/shard_map/all_to_all | solution.py:878
  34.6 0.5 shard_map.122
  35.2 0.4 shard_map.125
  35.6 8.5 %collective-permute-start.9 = (f32[128,128]{1,0:T(8,128)S(1)}, f32[128,128]{1,0:T(8,128)S(1)}, u32[]{:S(2)}, u32[]{:S(2)}) collective-permute-start(f32[128,128]{1,0:T(8,128)S(1)} %get-tuple-element.55.sent_b), channel_id=1, source_target_pairs={{1,2},{2,1},{3,4},{4,3},{5,6},{6,5},{7,8},{8,7},{9,10},{10,9},{11,... | collective-permute-start | bytes 196616 | tf_op jit(solution)/shard_map/ppermute | solution.py:962
  44.1 1.0 %shard_map.120 = (f32[5,8,8,128]{3,2,1,0:T(8,128)}, f32[8,128]{1,0:T(8,128)S(1)}) custom-call(f32[5,10,16,128]{3,2,1,0:T(8,128)S(1)} %get-tuple-element.46.second, f32[5,14,16,128]{3,2,1,0:T(8,128)S(1)} %get-tuple-element.47.derived, f32[5,8,8,128]{3,2,1,0:T(8,128)S(1)} %get-tuple-element.48.ends, f32[5,8,8,128]{3,2,1,0:T(8,128)S(1)} %pad_add_fusion.state), custom_call_target="tpu_custom_call" | custom-call | tf_op jit(solution)/shard_map/pallas_call | solution.py:52
  45.2 0.3 shard_map.123.partial
  45.5 0.5 shard_map.126
  46.1 3.7 %collective-permute-start.11 = (f32[128,128]{1,0:T(8,128)S(1)}, f32[128,128]{1,0:T(8,128)S(1)}, u32[]{:S(2)}, u32[]{:S(2)}) collective-permute-start(f32[128,128]{1,0:T(8,128)S(1)} %get-tuple-element.63), channel_id=1, source_target_pairs={{1,2},{2,1},{3,4},{4,3},{5,6},{6,5},{7,8},{8,7},{9,10},{10,9},{11,... | collective-permute-start | bytes 196616 | tf_op jit(solution)/shard_map/ppermute | solution.py:989
  49.8 0.3 shard_map.127
  50.2 0.3 shard_map.128.partial
  50.9 0.6 collective-permute-done.10.got_a
  51.4 3.8 %collective-permute-done.11.got_b = f32[128,128]{1,0:T(8,128)S(1)} collective-permute-done((f32[128,128]{1,0:T(8,128)S(1)}, f32[128,128]{1,0:T(8,128)S(1)}, u32[]{:S(2)}, u32[]{:S(2)}) %collective-permute-start.11) | collective-permute-done | bytes 65568 | tf_op jit(solution)/shard_map/ppermute | solution.py:989
  55.3 1.3 %shard_map.130 = f32[16,4,512]{2,1,0:T(4,128)} custom-call(f32[4,64,128]{2,1,0:T(8,128)S(1)} %shard_map.128.partial, f32[96,128]{1,0:T(8,128)S(1)} %collective-permute-done.10.got_a, f32[128,128]{1,0:T(8,128)S(1)} %collective-permute-done.11.got_b, f32[96,128]{1,0:T(8,128)S(1)} %get-tuple-element.58._.change, ...), custom_call_target="tpu_custom_call" | custom-call | tf_op jit(solution)/shard_map/pallas_call | solution.py:52
  (42 shorter events, 1.2 us)
Async XLA Ops:
  0.6 1.0 %copy-start.1 = (f32[3,8,8,128]{3,2,1,0:T(8,128)S(1)}, f32[3,8,8,128]{3,2,1,0:T(8,128)}, u32[]{:S(2)}) copy-start(f32[3,8,8,128]{3,2,1,0:T(8,128)} %param.11) | copy-start | bytes 294916
  0.6 1.0 %copy-start.2 = (f32[8,8,128]{2,1,0:T(8,128)S(1)}, f32[8,8,128]{2,1,0:T(8,128)}, u32[]{:S(2)}) copy-start(f32[8,8,128]{2,1,0:T(8,128)} %param.10) | copy-start | bytes 98308
  0.6 1.0 %copy-start.3 = (f32[8,8,128]{2,1,0:T(8,128)S(1)}, f32[8,8,128]{2,1,0:T(8,128)}, u32[]{:S(2)}) copy-start(f32[8,8,128]{2,1,0:T(8,128)} %param.12) | copy-start | bytes 98308
  1.7 3.7 %copy-start = (f32[16,4,512]{2,1,0:T(4,128)S(1)}, f32[16,4,512]{2,1,0:T(4,128)}, u32[]{:S(2)}) copy-start(f32[16,4,512]{2,1,0:T(4,128)} %given.1) | copy-start | bytes 393220
  1.8 3.6 %collective-permute-start = (f32[24,128]{1,0:T(8,128)S(1)}, f32[24,128]{1,0:T(8,128)S(1)}, u32[]{:S(2)}, u32[]{:S(2)}) collective-permute-start(f32[24,128]{1,0:T(8,128)S(1)} %get-tuple-element.33.sent_a), channel_id=1, source_target_pairs={{1,0},{0,1},{3,2},{2,3},{5,4},{4,5},{7,6},{6,7},{9,8},{8,9},{11,10... | collective-permute-start | bytes 36872 | tf_op jit(solution)/shard_map/ppermute | solution.py:791
  1.9 4.2 %collective-permute-start.1 = (f32[24,128]{1,0:T(8,128)S(1)}, f32[24,128]{1,0:T(8,128)S(1)}, u32[]{:S(2)}, u32[]{:S(2)}) collective-permute-start(f32[24,128]{1,0:T(8,128)S(1)} %get-tuple-element.34.sent_b), channel_id=1, source_target_pairs={{3,0},{2,1},{1,2},{0,3},{7,4},{6,5},{5,6},{4,7},{11,8},{10,9},{9,1... | collective-permute-start | bytes 36872 | tf_op jit(solution)/shard_map/ppermute | solution.py:792
  3.5 9.5 %collective-permute-start.2 = (f32[240,128]{1,0:T(8,128)S(1)}, f32[240,128]{1,0:T(8,128)S(1)}, u32[]{:S(2)}, u32[]{:S(2)}) collective-permute-start(f32[240,128]{1,0:T(8,128)S(1)} %get-tuple-element.36), channel_id=1, source_target_pairs={{16,0},{0,16},{17,1},{1,17},{18,2},{2,18},{19,3},{3,19},{20,4},{4,... | collective-permute-start | bytes 368648 | tf_op jit(solution)/shard_map/ppermute | solution.py:794
  4.1 0.7 %copy-start.4 = (s32[16,6]{0,1:T(8,128)S(1)}, s32[16,6]{0,1:T(8,128)}, u32[]{:S(2)}) copy-start(s32[16,6]{0,1:T(8,128)} %param.17) | copy-start | bytes 1156
  4.8 0.7 %copy-start.8 = (s32[1,1,1,16]{3,2,1,0:T(1,128)S(1)}, s32[1,1,1,16]{3,2,1,0:T(1,128)}, u32[]{:S(2)}) copy-start(s32[1,1,1,16]{3,2,1,0:T(1,128)} %param.19) | copy-start | bytes 196
  6.0 1.8 %copy-start.9 = (s32[1,1,1,16,1]{3,4,2,1,0:T(1,128)S(1)}, s32[1,1,1,16,1]{3,4,2,1,0:T(1,128)}, u32[]{:S(2)}) copy-start(s32[1,1,1,16,1]{3,4,2,1,0:T(1,128)} %param.18) | copy-start | bytes 196
  6.0 7.0 %collective-permute-start.4 = (f32[96,128]{1,0:T(8,128)S(1)}, f32[96,128]{1,0:T(8,128)S(1)}, u32[]{:S(2)}, u32[]{:S(2)}) collective-permute-start(f32[96,128]{1,0:T(8,128)S(1)} %get-tuple-element.35._), channel_id=1, source_target_pairs={{1,0},{0,1},{3,2},{2,3},{5,4},{4,5},{7,6},{6,7},{9,8},{8,9},{11,10... | collective-permute-start | bytes 147464 | tf_op jit(solution)/shard_map/ppermute | solution.py:803
  6.2 6.8 %collective-permute-start.3 = (f32[40,128]{1,0:T(8,128)S(1)}, f32[40,128]{1,0:T(8,128)S(1)}, u32[]{:S(2)}, u32[]{:S(2)}) collective-permute-start(f32[40,128]{1,0:T(8,128)S(1)} %shard_map.115.edge), channel_id=1, source_target_pairs={{16,0},{0,16},{17,1},{1,17},{18,2},{2,18},{19,3},{3,19},{20,4},{4,... | collective-permute-start | bytes 61448 | tf_op jit(solution)/shard_map/ppermute | solution.py:832
  7.8 9.5 %collective-permute-start.7 = (f32[104,128]{1,0:T(8,128)S(1)}, f32[104,128]{1,0:T(8,128)S(1)}, u32[]{:S(2)}, u32[]{:S(2)}) collective-permute-start(f32[104,128]{1,0:T(8,128)S(1)} %get-tuple-element.50), channel_id=1, source_target_pairs={{1,2},{2,1},{3,4},{4,3},{5,6},{6,5},{7,8},{8,7},{9,10},{10,9},{11,... | collective-permute-start | bytes 159752 | tf_op jit(solution)/shard_map/ppermute | solution.py:802
  13.1 0.8 %copy-start.6 = (f32[8,8]{1,0:T(8,128)S(1)}, f32[8,8]{1,0:T(8,128)}, u32[]{:S(2)}) copy-start(f32[8,8]{1,0:T(8,128)} %param.15) | copy-start | bytes 772
  13.1 0.7 %copy-start.5 = (f32[8,8]{1,0:T(8,128)S(1)}, f32[8,8]{1,0:T(8,128)}, u32[]{:S(2)}) copy-start(f32[8,8]{1,0:T(8,128)} %param.16) | copy-start | bytes 772
  13.2 6.4 %collective-permute-start.5 = (f32[176,128]{1,0:T(8,128)S(1)}, f32[176,128]{1,0:T(8,128)S(1)}, u32[]{:S(2)}, u32[]{:S(2)}) collective-permute-start(f32[176,128]{1,0:T(8,128)S(1)} %get-tuple-element.37), channel_id=1, source_target_pairs={{12,0},{8,4},{4,8},{0,12},{13,1},{9,5},{5,9},{1,13},{14,2},{10,6},... | collective-permute-start | bytes 270344 | tf_op jit(solution)/shard_map/ppermute | solution.py:835
  13.8 0.7 %copy-start.7 = (f32[16]{0:T(128)S(1)}, f32[16]{0:T(128)}, u32[]{:S(2)}) copy-start(f32[16]{0:T(128)} %param.14) | copy-start | bytes 196
  13.8 4.6 %collective-permute-start.6 = (f32[168,128]{1,0:T(8,128)S(1)}, f32[168,128]{1,0:T(8,128)S(1)}, u32[]{:S(2)}, u32[]{:S(2)}) collective-permute-start(f32[168,128]{1,0:T(8,128)S(1)} %get-tuple-element.38), channel_id=1, source_target_pairs={{4,0},{0,4},{12,8},{8,12},{5,1},{1,5},{13,9},{9,13},{6,2},{2,6},{1... | collective-permute-start | bytes 258056 | tf_op jit(solution)/shard_map/ppermute | solution.py:836
  20.9 10.1 %all-to-all-start = ((f32[4,104,128]{2,1,0:T(8,128)}), f32[4,104,128]{2,1,0:T(8,128)S(1)}, u32[]{:S(2)}, u32[]{:S(2)}) async-start(f32[4,104,128]{2,1,0:T(8,128)} %shard_map.121), calls=%async_computation | async-start | bytes 425984 | tf_op jit(solution)/shard_map/all_to_all | solution.py:878
  31.0 14.6 %all-to-all-start.1 = ((f32[4,192,128]{2,1,0:T(8,128)}), f32[4,192,128]{2,1,0:T(8,128)S(1)}, u32[]{:S(2)}, u32[]{:S(2)}) async-start(f32[4,192,128]{2,1,0:T(8,128)} %get-tuple-element.53._), calls=%async_computation.1 | async-start | bytes 786432 | tf_op jit(solution)/shard_map/all_to_all | solution.py:878
  35.5 10.0 %collective-permute-start.8 = (f32[96,128]{1,0:T(8,128)S(1)}, f32[96,128]{1,0:T(8,128)S(1)}, u32[]{:S(2)}, u32[]{:S(2)}) collective-permute-start(f32[96,128]{1,0:T(8,128)S(1)} %get-tuple-element.57), channel_id=1, source_target_pairs={{1,0},{0,1},{3,2},{2,3},{5,4},{4,5},{7,6},{6,7},{9,8},{8,9},{11,10... | collective-permute-start | bytes 147464 | tf_op jit(solution)/shard_map/ppermute | solution.py:972
  35.6 14.2 %collective-permute-start.9 = (f32[128,128]{1,0:T(8,128)S(1)}, f32[128,128]{1,0:T(8,128)S(1)}, u32[]{:S(2)}, u32[]{:S(2)}) collective-permute-start(f32[128,128]{1,0:T(8,128)S(1)} %get-tuple-element.55.sent_b), channel_id=1, source_target_pairs={{1,2},{2,1},{3,4},{4,3},{5,6},{6,5},{7,8},{8,7},{9,10},{10,9},{11,... | collective-permute-start | bytes 196616 | tf_op jit(solution)/shard_map/ppermute | solution.py:962
  46.1 9.2 %collective-permute-start.11 = (f32[128,128]{1,0:T(8,128)S(1)}, f32[128,128]{1,0:T(8,128)S(1)}, u32[]{:S(2)}, u32[]{:S(2)}) collective-permute-start(f32[128,128]{1,0:T(8,128)S(1)} %get-tuple-element.63), channel_id=1, source_target_pairs={{1,2},{2,1},{3,4},{4,3},{5,6},{6,5},{7,8},{8,7},{9,10},{10,9},{11,... | collective-permute-start | bytes 196616 | tf_op jit(solution)/shard_map/ppermute | solution.py:989
  50.1 1.3 %collective-permute-start.10 = (f32[96,128]{1,0:T(8,128)S(1)}, f32[96,128]{1,0:T(8,128)S(1)}, u32[]{:S(2)}, u32[]{:S(2)}) collective-permute-start(f32[96,128]{1,0:T(8,128)S(1)} %get-tuple-element.62), channel_id=1, source_target_pairs={{1,0},{0,1},{3,2},{2,3},{5,4},{4,5},{7,6},{6,7},{9,8},{8,9},{11,10... | collective-permute-start | bytes 147464 | tf_op jit(solution)/shard_map/ppermute | solution.py:993
